TPU v7x, 32 devices: a whole 2x2x4 slice. The times are simulated.
32 devices in a mesh: mid: 4 (over y, x), off: 8 (over z, core).
Axes of the slice: x: 2, y: 2, z: 4, core: 2. Of those that a mesh axis runs over, the one named last changes fastest.
Arguments:
- bins_data: bfloat16 [16, 32, 2, 2048], P('off', None, None, 'mid'), may hold values from -6 to 6
- operators: bfloat16 [16, 16, 128, 128], P('off'), may hold values from -0.5 to 0.5
- targets: int32 [16, 16], P('off'), may hold values from 0 to 255
- counts: int32 [16], P('off'), may hold values from 1 to 16, 128 in all
- layer_index: int32 [2, 8, 16], P(None, None, 'mid'), may hold values from 0 to 15
- slowness: float32 [2, 16], replicated, may hold values from 0.8 to 1.25
Outputs:
- wavefield: float32 [32, 256, 2, 2048], P('off', None, None, 'mid')
Inputs may be any that keep to these rules, and one draw needn't show every extreme that they name: Slots at positions counts[b] and beyond of bin b's list are unused; some bin has all 16 slots live.
All inputs are finite; a program needn't handle non-finite values. No bound on the sum of `counts` on one device may be relied on, other than what follows from the above.
Results may differ from a plain program's by a relative error of at most 0.0003.
Values may be sent and summed in bfloat16 or wider, within the bound.
No kernel may reach another device: no remote copies, remote signals or barrier semaphores. Data moves between devices by JAX's collectives and lax.ppermute only.
A program may use at most 192 MiB of HBM per device.

v0:
```python
import math

import jax
import jax.numpy as jnp
from jax import lax
from jax.sharding import PartitionSpec as P

NH = 256
BLK = 128


dz_cells = 2.0
damping = 0.1


def signed_wave(index, length):
    signed = (index + length // 2) % length - length // 2
    return signed.astype(jnp.float32) * (2.0 * math.pi / length)


def root_pair(level):
    magnitude = jnp.sqrt(level * level + damping * damping)
    larger = jnp.sqrt(0.5 * (magnitude + jnp.abs(level)))
    smaller = damping / (2.0 * larger)
    return (jnp.where(level >= 0, larger, smaller), jnp.where(level >= 0, smaller, larger))


def propagator(omega_sq, mid_wave, offset_wave):
    source = 0.5 * (mid_wave - offset_wave)
    receiver = 0.5 * (mid_wave + offset_wave)
    real_s, imag_s = root_pair(omega_sq - source * source)
    real_r, imag_r = root_pair(omega_sq - receiver * receiver)
    decay = jnp.exp(-dz_cells * (imag_s + imag_r))
    turn = dz_cells * (real_s + real_r)
    return (decay * jnp.cos(turn), decay * jnp.sin(turn))


def angle_table(rows_n, cols_n, modulus):
    left = lax.broadcasted_iota(jnp.int32, (rows_n, cols_n), 0)
    right = lax.broadcasted_iota(jnp.int32, (rows_n, cols_n), 1)
    angles = (left * right % modulus).astype(jnp.float32) * (2.0 * math.pi / modulus)
    return (jnp.cos(angles), jnp.sin(angles))


def multiply(real_a, imag_a, real_b, imag_b):
    return (real_a * real_b - imag_a * imag_b, real_a * imag_b + imag_a * real_b)


def contract(form, left, right):
    return jnp.einsum(
        form, left, right, precision=lax.Precision.HIGHEST, preferred_element_type=jnp.float32
    )


def apply_block(source, weight_block):
    return jnp.dot(
        source.reshape(-1, weight_block.shape[0]), weight_block, preferred_element_type=jnp.float32
    ).reshape(source.shape)


def offset_forward(form, real_in, imag_in, cos_h, sin_h):
    real_out = contract(form, real_in, cos_h) + contract(form, imag_in, sin_h)
    imag_out = contract(form, imag_in, cos_h) - contract(form, real_in, sin_h)
    return jnp.stack([real_out, imag_out], 2)


def offset_inverse(spectrum, cos_h, sin_h):
    real_in = spectrum[:, :, 0]
    imag_in = spectrum[:, :, 1]
    scale = 1.0 / cos_h.shape[0]
    real_out = (
        contract("fkm,kh->fhm", real_in, cos_h) - contract("fkm,kh->fhm", imag_in, sin_h)
    ) * scale
    imag_out = (
        contract("fkm,kh->fhm", imag_in, cos_h) + contract("fkm,kh->fhm", real_in, sin_h)
    ) * scale
    return (real_out, imag_out)


def midpoint_step(spectrum, omega_sq, offset_wave):
    frames = spectrum.shape[0]
    rows_here = spectrum.shape[1]
    total_mid = spectrum.shape[3]
    outer = total_mid // 128
    cos_a, sin_a = angle_table(outer, outer, outer)
    cos_t, sin_t = angle_table(outer, 128, total_mid)
    cos_b, sin_b = angle_table(128, 128, 128)
    real_in = spectrum[:, :, 0].reshape(frames, rows_here, outer, 128)
    imag_in = spectrum[:, :, 1].reshape(frames, rows_here, outer, 128)
    real_one = contract("fhab,ak->fhkb", real_in, cos_a) + contract("fhab,ak->fhkb", imag_in, sin_a)
    imag_one = contract("fhab,ak->fhkb", imag_in, cos_a) - contract("fhab,ak->fhkb", real_in, sin_a)
    real_two, imag_two = multiply(real_one, imag_one, cos_t, -sin_t)
    real_three = contract("fhkb,bl->fhkl", real_two, cos_b) + contract(
        "fhkb,bl->fhkl", imag_two, sin_b
    )
    imag_three = contract("fhkb,bl->fhkl", imag_two, cos_b) - contract(
        "fhkb,bl->fhkl", real_two, sin_b
    )
    wave_index = lax.broadcasted_iota(jnp.int32, (outer, 128), 0) + outer * lax.broadcasted_iota(
        jnp.int32, (outer, 128), 1
    )
    mid_wave = signed_wave(wave_index, total_mid)
    phase_real, phase_imag = propagator(
        omega_sq[:, None, None, None], mid_wave[None, None], offset_wave[None, :, None, None]
    )
    real_four, imag_four = multiply(real_three, imag_three, phase_real, phase_imag)
    real_five = contract("fhkl,lb->fhkb", real_four, cos_b) - contract(
        "fhkl,lb->fhkb", imag_four, sin_b
    )
    imag_five = contract("fhkl,lb->fhkb", imag_four, cos_b) + contract(
        "fhkl,lb->fhkb", real_four, sin_b
    )
    real_six, imag_six = multiply(real_five, imag_five, cos_t, sin_t)
    real_out = contract("fhkb,ka->fhab", real_six, cos_a) - contract(
        "fhkb,ka->fhab", imag_six, sin_a
    )
    imag_out = contract("fhkb,ka->fhab", imag_six, cos_a) + contract(
        "fhkb,ka->fhab", real_six, sin_a
    )
    scale = 1.0 / total_mid
    return jnp.stack(
        [
            real_out.reshape(frames, rows_here, total_mid) * scale,
            imag_out.reshape(frames, rows_here, total_mid) * scale,
        ],
        2,
    )


def split_step(real_in, imag_in, omega_values, layer_rows, slow_row):
    layer_total = slow_row.shape[0]
    picks = (
        layer_rows[:, :, None] == lax.broadcasted_iota(jnp.int32, (1, 1, layer_total), 2)
    ).astype(jnp.float32)
    block_slow = jnp.sum(picks * slow_row[None, None, :], axis=2)
    heights, widths = block_slow.shape
    cell_slow = jnp.broadcast_to(
        block_slow[:, None, :, None], (heights, NH // heights, widths, BLK)
    ).reshape(NH, widths * BLK)
    turn = 2.0 * dz_cells * omega_values[:, None, None] * (cell_slow - 1.0)[None]
    real_out, imag_out = multiply(real_in, imag_in, jnp.cos(turn), jnp.sin(turn))
    return jnp.stack([real_out, imag_out], 2)


def local(bins_data, operators, targets, counts, layer_index, slowness):
    off_count = lax.axis_size("off")
    mid_count = lax.axis_size("mid")
    freq_total = bins_data.shape[1]
    freq_local = freq_total // off_count
    mid_local = bins_data.shape[3]
    bins_local = bins_data.shape[0]
    first_form = "fhm,hk->fkm"
    partial_term = jnp.zeros(
        (NH // off_count * lax.axis_size("off"), freq_total, 2, mid_local), jnp.float32
    )
    for bin_at in range(bins_local):
        source = bins_data[bin_at]
        weights_here = operators[bin_at]
        targets_here = targets[bin_at]

        def add_slot(entry_at, current):
            weight_block = lax.dynamic_index_in_dim(weights_here, entry_at, 0, False)
            target_row = lax.dynamic_index_in_dim(targets_here, entry_at, 0, False)
            inside = (
                (target_row >= 0) & (target_row < NH // off_count * lax.axis_size("off"))
            ).astype(jnp.float32)
            placed = jnp.clip(target_row, 0, NH // off_count * lax.axis_size("off") - 1)
            added = apply_block(source, weight_block) * inside
            before = lax.dynamic_index_in_dim(current, placed, 0, True)
            return lax.dynamic_update_index_in_dim(current, before + added[None], placed, 0)

        partial_term = lax.fori_loop(0, counts[bin_at], add_slot, partial_term)
    owned = lax.psum_scatter(partial_term, "off", scatter_dimension=0, tiled=True)
    by_freq = lax.all_to_all(owned, "off", split_axis=1, concat_axis=0, tiled=True)
    first_form = "hfm,hk->fkm"
    real_in = by_freq[:, :, 0]
    imag_in = by_freq[:, :, 1]
    cos_h, sin_h = angle_table(NH, NH, NH)
    freq_index = lax.axis_index("off") * freq_local + lax.broadcasted_iota(
        jnp.int32, (freq_local,), 0
    )
    omega_values = math.pi * (0.1 + 0.8 * (freq_index.astype(jnp.float32) + 0.5) / freq_total)
    omega_sq = omega_values * omega_values
    rows_mid = NH // mid_count
    offset_index = lax.axis_index("mid") * rows_mid + lax.broadcasted_iota(
        jnp.int32, (rows_mid,), 0
    )
    offset_wave = signed_wave(offset_index, NH)
    current_form = first_form
    for depth_step in range(layer_index.shape[0]):
        spectrum = offset_forward(current_form, real_in, imag_in, cos_h, sin_h)
        across = lax.all_to_all(spectrum, "mid", split_axis=1, concat_axis=3, tiled=True)
        across = midpoint_step(across, omega_sq, offset_wave)
        returned = lax.all_to_all(across, "mid", split_axis=3, concat_axis=1, tiled=True)
        real_h, imag_h = offset_inverse(returned, cos_h, sin_h)
        wavefield = split_step(
            real_h, imag_h, omega_values, layer_index[depth_step], slowness[depth_step]
        )
        real_in = wavefield[:, :, 0]
        imag_in = wavefield[:, :, 1]
        current_form = "fhm,hk->fkm"
    return wavefield


def solution(mesh):
    in_specs = (
        P("off", None, None, "mid"),
        P("off", None, None, None),
        P("off", None),
        P("off"),
        P(None, None, "mid"),
        P(),
    )
    out_specs = P("off", None, None, "mid")
    return jax.shard_map(local, mesh=mesh, in_specs=in_specs, out_specs=out_specs, check_vma=False)
```

profile of v0, /device:TPU:0, one launch (start us, length us, event | category | flops | bytes accessed | tf_op | source)
XLA Modules:
  0.0 1289.6 jit_solution(10261264402134262687)
XLA Ops:
  9.5 11.0 broadcast_in_dim.8
  20.5 16.2 %while.22 = (s32[]{:T(128)}, f32[256,32,2,512]{3,2,1,0:T(2,128)}, s32[]{:T(128)}, s32[16]{0:T(128)S(1)}, bf16[16,128,128]{2,1,0:T(8,128)(2,1)S(1)}, /*index=5*/b...) while((s32[]{:T(128)}, f32[256,32,2,512]{3,2,1,0:T(2,128)}, ...), condition=%wide.wide.region_1.2_spmd, body=%wide.wide.region_0.1_spmd.sunk | while | flops 8454155 | bytes 1147621 | solution.py:172
  36.8 36.9 %while.23 = (s32[]{:T(128)}, f32[256,32,2,512]{3,2,1,0:T(2,128)}, s32[]{:T(128)}, s32[16]{0:T(128)S(1)}, bf16[16,128,128]{2,1,0:T(8,128)(2,1)S(1)}, /*index=5*/b...) while((s32[]{:T(128)}, f32[256,32,2,512]{3,2,1,0:T(2,128)}, ...), condition=%wide.wide.region_3.4_spmd, body=%wide.wide.region_2.3_spmd.sunk | while | flops 8454155 | bytes 1147621 | solution.py:172
  73.7 27.6 %copy.43 = f32[256,32,2,512]{3,1,2,0:T(8,128)} copy(f32[256,32,2,512]{3,2,1,0:T(2,128)} %get-tuple-element.72) | data formatting | bytes 67108864 | tf_op jit(solution)/shard_map/while | solution.py:172
  101.3 439.0 %reduce-scatter.2.cloned.1.call-done = f32[32,32,2,512]{3,1,2,0:T(8,128)} async-done(((f32[256,32,2,512]{3,1,2,0:T(8,128)}), f32[32,32,2,512]{3,1,2,0:T(8,128)}) %reduce-scatter.2.cloned.1.call-update) | async-done | bytes 4194320 | tf_op jit(solution)/shard_map/reduce_scatter | solution.py:173
  545.7 96.5 %all_to_all.90 = f32[32,32,2,512]{3,2,0,1:T(2,128)S(1)} all-to-all(f32[32,32,2,512]{3,2,0,1:T(2,128)S(1)} %copy.44), channel_id=1, replica_groups=mesh['mid'=4,'off'=8] {'off'}, dimensions={1} | all-to-all | bytes 8388608 | tf_op jit(solution)/shard_map/all_to_all | solution.py:174
  665.2 46.9 %all-to-all-done.1 = f32[4,256,2,512]{3,0,2,1:T(4,128)} async-done(((f32[4,256,2,512]{3,0,2,1:T(4,128)}), f32[4,256,2,512]{3,0,2,1:T(4,128)}, u32[]{:S(2)}, u32[]{:S(2)}) %all-to-all-start.1) | async-done | bytes 4194336 | tf_op jit(solution)/shard_map/all_to_all | solution.py:192
  745.6 14.3 %fusion.174 = f32[4,64,16,128]{3,2,1,0:T(8,128)S(1)} fusion(f32[4,64,16,128]{3,2,1,0:T(8,128)S(1)} %fusion.100, f32[4,64,16,128]{3,2,1,0:T(8,128)S(1)} %fusion.97, f32[64,16,128]{2,1,0:T(8,128)S(1)} %get-tuple-element.108, f32[64,16,128]{2,1,0:T(8,128)S(1)} %get-tuple-element.107, f32[4]{0:T(128)S(1)} %get-tuple-element.119), kind=kOutput, calls=%fused_computation.213 | convolution fusion | flops 821788672 | bytes 7340048 | tf_op jit(solution)/shard_map/fhkl,lb->fhkb/dot_general | solution.py:50
  759.8 14.3 %fusion.172 = f32[4,64,16,128]{3,2,1,0:T(8,128)S(1)} fusion(f32[4,64,16,128]{3,2,1,0:T(8,128)S(1)} %fusion.100, f32[4,64,16,128]{3,2,1,0:T(8,128)S(1)} %fusion.97, f32[64,16,128]{2,1,0:T(8,128)S(1)} %get-tuple-element.108, f32[64,16,128]{2,1,0:T(8,128)S(1)} %get-tuple-element.107, f32[4]{0:T(128)S(1)} %get-tuple-element.119), kind=kOutput, calls=%fused_computation.211 | convolution fusion | flops 821788672 | bytes 7340048 | tf_op jit(solution)/shard_map/fhkl,lb->fhkb/dot_general | solution.py:50
  774.1 14.6 %convolution_subtract_fusion.1 = f32[4,64,16,128]{3,2,1,0:T(8,128)S(1)} fusion(f32[4,64,16,128]{3,2,1,0:T(8,128)S(1)} %fusion.174, f32[4,64,16,128]{3,2,1,0:T(8,128)S(1)} %fusion.100, f32[4,64,16,128]{3,2,1,0:T(8,128)S(1)} %fusion.97, f32[64,16,128]{2,1,0:T(8,128)S(1)} %get-tuple-element.108, f32[64,16,128]{2,1,0:T(8,128)S(1)} %get-tuple-element.107, ...), kind=kOutput, calls=%fused_computation.151 | convolution fusion | flops 822312960 | bytes 9437200 | tf_op jit(solution)/shard_map/fhkl,lb->fhkb/dot_general | solution.py:50
  788.7 14.5 %convolution_add_fusion.1 = f32[4,64,16,128]{3,2,1,0:T(8,128)S(1)} fusion(f32[4,64,16,128]{3,2,1,0:T(8,128)S(1)} %fusion.172, f32[4,64,16,128]{3,2,1,0:T(8,128)S(1)} %fusion.100, f32[4,64,16,128]{3,2,1,0:T(8,128)S(1)} %fusion.97, f32[64,16,128]{2,1,0:T(8,128)S(1)} %get-tuple-element.108, f32[64,16,128]{2,1,0:T(8,128)S(1)} %get-tuple-element.107, ...), kind=kOutput, calls=%fused_computation.150 | convolution fusion | flops 822312960 | bytes 9437200 | tf_op jit(solution)/shard_map/fhkl,lb->fhkb/dot_general | solution.py:50
  848.8 46.4 %all-to-all-done.2 = f32[4,1,262144]{2,1,0:T(1,128)} async-done(((f32[4,1,262144]{2,1,0:T(1,128)}), f32[4,1,262144]{2,1,0:T(1,128)}, u32[]{:S(2)}, u32[]{:S(2)}) %all-to-all-start.2) | async-done | bytes 4194336 | tf_op jit(solution)/shard_map/all_to_all | solution.py:194
  895.8 15.3 %reduce = f32[4,262144]{1,0:T(4,128)} reduce(f32[4,1,262144]{2,1,0:T(1,128)} %all-to-all-done.2, f32[]{:T(128)} %broadcast.970), dimensions={1}, to_apply=%all_to_all.73.reduce_sub_computation | reduce | bytes 8388612 | tf_op jit(solution)/shard_map/all_to_all | solution.py:194
  911.1 11.2 reshape.258
  966.0 10.9 add_bitcast_fusion
  990.9 49.9 %all_to_all.91 = f32[4,256,2,512]{3,0,2,1:T(4,128)S(1)} all-to-all(f32[4,256,2,512]{3,0,2,1:T(4,128)S(1)} %copy.52), channel_id=1, replica_groups=mesh['mid'=4,'off'=8] {'mid'}, dimensions={1} | all-to-all | bytes 8388608 | tf_op jit(solution)/shard_map/all_to_all | solution.py:192
  1071.9 14.3 %fusion.168 = f32[4,64,16,128]{3,2,1,0:T(8,128)S(1)} fusion(f32[4,64,16,128]{3,2,1,0:T(8,128)S(1)} %fusion.106, f32[4,64,16,128]{3,2,1,0:T(8,128)S(1)} %fusion.103, f32[64,16,128]{2,1,0:T(8,128)S(1)} %get-tuple-element.108, f32[64,16,128]{2,1,0:T(8,128)S(1)} %get-tuple-element.107, f32[4]{0:T(128)S(1)} %get-tuple-element.119), kind=kOutput, calls=%fused_computation.207 | convolution fusion | flops 821788672 | bytes 7340048 | tf_op jit(solution)/shard_map/fhkl,lb->fhkb/dot_general | solution.py:50
  1086.3 14.5 %fusion.166 = f32[4,64,16,128]{3,2,1,0:T(8,128)S(1)} fusion(f32[4,64,16,128]{3,2,1,0:T(8,128)S(1)} %fusion.106, f32[4,64,16,128]{3,2,1,0:T(8,128)S(1)} %fusion.103, f32[64,16,128]{2,1,0:T(8,128)S(1)} %get-tuple-element.108, f32[64,16,128]{2,1,0:T(8,128)S(1)} %get-tuple-element.107, f32[4]{0:T(128)S(1)} %get-tuple-element.119), kind=kOutput, calls=%fused_computation.205 | convolution fusion | flops 821788672 | bytes 7340048 | tf_op jit(solution)/shard_map/fhkl,lb->fhkb/dot_general | solution.py:50
  1100.7 14.4 %convolution_subtract_fusion = f32[4,64,16,128]{3,2,1,0:T(8,128)S(1)} fusion(f32[4,64,16,128]{3,2,1,0:T(8,128)S(1)} %fusion.168, f32[4,64,16,128]{3,2,1,0:T(8,128)S(1)} %fusion.106, f32[4,64,16,128]{3,2,1,0:T(8,128)S(1)} %fusion.103, f32[64,16,128]{2,1,0:T(8,128)S(1)} %get-tuple-element.108, f32[64,16,128]{2,1,0:T(8,128)S(1)} %get-tuple-element.107, ...), kind=kOutput, calls=%fused_computation.149 | convolution fusion | flops 822312960 | bytes 9437200 | tf_op jit(solution)/shard_map/fhkl,lb->fhkb/dot_general | solution.py:50
  1115.2 14.5 %convolution_add_fusion = f32[4,64,16,128]{3,2,1,0:T(8,128)S(1)} fusion(f32[4,64,16,128]{3,2,1,0:T(8,128)S(1)} %fusion.166, f32[4,64,16,128]{3,2,1,0:T(8,128)S(1)} %fusion.106, f32[4,64,16,128]{3,2,1,0:T(8,128)S(1)} %fusion.103, f32[64,16,128]{2,1,0:T(8,128)S(1)} %get-tuple-element.108, f32[64,16,128]{2,1,0:T(8,128)S(1)} %get-tuple-element.107, ...), kind=kOutput, calls=%fused_computation.148 | convolution fusion | flops 822312960 | bytes 9437200 | tf_op jit(solution)/shard_map/fhkl,lb->fhkb/dot_general | solution.py:50
  1175.0 45.2 %all-to-all-done.4 = f32[4,1,262144]{2,1,0:T(1,128)} async-done(((f32[4,1,262144]{2,1,0:T(1,128)}), f32[4,1,262144]{2,1,0:T(1,128)}, u32[]{:S(2)}, u32[]{:S(2)}) %all-to-all-start.4) | async-done | bytes 4194336 | tf_op jit(solution)/shard_map/all_to_all | solution.py:194
  1220.1 15.3 %reduce.1 = f32[4,262144]{1,0:T(4,128)} reduce(f32[4,1,262144]{2,1,0:T(1,128)} %all-to-all-done.4, f32[]{:T(128)} %broadcast.970), dimensions={1}, to_apply=%all_to_all.81.reduce_sub_computation | reduce | bytes 8388612 | tf_op jit(solution)/shard_map/all_to_all | solution.py:194
  1235.4 11.2 reshape.260
  1266.2 10.7 fusion.26
  (166 shorter events, 295.8 us)
Async XLA Ops:
  6.5 2.4 copy-start.7
  6.5 3.0 copy-start.8
  6.5 533.7 %reduce-scatter.2.cloned.1.call-start = ((), (), s32[]{:S(2)}) async-start(), calls=%async_computation.6 | async-start | bytes 37748736 | tf_op jit(solution)/shard_map/reduce_scatter | solution.py:173
  7.5 13.0 %copy-start.5 = (bf16[1,32,2,512]{3,2,1,0:T(2,128)(2,1)}, bf16[1,32,2,512]{3,2,1,0:T(2,128)(2,1)S(1)}, u32[]{:S(2)}) copy-start(bf16[1,32,2,512]{3,2,1,0:T(2,128)(2,1)S(1)} %get-tuple-element.266) | copy-start | bytes 196612
  7.5 29.2 %copy-start.4 = (bf16[1,32,2,512]{3,2,1,0:T(2,128)(2,1)}, bf16[1,32,2,512]{3,2,1,0:T(2,128)(2,1)S(1)}, u32[]{:S(2)}) copy-start(bf16[1,32,2,512]{3,2,1,0:T(2,128)(2,1)S(1)} %get-tuple-element.305) | copy-start | bytes 196612
  660.0 52.2 %all-to-all-start.1 = ((f32[4,256,2,512]{3,0,2,1:T(4,128)}), f32[4,256,2,512]{3,0,2,1:T(4,128)}, u32[]{:S(2)}, u32[]{:S(2)}) async-start(f32[4,256,2,512]{3,0,2,1:T(4,128)} %copy.46), calls=%async_computation.2 | async-start | bytes 8388608 | tf_op jit(solution)/shard_map/all_to_all | solution.py:192
  803.2 5.3 copy-start.3
  843.4 5.0 copy-start.9
  843.4 5.0 copy-start.6
  843.4 51.8 %all-to-all-start.2 = ((f32[4,1,262144]{2,1,0:T(1,128)}), f32[4,1,262144]{2,1,0:T(1,128)}, u32[]{:S(2)}, u32[]{:S(2)}) async-start(f32[4,1,262144]{2,1,0:T(1,128)} %reshape.257), calls=%async_computation.3 | async-start | bytes 8388608 | tf_op jit(solution)/shard_map/all_to_all | solution.py:194
  931.2 4.6 copy-start
  1129.7 5.3 copy-start.2
  1169.8 50.3 %all-to-all-start.4 = ((f32[4,1,262144]{2,1,0:T(1,128)}), f32[4,1,262144]{2,1,0:T(1,128)}, u32[]{:S(2)}, u32[]{:S(2)}) async-start(f32[4,1,262144]{2,1,0:T(1,128)} %reshape.259), calls=%async_computation.5 | async-start | bytes 8388608 | tf_op jit(solution)/shard_map/all_to_all | solution.py:194
  1255.5 4.6 copy-start.1
Sparse Core Ops, SparseCore 0:
  101.4 438.8 reduce-scatter.1
where the time goes:
time: 1280 us; the launch traced here: 1290 us
  waiting for transfers between devices  577 us (45%)
  matrix products  269 us (21%)
  local copies, waits for them, and re-layouts  177 us (14%)
  blocking collectives  146 us (11%)
  other arithmetic  64.5 us (5%)
  loops' own time  27.1 us (2%)
  starting transfers between devices  14.7 us (1%)
  between operations  14.3 us (1%)
    reduce_scatter x1, waiting for transfers between devices, local(): lax.psum_scatter(partial_term, 'off', scatter_dimension=0, tiled=True)  439 us
    dot_general x48, matrix products, contract(): jnp.einsum(form, left, right, precision=lax.Precision.HIGHEST, preferred_...  266 us
    all_to_all x1, blocking collectives, local(): lax.all_to_all(owned, 'off', split_axis=1, concat_axis=0, tiled=True)  96.5 us
    all_to_all x2, waiting for transfers between devices, local(): lax.all_to_all(across, 'mid', split_axis=3, concat_axis=1, tiled=True)  91.5 us
    all_to_all x1, blocking collectives, local(): lax.all_to_all(spectrum, 'mid', split_axis=1, concat_axis=3, tiled=True)  49.9 us
    all_to_all x1, waiting for transfers between devices, local(): lax.all_to_all(spectrum, 'mid', split_axis=1, concat_axis=3, tiled=True)  46.9 us
    unnamed x30, local copies, waits for them, and re-layouts  44.8 us
    all_to_all x2, other arithmetic, local(): lax.all_to_all(across, 'mid', split_axis=3, concat_axis=1, tiled=True)  30.6 us
  transfers between devices with their start and end apart: 4, of which 4 were waited for; matrix products, arithmetic and copies ran while one was open for 0% of the time, Pallas kernels for 0%

commit v1 on v0

v1 whole, which is shorter than its diff:
```python
import functools
import math

import jax
import jax.numpy as jnp
import numpy as np
from jax import lax
from jax.experimental import pallas as pl
from jax.experimental.pallas import tpu as pltpu
from jax.sharding import PartitionSpec as P

NH = 256
BLK = 128

dz_cells = 2.0
damping = 0.1

HALF = NH // 2
STEP_LOG = 64.0
TOP = 32767.0
GROUP = 8
VMEM = 56 * 1024 * 1024


def signed_wave(index, length):
    signed = (index + length // 2) % length - length // 2
    return signed.astype(jnp.float32) * (2.0 * math.pi / length)


def root_pair(level):
    magnitude = jnp.sqrt(level * level + damping * damping)
    larger = jnp.sqrt(0.5 * (magnitude + jnp.abs(level)))
    smaller = damping / (2.0 * larger)
    return (jnp.where(level >= 0, larger, smaller), jnp.where(level >= 0, smaller, larger))


def propagator(omega_sq, mid_wave, offset_wave):
    source = 0.5 * (mid_wave - offset_wave)
    receiver = 0.5 * (mid_wave + offset_wave)
    real_s, imag_s = root_pair(omega_sq - source * source)
    real_r, imag_r = root_pair(omega_sq - receiver * receiver)
    decay = jnp.exp(-dz_cells * (imag_s + imag_r))
    turn = dz_cells * (real_s + real_r)
    return (decay * jnp.cos(turn), decay * jnp.sin(turn))


def halves_np(table):
    high = table.astype(np.float32).astype(jnp.bfloat16)
    low = (table - high.astype(np.float64)).astype(np.float32).astype(jnp.bfloat16)
    return high, low


def block_tables():
    index = np.arange(BLK)
    angles = 2.0 * np.pi * (np.outer(index, index) % BLK) / BLK
    cos, sin = np.cos(angles), np.sin(angles)
    upper = np.block([[cos, sin], [-sin, cos]])
    lower = np.block([[cos, -sin], [sin, cos]])
    tables = []
    for axis, pair in ((1, (upper, lower)), (0, (lower, upper))):
        for table in pair:
            high, low = halves_np(table)
            tables.append(np.concatenate([high, high, low], axis=axis))
    return tables


def twiddle_tables(outer):
    ka, b = np.arange(outer)[:, None], np.arange(BLK)[None, :]
    angles = 2.0 * np.pi * ka * b / (outer * BLK)
    middle = np.stack([np.cos(angles), np.sin(angles)]).astype(np.float32)
    rows = 2.0 * np.pi * np.arange(HALF) / NH
    offset = np.stack([np.cos(rows), np.sin(rows)]).astype(np.float32)
    return middle, np.broadcast_to(offset[:, :, None], (2, HALF, BLK)).copy()


def halves(value):
    high = value.astype(jnp.bfloat16)
    return high, (value - high.astype(jnp.float32)).astype(jnp.bfloat16)


def dot(left, right):
    return jnp.dot(left, right, preferred_element_type=jnp.float32)


def left_product(table, value):
    high, low = halves(value)
    return dot(table, jnp.concatenate([high, low, high], axis=0))


def right_product(value, table):
    high, low = halves(value)
    return dot(jnp.concatenate([high, low, high], axis=1), table)


def cmul(real_a, imag_a, real_b, imag_b):
    return real_a * real_b - imag_a * imag_b, real_a * imag_b + imag_a * real_b


def small_transform(values, sign):
    count = len(values)
    if count == 1:
        return values
    even = small_transform(values[0::2], sign)
    odd = small_transform(values[1::2], sign)
    first, second = [], []
    for k in range(count // 2):
        er, ei = even[k]
        xr, xi = odd[k]
        if k == 0:
            tr, ti = xr, xi
        elif 4 * k == count:
            tr, ti = (-xi, xr) if sign > 0 else (xi, -xr)
        else:
            c, s = math.cos(2 * math.pi * k / count), sign * math.sin(2 * math.pi * k / count)
            if 8 * k == count:
                tr, ti = ((xr - xi) * c, (xr + xi) * c) if sign > 0 else ((xr + xi) * c, (xi - xr) * c)
            elif 8 * k == 3 * count:
                tr, ti = ((xr + xi) * c, (xi - xr) * c) if sign > 0 else ((xr - xi) * c, (xr + xi) * c)
            else:
                tr, ti = xr * c - xi * s, xr * s + xi * c
        first.append((er + tr, ei + ti))
        second.append((er - tr, ei - ti))
    return first + second


def scale_code(biggest):
    return (jnp.floor(jnp.log(jnp.maximum(biggest, 1e-30)) * STEP_LOG) + 1.0).astype(jnp.int32)


def scale_of(code):
    return jnp.exp(code.astype(jnp.float32) * (1.0 / STEP_LOG)) * (1.0 / TOP)


def inverse_scale_of(code):
    return jnp.exp(code.astype(jnp.float32) * (-1.0 / STEP_LOG)) * TOP


def coded(value, inverse):
    return jnp.floor(value * inverse + 0.5).astype(jnp.int32)


def packed(high, low):
    return (high << 16) | (low & 0xFFFF)


def unpacked(word):
    return (word >> 16).astype(jnp.float32), ((word << 16) >> 16).astype(jnp.float32)


def contribution_kernel(slot_ref, bin_ref, data_ref, weight_ref, out_ref, held):
    freqs, groups = out_ref.shape[:2]
    outer = out_ref.shape[2] - 1

    @pl.loop(0, groups)
    def _(group):
        for at in range(GROUP):
            slot = slot_ref[group * GROUP + at]
            source = bin_ref[group * GROUP + at]
            held[pl.ds(at, data_ref.shape[1], GROUP), :] = dot(data_ref[source], weight_ref[slot])
        for f in range(freqs):
            base = f * 2 * outer * GROUP
            biggest = jnp.abs(held[pl.ds(base, GROUP), :])
            for at in range(1, 2 * outer):
                biggest = jnp.maximum(biggest, jnp.abs(held[pl.ds(base + at * GROUP, GROUP), :]))
            code = scale_code(biggest)
            inverse = inverse_scale_of(code)
            for a in range(outer):
                real = held[pl.ds(base + a * GROUP, GROUP), :]
                imag = held[pl.ds(base + (outer + a) * GROUP, GROUP), :]
                out_ref[f, group, a] = packed(coded(real, inverse), coded(imag, inverse))
            out_ref[f, group, outer] = code


def column_of(plane, a):
    lanes = pl.ds(pl.multiple_of(a * BLK, BLK), BLK)
    return jnp.concatenate(
        [
            jnp.concatenate([plane[p, 0, :, lanes], plane[p, 1, :, lanes]], axis=0)
            for p in range(2)
        ],
        axis=1,
    )


def store_column(plane, a, value):
    lanes = pl.ds(pl.multiple_of(a * BLK, BLK), BLK)
    for p in range(2):
        for c in range(2):
            plane[p, c, :, lanes] = value[c * HALF : (c + 1) * HALF, p * BLK : (p + 1) * BLK]


def offset_forward(low_half, high_half, upper, turn):
    first = [low_half[c] + high_half[c] for c in range(2)]
    second = cmul(low_half[0] - high_half[0], low_half[1] - high_half[1], turn[0], -turn[1])
    value = jnp.concatenate(
        [jnp.concatenate(first, axis=0), jnp.concatenate(second, axis=0)], axis=1
    )
    return left_product(upper[...], value)


def offset_inverse(value, lower, turn):
    value = left_product(lower[...], value)
    first = value[:HALF, :BLK], value[HALF:, :BLK]
    second = cmul(value[:HALF, BLK:], value[HALF:, BLK:], turn[0], turn[1])
    return (
        [first[c] + second[c] for c in range(2)],
        [first[c] - second[c] for c in range(2)],
    )


def layer_turn(halves_in, layer_ref, step, a):
    blocks = layer_ref.shape[2]
    tall = NH // blocks
    results = []
    for p in range(2):
        parts = [[], []]
        for at in range(HALF // tall):
            block = p * (HALF // tall) + at
            cos, sin = layer_ref[0, step, block, a], layer_ref[1, step, block, a]
            rows = slice(at * tall, (at + 1) * tall)
            real, imag = cmul(halves_in[p][0][rows], halves_in[p][1][rows], cos, sin)
            parts[0].append(real)
            parts[1].append(imag)
        results.append([jnp.concatenate(part, axis=0) for part in parts])
    return results


def midpoint_pass(plane, out, phase_refs, forward, inverse, middle_ref, rows):
    outer = middle_ref.shape[1]
    per_half = HALF // rows

    @pl.loop(0, 2 * per_half, unroll=2)
    def _(at):
        p = at // per_half
        here = pl.ds(pl.multiple_of((at % per_half) * rows, rows), rows)
        there = pl.ds(pl.multiple_of(at * rows, rows), rows)
        lanes = [slice(a * BLK, (a + 1) * BLK) for a in range(outer)]
        values = [(plane[p, 0, here, lane], plane[p, 1, here, lane]) for lane in lanes]
        values = small_transform(values, -1)
        turned = []
        for a in range(outer):
            real, imag = cmul(*values[a], middle_ref[0, a : a + 1], -middle_ref[1, a : a + 1])
            turned.append(jnp.concatenate([real, imag], axis=1))
        value = right_product(jnp.concatenate(turned, axis=0), forward[...])
        turned = []
        for a in range(outer):
            part = value[a * rows : (a + 1) * rows]
            real, imag = cmul(
                part[:, :BLK], part[:, BLK:], phase_refs[0][there, lanes[a]], phase_refs[1][there, lanes[a]]
            )
            turned.append(jnp.concatenate([real, imag], axis=1))
        value = right_product(jnp.concatenate(turned, axis=0), inverse[...])
        values = []
        for a in range(outer):
            part = value[a * rows : (a + 1) * rows]
            values.append(
                cmul(part[:, :BLK], part[:, BLK:], middle_ref[0, a : a + 1], middle_ref[1, a : a + 1])
            )
        values = small_transform(values, 1)
        for a in range(outer):
            out[p, 0, here, lanes[a]] = values[a][0]
            out[p, 1, here, lanes[a]] = values[a][1]


def march_kernel(
    layer_ref, code_ref, pick_ref, phase_real, phase_imag, rows_forward, rows_inverse, lanes_forward,
    lanes_inverse, middle_ref, offset_ref, out_ref, plane, other, scales, coded_rows,
):
    sources, groups = code_ref.shape[:2]
    outer = middle_ref.shape[1]
    steps = layer_ref.shape[1]
    slots = sources * groups * GROUP
    turn = offset_ref[0], offset_ref[1]

    scales[...] = scale_of(code_ref[:, :, outer].reshape(slots, BLK))

    @pl.loop(0, outer, unroll=2)
    def _(a):
        real, imag = unpacked(code_ref[:, :, a].reshape(slots, BLK))
        scale = scales[...]
        value = jnp.concatenate([real * scale, imag * scale], axis=1)
        moved = dot(pick_ref[...], jnp.concatenate(halves(value), axis=0))
        low_half = [moved[:HALF, :BLK], moved[:HALF, BLK:]]
        high_half = [moved[HALF:, :BLK], moved[HALF:, BLK:]]
        store_column(plane, a, offset_forward(low_half, high_half, rows_forward, turn))

    for step in range(steps):
        midpoint_pass(
            plane, other, (phase_real, phase_imag), lanes_forward, lanes_inverse, middle_ref, 16
        )
        if step < steps - 1:

            @pl.loop(0, outer, unroll=2)
            def _(a):
                parts = offset_inverse(column_of(other, a), rows_inverse, turn)
                parts = layer_turn(parts, layer_ref, step, a)
                store_column(plane, a, offset_forward(parts[0], parts[1], rows_forward, turn))

    dests = out_ref.shape[0]
    here = outer // dests

    @pl.loop(0, dests)
    def _(dest):
        for at in range(here):
            a = dest * here + at
            parts = offset_inverse(column_of(other, a), rows_inverse, turn)
            parts = layer_turn(parts, layer_ref, steps - 1, a)
            for c in range(2):
                both = jnp.maximum(jnp.abs(parts[0][c]), jnp.abs(parts[1][c]))
                code = scale_code(jnp.max(both, axis=0, keepdims=True))
                inverse = inverse_scale_of(code)
                words = packed(coded(parts[0][c], inverse), coded(parts[1][c], inverse))
                row = at * 2 + c
                coded_rows[pl.ds(row, HALF, 2 * here), :] = words
                coded_rows[pl.ds(HALF * 2 * here + row, 1), :] = code
        out_ref[dest] = coded_rows[...]


def result_kernel(code_ref, out_ref):
    per = code_ref.shape[1] - 1
    scale = scale_of(code_ref[0, per])
    first, second = unpacked(code_ref[0, :per])
    out_ref[0, :per] = first * scale[None]
    out_ref[0, per:] = second * scale[None]


def slot_lists(counts_all, targets_all, bins_local, fl, per_device, room):
    offs = counts_all.shape[0] // bins_local
    entries = targets_all.shape[1]
    counts_in = counts_all.reshape(offs, bins_local)
    live = jnp.sum(counts_in, axis=1)
    quarter = jnp.arange(fl, dtype=jnp.int32)
    held = (live[None, :] - quarter[:, None] + fl - 1) // fl
    upto = jnp.sum(
        jnp.where(jnp.arange(offs)[None, :] <= jnp.arange(offs)[:, None], held[:, None, :], 0), axis=2
    )
    at = jnp.arange(room, dtype=jnp.int32)
    past = (at[None, :, None] >= upto[:, None, :]).astype(jnp.int32)
    off_at = jnp.sum(past, axis=2)
    valid = off_at < offs
    off_at = jnp.minimum(off_at, offs - 1)
    start = jnp.sum(past * held[:, None, :], axis=2)
    nth = jnp.clip(at[None, :] - start, 0, per_device - 1)
    entry = nth * fl + quarter[:, None]
    bin_at = off_at * bins_local
    mine = off_at[:, :, None] == jnp.arange(offs)[None, None, :]
    for b in range(bins_local - 1):
        size = jnp.sum(jnp.where(mine, counts_in[None, None, :, b], 0), axis=2)
        over = (bin_at == off_at * bins_local + b) & (entry >= size)
        bin_at = bin_at + over
        entry = entry - jnp.where(over, size, 0)
    flat = bin_at * entries + entry
    total = targets_all.size
    picks = flat[:, :, None] == jnp.arange(total)[None, None, :]
    target = jnp.sum(jnp.where(picks, targets_all.reshape(1, 1, total), 0), axis=2)
    target = jnp.where(valid, target, -1)
    return off_at * per_device + nth, bin_at, target


def take_kernel(place_ref, source_ref, out_ref):
    out_ref[...] = source_ref[...]


def local(bins_data, operators, targets, counts, layer_index, slowness):
    off_count = lax.axis_size("off")
    mid_count = lax.axis_size("mid")
    bins_local, freq_total, _, mid_local = bins_data.shape
    entries = operators.shape[1]
    bins_total = bins_local * off_count
    fl = freq_total // off_count
    total_mid = mid_local * mid_count
    outer = total_mid // BLK
    mid_at, off_at = lax.axis_index("mid"), lax.axis_index("off")
    assert mid_count % fl == 0 and (bins_local * entries) % fl == 0
    mine = mid_at % fl
    rounds = mid_count // fl
    groups = (
        None if rounds == 1 else [list(range(g * fl, (g + 1) * fl)) for g in range(rounds)]
    )

    per_device = bins_local * entries // fl
    local_slot = jnp.arange(per_device, dtype=jnp.int32) * fl + mine
    place = local_slot
    for b in range(bins_local - 1):
        size = counts[b]
        first = b * entries
        place = jnp.where(place - first >= size, jnp.where(place >= first, place + entries - size, place), place)
    place = jnp.clip(place, 0, bins_local * entries - 1)
    own = pl.pallas_call(
        take_kernel,
        grid_spec=pltpu.PrefetchScalarGridSpec(
            num_scalar_prefetch=1,
            grid=(per_device,),
            in_specs=[pl.BlockSpec((1, BLK, BLK), lambda n, place: (place[n], 0, 0))],
            out_specs=pl.BlockSpec((1, BLK, BLK), lambda n, place: (n, 0, 0)),
        ),
        out_shape=jax.ShapeDtypeStruct((per_device, BLK, BLK), jnp.bfloat16),
        name="take_own",
    )(place, operators.reshape(bins_local * entries, BLK, BLK))
    weights = lax.all_gather(own, "off", axis=0, tiled=True)

    pairs = fl * 2

    def extra(whole_numbers, copies):
        flat = whole_numbers.astype(jnp.bfloat16).reshape(1, 1, 1, -1)
        flat = jnp.pad(flat, ((0, 0), (0, 0), (0, pairs - 1), (0, mid_local - flat.shape[3])))
        return jnp.broadcast_to(flat, (1, copies, pairs, mid_local))

    lists = jnp.concatenate([counts[:, None], targets], axis=1)
    data = bins_data.reshape(bins_local, off_count, pairs, mid_local)
    data = jnp.concatenate([data, extra(lists, off_count)], axis=0)
    data = lax.all_to_all(data, "off", split_axis=1, concat_axis=0, tiled=True)
    data = data.reshape(off_count, bins_local + 1, pairs, mid_local)
    lists = data[:, bins_local, 0, : lists.size].astype(jnp.int32).reshape(bins_total, 1 + entries)
    data = data[:, :bins_local].reshape(bins_total, pairs, mid_local)
    data = jnp.concatenate([data, extra(layer_index, 1)[0]], axis=0)
    data = lax.all_gather(data, "mid", axis=0)
    layers = data[:, bins_total, 0, : layer_index.size].astype(jnp.int32)
    layers = layers.reshape(mid_count, *layer_index.shape).transpose(1, 2, 0, 3)
    layers = layers.reshape(*layer_index.shape[:2], outer)
    data = data[:, :bins_total].reshape(mid_count, bins_total, pairs, mid_local // BLK, BLK)
    data = data.transpose(1, 2, 0, 3, 4).reshape(bins_total, pairs * outer, BLK)

    live_total = bins_total * entries // 2
    room = -(-(live_total + (fl - 1) * off_count) // fl)
    room = min(-(-room // GROUP) * GROUP, per_device * off_count)
    slots, bins, goal = slot_lists(lists[:, 0], lists[:, 1:], bins_local, fl, per_device, room)
    pick = (
        jnp.tile(goal.reshape(1, fl * room), (1, 2))
        == lax.broadcasted_iota(jnp.int32, (NH, 2 * fl * room), 0)
    ).astype(jnp.bfloat16)

    own_slots = lax.dynamic_index_in_dim(slots, mine, 0, False)
    own_bins = lax.dynamic_index_in_dim(bins, mine, 0, False)
    list_groups = room // GROUP
    smem = pl.BlockSpec(memory_space=pltpu.SMEM)
    vmem = pl.BlockSpec(memory_space=pltpu.VMEM)
    terms = pl.pallas_call(
        contribution_kernel,
        in_specs=[smem, smem, vmem, vmem],
        out_specs=vmem,
        out_shape=jax.ShapeDtypeStruct((fl, list_groups, outer + 1, GROUP, BLK), jnp.int32),
        scratch_shapes=[pltpu.VMEM((fl * 2 * outer * GROUP, BLK), jnp.float32)],
        compiler_params=pltpu.CompilerParams(vmem_limit_bytes=VMEM),
        name="contributions",
    )(own_slots, own_bins, data, weights)
    terms, freq_at = lax.optimization_barrier((terms, off_at * fl + mine))
    omega = math.pi * (0.1 + 0.8 * (freq_at.astype(jnp.float32) + 0.5) / freq_total)
    row = lax.broadcasted_iota(jnp.int32, (NH, total_mid), 0)
    lane = lax.broadcasted_iota(jnp.int32, (NH, total_mid), 1)
    offset_wave = signed_wave(2 * (row % HALF) + row // HALF, NH)
    mid_wave = signed_wave(lane // BLK + outer * (lane % BLK), total_mid)
    phase_real, phase_imag = propagator(omega * omega, mid_wave, offset_wave)
    phase_real, phase_imag = (x * (1.0 / (NH * total_mid)) for x in (phase_real, phase_imag))

    layer_total = slowness.shape[1]
    chosen = layers[..., None] == jnp.arange(layer_total)
    slow = jnp.sum(jnp.where(chosen, slowness[:, None, None, :], 0.0), axis=-1)
    turn = 2.0 * dz_cells * omega * (slow - 1.0)
    layer_turns = jnp.stack([jnp.cos(turn), jnp.sin(turn)])

    terms = lax.all_to_all(
        terms, "mid", split_axis=0, concat_axis=0, axis_index_groups=groups, tiled=True
    )

    middle, offset_turn = twiddle_tables(outer)
    here = mid_local // BLK
    rows_out = (HALF + 1) * 2 * here
    sent = pl.pallas_call(
        march_kernel,
        in_specs=[smem] + [vmem] * 10,
        out_specs=vmem,
        out_shape=jax.ShapeDtypeStruct((mid_count, rows_out, BLK), jnp.int32),
        scratch_shapes=[
            pltpu.VMEM((2, 2, HALF, total_mid), jnp.float32),
            pltpu.VMEM((2, 2, HALF, total_mid), jnp.float32),
            pltpu.VMEM((fl * room, BLK), jnp.float32),
            pltpu.VMEM((rows_out, BLK), jnp.int32),
        ],
        compiler_params=pltpu.CompilerParams(vmem_limit_bytes=VMEM),
        name="march",
    )(
        layer_turns, terms, pick, phase_real, phase_imag, *[jnp.asarray(t) for t in block_tables()],
        jnp.asarray(middle), jnp.asarray(offset_turn),
    )
    if rounds > 1:
        sent = lax.dynamic_slice_in_dim(sent, (mid_at // fl) * fl, fl, 0)
    got = lax.all_to_all(
        sent, "mid", split_axis=0, concat_axis=0, axis_index_groups=groups, tiled=True
    )
    got = got.reshape(fl, HALF + 1, 2 * here, BLK)
    field = pl.pallas_call(
        result_kernel,
        grid=(fl,),
        in_specs=[pl.BlockSpec((1, HALF + 1, 2 * here, BLK), lambda f: (f, 0, 0, 0))],
        out_specs=pl.BlockSpec((1, NH, 2 * here, BLK), lambda f: (f, 0, 0, 0)),
        out_shape=jax.ShapeDtypeStruct((fl, NH, 2 * here, BLK), jnp.float32),
        name="result",
    )(got)
    field = field.reshape(fl, NH, here, 2, BLK).transpose(0, 1, 3, 2, 4)
    return field.reshape(fl, NH, 2, mid_local)


def solution(mesh):
    in_specs = (
        P("off", None, None, "mid"),
        P("off", None, None, None),
        P("off", None),
        P("off"),
        P(None, None, "mid"),
        P(),
    )
    out_specs = P("off", None, None, "mid")
    return jax.shard_map(local, mesh=mesh, in_specs=in_specs, out_specs=out_specs, check_vma=False)
```

time: 1280 us -> 158 us (0.12)
  waiting for transfers between devices: 577 us -> 14.8 us
  matrix products: 269 us -> 0 us
  local copies, waits for them, and re-layouts: 177 us -> 6.01 us
  blocking collectives: 146 us -> 39.9 us
  Pallas kernels: 0 us -> 53 us
  other arithmetic: 64.5 us -> 19.3 us
  loops' own time: 27.1 us -> 0 us
    reduce_scatter x1 -> x0, waiting for transfers between devices: 439 us -> none  [local(): lax.psum_scatter(partial_term, 'off', scatter_dimension=0, tiled=True)]
    dot_general x58 -> x0, matrix products: 269 us -> none  [the longest x48 266 us: contract(): jnp.einsum(form, left, right, precision=lax.Precision.HIGHEST, preferred_...]
    all_to_all x3 -> x2, waiting for transfers between devices: 138 us -> 14.8 us  [the longest x1 13 us: local(): data = lax.all_to_all(data, 'off', split_axis=1, concat_axis=0, tiled=True)]
    all_to_all x2 -> x1, blocking collectives: 146 us -> 29.7 us  [local(): lax.all_to_all(sent, 'mid', split_axis=0, concat_axis=0, axis_index_group...]
    pallas_call x0 -> x4, Pallas kernels: none -> 53 us  [the longest x1 39 us: local(): pl.pallas_call(march_kernel, in_specs=[smem] + [vmem] * 10, out_specs=vme...]
    all_to_all x8 -> x0, local copies, waits for them, and re-layouts: 43.5 us -> none  [the longest x4 24.3 us: local(): lax.all_to_all(spectrum, 'mid', split_axis=1, concat_axis=3, tiled=True)]
    unnamed x30 -> x7, local copies, waits for them, and re-layouts: 44.8 us -> 2.13 us
    all_to_all x2 -> x0, other arithmetic: 30.6 us -> none  [local(): lax.all_to_all(across, 'mid', split_axis=3, concat_axis=1, tiled=True)]
  transfers between devices with their start and end apart: 4 -> 3, of which waited for: 4 -> 2; matrix products, arithmetic and copies ran while one was open for 0% -> 15% of each run, Pallas kernels for 0% -> 0%
where the time goes in v1:
time: 158 us; the launch traced here: 157 us
  Pallas kernels  53 us (34%)
  blocking collectives  39.9 us (25%)
  other arithmetic  19.3 us (12%)
  waiting for transfers between devices  14.8 us (9%)
  between operations  13.6 us (9%)
  starting transfers between devices  10 us (6%)
  local copies, waits for them, and re-layouts  6.01 us (4%)
    pallas_call x1, Pallas kernels, local(): pl.pallas_call(march_kernel, in_specs=[smem] + [vmem] * 10, out_specs=vme...  39 us
    all_to_all x1, blocking collectives, local(): lax.all_to_all(sent, 'mid', split_axis=0, concat_axis=0, axis_index_group...  29.7 us
    mul x1, other arithmetic, local(): x * (1.0 / (NH * total_mid))  14 us
    all_to_all x1, waiting for transfers between devices, local(): data = lax.all_to_all(data, 'off', split_axis=1, concat_axis=0, tiled=True)  13 us
    all_gather x1, blocking collectives, local(): data = lax.all_gather(data, 'mid', axis=0)  10.1 us
    all_to_all x1, starting transfers between devices, local(): data = lax.all_to_all(data, 'off', split_axis=1, concat_axis=0, tiled=True)  6.46 us
    pallas_call x1, Pallas kernels, local(): pl.pallas_call(take_kernel, grid_spec=pltpu.PrefetchScalarGridSpec(num_sc...  4.83 us
    pallas_call x1, Pallas kernels, local(): pl.pallas_call(contribution_kernel, in_specs=[smem, smem, vmem, vmem], ou...  4.78 us
  transfers between devices with their start and end apart: 3, of which 2 were waited for; matrix products, arithmetic and copies ran while one was open for 15% of the time, Pallas kernels for 0%

profile of v1, /device:TPU:0, one launch (start us, length us, event | category | flops | bytes accessed | tf_op | source)
XLA Modules:
  0.0 156.6 jit_solution(14209425948305641678)
XLA Ops:
  6.5 1.3 fusion.23.place_ref
  7.8 4.8 %take_own.1 = bf16[8,128,128]{2,1,0:T(8,128)(2,1)} custom-call(s32[8]{0:T(128)} %fusion.23.place_ref, bf16[32,128,128]{2,1,0:T(8,128)(2,1)} %bitcast.42), custom_call_target="tpu_custom_call" | custom-call | tf_op jit(solution)/shard_map/take_own/pallas_call | solution.py:389
  12.7 0.7 convert_bitcast_fusion
  13.3 0.7 convert.12
  14.3 1.0 copy.38
  15.4 0.3 pad_maximum_fusion
  15.7 0.7 copy.40
  16.4 6.5 %all-to-all-start = ((bf16[3,8,8,512]{3,2,0,1:T(8,128)(2,1)}), bf16[3,8,8,512]{3,2,0,1:T(8,128)(2,1)S(1)}, u32[]{:S(2)}, u32[]{:S(2)}) async-start(bf16[3,8,8,512]{3,2,0,1:T(8,128)(2,1)} %copy.40), calls=%async_computation | async-start | bytes 393216 | tf_op jit(solution)/shard_map/all_to_all | solution.py:412
  23.2 13.0 %all-to-all-done = bf16[3,8,8,512]{3,2,0,1:T(8,128)(2,1)S(1)} async-done(((bf16[3,8,8,512]{3,2,0,1:T(8,128)(2,1)}), bf16[3,8,8,512]{3,2,0,1:T(8,128)(2,1)S(1)}, u32[]{:S(2)}, u32[]{:S(2)}) %all-to-all-start) | async-done | bytes 196640 | tf_op jit(solution)/shard_map/all_to_all | solution.py:412
  37.3 0.2 select_reduce_fusion
  37.7 10.1 %all-gather = bf16[68,8,512]{2,1,0:T(8,128)(2,1)S(1)} all-gather(bf16[17,8,512]{2,1,0:T(8,128)(2,1)S(1)} %pad_maximum_fusion.1), channel_id=2, replica_groups=mesh['mid'=4,'off'=8] {'mid'}, dimensions={0}, use_global_device_ids=true | all-gather | bytes 696320 | tf_op jit(solution)/shard_map/all_gather | solution.py:417
  47.9 1.0 copy.42
  49.2 0.6 dynamic-slice_bitcast_fusion
  49.8 0.2 select_reduce_fusion.1
  50.0 0.7 fusion.8.pick_ref
  50.8 4.8 %contributions.1 = s32[4,5,17,8,128]{4,3,2,1,0:T(8,128)} custom-call(s32[40]{0:T(128)} %get-tuple-element.19.slot_ref, s32[40]{0:T(128)} %get-tuple-element.18.bin_ref, bf16[16,128,128]{2,1,0:T(8,128)(2,1)} %bitcast.41, bf16[64,128,128]{2,1,0:T(8,128)(2,1)} %all-gather.3.cloned.1.call-done.weight_ref), custom_call_target="tpu_custom_call" | custom-call | tf_op jit(solution)/shard_map/contributions/pallas_call | solution.py:438
  55.5 3.5 %all-to-all-start.1 = ((s32[4,5,17,8,128]{4,3,2,1,0:T(8,128)}), s32[4,5,17,8,128]{4,3,2,1,0:T(8,128)S(1)}, u32[]{:S(2)}, u32[]{:S(2)}) async-start(s32[4,5,17,8,128]{4,3,2,1,0:T(8,128)} %contributions.1), calls=%async_computation.1 | async-start | bytes 2785280 | tf_op jit(solution)/shard_map/all_to_all | solution.py:462
  59.1 0.6 pad_maximum_fusion.2.layer_ref
  59.8 14.0 %multiply_multiply_fusion = (f32[256,2048]{1,0:T(8,128)}, f32[256,2048]{1,0:T(8,128)}) fusion(s32[256]{0:T(256)S(1)} %get-tuple-element.26, s32[256]{0:T(256)S(1)} %get-tuple-element.31, pred[256]{0:T(512)(128)(4,1)S(1)} %get-tuple-element.28, s32[256]{0:T(256)S(1)} %get-tuple-element.27, s32[256]{0:T(256)S(1)} %get-tuple-element.30, ...), kind=kLoop, calls=%fused_computation.14 | loop fusion | flops 38797312 | bytes 4235780 | tf_op jit(solution)/shard_map/mul | solution.py:454
  73.7 1.8 %all-to-all-done.1.code_ref = s32[4,5,17,8,128]{4,3,2,1,0:T(8,128)S(1)} async-done(((s32[4,5,17,8,128]{4,3,2,1,0:T(8,128)}), s32[4,5,17,8,128]{4,3,2,1,0:T(8,128)S(1)}, u32[]{:S(2)}, u32[]{:S(2)}) %all-to-all-start.1) | async-done | bytes 1392672 | tf_op jit(solution)/shard_map/all_to_all | solution.py:462
  75.6 1.1 copy-done
  76.6 39.0 %march.1 = s32[4,1032,128]{2,1,0:T(8,128)} custom-call(f32[2,2,8,16]{3,2,1,0:T(8,128)} %pad_maximum_fusion.2.layer_ref, s32[4,5,17,8,128]{4,3,2,1,0:T(8,128)} %copy-done, bf16[256,320]{1,0:T(8,128)(2,1)} %fusion.8.pick_ref, f32[256,2048]{1,0:T(8,128)} %get-tuple-element.12.phase_real, f32[256,2048]{1,0:T(8,128)} %get-tuple-element.11.phase_imag, ...), custom_call_target="tpu_custom_call" | custom-call | tf_op jit(solution)/shard_map/march/pallas_call | solution.py:469
  115.7 29.7 %all_to_all.25 = s32[4,1032,128]{2,1,0:T(8,128)} all-to-all(s32[4,1032,128]{2,1,0:T(8,128)} %march.1), channel_id=1, replica_groups=mesh['mid'=4,'off'=8] {'mid'}, dimensions={0} | all-to-all | bytes 4227072 | tf_op jit(solution)/shard_map/all_to_all | solution.py:488
  145.4 4.3 %result.1 = f32[4,256,8,128]{3,2,1,0:T(8,128)} custom-call(s32[4,129,8,128]{3,2,1,0:T(8,128)} %bitcast.38), custom_call_target="tpu_custom_call" | custom-call | tf_op jit(solution)/shard_map/result/pallas_call | solution.py:492
  (50 shorter events, 2.3 us)
Async XLA Ops:
  6.5 16.4 %copy-start.1 = (s32[2,8,4]{1,2,0:T(4,128)S(1)}, s32[2,8,4]{1,2,0:T(4,128)}, u32[]{:S(2)}) copy-start(s32[2,8,4]{1,2,0:T(4,128)} %param.16) | copy-start | bytes 772
  6.5 44.2 %all-gather.3.cloned.1.call-start = ((), (), s32[]{:S(2)}) async-start(), calls=%async_computation.3 | async-start | bytes 2359296 | tf_op jit(solution)/shard_map/all_gather | solution.py:400
  16.4 33.4 %copy-start.2 = (f32[2,16]{1,0:T(2,128)S(1)}, f32[2,16]{1,0:T(2,128)}, u32[]{:S(2)}) copy-start(f32[2,16]{1,0:T(2,128)} %param.17) | copy-start | bytes 388
  16.4 19.7 %all-to-all-start = ((bf16[3,8,8,512]{3,2,0,1:T(8,128)(2,1)}), bf16[3,8,8,512]{3,2,0,1:T(8,128)(2,1)S(1)}, u32[]{:S(2)}, u32[]{:S(2)}) async-start(bf16[3,8,8,512]{3,2,0,1:T(8,128)(2,1)} %copy.40), calls=%async_computation | async-start | bytes 393216 | tf_op jit(solution)/shard_map/all_to_all | solution.py:412
  55.5 20.0 %all-to-all-start.1 = ((s32[4,5,17,8,128]{4,3,2,1,0:T(8,128)}), s32[4,5,17,8,128]{4,3,2,1,0:T(8,128)S(1)}, u32[]{:S(2)}, u32[]{:S(2)}) async-start(s32[4,5,17,8,128]{4,3,2,1,0:T(8,128)} %contributions.1), calls=%async_computation.1 | async-start | bytes 2785280 | tf_op jit(solution)/shard_map/all_to_all | solution.py:462
  75.5 1.1 copy-start
Sparse Core Ops, SparseCore 0:
  12.8 36.4 all-gather.2

commit v2 on v1

--- a/solution.py
+++ b/solution.py
@@ -147,7 +147,16 @@
     return (word >> 16).astype(jnp.float32), ((word << 16) >> 16).astype(jnp.float32)
 
 
-def contribution_kernel(slot_ref, bin_ref, data_ref, weight_ref, out_ref, held):
+def contribution_kernel(
+    slot_ref, bin_ref, data_ref, near_ref, far_ref, out_ref, held, weight_ref, near_sem, far_sem
+):
+    count = near_ref.shape[0]
+    near = pltpu.make_async_copy(near_ref, weight_ref.at[pl.ds(0, count)], near_sem)
+    far = pltpu.make_async_copy(far_ref, weight_ref.at[pl.ds(count, count)], far_sem)
+    near.start()
+    far.start()
+    near.wait()
+    far.wait()
     freqs, groups = out_ref.shape[:2]
     outer = out_ref.shape[2] - 1
 
@@ -264,7 +273,7 @@
 
 def march_kernel(
     layer_ref, code_ref, pick_ref, phase_real, phase_imag, rows_forward, rows_inverse, lanes_forward,
-    lanes_inverse, middle_ref, offset_ref, out_ref, plane, other, scales, coded_rows,
+    lanes_inverse, middle_ref, offset_ref, other, plane, scales,
 ):
     sources, groups = code_ref.shape[:2]
     outer = middle_ref.shape[1]
@@ -286,7 +295,7 @@
 
     for step in range(steps):
         midpoint_pass(
-            plane, other, (phase_real, phase_imag), lanes_forward, lanes_inverse, middle_ref, 16
+            plane, other, (phase_real, phase_imag), lanes_forward, lanes_inverse, middle_ref, 32
         )
         if step < steps - 1:
 
@@ -296,32 +305,50 @@
                 parts = layer_turn(parts, layer_ref, step, a)
                 store_column(plane, a, offset_forward(parts[0], parts[1], rows_forward, turn))
 
-    dests = out_ref.shape[0]
-    here = outer // dests
-
-    @pl.loop(0, dests)
-    def _(dest):
-        for at in range(here):
-            a = dest * here + at
-            parts = offset_inverse(column_of(other, a), rows_inverse, turn)
-            parts = layer_turn(parts, layer_ref, steps - 1, a)
-            for c in range(2):
-                both = jnp.maximum(jnp.abs(parts[0][c]), jnp.abs(parts[1][c]))
-                code = scale_code(jnp.max(both, axis=0, keepdims=True))
-                inverse = inverse_scale_of(code)
-                words = packed(coded(parts[0][c], inverse), coded(parts[1][c], inverse))
-                row = at * 2 + c
-                coded_rows[pl.ds(row, HALF, 2 * here), :] = words
-                coded_rows[pl.ds(HALF * 2 * here + row, 1), :] = code
-        out_ref[dest] = coded_rows[...]
-
-
-def result_kernel(code_ref, out_ref):
-    per = code_ref.shape[1] - 1
-    scale = scale_of(code_ref[0, per])
-    first, second = unpacked(code_ref[0, :per])
+
+def finish_kernel(dest_ref, layer_ref, plane_ref, rows_inverse, offset_ref, out_ref):
+    here = plane_ref.shape[3] // BLK
+    turn = offset_ref[0], offset_ref[1]
+    for at in range(here):
+        parts = offset_inverse(column_of(plane_ref, at), rows_inverse, turn)
+        parts = layer_turn(parts, layer_ref, layer_ref.shape[1] - 1, dest_ref[0] * here + at)
+        for c in range(2):
+            both = jnp.maximum(jnp.abs(parts[0][c]), jnp.abs(parts[1][c]))
+            code = scale_code(jnp.max(both, axis=0, keepdims=True))
+            inverse = inverse_scale_of(code)
+            words = packed(coded(parts[0][c], inverse), coded(parts[1][c], inverse))
+            row = at * 2 + c
+            out_ref[pl.ds(row, HALF, 2 * here), :] = words
+            out_ref[pl.ds(HALF * 2 * here + row, 1), :] = code
+
+
+def result_kernel(freq_ref, code_ref, *rest):
+    out_ref = rest[-1]
+    tall = out_ref.shape[2]
+    per = code_ref.shape[0] // tall - 1
+    scale = scale_of(code_ref[per * tall :])
+    first, second = unpacked(code_ref[: per * tall].reshape(per, tall, BLK))
     out_ref[0, :per] = first * scale[None]
     out_ref[0, per:] = second * scale[None]
+
+
+def take_kernel(mine_ref, counts_ref, source_ref, out_ref, sems):
+    taken, entries = out_ref.shape[0], source_ref.shape[1]
+    bins_here, stride = source_ref.shape[0], source_ref.shape[0] * entries // taken
+    copies = []
+    for n in range(taken):
+        entry, bin_at = n * stride + mine_ref[0], 0
+        for b in range(bins_here - 1):
+            over = (bin_at == b) & (entry >= counts_ref[b])
+            entry = jnp.where(over, entry - counts_ref[b], entry)
+            bin_at = jnp.where(over, b + 1, bin_at)
+        entry = jnp.minimum(entry, entries - 1)
+        copies.append(
+            pltpu.make_async_copy(source_ref.at[bin_at, entry], out_ref.at[n], sems.at[n])
+        )
+        copies[-1].start()
+    for copy in copies:
+        copy.wait()
 
 
 def slot_lists(counts_all, targets_all, bins_local, fl, per_device, room):
@@ -354,11 +381,7 @@
     picks = flat[:, :, None] == jnp.arange(total)[None, None, :]
     target = jnp.sum(jnp.where(picks, targets_all.reshape(1, 1, total), 0), axis=2)
     target = jnp.where(valid, target, -1)
-    return off_at * per_device + nth, bin_at, target
-
-
-def take_kernel(place_ref, source_ref, out_ref):
-    out_ref[...] = source_ref[...]
+    return off_at, nth, bin_at, target
 
 
 def local(bins_data, operators, targets, counts, layer_index, slowness):
@@ -379,25 +402,21 @@
     )
 
     per_device = bins_local * entries // fl
-    local_slot = jnp.arange(per_device, dtype=jnp.int32) * fl + mine
-    place = local_slot
-    for b in range(bins_local - 1):
-        size = counts[b]
-        first = b * entries
-        place = jnp.where(place - first >= size, jnp.where(place >= first, place + entries - size, place), place)
-    place = jnp.clip(place, 0, bins_local * entries - 1)
+    smem = pl.BlockSpec(memory_space=pltpu.SMEM)
+    vmem = pl.BlockSpec(memory_space=pltpu.VMEM)
+    hbm = pl.BlockSpec(memory_space=pl.ANY)
     own = pl.pallas_call(
         take_kernel,
-        grid_spec=pltpu.PrefetchScalarGridSpec(
-            num_scalar_prefetch=1,
-            grid=(per_device,),
-            in_specs=[pl.BlockSpec((1, BLK, BLK), lambda n, place: (place[n], 0, 0))],
-            out_specs=pl.BlockSpec((1, BLK, BLK), lambda n, place: (n, 0, 0)),
-        ),
+        in_specs=[smem, smem, hbm],
+        out_specs=hbm,
         out_shape=jax.ShapeDtypeStruct((per_device, BLK, BLK), jnp.bfloat16),
+        scratch_shapes=[pltpu.SemaphoreType.DMA((per_device,))],
         name="take_own",
-    )(place, operators.reshape(bins_local * entries, BLK, BLK))
-    weights = lax.all_gather(own, "off", axis=0, tiled=True)
+    )(mine.reshape(1), counts, operators)
+    cores = 2 if off_count % 2 == 0 else 1
+    lines = [list(range(c, off_count, cores)) for c in range(cores)]
+    near = lax.all_gather(own, "off", axis=0, tiled=True, axis_index_groups=lines)
+    far = near if cores == 1 else lax.ppermute(near, "off", [(i, i ^ 1) for i in range(off_count)])
 
     pairs = fl * 2
 
@@ -424,7 +443,9 @@
     live_total = bins_total * entries // 2
     room = -(-(live_total + (fl - 1) * off_count) // fl)
     room = min(-(-room // GROUP) * GROUP, per_device * off_count)
-    slots, bins, goal = slot_lists(lists[:, 0], lists[:, 1:], bins_local, fl, per_device, room)
+    offs, nth, bins, goal = slot_lists(lists[:, 0], lists[:, 1:], bins_local, fl, per_device, room)
+    side = (offs % cores != off_at % cores).astype(jnp.int32) * (off_count // cores)
+    slots = (side + offs // cores) * per_device + nth
     pick = (
         jnp.tile(goal.reshape(1, fl * room), (1, 2))
         == lax.broadcasted_iota(jnp.int32, (NH, 2 * fl * room), 0)
@@ -433,17 +454,20 @@
     own_slots = lax.dynamic_index_in_dim(slots, mine, 0, False)
     own_bins = lax.dynamic_index_in_dim(bins, mine, 0, False)
     list_groups = room // GROUP
-    smem = pl.BlockSpec(memory_space=pltpu.SMEM)
-    vmem = pl.BlockSpec(memory_space=pltpu.VMEM)
     terms = pl.pallas_call(
         contribution_kernel,
-        in_specs=[smem, smem, vmem, vmem],
+        in_specs=[smem, smem, vmem, hbm, hbm],
         out_specs=vmem,
         out_shape=jax.ShapeDtypeStruct((fl, list_groups, outer + 1, GROUP, BLK), jnp.int32),
-        scratch_shapes=[pltpu.VMEM((fl * 2 * outer * GROUP, BLK), jnp.float32)],
+        scratch_shapes=[
+            pltpu.VMEM((fl * 2 * outer * GROUP, BLK), jnp.float32),
+            pltpu.VMEM((2 * near.shape[0], BLK, BLK), jnp.bfloat16),
+            pltpu.SemaphoreType.DMA,
+            pltpu.SemaphoreType.DMA,
+        ],
         compiler_params=pltpu.CompilerParams(vmem_limit_bytes=VMEM),
         name="contributions",
-    )(own_slots, own_bins, data, weights)
+    )(own_slots, own_bins, data, near, far)
     terms, freq_at = lax.optimization_barrier((terms, off_at * fl + mine))
     omega = math.pi * (0.1 + 0.8 * (freq_at.astype(jnp.float32) + 0.5) / freq_total)
     row = lax.broadcasted_iota(jnp.int32, (NH, total_mid), 0)
@@ -466,37 +490,63 @@
     middle, offset_turn = twiddle_tables(outer)
     here = mid_local // BLK
     rows_out = (HALF + 1) * 2 * here
-    sent = pl.pallas_call(
+    tables = [jnp.asarray(t) for t in block_tables()]
+    middle, offset_turn = jnp.asarray(middle), jnp.asarray(offset_turn)
+    plane = pl.pallas_call(
         march_kernel,
         in_specs=[smem] + [vmem] * 10,
         out_specs=vmem,
-        out_shape=jax.ShapeDtypeStruct((mid_count, rows_out, BLK), jnp.int32),
+        out_shape=jax.ShapeDtypeStruct((2, 2, HALF, total_mid), jnp.float32),
         scratch_shapes=[
             pltpu.VMEM((2, 2, HALF, total_mid), jnp.float32),
-            pltpu.VMEM((2, 2, HALF, total_mid), jnp.float32),
             pltpu.VMEM((fl * room, BLK), jnp.float32),
-            pltpu.VMEM((rows_out, BLK), jnp.int32),
         ],
         compiler_params=pltpu.CompilerParams(vmem_limit_bytes=VMEM),
         name="march",
-    )(
-        layer_turns, terms, pick, phase_real, phase_imag, *[jnp.asarray(t) for t in block_tables()],
-        jnp.asarray(middle), jnp.asarray(offset_turn),
-    )
-    if rounds > 1:
-        sent = lax.dynamic_slice_in_dim(sent, (mid_at // fl) * fl, fl, 0)
-    got = lax.all_to_all(
-        sent, "mid", split_axis=0, concat_axis=0, axis_index_groups=groups, tiled=True
-    )
-    got = got.reshape(fl, HALF + 1, 2 * here, BLK)
-    field = pl.pallas_call(
-        result_kernel,
-        grid=(fl,),
-        in_specs=[pl.BlockSpec((1, HALF + 1, 2 * here, BLK), lambda f: (f, 0, 0, 0))],
-        out_specs=pl.BlockSpec((1, NH, 2 * here, BLK), lambda f: (f, 0, 0, 0)),
-        out_shape=jax.ShapeDtypeStruct((fl, NH, 2 * here, BLK), jnp.float32),
-        name="result",
-    )(got)
+    )(layer_turns, terms, pick, phase_real, phase_imag, *tables, middle, offset_turn)
+
+    finish = pl.pallas_call(
+        finish_kernel,
+        grid_spec=pltpu.PrefetchScalarGridSpec(
+            num_scalar_prefetch=1,
+            grid=(1,),
+            in_specs=[
+                smem,
+                pl.BlockSpec((2, 2, HALF, mid_local), lambda i, dest: (0, 0, 0, dest[0])),
+                vmem,
+                vmem,
+            ],
+            out_specs=pl.BlockSpec((rows_out, BLK), lambda i, dest: (0, 0)),
+        ),
+        out_shape=jax.ShapeDtypeStruct((rows_out, BLK), jnp.int32),
+        name="finish",
+    )
+    got = {}
+    for ahead in [*range(fl - 1, 0, -1), 0]:
+        dest = (mid_at // fl) * fl + (mine + ahead) % fl
+        block = finish(dest.reshape(1), layer_turns, plane, tables[1], offset_turn)
+        plane, block = lax.optimization_barrier((plane, block))
+        if ahead:
+            pairs_of = [(s, s // fl * fl + (s % fl + ahead) % fl) for s in range(mid_count)]
+            block = lax.ppermute(block, "mid", pairs_of)
+        got[ahead] = block
+
+    field = None
+    for ahead in [0, *range(fl - 1, 0, -1)]:
+        freq = (mine - ahead) % fl
+        first = field is None
+        field = pl.pallas_call(
+            result_kernel,
+            grid_spec=pltpu.PrefetchScalarGridSpec(
+                num_scalar_prefetch=1,
+                grid=(1,),
+                in_specs=[pl.BlockSpec((rows_out, BLK), lambda i, f: (0, 0))] + ([] if first else [hbm]),
+                out_specs=pl.BlockSpec((1, NH, 2 * here, BLK), lambda i, f: (f[0], 0, 0, 0)),
+            ),
+            out_shape=jax.ShapeDtypeStruct((fl, NH, 2 * here, BLK), jnp.float32),
+            input_output_aliases={} if first else {2: 0},
+            name="result",
+        )(freq.reshape(1), got[ahead], *([] if first else [field]))
     field = field.reshape(fl, NH, here, 2, BLK).transpose(0, 1, 3, 2, 4)
     return field.reshape(fl, NH, 2, mid_local)
 

time: 158 us -> 173 us (1.095)
  blocking collectives: 39.9 us -> 10.9 us
  waiting for transfers between devices: 14.8 us -> 35.2 us
  Pallas kernels: 53 us -> 71.1 us
  starting transfers between devices: 10 us -> 13.6 us
  local copies, waits for them, and re-layouts: 6.01 us -> 9.4 us
    all_to_all x1 -> x0, blocking collectives: 29.7 us -> none  [local(): lax.all_to_all(sent, 'mid', split_axis=0, concat_axis=0, axis_index_group...]
    pallas_call x3 -> x10, Pallas kernels: 13.9 us -> 36.7 us  [the longest x4 12.8 us: local(): block = finish(dest.reshape(1), layer_turns, plane, tables[1], offset_turn)]
    all_gather x1, waiting for transfers between devices: 0.01 us -> 17.2 us  [local(): lax.all_gather(own, 'off', axis=0, tiled=True, axis_index_groups=lines)]
    ppermute x0 -> x4, waiting for transfers between devices: none -> 14.5 us  [the longest x3 14.5 us: local(): block = lax.ppermute(block, 'mid', pairs_of)]
    all_to_all x1, waiting for transfers between devices: 13 us -> 0.01 us  [local(): data = lax.all_to_all(data, 'off', split_axis=1, concat_axis=0, tiled=True)]
    pallas_call x1, Pallas kernels: 39 us -> 34.4 us  [local(): pl.pallas_call(march_kernel, in_specs=[smem] + [vmem] * 10, out_specs=vme...]
    ppermute x0 -> x4, starting transfers between devices: none -> 3.49 us  [the longest x3 3.49 us: local(): block = lax.ppermute(block, 'mid', pairs_of)]
    unnamed x7 -> x19, local copies, waits for them, and re-layouts: 2.13 us -> 5.58 us
  transfers between devices with their start and end apart: 3 -> 7, of which waited for: 2 -> 4; matrix products, arithmetic and copies ran while one was open for 15% -> 11% of each run, Pallas kernels for 0% -> 13%
where the time goes in v2:
time: 173 us; the launch traced here: 172 us
  Pallas kernels  71.1 us (41%)
  waiting for transfers between devices  35.2 us (20%)
  other arithmetic  18.1 us (10%)
  between operations  13.8 us (8%)
  starting transfers between devices  13.6 us (8%)
  blocking collectives  10.9 us (6%)
  local copies, waits for them, and re-layouts  9.4 us (5%)
    pallas_call x1, Pallas kernels, local(): pl.pallas_call(march_kernel, in_specs=[smem] + [vmem] * 10, out_specs=vme...  34.4 us
    all_gather x1, waiting for transfers between devices, local(): lax.all_gather(own, 'off', axis=0, tiled=True, axis_index_groups=lines)  17.2 us
    ppermute x3, waiting for transfers between devices, local(): block = lax.ppermute(block, 'mid', pairs_of)  14.5 us
    mul x1, other arithmetic, local(): x * (1.0 / (NH * total_mid))  14 us
    pallas_call x4, Pallas kernels, local(): block = finish(dest.reshape(1), layer_turns, plane, tables[1], offset_turn)  12.8 us
    all_gather x1, blocking collectives, local(): data = lax.all_gather(data, 'mid', axis=0)  10.9 us
    pallas_call x1, Pallas kernels, local(): pl.pallas_call(take_kernel, in_specs=[smem, smem, hbm], out_specs=hbm, ou...  9.79 us
    pallas_call x4, Pallas kernels, local(): pl.pallas_call(result_kernel, grid_spec=pltpu.PrefetchScalarGridSpec(num_...  8.53 us
  transfers between devices with their start and end apart: 7, of which 4 were waited for; matrix products, arithmetic and copies ran while one was open for 11% of the time, Pallas kernels for 13%

profile of v2, /device:TPU:0, one launch (start us, length us, event | category | flops | bytes accessed | tf_op | source)
XLA Modules:
  0.0 171.9 jit_solution(4728290115239171358)
XLA Ops:
  8.2 1.0 copy.41
  10.3 6.3 %all-to-all-start = ((bf16[3,8,8,512]{3,2,0,1:T(8,128)(2,1)}), bf16[3,8,8,512]{3,2,0,1:T(8,128)(2,1)S(1)}, u32[]{:S(2)}, u32[]{:S(2)}) async-start(bf16[3,8,8,512]{3,2,0,1:T(8,128)(2,1)} %copy.43), calls=%async_computation | async-start | bytes 393216 | tf_op jit(solution)/shard_map/all_to_all | solution.py:431
  16.7 9.8 %take_own.1 = bf16[8,128,128]{2,1,0:T(8,128)(2,1)} custom-call(s32[1]{0:T(128)} %bitcast.17.mine_ref, s32[2]{0:T(128)} %counts_ref.1, bf16[2,16,128,128]{3,2,1,0:T(8,128)(2,1)} %source_ref.1), custom_call_target="tpu_custom_call" | custom-call | tf_op jit(solution)/shard_map/take_own/pallas_call | solution.py:408
  27.4 10.9 %all-gather = bf16[68,8,512]{2,1,0:T(8,128)(2,1)S(1)} all-gather(bf16[17,8,512]{2,1,0:T(8,128)(2,1)S(1)} %pad_maximum_fusion.1), channel_id=2, replica_groups=mesh['mid'=4,'off'=8] {'mid'}, dimensions={0}, use_global_device_ids=true | all-gather | bytes 696320 | tf_op jit(solution)/shard_map/all_gather | solution.py:436
  38.8 17.2 %all-gather.3.cloned.1.call-done.near_ref = bf16[32,128,128]{2,1,0:T(8,128)(2,1)} async-done(((bf16[8,128,128]{2,1,0:T(8,128)(2,1)}), bf16[32,128,128]{2,1,0:T(8,128)(2,1)}) %all-gather.3.cloned.1.call-update) | async-done | bytes 1048592 | tf_op jit(solution)/shard_map/all_gather | solution.py:418
  56.1 1.0 copy.45
  60.5 5.6 %contributions.1 = s32[4,5,17,8,128]{4,3,2,1,0:T(8,128)} custom-call(s32[40]{0:T(128)} %get-tuple-element.33.slot_ref, s32[40]{0:T(128)} %get-tuple-element.32.bin_ref, bf16[16,128,128]{2,1,0:T(8,128)(2,1)} %bitcast.45, bf16[32,128,128]{2,1,0:T(8,128)(2,1)} %all-gather.3.cloned.1.call-done.near_ref, bf16[32,128,128]{2,1,0:T(8,128)(2,1)} %copy-done.1), custom_call_target="tpu_custom_call" | custom-call | tf_op jit(solution)/shard_map/contributions/pallas_call | solution.py:457
  66.1 3.7 %all-to-all-start.1 = ((s32[4,5,17,8,128]{4,3,2,1,0:T(8,128)}), s32[4,5,17,8,128]{4,3,2,1,0:T(8,128)S(1)}, u32[]{:S(2)}, u32[]{:S(2)}) async-start(s32[4,5,17,8,128]{4,3,2,1,0:T(8,128)} %contributions.1), calls=%async_computation.1 | async-start | bytes 2785280 | tf_op jit(solution)/shard_map/all_to_all | solution.py:486
  70.5 14.0 %multiply_multiply_fusion = (f32[256,2048]{1,0:T(8,128)}, f32[256,2048]{1,0:T(8,128)}) fusion(s32[256]{0:T(256)S(1)} %get-tuple-element.40, s32[256]{0:T(256)S(1)} %get-tuple-element.45, pred[256]{0:T(512)(128)(4,1)S(1)} %get-tuple-element.42, s32[256]{0:T(256)S(1)} %get-tuple-element.41, s32[256]{0:T(256)S(1)} %get-tuple-element.44, ...), kind=kLoop, calls=%fused_computation.14 | loop fusion | flops 38797312 | bytes 4235780 | tf_op jit(solution)/shard_map/mul | solution.py:478
  84.5 3.4 %all-to-all-done.1.code_ref = s32[4,5,17,8,128]{4,3,2,1,0:T(8,128)S(1)} async-done(((s32[4,5,17,8,128]{4,3,2,1,0:T(8,128)}), s32[4,5,17,8,128]{4,3,2,1,0:T(8,128)S(1)}, u32[]{:S(2)}, u32[]{:S(2)}) %all-to-all-start.1) | async-done | bytes 1392672 | tf_op jit(solution)/shard_map/all_to_all | solution.py:486
  87.9 1.1 copy-done
  89.0 34.4 %march.1.plane_ref = f32[2,2,128,2048]{3,2,1,0:T(8,128)} custom-call(f32[2,2,8,16]{3,2,1,0:T(8,128)} %pad_maximum_fusion.2.layer_ref, s32[4,5,17,8,128]{4,3,2,1,0:T(8,128)} %copy-done, bf16[256,320]{1,0:T(8,128)(2,1)} %fusion.8.pick_ref, f32[256,2048]{1,0:T(8,128)} %get-tuple-element.26.phase_real, f32[256,2048]{1,0:T(8,128)} %get-tuple-element.25.phase_imag, ...), custom_call_target="tpu_custom_call" | custom-call | tf_op jit(solution)/shard_map/march/pallas_call | solution.py:495
  123.3 3.1 %finish.4 = s32[1032,128]{1,0:T(8,128)} custom-call(s32[1]{0:T(128)} %bitcast.22.dest_ref, f32[2,2,8,16]{3,2,1,0:T(8,128)} %pad_maximum_fusion.2.layer_ref, f32[2,2,128,2048]{3,2,1,0:T(8,128)} %march.1.plane_ref, bf16[256,768]{1,0:T(8,128)(2,1)} %constant.261.clone.rows_inverse, f32[2,128,128]{2,1,0:T(8,128)} %constant.265.clone.offset_ref), custom_call_target="tpu_custom_call" | custom-call | tf_op jit(solution)/shard_map/finish/pallas_call | solution.py:527
  126.5 3.2 %finish.5 = s32[1032,128]{1,0:T(8,128)} custom-call(s32[1]{0:T(128)} %bitcast.23.dest_ref, f32[2,2,8,16]{3,2,1,0:T(8,128)} %pad_maximum_fusion.2.layer_ref, f32[2,2,128,2048]{3,2,1,0:T(8,128)} %march.1.plane_ref, bf16[256,768]{1,0:T(8,128)(2,1)} %constant.261.clone.rows_inverse, f32[2,128,128]{2,1,0:T(8,128)} %constant.265.clone.offset_ref), custom_call_target="tpu_custom_call" | custom-call | tf_op jit(solution)/shard_map/finish/pallas_call | solution.py:527
  129.7 1.4 collective-permute-start.3
  131.1 3.2 %finish.6 = s32[1032,128]{1,0:T(8,128)} custom-call(s32[1]{0:T(128)} %bitcast.24.dest_ref, f32[2,2,8,16]{3,2,1,0:T(8,128)} %pad_maximum_fusion.2.layer_ref, f32[2,2,128,2048]{3,2,1,0:T(8,128)} %march.1.plane_ref, bf16[256,768]{1,0:T(8,128)(2,1)} %constant.261.clone.rows_inverse, f32[2,128,128]{2,1,0:T(8,128)} %constant.265.clone.offset_ref), custom_call_target="tpu_custom_call" | custom-call | tf_op jit(solution)/shard_map/finish/pallas_call | solution.py:527
  134.4 1.5 collective-permute-start.2
  136.4 3.2 %finish.7.code_ref = s32[1032,128]{1,0:T(8,128)} custom-call(s32[1]{0:T(128)} %bitcast.28.dest_ref, f32[2,2,8,16]{3,2,1,0:T(8,128)} %pad_maximum_fusion.2.layer_ref, f32[2,2,128,2048]{3,2,1,0:T(8,128)} %march.1.plane_ref, bf16[256,768]{1,0:T(8,128)(2,1)} %constant.261.clone.rows_inverse, f32[2,128,128]{2,1,0:T(8,128)} %constant.265.clone.offset_ref), custom_call_target="tpu_custom_call" | custom-call | tf_op jit(solution)/shard_map/finish/pallas_call | solution.py:527
  139.6 2.1 %result.4.rest_0_ = f32[4,256,8,128]{3,2,1,0:T(8,128)} custom-call(s32[1]{0:T(128)} %bitcast.27.freq_ref, s32[1032,128]{1,0:T(8,128)} %finish.7.code_ref), custom_call_target="tpu_custom_call" | custom-call | tf_op jit(solution)/shard_map/result/pallas_call | solution.py:538
  141.7 2.9 %collective-permute-done.3.code_ref = s32[1032,128]{1,0:T(8,128)S(1)} collective-permute-done((s32[1032,128]{1,0:T(8,128)S(1)}, s32[1032,128]{1,0:T(8,128)S(1)}, u32[]{:S(2)}, u32[]{:S(2)}) %collective-permute-start.3) | collective-permute-done | bytes 528416 | tf_op jit(solution)/shard_map/ppermute | solution.py:531
  145.5 2.1 %result.5.rest_0_ = f32[4,256,8,128]{3,2,1,0:T(8,128)} custom-call(s32[1]{0:T(128)} %bitcast.26.freq_ref, s32[1032,128]{1,0:T(8,128)} %copy-done.6, f32[4,256,8,128]{3,2,1,0:T(8,128)} %result.4.rest_0_), custom_call_target="tpu_custom_call", output_to_operand_aliasing={{}: (2, {})} | custom-call | tf_op jit(solution)/shard_map/result/pallas_call | solution.py:538
  147.6 11.6 %collective-permute-done.2.code_ref = s32[1032,128]{1,0:T(8,128)S(1)} collective-permute-done((s32[1032,128]{1,0:T(8,128)S(1)}, s32[1032,128]{1,0:T(8,128)S(1)}, u32[]{:S(2)}, u32[]{:S(2)}) %collective-permute-start.2) | collective-permute-done | bytes 528416 | tf_op jit(solution)/shard_map/ppermute | solution.py:531
  160.0 2.1 %result.6.rest_0_ = f32[4,256,8,128]{3,2,1,0:T(8,128)} custom-call(s32[1]{0:T(128)} %bitcast.25.freq_ref, s32[1032,128]{1,0:T(8,128)} %copy-done.5, f32[4,256,8,128]{3,2,1,0:T(8,128)} %result.5.rest_0_), custom_call_target="tpu_custom_call", output_to_operand_aliasing={{}: (2, {})} | custom-call | tf_op jit(solution)/shard_map/result/pallas_call | solution.py:538
  162.9 2.1 %result.7 = f32[4,256,8,128]{3,2,1,0:T(8,128)} custom-call(s32[1]{0:T(128)} %bitcast.freq_ref, s32[1032,128]{1,0:T(8,128)} %copy-done.3, f32[4,256,8,128]{3,2,1,0:T(8,128)} %result.6.rest_0_), custom_call_target="tpu_custom_call", output_to_operand_aliasing={{}: (2, {})} | custom-call | tf_op jit(solution)/shard_map/result/pallas_call | solution.py:538
  (75 shorter events, 11.0 us)
Async XLA Ops:
  6.5 20.1 %copy-start.7 = (s32[2,8,4]{1,2,0:T(4,128)S(1)}, s32[2,8,4]{1,2,0:T(4,128)}, u32[]{:S(2)}) copy-start(s32[2,8,4]{1,2,0:T(4,128)} %param.16) | copy-start | bytes 772
  10.3 16.7 %all-to-all-start = ((bf16[3,8,8,512]{3,2,0,1:T(8,128)(2,1)}), bf16[3,8,8,512]{3,2,0,1:T(8,128)(2,1)S(1)}, u32[]{:S(2)}, u32[]{:S(2)}) async-start(bf16[3,8,8,512]{3,2,0,1:T(8,128)(2,1)} %copy.43), calls=%async_computation | async-start | bytes 393216 | tf_op jit(solution)/shard_map/all_to_all | solution.py:431
  16.6 39.4 %all-gather.3.cloned.1.call-start = ((), (), s32[]{:S(2)}) async-start(), calls=%async_computation.2 | async-start | bytes 1310720 | tf_op jit(solution)/shard_map/all_gather | solution.py:418
  26.5 32.0 %copy-start.8 = (f32[2,16]{1,0:T(2,128)S(1)}, f32[2,16]{1,0:T(2,128)}, u32[]{:S(2)}) copy-start(f32[2,16]{1,0:T(2,128)} %param.17) | copy-start | bytes 388
  56.0 3.4 %collective-permute-start = (bf16[32,128,128]{2,1,0:T(8,128)(2,1)}, bf16[32,128,128]{2,1,0:T(8,128)(2,1)S(1)}, u32[]{:S(2)}, u32[]{:S(2)}) collective-permute-start(bf16[32,128,128]{2,1,0:T(8,128)(2,1)} %all-gather.3.cloned.1.call-done.near_ref), channel_id=1, source_target_pairs={{0,1},{1,0},{2,3},{3,2},{4,5},{5,4},{6,7},{7,6},{8,9},{9,8},{10,11... | collective-permute-start | bytes 3145736 | tf_op jit(solution)/shard_map/ppermute | solution.py:419
  59.4 1.0 copy-start.1
  66.1 21.8 %all-to-all-start.1 = ((s32[4,5,17,8,128]{4,3,2,1,0:T(8,128)}), s32[4,5,17,8,128]{4,3,2,1,0:T(8,128)S(1)}, u32[]{:S(2)}, u32[]{:S(2)}) async-start(s32[4,5,17,8,128]{4,3,2,1,0:T(8,128)} %contributions.1), calls=%async_computation.1 | async-start | bytes 2785280 | tf_op jit(solution)/shard_map/all_to_all | solution.py:486
  87.9 1.1 copy-start
  126.5 3.2 %copy-start.4 = (s32[1032,128]{1,0:T(8,128)S(1)}, s32[1032,128]{1,0:T(8,128)}, u32[]{:S(2)}) copy-start(s32[1032,128]{1,0:T(8,128)} %finish.4) | copy-start | bytes 1585156
  129.7 14.9 %collective-permute-start.3 = (s32[1032,128]{1,0:T(8,128)S(1)}, s32[1032,128]{1,0:T(8,128)S(1)}, u32[]{:S(2)}, u32[]{:S(2)}) collective-permute-start(s32[1032,128]{1,0:T(8,128)S(1)} %copy-done.4), channel_id=1, source_target_pairs={{0,24},{8,0},{16,8},{24,16},{1,25},{9,1},{17,9},{25,17},{2,26},{10... | collective-permute-start | bytes 1585160 | tf_op jit(solution)/shard_map/ppermute | solution.py:531
  131.1 3.2 %copy-start.2 = (s32[1032,128]{1,0:T(8,128)S(1)}, s32[1032,128]{1,0:T(8,128)}, u32[]{:S(2)}) copy-start(s32[1032,128]{1,0:T(8,128)} %finish.5) | copy-start | bytes 1585156
  134.4 24.8 %collective-permute-start.2 = (s32[1032,128]{1,0:T(8,128)S(1)}, s32[1032,128]{1,0:T(8,128)S(1)}, u32[]{:S(2)}, u32[]{:S(2)}) collective-permute-start(s32[1032,128]{1,0:T(8,128)S(1)} %copy-done.2), channel_id=1, source_target_pairs={{0,16},{8,24},{16,0},{24,8},{1,17},{9,25},{17,1},{25,9},{2,18},{10... | collective-permute-start | bytes 1585160 | tf_op jit(solution)/shard_map/ppermute | solution.py:531
  135.8 26.3 %collective-permute-start.1 = (s32[1032,128]{1,0:T(8,128)}, s32[1032,128]{1,0:T(8,128)S(1)}, u32[]{:S(2)}, u32[]{:S(2)}) collective-permute-start(s32[1032,128]{1,0:T(8,128)} %finish.6), channel_id=1, source_target_pairs={{0,8},{8,16},{16,24},{24,0},{1,9},{9,17},{17,25},{25,1},{2,10},{10... | collective-permute-start | bytes 1585160 | tf_op jit(solution)/shard_map/ppermute | solution.py:531
  144.7 0.8 copy-start.6
  159.2 0.8 copy-start.5
  162.1 0.8 copy-start.3
Sparse Core Ops, SparseCore 0:
  26.6 29.3 all-gather.2

commit v3 on v2

--- a/solution.py
+++ b/solution.py
@@ -147,16 +147,17 @@
     return (word >> 16).astype(jnp.float32), ((word << 16) >> 16).astype(jnp.float32)
 
 
-def contribution_kernel(
-    slot_ref, bin_ref, data_ref, near_ref, far_ref, out_ref, held, weight_ref, near_sem, far_sem
-):
-    count = near_ref.shape[0]
-    near = pltpu.make_async_copy(near_ref, weight_ref.at[pl.ds(0, count)], near_sem)
-    far = pltpu.make_async_copy(far_ref, weight_ref.at[pl.ds(count, count)], far_sem)
-    near.start()
-    far.start()
-    near.wait()
-    far.wait()
+def contribution_kernel(slot_ref, bin_ref, data_ref, *rest):
+    *sources, out_ref, held, weight_ref, sems = rest
+    count = sources[0].shape[0]
+    copies = [
+        pltpu.make_async_copy(ref, weight_ref.at[pl.ds(n * count, count)], sems.at[n])
+        for n, ref in enumerate(sources)
+    ]
+    for copy in copies:
+        copy.start()
+    for copy in copies:
+        copy.wait()
     freqs, groups = out_ref.shape[:2]
     outer = out_ref.shape[2] - 1
 
@@ -238,7 +239,7 @@
     outer = middle_ref.shape[1]
     per_half = HALF // rows
 
-    @pl.loop(0, 2 * per_half, unroll=2)
+    @pl.loop(0, 2 * per_half, unroll=4)
     def _(at):
         p = at // per_half
         here = pl.ds(pl.multiple_of((at % per_half) * rows, rows), rows)
@@ -283,7 +284,7 @@
 
     scales[...] = scale_of(code_ref[:, :, outer].reshape(slots, BLK))
 
-    @pl.loop(0, outer, unroll=2)
+    @pl.loop(0, outer, unroll=4)
     def _(a):
         real, imag = unpacked(code_ref[:, :, a].reshape(slots, BLK))
         scale = scales[...]
@@ -295,11 +296,11 @@
 
     for step in range(steps):
         midpoint_pass(
-            plane, other, (phase_real, phase_imag), lanes_forward, lanes_inverse, middle_ref, 32
+            plane, other, (phase_real, phase_imag), lanes_forward, lanes_inverse, middle_ref, 16
         )
         if step < steps - 1:
 
-            @pl.loop(0, outer, unroll=2)
+            @pl.loop(0, outer, unroll=4)
             def _(a):
                 parts = offset_inverse(column_of(other, a), rows_inverse, turn)
                 parts = layer_turn(parts, layer_ref, step, a)
@@ -408,15 +409,21 @@
     own = pl.pallas_call(
         take_kernel,
         in_specs=[smem, smem, hbm],
-        out_specs=hbm,
+        out_specs=vmem,
         out_shape=jax.ShapeDtypeStruct((per_device, BLK, BLK), jnp.bfloat16),
         scratch_shapes=[pltpu.SemaphoreType.DMA((per_device,))],
         name="take_own",
     )(mine.reshape(1), counts, operators)
+    bins_data, own = lax.optimization_barrier((bins_data, own))
     cores = 2 if off_count % 2 == 0 else 1
-    lines = [list(range(c, off_count, cores)) for c in range(cores)]
-    near = lax.all_gather(own, "off", axis=0, tiled=True, axis_index_groups=lines)
-    far = near if cores == 1 else lax.ppermute(near, "off", [(i, i ^ 1) for i in range(off_count)])
+    line = off_count // cores
+    assert line & (line - 1) == 0 and fl & (fl - 1) == 0
+    shares = [own] + [
+        lax.ppermute(own, "off", [(i, (i // cores ^ away) * cores + i % cores) for i in range(off_count)])
+        for away in range(1, line)
+    ]
+    if cores > 1:
+        shares += [lax.ppermute(x, "off", [(i, i ^ 1) for i in range(off_count)]) for x in shares]
 
     pairs = fl * 2
 
@@ -444,8 +451,8 @@
     room = -(-(live_total + (fl - 1) * off_count) // fl)
     room = min(-(-room // GROUP) * GROUP, per_device * off_count)
     offs, nth, bins, goal = slot_lists(lists[:, 0], lists[:, 1:], bins_local, fl, per_device, room)
-    side = (offs % cores != off_at % cores).astype(jnp.int32) * (off_count // cores)
-    slots = (side + offs // cores) * per_device + nth
+    side = (offs % cores != off_at % cores).astype(jnp.int32) * line
+    slots = (side + ((offs // cores) ^ (off_at // cores))) * per_device + nth
     pick = (
         jnp.tile(goal.reshape(1, fl * room), (1, 2))
         == lax.broadcasted_iota(jnp.int32, (NH, 2 * fl * room), 0)
@@ -456,18 +463,17 @@
     list_groups = room // GROUP
     terms = pl.pallas_call(
         contribution_kernel,
-        in_specs=[smem, smem, vmem, hbm, hbm],
+        in_specs=[smem, smem, vmem] + [hbm] * len(shares),
         out_specs=vmem,
         out_shape=jax.ShapeDtypeStruct((fl, list_groups, outer + 1, GROUP, BLK), jnp.int32),
         scratch_shapes=[
             pltpu.VMEM((fl * 2 * outer * GROUP, BLK), jnp.float32),
-            pltpu.VMEM((2 * near.shape[0], BLK, BLK), jnp.bfloat16),
-            pltpu.SemaphoreType.DMA,
-            pltpu.SemaphoreType.DMA,
+            pltpu.VMEM((len(shares) * per_device, BLK, BLK), jnp.bfloat16),
+            pltpu.SemaphoreType.DMA((len(shares),)),
         ],
         compiler_params=pltpu.CompilerParams(vmem_limit_bytes=VMEM),
         name="contributions",
-    )(own_slots, own_bins, data, near, far)
+    )(own_slots, own_bins, data, *shares)
     terms, freq_at = lax.optimization_barrier((terms, off_at * fl + mine))
     omega = math.pi * (0.1 + 0.8 * (freq_at.astype(jnp.float32) + 0.5) / freq_total)
     row = lax.broadcasted_iota(jnp.int32, (NH, total_mid), 0)
@@ -519,21 +525,23 @@
             out_specs=pl.BlockSpec((rows_out, BLK), lambda i, dest: (0, 0)),
         ),
         out_shape=jax.ShapeDtypeStruct((rows_out, BLK), jnp.int32),
+        cost_estimate=pl.CostEstimate(
+            flops=6 * NH * NH * 2 * BLK * here, bytes_accessed=6 * NH * mid_local, transcendentals=0
+        ),
         name="finish",
     )
     got = {}
     for ahead in [*range(fl - 1, 0, -1), 0]:
-        dest = (mid_at // fl) * fl + (mine + ahead) % fl
+        dest = (mid_at // fl) * fl + (mine ^ ahead)
         block = finish(dest.reshape(1), layer_turns, plane, tables[1], offset_turn)
         plane, block = lax.optimization_barrier((plane, block))
         if ahead:
-            pairs_of = [(s, s // fl * fl + (s % fl + ahead) % fl) for s in range(mid_count)]
-            block = lax.ppermute(block, "mid", pairs_of)
+            block = lax.ppermute(block, "mid", [(s, s ^ ahead) for s in range(mid_count)])
         got[ahead] = block
 
     field = None
     for ahead in [0, *range(fl - 1, 0, -1)]:
-        freq = (mine - ahead) % fl
+        freq = mine ^ ahead
         first = field is None
         field = pl.pallas_call(
             result_kernel,
@@ -545,6 +553,10 @@
             ),
             out_shape=jax.ShapeDtypeStruct((fl, NH, 2 * here, BLK), jnp.float32),
             input_output_aliases={} if first else {2: 0},
+            compiler_params=pltpu.CompilerParams(vmem_limit_bytes=VMEM),
+            cost_estimate=pl.CostEstimate(
+                flops=4 * NH * mid_local, bytes_accessed=12 * NH * mid_local, transcendentals=0
+            ),
             name="result",
         )(freq.reshape(1), got[ahead], *([] if first else [field]))
     field = field.reshape(fl, NH, here, 2, BLK).transpose(0, 1, 3, 2, 4)

time: 173 us -> 143 us (0.83)
  between operations: 13.8 us -> 0.37 us
  Pallas kernels: 71.1 us -> 57.7 us
  waiting for transfers between devices: 35.2 us -> 27.7 us
  starting transfers between devices: 13.6 us -> 19 us
    all_gather x1 -> x0, waiting for transfers between devices: 17.2 us -> none  [local(): lax.all_gather(own, 'off', axis=0, tiled=True, axis_index_groups=lines)]
    pallas_call x2, Pallas kernels: 15.4 us -> 8.08 us  [the longest x1 5.62 us: local(): pl.pallas_call(contribution_kernel, in_specs=[smem, smem, vmem] + [hbm] *...]
    ppermute x4 -> x10, starting transfers between devices: 3.49 us -> 10.2 us  [the longest x3 5.66 us: local(): lax.ppermute(own, 'off', [(i, (i // cores ^ away) * cores + i % cores) fo...]
    ppermute x4 -> x10, waiting for transfers between devices: 14.5 us -> 21 us  [the longest x3 11.2 us: local(): lax.ppermute(own, 'off', [(i, (i // cores ^ away) * cores + i % cores) fo...]
    pallas_call x1, Pallas kernels: 34.4 us -> 28.3 us  [local(): pl.pallas_call(march_kernel, in_specs=[smem] + [vmem] * 10, out_specs=vme...]
    all_to_all x1, waiting for transfers between devices: 0.01 us -> 5.82 us  [local(): data = lax.all_to_all(data, 'off', split_axis=1, concat_axis=0, tiled=True)]
    all_to_all x1, waiting for transfers between devices: 3.41 us -> 0.87 us  [local(): lax.all_to_all(terms, 'mid', split_axis=0, concat_axis=0, axis_index_grou...]
    unnamed x19 -> x28, local copies, waits for them, and re-layouts: 5.58 us -> 4.43 us
  transfers between devices with their start and end apart: 7 -> 12, of which waited for: 4 -> 5; matrix products, arithmetic and copies ran while one was open for 11% -> 16% of each run, Pallas kernels for 13% -> 9%
where the time goes in v3:
time: 143 us; the launch traced here: 142 us
  Pallas kernels  57.7 us (40%)
  waiting for transfers between devices  27.7 us (19%)
  starting transfers between devices  19 us (13%)
  other arithmetic  18 us (13%)
  blocking collectives  10.2 us (7%)
  local copies, waits for them, and re-layouts  9.34 us (7%)
    pallas_call x1, Pallas kernels, local(): pl.pallas_call(march_kernel, in_specs=[smem] + [vmem] * 10, out_specs=vme...  28.3 us
    mul x1, other arithmetic, local(): x * (1.0 / (NH * total_mid))  14 us
    pallas_call x4, Pallas kernels, local(): block = finish(dest.reshape(1), layer_turns, plane, tables[1], offset_turn)  12.7 us
    ppermute x3, waiting for transfers between devices, local(): lax.ppermute(own, 'off', [(i, (i // cores ^ away) * cores + i % cores) fo...  11.2 us
    all_gather x1, blocking collectives, local(): data = lax.all_gather(data, 'mid', axis=0)  10.2 us
    ppermute x3, waiting for transfers between devices, local(): lax.ppermute(block, 'mid', [(s, s ^ ahead) for s in range(mid_count)])  9.77 us
    pallas_call x4, Pallas kernels, local(): pl.pallas_call(result_kernel, grid_spec=pltpu.PrefetchScalarGridSpec(num_...  8.53 us
    all_to_all x1, waiting for transfers between devices, local(): data = lax.all_to_all(data, 'off', split_axis=1, concat_axis=0, tiled=True)  5.82 us
  transfers between devices with their start and end apart: 12, of which 5 were waited for; matrix products, arithmetic and copies ran while one was open for 16% of the time, Pallas kernels for 9%

profile of v3, /device:TPU:0, one launch (start us, length us, event | category | flops | bytes accessed | tf_op | source)
XLA Modules:
  0.0 142.3 jit_solution(534768899743885607)
XLA Ops:
  0.0 2.5 %take_own.1.rest_0_ = bf16[8,128,128]{2,1,0:T(8,128)(2,1)} custom-call(s32[1]{0:T(128)} %bitcast.1.mine_ref.freq_ref, s32[2]{0:T(128)} %counts_ref.1, bf16[2,16,128,128]{3,2,1,0:T(8,128)(2,1)} %source_ref.1), custom_call_target="tpu_custom_call" | custom-call | tf_op jit(solution)/shard_map/take_own/pallas_call | solution.py:409
  2.5 3.1 %collective-permute-start = (bf16[8,128,128]{2,1,0:T(8,128)(2,1)}, bf16[8,128,128]{2,1,0:T(8,128)(2,1)S(1)}, u32[]{:S(2)}, u32[]{:S(2)}) collective-permute-start(bf16[8,128,128]{2,1,0:T(8,128)(2,1)} %take_own.1.rest_0_), channel_id=1, source_target_pairs={{0,2},{1,3},{2,0},{3,1},{4,6},{5,7},{6,4},{7,5},{8,10},{9,11},{10,... | collective-permute-start | bytes 786440 | tf_op jit(solution)/shard_map/ppermute | solution.py:422
  5.5 2.6 %collective-permute-start.1 = (bf16[8,128,128]{2,1,0:T(8,128)(2,1)}, bf16[8,128,128]{2,1,0:T(8,128)(2,1)S(1)}, u32[]{:S(2)}, u32[]{:S(2)}) collective-permute-start(bf16[8,128,128]{2,1,0:T(8,128)(2,1)} %take_own.1.rest_0_), channel_id=1, source_target_pairs={{0,4},{1,5},{2,6},{3,7},{4,0},{5,1},{6,2},{7,3},{8,12},{9,13},{10,... | collective-permute-start | bytes 786440 | tf_op jit(solution)/shard_map/ppermute | solution.py:422
  8.8 1.0 copy.41
  11.9 5.2 %all-to-all-start = ((bf16[3,8,8,512]{3,2,0,1:T(8,128)(2,1)}), bf16[3,8,8,512]{3,2,0,1:T(8,128)(2,1)S(1)}, u32[]{:S(2)}, u32[]{:S(2)}) async-start(bf16[3,8,8,512]{3,2,0,1:T(8,128)(2,1)} %copy.43), calls=%async_computation | async-start | bytes 393216 | tf_op jit(solution)/shard_map/all_to_all | solution.py:438
  18.1 11.2 %collective-permute-done.1.rest_2_ = bf16[8,128,128]{2,1,0:T(8,128)(2,1)S(1)} collective-permute-done((bf16[8,128,128]{2,1,0:T(8,128)(2,1)}, bf16[8,128,128]{2,1,0:T(8,128)(2,1)S(1)}, u32[]{:S(2)}, u32[]{:S(2)}) %collective-permute-start.1) | collective-permute-done | bytes 262176 | tf_op jit(solution)/shard_map/ppermute | solution.py:422
  29.8 5.8 %all-to-all-done = bf16[3,8,8,512]{3,2,0,1:T(8,128)(2,1)S(1)} async-done(((bf16[3,8,8,512]{3,2,0,1:T(8,128)(2,1)}), bf16[3,8,8,512]{3,2,0,1:T(8,128)(2,1)S(1)}, u32[]{:S(2)}, u32[]{:S(2)}) %all-to-all-start) | async-done | bytes 196640 | tf_op jit(solution)/shard_map/all_to_all | solution.py:438
  36.2 10.2 %all-gather = bf16[68,8,512]{2,1,0:T(8,128)(2,1)S(1)} all-gather(bf16[17,8,512]{2,1,0:T(8,128)(2,1)S(1)} %pad_maximum_fusion.1), channel_id=2, replica_groups=mesh['mid'=4,'off'=8] {'mid'}, dimensions={0}, use_global_device_ids=true | all-gather | bytes 696320 | tf_op jit(solution)/shard_map/all_gather | solution.py:443
  51.2 5.6 %contributions.1 = s32[4,5,17,8,128]{4,3,2,1,0:T(8,128)} custom-call(s32[40]{0:T(128)} %get-tuple-element.37.slot_ref, s32[40]{0:T(128)} %get-tuple-element.36.bin_ref, bf16[16,128,128]{2,1,0:T(8,128)(2,1)} %bitcast.44, bf16[8,128,128]{2,1,0:T(8,128)(2,1)} %take_own.1.rest_0_, bf16[8,128,128]{2,1,0:T(8,128)(2,1)} %copy-done.5, ...), custom_call_target="tpu_custom_call" | custom-call | tf_op jit(solution)/shard_map/contributions/pallas_call | solution.py:464
  56.9 3.6 %all-to-all-start.1 = ((s32[4,5,17,8,128]{4,3,2,1,0:T(8,128)}), s32[4,5,17,8,128]{4,3,2,1,0:T(8,128)S(1)}, u32[]{:S(2)}, u32[]{:S(2)}) async-start(s32[4,5,17,8,128]{4,3,2,1,0:T(8,128)} %contributions.1), calls=%async_computation.1 | async-start | bytes 2785280 | tf_op jit(solution)/shard_map/all_to_all | solution.py:492
  61.1 14.0 %multiply_multiply_fusion = (f32[256,2048]{1,0:T(8,128)}, f32[256,2048]{1,0:T(8,128)}) fusion(s32[256]{0:T(256)S(1)} %get-tuple-element.44, s32[256]{0:T(256)S(1)} %get-tuple-element.49, pred[256]{0:T(512)(128)(4,1)S(1)} %get-tuple-element.46, s32[256]{0:T(256)S(1)} %get-tuple-element.45, s32[256]{0:T(256)S(1)} %get-tuple-element.48, ...), kind=kLoop, calls=%fused_computation.14 | loop fusion | flops 38797312 | bytes 4235780 | tf_op jit(solution)/shard_map/mul | solution.py:484
  75.9 1.1 copy-done
  77.0 28.3 %march.1.plane_ref = f32[2,2,128,2048]{3,2,1,0:T(8,128)} custom-call(f32[2,2,8,16]{3,2,1,0:T(8,128)} %pad_maximum_fusion.2.layer_ref, s32[4,5,17,8,128]{4,3,2,1,0:T(8,128)} %copy-done, bf16[256,320]{1,0:T(8,128)(2,1)} %fusion.8.pick_ref, f32[256,2048]{1,0:T(8,128)} %get-tuple-element.30.phase_real, f32[256,2048]{1,0:T(8,128)} %get-tuple-element.29.phase_imag, ...), custom_call_target="tpu_custom_call" | custom-call | tf_op jit(solution)/shard_map/march/pallas_call | solution.py:501
  105.3 3.2 %finish.4 = s32[1032,128]{1,0:T(8,128)} custom-call(s32[1]{0:T(128)} %bitcast.22.dest_ref, f32[2,2,8,16]{3,2,1,0:T(8,128)} %pad_maximum_fusion.2.layer_ref, f32[2,2,128,2048]{3,2,1,0:T(8,128)} %march.1.plane_ref, bf16[256,768]{1,0:T(8,128)(2,1)} %constant.233.clone.rows_inverse, f32[2,128,128]{2,1,0:T(8,128)} %constant.237.clone.offset_ref), custom_call_target="tpu_custom_call" | custom-call | flops 402653184 | bytes 786432 | tf_op jit(solution)/shard_map/finish/pallas_call | solution.py:536
  108.5 3.2 %finish.5 = s32[1032,128]{1,0:T(8,128)} custom-call(s32[1]{0:T(128)} %bitcast.23.dest_ref, f32[2,2,8,16]{3,2,1,0:T(8,128)} %pad_maximum_fusion.2.layer_ref, f32[2,2,128,2048]{3,2,1,0:T(8,128)} %march.1.plane_ref, bf16[256,768]{1,0:T(8,128)(2,1)} %constant.233.clone.rows_inverse, f32[2,128,128]{2,1,0:T(8,128)} %constant.237.clone.offset_ref), custom_call_target="tpu_custom_call" | custom-call | flops 402653184 | bytes 786432 | tf_op jit(solution)/shard_map/finish/pallas_call | solution.py:536
  111.7 2.0 %collective-permute-start.9 = (s32[1032,128]{1,0:T(8,128)S(1)}, s32[1032,128]{1,0:T(8,128)S(1)}, u32[]{:S(2)}, u32[]{:S(2)}) collective-permute-start(s32[1032,128]{1,0:T(8,128)S(1)} %copy-done.3), channel_id=1, source_target_pairs={{0,24},{8,16},{16,8},{24,0},{1,25},{9,17},{17,9},{25,1},{2,26},{10... | collective-permute-start | bytes 1585160 | tf_op jit(solution)/shard_map/ppermute | solution.py:539
  114.6 3.2 %finish.6 = s32[1032,128]{1,0:T(8,128)} custom-call(s32[1]{0:T(128)} %bitcast.24.dest_ref, f32[2,2,8,16]{3,2,1,0:T(8,128)} %pad_maximum_fusion.2.layer_ref, f32[2,2,128,2048]{3,2,1,0:T(8,128)} %march.1.plane_ref, bf16[256,768]{1,0:T(8,128)(2,1)} %constant.233.clone.rows_inverse, f32[2,128,128]{2,1,0:T(8,128)} %constant.237.clone.offset_ref), custom_call_target="tpu_custom_call" | custom-call | flops 402653184 | bytes 786432 | tf_op jit(solution)/shard_map/finish/pallas_call | solution.py:536
  118.4 3.2 %finish.7.code_ref = s32[1032,128]{1,0:T(8,128)} custom-call(s32[1]{0:T(128)} %bitcast.27.dest_ref, f32[2,2,8,16]{3,2,1,0:T(8,128)} %pad_maximum_fusion.2.layer_ref, f32[2,2,128,2048]{3,2,1,0:T(8,128)} %march.1.plane_ref, bf16[256,768]{1,0:T(8,128)(2,1)} %constant.233.clone.rows_inverse, f32[2,128,128]{2,1,0:T(8,128)} %constant.237.clone.offset_ref), custom_call_target="tpu_custom_call" | custom-call | flops 402653184 | bytes 786432 | tf_op jit(solution)/shard_map/finish/pallas_call | solution.py:536
  121.6 2.1 %result.4.rest_0_ = f32[4,256,8,128]{3,2,1,0:T(8,128)} custom-call(s32[1]{0:T(128)} %bitcast.1.mine_ref.freq_ref, s32[1032,128]{1,0:T(8,128)} %finish.7.code_ref), custom_call_target="tpu_custom_call" | custom-call | flops 524288 | bytes 1572864 | tf_op jit(solution)/shard_map/result/pallas_call | solution.py:546
  123.7 3.9 %collective-permute-done.9.code_ref = s32[1032,128]{1,0:T(8,128)S(1)} collective-permute-done((s32[1032,128]{1,0:T(8,128)S(1)}, s32[1032,128]{1,0:T(8,128)S(1)}, u32[]{:S(2)}, u32[]{:S(2)}) %collective-permute-start.9) | collective-permute-done | bytes 528416 | tf_op jit(solution)/shard_map/ppermute | solution.py:539
  128.4 2.1 %result.5.rest_0_ = f32[4,256,8,128]{3,2,1,0:T(8,128)} custom-call(s32[1]{0:T(128)} %bitcast.26.freq_ref, s32[1032,128]{1,0:T(8,128)} %copy-done.4, f32[4,256,8,128]{3,2,1,0:T(8,128)} %result.4.rest_0_), custom_call_target="tpu_custom_call", output_to_operand_aliasing={{}: (2, {})} | custom-call | flops 524288 | bytes 1572864 | tf_op jit(solution)/shard_map/result/pallas_call | solution.py:546
  130.5 5.9 %collective-permute-done.8.code_ref = s32[1032,128]{1,0:T(8,128)S(1)} collective-permute-done((s32[1032,128]{1,0:T(8,128)}, s32[1032,128]{1,0:T(8,128)S(1)}, u32[]{:S(2)}, u32[]{:S(2)}) %collective-permute-start.8) | collective-permute-done | bytes 528416 | tf_op jit(solution)/shard_map/ppermute | solution.py:539
  137.2 2.1 %result.6.rest_0_ = f32[4,256,8,128]{3,2,1,0:T(8,128)} custom-call(s32[1]{0:T(128)} %bitcast.25.freq_ref, s32[1032,128]{1,0:T(8,128)} %copy-done.2, f32[4,256,8,128]{3,2,1,0:T(8,128)} %result.5.rest_0_), custom_call_target="tpu_custom_call", output_to_operand_aliasing={{}: (2, {})} | custom-call | flops 524288 | bytes 1572864 | tf_op jit(solution)/shard_map/result/pallas_call | solution.py:546
  140.1 2.1 %result.7 = f32[4,256,8,128]{3,2,1,0:T(8,128)} custom-call(s32[1]{0:T(128)} %bitcast.freq_ref, s32[1032,128]{1,0:T(8,128)} %copy-done.1, f32[4,256,8,128]{3,2,1,0:T(8,128)} %result.6.rest_0_), custom_call_target="tpu_custom_call", output_to_operand_aliasing={{}: (2, {})} | custom-call | flops 524288 | bytes 1572864 | tf_op jit(solution)/shard_map/result/pallas_call | solution.py:546
  (94 shorter events, 14.7 us)
Async XLA Ops:
  0.0 17.1 %copy-start.12 = (s32[2,8,4]{1,2,0:T(4,128)S(1)}, s32[2,8,4]{1,2,0:T(4,128)}, u32[]{:S(2)}) copy-start(s32[2,8,4]{1,2,0:T(4,128)} %param.16) | copy-start | bytes 772
  2.5 15.0 %collective-permute-start = (bf16[8,128,128]{2,1,0:T(8,128)(2,1)}, bf16[8,128,128]{2,1,0:T(8,128)(2,1)S(1)}, u32[]{:S(2)}, u32[]{:S(2)}) collective-permute-start(bf16[8,128,128]{2,1,0:T(8,128)(2,1)} %take_own.1.rest_0_), channel_id=1, source_target_pairs={{0,2},{1,3},{2,0},{3,1},{4,6},{5,7},{6,4},{7,5},{8,10},{9,11},{10,... | collective-permute-start | bytes 786440 | tf_op jit(solution)/shard_map/ppermute | solution.py:422
  5.5 23.7 %collective-permute-start.1 = (bf16[8,128,128]{2,1,0:T(8,128)(2,1)}, bf16[8,128,128]{2,1,0:T(8,128)(2,1)S(1)}, u32[]{:S(2)}, u32[]{:S(2)}) collective-permute-start(bf16[8,128,128]{2,1,0:T(8,128)(2,1)} %take_own.1.rest_0_), channel_id=1, source_target_pairs={{0,4},{1,5},{2,6},{3,7},{4,0},{5,1},{6,2},{7,3},{8,12},{9,13},{10,... | collective-permute-start | bytes 786440 | tf_op jit(solution)/shard_map/ppermute | solution.py:422
  8.1 21.1 %collective-permute-start.2 = (bf16[8,128,128]{2,1,0:T(8,128)(2,1)}, bf16[8,128,128]{2,1,0:T(8,128)(2,1)S(1)}, u32[]{:S(2)}, u32[]{:S(2)}) collective-permute-start(bf16[8,128,128]{2,1,0:T(8,128)(2,1)} %take_own.1.rest_0_), channel_id=1, source_target_pairs={{0,6},{1,7},{2,4},{3,5},{4,2},{5,3},{6,0},{7,1},{8,14},{9,15},{10,... | collective-permute-start | bytes 786440 | tf_op jit(solution)/shard_map/ppermute | solution.py:422
  8.1 42.1 %collective-permute-start.3 = (bf16[8,128,128]{2,1,0:T(8,128)(2,1)}, bf16[8,128,128]{2,1,0:T(8,128)(2,1)S(1)}, u32[]{:S(2)}, u32[]{:S(2)}) collective-permute-start(bf16[8,128,128]{2,1,0:T(8,128)(2,1)} %take_own.1.rest_0_), channel_id=1, source_target_pairs={{0,1},{1,0},{2,3},{3,2},{4,5},{5,4},{6,7},{7,6},{8,9},{9,8},{10,11... | collective-permute-start | bytes 786440 | tf_op jit(solution)/shard_map/ppermute | solution.py:426
  10.8 36.7 %copy-start.13 = (f32[2,16]{1,0:T(2,128)S(1)}, f32[2,16]{1,0:T(2,128)}, u32[]{:S(2)}) copy-start(f32[2,16]{1,0:T(2,128)} %param.17) | copy-start | bytes 388
  11.9 23.7 %all-to-all-start = ((bf16[3,8,8,512]{3,2,0,1:T(8,128)(2,1)}), bf16[3,8,8,512]{3,2,0,1:T(8,128)(2,1)S(1)}, u32[]{:S(2)}, u32[]{:S(2)}) async-start(bf16[3,8,8,512]{3,2,0,1:T(8,128)(2,1)} %copy.43), calls=%async_computation | async-start | bytes 393216 | tf_op jit(solution)/shard_map/all_to_all | solution.py:438
  17.5 32.8 %copy-start.5 = (bf16[8,128,128]{2,1,0:T(8,128)(2,1)}, bf16[8,128,128]{2,1,0:T(8,128)(2,1)S(1)}, u32[]{:S(2)}) copy-start(bf16[8,128,128]{2,1,0:T(8,128)(2,1)S(1)} %collective-permute-done.rest_1_) | copy-start | bytes 786436
  17.5 32.8 %collective-permute-start.4 = (bf16[8,128,128]{2,1,0:T(8,128)(2,1)S(1)}, bf16[8,128,128]{2,1,0:T(8,128)(2,1)S(1)}, u32[]{:S(2)}, u32[]{:S(2)}) collective-permute-start(bf16[8,128,128]{2,1,0:T(8,128)(2,1)S(1)} %collective-permute-done.rest_1_), channel_id=1, source_target_pairs={{0,1},{1,0},{2,3},{3,2},{4,5},{5,4},{6,7},{7,6},{8,9},{9,8},{10,11... | collective-permute-start | bytes 786440 | tf_op jit(solution)/shard_map/ppermute | solution.py:426
  29.3 21.0 %copy-start.6 = (bf16[8,128,128]{2,1,0:T(8,128)(2,1)}, bf16[8,128,128]{2,1,0:T(8,128)(2,1)S(1)}, u32[]{:S(2)}) copy-start(bf16[8,128,128]{2,1,0:T(8,128)(2,1)S(1)} %collective-permute-done.1.rest_2_) | copy-start | bytes 786436
  29.3 21.0 %collective-permute-start.5 = (bf16[8,128,128]{2,1,0:T(8,128)(2,1)S(1)}, bf16[8,128,128]{2,1,0:T(8,128)(2,1)S(1)}, u32[]{:S(2)}, u32[]{:S(2)}) collective-permute-start(bf16[8,128,128]{2,1,0:T(8,128)(2,1)S(1)} %collective-permute-done.1.rest_2_), channel_id=1, source_target_pairs={{0,1},{1,0},{2,3},{3,2},{4,5},{5,4},{6,7},{7,6},{8,9},{9,8},{10,11... | collective-permute-start | bytes 786440 | tf_op jit(solution)/shard_map/ppermute | solution.py:426
  29.3 21.0 %copy-start.7 = (bf16[8,128,128]{2,1,0:T(8,128)(2,1)}, bf16[8,128,128]{2,1,0:T(8,128)(2,1)S(1)}, u32[]{:S(2)}) copy-start(bf16[8,128,128]{2,1,0:T(8,128)(2,1)S(1)} %collective-permute-done.2.rest_3_) | copy-start | bytes 786436
  29.3 21.0 %collective-permute-start.6 = (bf16[8,128,128]{2,1,0:T(8,128)(2,1)S(1)}, bf16[8,128,128]{2,1,0:T(8,128)(2,1)S(1)}, u32[]{:S(2)}, u32[]{:S(2)}) collective-permute-start(bf16[8,128,128]{2,1,0:T(8,128)(2,1)S(1)} %collective-permute-done.2.rest_3_), channel_id=1, source_target_pairs={{0,1},{1,0},{2,3},{3,2},{4,5},{5,4},{6,7},{7,6},{8,9},{9,8},{10,11... | collective-permute-start | bytes 786440 | tf_op jit(solution)/shard_map/ppermute | solution.py:426
  50.2 0.8 copy-start.9
  50.3 0.9 copy-start.10
  50.3 0.9 copy-start.11
  56.9 19.0 %all-to-all-start.1 = ((s32[4,5,17,8,128]{4,3,2,1,0:T(8,128)}), s32[4,5,17,8,128]{4,3,2,1,0:T(8,128)S(1)}, u32[]{:S(2)}, u32[]{:S(2)}) async-start(s32[4,5,17,8,128]{4,3,2,1,0:T(8,128)} %contributions.1), calls=%async_computation.1 | async-start | bytes 2785280 | tf_op jit(solution)/shard_map/all_to_all | solution.py:492
  75.9 1.1 copy-start
  108.5 3.2 %copy-start.3 = (s32[1032,128]{1,0:T(8,128)S(1)}, s32[1032,128]{1,0:T(8,128)}, u32[]{:S(2)}) copy-start(s32[1032,128]{1,0:T(8,128)} %finish.4) | copy-start | bytes 1585156
  111.7 15.8 %collective-permute-start.9 = (s32[1032,128]{1,0:T(8,128)S(1)}, s32[1032,128]{1,0:T(8,128)S(1)}, u32[]{:S(2)}, u32[]{:S(2)}) collective-permute-start(s32[1032,128]{1,0:T(8,128)S(1)} %copy-done.3), channel_id=1, source_target_pairs={{0,24},{8,16},{16,8},{24,0},{1,25},{9,17},{17,9},{25,1},{2,26},{10... | collective-permute-start | bytes 1585160 | tf_op jit(solution)/shard_map/ppermute | solution.py:539
  113.8 22.6 %collective-permute-start.8 = (s32[1032,128]{1,0:T(8,128)}, s32[1032,128]{1,0:T(8,128)S(1)}, u32[]{:S(2)}, u32[]{:S(2)}) collective-permute-start(s32[1032,128]{1,0:T(8,128)} %finish.5), channel_id=1, source_target_pairs={{0,16},{8,24},{16,0},{24,8},{1,17},{9,25},{17,1},{25,9},{2,18},{10... | collective-permute-start | bytes 1585160 | tf_op jit(solution)/shard_map/ppermute | solution.py:539
  117.8 21.6 %collective-permute-start.7 = (s32[1032,128]{1,0:T(8,128)}, s32[1032,128]{1,0:T(8,128)S(1)}, u32[]{:S(2)}, u32[]{:S(2)}) collective-permute-start(s32[1032,128]{1,0:T(8,128)} %finish.6), channel_id=1, source_target_pairs={{0,8},{8,0},{16,24},{24,16},{1,9},{9,1},{17,25},{25,17},{2,10},{10... | collective-permute-start | bytes 1585160 | tf_op jit(solution)/shard_map/ppermute | solution.py:539
  127.6 0.8 copy-start.4
  136.4 0.8 copy-start.2
  (2 other events, 1.5 us)

commit v4 on v3

--- a/solution.py
+++ b/solution.py
@@ -19,6 +19,7 @@
 STEP_LOG = 64.0
 TOP = 32767.0
 GROUP = 8
+COLUMNS = 2
 VMEM = 56 * 1024 * 1024
 
 
@@ -199,23 +200,30 @@
             plane[p, c, :, lanes] = value[c * HALF : (c + 1) * HALF, p * BLK : (p + 1) * BLK]
 
 
-def offset_forward(low_half, high_half, upper, turn):
-    first = [low_half[c] + high_half[c] for c in range(2)]
-    second = cmul(low_half[0] - high_half[0], low_half[1] - high_half[1], turn[0], -turn[1])
-    value = jnp.concatenate(
-        [jnp.concatenate(first, axis=0), jnp.concatenate(second, axis=0)], axis=1
-    )
-    return left_product(upper[...], value)
-
-
-def offset_inverse(value, lower, turn):
-    value = left_product(lower[...], value)
-    first = value[:HALF, :BLK], value[HALF:, :BLK]
-    second = cmul(value[:HALF, BLK:], value[HALF:, BLK:], turn[0], turn[1])
-    return (
-        [first[c] + second[c] for c in range(2)],
-        [first[c] - second[c] for c in range(2)],
-    )
+def offset_forward(pairs, upper, turn):
+    parts = []
+    for low_half, high_half in pairs:
+        first = [low_half[c] + high_half[c] for c in range(2)]
+        second = cmul(low_half[0] - high_half[0], low_half[1] - high_half[1], turn[0], -turn[1])
+        parts += [jnp.concatenate(first, axis=0), jnp.concatenate(second, axis=0)]
+    value = left_product(upper[...], jnp.concatenate(parts, axis=1))
+    return [value[:, n * 2 * BLK : (n + 1) * 2 * BLK] for n in range(len(pairs))]
+
+
+def offset_inverse(columns, lower, turn):
+    value = left_product(lower[...], jnp.concatenate(columns, axis=1))
+    pairs = []
+    for n in range(len(columns)):
+        part = value[:, n * 2 * BLK : (n + 1) * 2 * BLK]
+        first = part[:HALF, :BLK], part[HALF:, :BLK]
+        second = cmul(part[:HALF, BLK:], part[HALF:, BLK:], turn[0], turn[1])
+        pairs.append(
+            (
+                [first[c] + second[c] for c in range(2)],
+                [first[c] - second[c] for c in range(2)],
+            )
+        )
+    return pairs
 
 
 def layer_turn(halves_in, layer_ref, step, a):
@@ -284,15 +292,22 @@
 
     scales[...] = scale_of(code_ref[:, :, outer].reshape(slots, BLK))
 
-    @pl.loop(0, outer, unroll=4)
-    def _(a):
-        real, imag = unpacked(code_ref[:, :, a].reshape(slots, BLK))
-        scale = scales[...]
-        value = jnp.concatenate([real * scale, imag * scale], axis=1)
-        moved = dot(pick_ref[...], jnp.concatenate(halves(value), axis=0))
-        low_half = [moved[:HALF, :BLK], moved[:HALF, BLK:]]
-        high_half = [moved[HALF:, :BLK], moved[HALF:, BLK:]]
-        store_column(plane, a, offset_forward(low_half, high_half, rows_forward, turn))
+    @pl.loop(0, outer // COLUMNS, unroll=2)
+    def _(at):
+        pairs = []
+        for a in range(COLUMNS):
+            real, imag = unpacked(code_ref[:, :, at * COLUMNS + a].reshape(slots, BLK))
+            scale = scales[...]
+            value = jnp.concatenate([real * scale, imag * scale], axis=1)
+            moved = dot(pick_ref[...], jnp.concatenate(halves(value), axis=0))
+            pairs.append(
+                (
+                    [moved[:HALF, :BLK], moved[:HALF, BLK:]],
+                    [moved[HALF:, :BLK], moved[HALF:, BLK:]],
+                )
+            )
+        for a, value in enumerate(offset_forward(pairs, rows_forward, turn)):
+            store_column(plane, at * COLUMNS + a, value)
 
     for step in range(steps):
         midpoint_pass(
@@ -300,19 +315,21 @@
         )
         if step < steps - 1:
 
-            @pl.loop(0, outer, unroll=4)
-            def _(a):
-                parts = offset_inverse(column_of(other, a), rows_inverse, turn)
-                parts = layer_turn(parts, layer_ref, step, a)
-                store_column(plane, a, offset_forward(parts[0], parts[1], rows_forward, turn))
+            @pl.loop(0, outer // COLUMNS, unroll=2)
+            def _(at):
+                places = [at * COLUMNS + a for a in range(COLUMNS)]
+                pairs = offset_inverse([column_of(other, a) for a in places], rows_inverse, turn)
+                pairs = [layer_turn(p, layer_ref, step, a) for p, a in zip(pairs, places)]
+                for a, value in zip(places, offset_forward(pairs, rows_forward, turn)):
+                    store_column(plane, a, value)
 
 
 def finish_kernel(dest_ref, layer_ref, plane_ref, rows_inverse, offset_ref, out_ref):
     here = plane_ref.shape[3] // BLK
     turn = offset_ref[0], offset_ref[1]
+    pairs = offset_inverse([column_of(plane_ref, at) for at in range(here)], rows_inverse, turn)
     for at in range(here):
-        parts = offset_inverse(column_of(plane_ref, at), rows_inverse, turn)
-        parts = layer_turn(parts, layer_ref, layer_ref.shape[1] - 1, dest_ref[0] * here + at)
+        parts = layer_turn(pairs[at], layer_ref, layer_ref.shape[1] - 1, dest_ref[0] * here + at)
         for c in range(2):
             both = jnp.maximum(jnp.abs(parts[0][c]), jnp.abs(parts[1][c]))
             code = scale_code(jnp.max(both, axis=0, keepdims=True))
@@ -324,13 +341,29 @@
 
 
 def result_kernel(freq_ref, code_ref, *rest):
-    out_ref = rest[-1]
-    tall = out_ref.shape[2]
-    per = code_ref.shape[0] // tall - 1
-    scale = scale_of(code_ref[per * tall :])
-    first, second = unpacked(code_ref[: per * tall].reshape(per, tall, BLK))
-    out_ref[0, :per] = first * scale[None]
-    out_ref[0, per:] = second * scale[None]
+    out_ref, words, sem = rest[-3:]
+    chunk, tall = out_ref.shape[1:3]
+    per = words.shape[0] // tall - 1
+    at = pl.program_id(0)
+    chunks = per // chunk
+
+    @pl.when(at == 0)
+    def _():
+        copy = pltpu.make_async_copy(code_ref, words, sem)
+        copy.start()
+        copy.wait()
+
+    scale = scale_of(words[per * tall :])[None]
+    rows = pl.ds(pl.multiple_of((at % chunks) * chunk * tall, chunk * tall), chunk * tall)
+    here = words[rows].reshape(chunk, tall, BLK)
+
+    @pl.when(at < chunks)
+    def _():
+        out_ref[0] = unpacked(here)[0] * scale
+
+    @pl.when(at >= chunks)
+    def _():
+        out_ref[0] = unpacked(here)[1] * scale
 
 
 def take_kernel(mine_ref, counts_ref, source_ref, out_ref, sems):
@@ -406,6 +439,18 @@
     smem = pl.BlockSpec(memory_space=pltpu.SMEM)
     vmem = pl.BlockSpec(memory_space=pltpu.VMEM)
     hbm = pl.BlockSpec(memory_space=pl.ANY)
+    pairs = fl * 2
+
+    def extra(whole_numbers, copies):
+        flat = whole_numbers.astype(jnp.bfloat16).reshape(1, 1, 1, -1)
+        flat = jnp.pad(flat, ((0, 0), (0, 0), (0, pairs - 1), (0, mid_local - flat.shape[3])))
+        return jnp.broadcast_to(flat, (1, copies, pairs, mid_local))
+
+    lists = jnp.concatenate([counts[:, None], targets], axis=1)
+    data = bins_data.reshape(bins_local, off_count, pairs, mid_local)
+    data = jnp.concatenate([data, extra(lists, off_count)], axis=0)
+    data = lax.all_to_all(data, "off", split_axis=1, concat_axis=0, tiled=True)
+
     own = pl.pallas_call(
         take_kernel,
         in_specs=[smem, smem, hbm],
@@ -414,7 +459,7 @@
         scratch_shapes=[pltpu.SemaphoreType.DMA((per_device,))],
         name="take_own",
     )(mine.reshape(1), counts, operators)
-    bins_data, own = lax.optimization_barrier((bins_data, own))
+    data, own = lax.optimization_barrier((data, own))
     cores = 2 if off_count % 2 == 0 else 1
     line = off_count // cores
     assert line & (line - 1) == 0 and fl & (fl - 1) == 0
@@ -425,17 +470,6 @@
     if cores > 1:
         shares += [lax.ppermute(x, "off", [(i, i ^ 1) for i in range(off_count)]) for x in shares]
 
-    pairs = fl * 2
-
-    def extra(whole_numbers, copies):
-        flat = whole_numbers.astype(jnp.bfloat16).reshape(1, 1, 1, -1)
-        flat = jnp.pad(flat, ((0, 0), (0, 0), (0, pairs - 1), (0, mid_local - flat.shape[3])))
-        return jnp.broadcast_to(flat, (1, copies, pairs, mid_local))
-
-    lists = jnp.concatenate([counts[:, None], targets], axis=1)
-    data = bins_data.reshape(bins_local, off_count, pairs, mid_local)
-    data = jnp.concatenate([data, extra(lists, off_count)], axis=0)
-    data = lax.all_to_all(data, "off", split_axis=1, concat_axis=0, tiled=True)
     data = data.reshape(off_count, bins_local + 1, pairs, mid_local)
     lists = data[:, bins_local, 0, : lists.size].astype(jnp.int32).reshape(bins_total, 1 + entries)
     data = data[:, :bins_local].reshape(bins_total, pairs, mid_local)
@@ -453,11 +487,6 @@
     offs, nth, bins, goal = slot_lists(lists[:, 0], lists[:, 1:], bins_local, fl, per_device, room)
     side = (offs % cores != off_at % cores).astype(jnp.int32) * line
     slots = (side + ((offs // cores) ^ (off_at // cores))) * per_device + nth
-    pick = (
-        jnp.tile(goal.reshape(1, fl * room), (1, 2))
-        == lax.broadcasted_iota(jnp.int32, (NH, 2 * fl * room), 0)
-    ).astype(jnp.bfloat16)
-
     own_slots = lax.dynamic_index_in_dim(slots, mine, 0, False)
     own_bins = lax.dynamic_index_in_dim(bins, mine, 0, False)
     list_groups = room // GROUP
@@ -474,7 +503,12 @@
         compiler_params=pltpu.CompilerParams(vmem_limit_bytes=VMEM),
         name="contributions",
     )(own_slots, own_bins, data, *shares)
-    terms, freq_at = lax.optimization_barrier((terms, off_at * fl + mine))
+    terms, goal, layers, freq_at = lax.optimization_barrier((terms, goal, layers, off_at * fl + mine))
+    pick = (
+        jnp.tile(goal.reshape(1, fl * room), (1, 2))
+        == lax.broadcasted_iota(jnp.int32, (NH, 2 * fl * room), 0)
+    ).astype(jnp.bfloat16)
+
     omega = math.pi * (0.1 + 0.8 * (freq_at.astype(jnp.float32) + 0.5) / freq_total)
     row = lax.broadcasted_iota(jnp.int32, (NH, total_mid), 0)
     lane = lax.broadcasted_iota(jnp.int32, (NH, total_mid), 1)
@@ -534,7 +568,6 @@
     for ahead in [*range(fl - 1, 0, -1), 0]:
         dest = (mid_at // fl) * fl + (mine ^ ahead)
         block = finish(dest.reshape(1), layer_turns, plane, tables[1], offset_turn)
-        plane, block = lax.optimization_barrier((plane, block))
         if ahead:
             block = lax.ppermute(block, "mid", [(s, s ^ ahead) for s in range(mid_count)])
         got[ahead] = block
@@ -547,9 +580,10 @@
             result_kernel,
             grid_spec=pltpu.PrefetchScalarGridSpec(
                 num_scalar_prefetch=1,
-                grid=(1,),
-                in_specs=[pl.BlockSpec((rows_out, BLK), lambda i, f: (0, 0))] + ([] if first else [hbm]),
-                out_specs=pl.BlockSpec((1, NH, 2 * here, BLK), lambda i, f: (f[0], 0, 0, 0)),
+                grid=(NH // (HALF // 2),),
+                in_specs=[hbm] if first else [hbm, hbm],
+                out_specs=pl.BlockSpec((1, HALF // 2, 2 * here, BLK), lambda i, f: (f[0], i, 0, 0)),
+                scratch_shapes=[pltpu.VMEM((rows_out, BLK), jnp.int32), pltpu.SemaphoreType.DMA],
             ),
             out_shape=jax.ShapeDtypeStruct((fl, NH, 2 * here, BLK), jnp.float32),
             input_output_aliases={} if first else {2: 0},

time: 143 us -> 139 us (0.972); the launches traced: 142 us -> 137 us
  waiting for transfers between devices: 27.7 us -> 19 us
  Pallas kernels: 57.7 us -> 59.6 us
    ppermute x3, waiting for transfers between devices: 11.2 us -> 5.67 us  [local(): lax.ppermute(own, 'off', [(i, (i // cores ^ away) * cores + i % cores) fo...]
    ppermute x3, waiting for transfers between devices: 9.77 us -> 6.46 us  [local(): lax.ppermute(block, 'mid', [(s, s ^ ahead) for s in range(mid_count)])]
    pallas_call x4, Pallas kernels: 8.53 us -> 10.5 us  [local(): pl.pallas_call(result_kernel, grid_spec=pltpu.PrefetchScalarGridSpec(num_...]
    unnamed x28 -> x25, local copies, waits for them, and re-layouts: 4.43 us -> 5.47 us
  transfers between devices with their start and end apart: 12 -> 12, of which waited for: 5 -> 6; matrix products, arithmetic and copies ran while one was open for 16% -> 14% of each run, Pallas kernels for 9% -> 14%
where the time goes in v4:
time: 139 us; the launch traced here: 137 us
  Pallas kernels  59.6 us (43%)
  waiting for transfers between devices  19 us (14%)
  other arithmetic  18.7 us (13%)
  starting transfers between devices  18.5 us (13%)
  blocking collectives  11 us (8%)
  local copies, waits for them, and re-layouts  9.33 us (7%)
    pallas_call x1, Pallas kernels, local(): pl.pallas_call(march_kernel, in_specs=[smem] + [vmem] * 10, out_specs=vme...  28.6 us
    mul x1, other arithmetic, local(): x * (1.0 / (NH * total_mid))  13.9 us
    pallas_call x4, Pallas kernels, local(): block = finish(dest.reshape(1), layer_turns, plane, tables[1], offset_turn)  12.5 us
    all_gather x1, blocking collectives, local(): data = lax.all_gather(data, 'mid', axis=0)  11 us
    pallas_call x4, Pallas kernels, local(): pl.pallas_call(result_kernel, grid_spec=pltpu.PrefetchScalarGridSpec(num_...  10.5 us
    ppermute x3, waiting for transfers between devices, local(): lax.ppermute(block, 'mid', [(s, s ^ ahead) for s in range(mid_count)])  6.46 us
    all_to_all x1, starting transfers between devices, local(): data = lax.all_to_all(data, 'off', split_axis=1, concat_axis=0, tiled=True)  6.33 us
    ppermute x3, waiting for transfers between devices, local(): lax.ppermute(own, 'off', [(i, (i // cores ^ away) * cores + i % cores) fo...  5.67 us
  transfers between devices with their start and end apart: 12, of which 6 were waited for; matrix products, arithmetic and copies ran while one was open for 14% of the time, Pallas kernels for 14%

profile of v4, /device:TPU:0, one launch (start us, length us, event | category | flops | bytes accessed | tf_op | source)
XLA Modules:
  0.0 136.7 jit_solution(10021135743436762792)
XLA Ops:
  3.8 6.3 %all-to-all-start = ((bf16[3,8,8,512]{3,2,0,1:T(8,128)(2,1)}), bf16[3,8,8,512]{3,2,0,1:T(8,128)(2,1)S(1)}, u32[]{:S(2)}, u32[]{:S(2)}) async-start(bf16[3,8,8,512]{3,2,0,1:T(8,128)(2,1)} %copy.46), calls=%async_computation | async-start | bytes 393216 | tf_op jit(solution)/shard_map/all_to_all | solution.py:452
  11.1 2.3 %take_own.1.rest_0_ = bf16[8,128,128]{2,1,0:T(8,128)(2,1)} custom-call(s32[1]{0:T(128)} %bitcast.8.mine_ref.freq_ref, s32[2]{0:T(128)} %counts_ref.1, bf16[2,16,128,128]{3,2,1,0:T(8,128)(2,1)} %source_ref.1), custom_call_target="tpu_custom_call" | custom-call | tf_op jit(solution)/shard_map/take_own/pallas_call | solution.py:454
  13.5 4.9 %all-to-all-done = bf16[3,8,8,512]{3,2,0,1:T(8,128)(2,1)S(1)} async-done(((bf16[3,8,8,512]{3,2,0,1:T(8,128)(2,1)}), bf16[3,8,8,512]{3,2,0,1:T(8,128)(2,1)S(1)}, u32[]{:S(2)}, u32[]{:S(2)}) %all-to-all-start) | async-done | bytes 196640 | tf_op jit(solution)/shard_map/all_to_all | solution.py:452
  19.4 1.4 %collective-permute-start.1 = (bf16[8,128,128]{2,1,0:T(8,128)(2,1)}, bf16[8,128,128]{2,1,0:T(8,128)(2,1)S(1)}, u32[]{:S(2)}, u32[]{:S(2)}) collective-permute-start(bf16[8,128,128]{2,1,0:T(8,128)(2,1)} %take_own.1.rest_0_), channel_id=1, source_target_pairs={{0,4},{1,5},{2,6},{3,7},{4,0},{5,1},{6,2},{7,3},{8,12},{9,13},{10,... | collective-permute-start | bytes 786440 | tf_op jit(solution)/shard_map/ppermute | solution.py:467
  20.9 2.6 %collective-permute-start.2 = (bf16[8,128,128]{2,1,0:T(8,128)(2,1)}, bf16[8,128,128]{2,1,0:T(8,128)(2,1)S(1)}, u32[]{:S(2)}, u32[]{:S(2)}) collective-permute-start(bf16[8,128,128]{2,1,0:T(8,128)(2,1)} %take_own.1.rest_0_), channel_id=1, source_target_pairs={{0,6},{1,7},{2,4},{3,5},{4,2},{5,3},{6,0},{7,1},{8,14},{9,15},{10,... | collective-permute-start | bytes 786440 | tf_op jit(solution)/shard_map/ppermute | solution.py:467
  23.8 11.0 %all-gather = bf16[68,8,512]{2,1,0:T(8,128)(2,1)S(1)} all-gather(bf16[17,8,512]{2,1,0:T(8,128)(2,1)S(1)} %pad_maximum_fusion.1), channel_id=2, replica_groups=mesh['mid'=4,'off'=8] {'mid'}, dimensions={0}, use_global_device_ids=true | all-gather | bytes 696320 | tf_op jit(solution)/shard_map/all_gather | solution.py:477
  35.4 5.7 %collective-permute-done.1.rest_2_ = bf16[8,128,128]{2,1,0:T(8,128)(2,1)S(1)} collective-permute-done((bf16[8,128,128]{2,1,0:T(8,128)(2,1)}, bf16[8,128,128]{2,1,0:T(8,128)(2,1)S(1)}, u32[]{:S(2)}, u32[]{:S(2)}) %collective-permute-start.1) | collective-permute-done | bytes 262176 | tf_op jit(solution)/shard_map/ppermute | solution.py:467
  44.4 5.6 %contributions.1 = s32[4,5,17,8,128]{4,3,2,1,0:T(8,128)} custom-call(s32[40]{0:T(128)} %get-tuple-element.27.slot_ref, s32[40]{0:T(128)} %get-tuple-element.26.bin_ref, bf16[16,128,128]{2,1,0:T(8,128)(2,1)} %bitcast.49, bf16[8,128,128]{2,1,0:T(8,128)(2,1)} %take_own.1.rest_0_, bf16[8,128,128]{2,1,0:T(8,128)(2,1)} %copy-done.4, ...), custom_call_target="tpu_custom_call" | custom-call | tf_op jit(solution)/shard_map/contributions/pallas_call | solution.py:493
  50.1 3.7 %all-to-all-start.1 = ((s32[4,5,17,8,128]{4,3,2,1,0:T(8,128)}), s32[4,5,17,8,128]{4,3,2,1,0:T(8,128)S(1)}, u32[]{:S(2)}, u32[]{:S(2)}) async-start(s32[4,5,17,8,128]{4,3,2,1,0:T(8,128)} %contributions.1), calls=%async_computation.1 | async-start | bytes 2785280 | tf_op jit(solution)/shard_map/all_to_all | solution.py:526
  55.6 13.9 %multiply_multiply_fusion = (f32[256,2048]{1,0:T(8,128)}, f32[256,2048]{1,0:T(8,128)}) fusion(s32[256]{0:T(256)S(1)} %get-tuple-element.34, s32[256]{0:T(256)S(1)} %get-tuple-element.39, pred[256]{0:T(512)(128)(4,1)S(1)} %get-tuple-element.36, s32[256]{0:T(256)S(1)} %get-tuple-element.35, s32[256]{0:T(256)S(1)} %get-tuple-element.38, ...), kind=kLoop, calls=%fused_computation.14 | loop fusion | flops 38797312 | bytes 4235780 | tf_op jit(solution)/shard_map/mul | solution.py:518
  69.5 2.0 %all-to-all-done.1.code_ref = s32[4,5,17,8,128]{4,3,2,1,0:T(8,128)S(1)} async-done(((s32[4,5,17,8,128]{4,3,2,1,0:T(8,128)}), s32[4,5,17,8,128]{4,3,2,1,0:T(8,128)S(1)}, u32[]{:S(2)}, u32[]{:S(2)}) %all-to-all-start.1) | async-done | bytes 1392672 | tf_op jit(solution)/shard_map/all_to_all | solution.py:526
  71.5 1.1 copy-done
  72.6 28.6 %march.1.plane_ref = f32[2,2,128,2048]{3,2,1,0:T(8,128)} custom-call(f32[2,2,8,16]{3,2,1,0:T(8,128)} %pad_maximum_fusion.2.layer_ref, s32[4,5,17,8,128]{4,3,2,1,0:T(8,128)} %copy-done, bf16[256,320]{1,0:T(8,128)(2,1)} %fusion.8.pick_ref, f32[256,2048]{1,0:T(8,128)} %get-tuple-element.20.phase_real, f32[256,2048]{1,0:T(8,128)} %get-tuple-element.19.phase_imag, ...), custom_call_target="tpu_custom_call" | custom-call | tf_op jit(solution)/shard_map/march/pallas_call | solution.py:535
  101.2 3.1 %finish.5 = s32[1032,128]{1,0:T(8,128)} custom-call(s32[1]{0:T(128)} %bitcast.23.dest_ref, f32[2,2,8,16]{3,2,1,0:T(8,128)} %pad_maximum_fusion.2.layer_ref, f32[2,2,128,2048]{3,2,1,0:T(8,128)} %march.1.plane_ref, bf16[256,768]{1,0:T(8,128)(2,1)} %constant.233.clone.rows_inverse, f32[2,128,128]{2,1,0:T(8,128)} %constant.237.clone.offset_ref), custom_call_target="tpu_custom_call" | custom-call | flops 402653184 | bytes 786432 | tf_op jit(solution)/shard_map/finish/pallas_call | solution.py:570
  104.3 1.5 %collective-permute-start.8 = (s32[1032,128]{1,0:T(8,128)}, s32[1032,128]{1,0:T(8,128)S(1)}, u32[]{:S(2)}, u32[]{:S(2)}) collective-permute-start(s32[1032,128]{1,0:T(8,128)} %finish.5), channel_id=1, source_target_pairs={{0,16},{8,24},{16,0},{24,8},{1,17},{9,25},{17,1},{25,9},{2,18},{10... | collective-permute-start | bytes 1585160 | tf_op jit(solution)/shard_map/ppermute | solution.py:572
  105.7 3.1 %finish.6 = s32[1032,128]{1,0:T(8,128)} custom-call(s32[1]{0:T(128)} %bitcast.25.dest_ref, f32[2,2,8,16]{3,2,1,0:T(8,128)} %pad_maximum_fusion.2.layer_ref, f32[2,2,128,2048]{3,2,1,0:T(8,128)} %march.1.plane_ref, bf16[256,768]{1,0:T(8,128)(2,1)} %constant.233.clone.rows_inverse, f32[2,128,128]{2,1,0:T(8,128)} %constant.237.clone.offset_ref), custom_call_target="tpu_custom_call" | custom-call | flops 402653184 | bytes 786432 | tf_op jit(solution)/shard_map/finish/pallas_call | solution.py:570
  108.9 1.4 %collective-permute-start.9 = (s32[1032,128]{1,0:T(8,128)}, s32[1032,128]{1,0:T(8,128)S(1)}, u32[]{:S(2)}, u32[]{:S(2)}) collective-permute-start(s32[1032,128]{1,0:T(8,128)} %finish.6), channel_id=1, source_target_pairs={{0,24},{8,16},{16,8},{24,0},{1,25},{9,17},{17,9},{25,1},{2,26},{10... | collective-permute-start | bytes 1585160 | tf_op jit(solution)/shard_map/ppermute | solution.py:572
  110.3 3.1 %finish.4 = s32[1032,128]{1,0:T(8,128)} custom-call(s32[1]{0:T(128)} %bitcast.1.dest_ref, f32[2,2,8,16]{3,2,1,0:T(8,128)} %pad_maximum_fusion.2.layer_ref, f32[2,2,128,2048]{3,2,1,0:T(8,128)} %march.1.plane_ref, bf16[256,768]{1,0:T(8,128)(2,1)} %constant.233.clone.rows_inverse, f32[2,128,128]{2,1,0:T(8,128)} %constant.237.clone.offset_ref), custom_call_target="tpu_custom_call" | custom-call | flops 402653184 | bytes 786432 | tf_op jit(solution)/shard_map/finish/pallas_call | solution.py:570
  114.0 3.1 %finish.7.code_ref = s32[1032,128]{1,0:T(8,128)} custom-call(s32[1]{0:T(128)} %bitcast.26.dest_ref, f32[2,2,8,16]{3,2,1,0:T(8,128)} %pad_maximum_fusion.2.layer_ref, f32[2,2,128,2048]{3,2,1,0:T(8,128)} %march.1.plane_ref, bf16[256,768]{1,0:T(8,128)(2,1)} %constant.233.clone.rows_inverse, f32[2,128,128]{2,1,0:T(8,128)} %constant.237.clone.offset_ref), custom_call_target="tpu_custom_call" | custom-call | flops 402653184 | bytes 786432 | tf_op jit(solution)/shard_map/finish/pallas_call | solution.py:570
  117.2 2.6 %result.4.rest_0_ = f32[4,256,8,128]{3,2,1,0:T(8,128)} custom-call(s32[1]{0:T(128)} %bitcast.8.mine_ref.freq_ref, s32[1032,128]{1,0:T(8,128)} %finish.7.code_ref), custom_call_target="tpu_custom_call" | custom-call | flops 524288 | bytes 1572864 | tf_op jit(solution)/shard_map/result/pallas_call | solution.py:579
  119.8 5.2 %collective-permute-done.9.code_ref = s32[1032,128]{1,0:T(8,128)S(1)} collective-permute-done((s32[1032,128]{1,0:T(8,128)}, s32[1032,128]{1,0:T(8,128)S(1)}, u32[]{:S(2)}, u32[]{:S(2)}) %collective-permute-start.9) | collective-permute-done | bytes 528416 | tf_op jit(solution)/shard_map/ppermute | solution.py:572
  125.8 2.6 %result.5.rest_0_ = f32[4,256,8,128]{3,2,1,0:T(8,128)} custom-call(s32[1]{0:T(128)} %bitcast.24.freq_ref, s32[1032,128]{1,0:T(8,128)} %copy-done.3, f32[4,256,8,128]{3,2,1,0:T(8,128)} %result.4.rest_0_), custom_call_target="tpu_custom_call", output_to_operand_aliasing={{}: (2, {})} | custom-call | flops 524288 | bytes 1572864 | tf_op jit(solution)/shard_map/result/pallas_call | solution.py:579
  129.6 2.6 %result.6.rest_0_ = f32[4,256,8,128]{3,2,1,0:T(8,128)} custom-call(s32[1]{0:T(128)} %bitcast.22.freq_ref, s32[1032,128]{1,0:T(8,128)} %copy-done.1, f32[4,256,8,128]{3,2,1,0:T(8,128)} %result.5.rest_0_), custom_call_target="tpu_custom_call", output_to_operand_aliasing={{}: (2, {})} | custom-call | flops 524288 | bytes 1572864 | tf_op jit(solution)/shard_map/result/pallas_call | solution.py:579
  134.0 2.6 %result.7 = f32[4,256,8,128]{3,2,1,0:T(8,128)} custom-call(s32[1]{0:T(128)} %bitcast.freq_ref, s32[1032,128]{1,0:T(8,128)} %copy-done.2, f32[4,256,8,128]{3,2,1,0:T(8,128)} %result.6.rest_0_), custom_call_target="tpu_custom_call", output_to_operand_aliasing={{}: (2, {})} | custom-call | flops 524288 | bytes 1572864 | tf_op jit(solution)/shard_map/result/pallas_call | solution.py:579
  (91 shorter events, 16.0 us)
Async XLA Ops:
  3.8 14.7 %all-to-all-start = ((bf16[3,8,8,512]{3,2,0,1:T(8,128)(2,1)}), bf16[3,8,8,512]{3,2,0,1:T(8,128)(2,1)S(1)}, u32[]{:S(2)}, u32[]{:S(2)}) async-start(bf16[3,8,8,512]{3,2,0,1:T(8,128)(2,1)} %copy.46), calls=%async_computation | async-start | bytes 393216 | tf_op jit(solution)/shard_map/all_to_all | solution.py:452
  19.0 16.3 %collective-permute-start = (bf16[8,128,128]{2,1,0:T(8,128)(2,1)}, bf16[8,128,128]{2,1,0:T(8,128)(2,1)S(1)}, u32[]{:S(2)}, u32[]{:S(2)}) collective-permute-start(bf16[8,128,128]{2,1,0:T(8,128)(2,1)} %take_own.1.rest_0_), channel_id=1, source_target_pairs={{0,2},{1,3},{2,0},{3,1},{4,6},{5,7},{6,4},{7,5},{8,10},{9,11},{10,... | collective-permute-start | bytes 786440 | tf_op jit(solution)/shard_map/ppermute | solution.py:467
  19.4 21.6 %collective-permute-start.1 = (bf16[8,128,128]{2,1,0:T(8,128)(2,1)}, bf16[8,128,128]{2,1,0:T(8,128)(2,1)S(1)}, u32[]{:S(2)}, u32[]{:S(2)}) collective-permute-start(bf16[8,128,128]{2,1,0:T(8,128)(2,1)} %take_own.1.rest_0_), channel_id=1, source_target_pairs={{0,4},{1,5},{2,6},{3,7},{4,0},{5,1},{6,2},{7,3},{8,12},{9,13},{10,... | collective-permute-start | bytes 786440 | tf_op jit(solution)/shard_map/ppermute | solution.py:467
  20.9 20.2 %collective-permute-start.2 = (bf16[8,128,128]{2,1,0:T(8,128)(2,1)}, bf16[8,128,128]{2,1,0:T(8,128)(2,1)S(1)}, u32[]{:S(2)}, u32[]{:S(2)}) collective-permute-start(bf16[8,128,128]{2,1,0:T(8,128)(2,1)} %take_own.1.rest_0_), channel_id=1, source_target_pairs={{0,6},{1,7},{2,4},{3,5},{4,2},{5,3},{6,0},{7,1},{8,14},{9,15},{10,... | collective-permute-start | bytes 786440 | tf_op jit(solution)/shard_map/ppermute | solution.py:467
  23.4 20.0 %collective-permute-start.3 = (bf16[8,128,128]{2,1,0:T(8,128)(2,1)}, bf16[8,128,128]{2,1,0:T(8,128)(2,1)S(1)}, u32[]{:S(2)}, u32[]{:S(2)}) collective-permute-start(bf16[8,128,128]{2,1,0:T(8,128)(2,1)} %take_own.1.rest_0_), channel_id=1, source_target_pairs={{0,1},{1,0},{2,3},{3,2},{4,5},{5,4},{6,7},{7,6},{8,9},{9,8},{10,11... | collective-permute-start | bytes 786440 | tf_op jit(solution)/shard_map/ppermute | solution.py:471
  35.3 8.2 %copy-start.4 = (bf16[8,128,128]{2,1,0:T(8,128)(2,1)}, bf16[8,128,128]{2,1,0:T(8,128)(2,1)S(1)}, u32[]{:S(2)}) copy-start(bf16[8,128,128]{2,1,0:T(8,128)(2,1)S(1)} %collective-permute-done.rest_1_) | copy-start | bytes 786436
  35.3 8.1 %collective-permute-start.4 = (bf16[8,128,128]{2,1,0:T(8,128)(2,1)S(1)}, bf16[8,128,128]{2,1,0:T(8,128)(2,1)S(1)}, u32[]{:S(2)}, u32[]{:S(2)}) collective-permute-start(bf16[8,128,128]{2,1,0:T(8,128)(2,1)S(1)} %collective-permute-done.rest_1_), channel_id=1, source_target_pairs={{0,1},{1,0},{2,3},{3,2},{4,5},{5,4},{6,7},{7,6},{8,9},{9,8},{10,11... | collective-permute-start | bytes 786440 | tf_op jit(solution)/shard_map/ppermute | solution.py:471
  41.0 2.4 %copy-start.5 = (bf16[8,128,128]{2,1,0:T(8,128)(2,1)}, bf16[8,128,128]{2,1,0:T(8,128)(2,1)S(1)}, u32[]{:S(2)}) copy-start(bf16[8,128,128]{2,1,0:T(8,128)(2,1)S(1)} %collective-permute-done.1.rest_2_) | copy-start | bytes 786436
  41.0 2.4 %collective-permute-start.5 = (bf16[8,128,128]{2,1,0:T(8,128)(2,1)S(1)}, bf16[8,128,128]{2,1,0:T(8,128)(2,1)S(1)}, u32[]{:S(2)}, u32[]{:S(2)}) collective-permute-start(bf16[8,128,128]{2,1,0:T(8,128)(2,1)S(1)} %collective-permute-done.1.rest_2_), channel_id=1, source_target_pairs={{0,1},{1,0},{2,3},{3,2},{4,5},{5,4},{6,7},{7,6},{8,9},{9,8},{10,11... | collective-permute-start | bytes 786440 | tf_op jit(solution)/shard_map/ppermute | solution.py:471
  41.0 2.4 %copy-start.6 = (bf16[8,128,128]{2,1,0:T(8,128)(2,1)}, bf16[8,128,128]{2,1,0:T(8,128)(2,1)S(1)}, u32[]{:S(2)}) copy-start(bf16[8,128,128]{2,1,0:T(8,128)(2,1)S(1)} %collective-permute-done.2.rest_3_) | copy-start | bytes 786436
  41.1 2.4 %collective-permute-start.6 = (bf16[8,128,128]{2,1,0:T(8,128)(2,1)S(1)}, bf16[8,128,128]{2,1,0:T(8,128)(2,1)S(1)}, u32[]{:S(2)}, u32[]{:S(2)}) collective-permute-start(bf16[8,128,128]{2,1,0:T(8,128)(2,1)S(1)} %collective-permute-done.2.rest_3_), channel_id=1, source_target_pairs={{0,1},{1,0},{2,3},{3,2},{4,5},{5,4},{6,7},{7,6},{8,9},{9,8},{10,11... | collective-permute-start | bytes 786440 | tf_op jit(solution)/shard_map/ppermute | solution.py:471
  43.4 0.7 copy-start.7
  43.4 0.8 copy-start.8
  43.4 0.9 copy-start.9
  43.5 0.9 copy-start.10
  50.0 4.7 %copy-start.11 = (f32[2,16]{1,0:T(2,128)S(1)}, f32[2,16]{1,0:T(2,128)}, u32[]{:S(2)}) copy-start(f32[2,16]{1,0:T(2,128)} %param.17) | copy-start | bytes 388
  50.1 21.4 %all-to-all-start.1 = ((s32[4,5,17,8,128]{4,3,2,1,0:T(8,128)}), s32[4,5,17,8,128]{4,3,2,1,0:T(8,128)S(1)}, u32[]{:S(2)}, u32[]{:S(2)}) async-start(s32[4,5,17,8,128]{4,3,2,1,0:T(8,128)} %contributions.1), calls=%async_computation.1 | async-start | bytes 2785280 | tf_op jit(solution)/shard_map/all_to_all | solution.py:526
  71.5 1.1 copy-start
  104.3 24.5 %collective-permute-start.8 = (s32[1032,128]{1,0:T(8,128)}, s32[1032,128]{1,0:T(8,128)S(1)}, u32[]{:S(2)}, u32[]{:S(2)}) collective-permute-start(s32[1032,128]{1,0:T(8,128)} %finish.5), channel_id=1, source_target_pairs={{0,16},{8,24},{16,0},{24,8},{1,17},{9,25},{17,1},{25,9},{2,18},{10... | collective-permute-start | bytes 1585160 | tf_op jit(solution)/shard_map/ppermute | solution.py:572
  108.9 16.1 %collective-permute-start.9 = (s32[1032,128]{1,0:T(8,128)}, s32[1032,128]{1,0:T(8,128)S(1)}, u32[]{:S(2)}, u32[]{:S(2)}) collective-permute-start(s32[1032,128]{1,0:T(8,128)} %finish.6), channel_id=1, source_target_pairs={{0,24},{8,16},{16,8},{24,0},{1,25},{9,17},{17,9},{25,1},{2,26},{10... | collective-permute-start | bytes 1585160 | tf_op jit(solution)/shard_map/ppermute | solution.py:572
  113.4 19.7 %collective-permute-start.7 = (s32[1032,128]{1,0:T(8,128)}, s32[1032,128]{1,0:T(8,128)S(1)}, u32[]{:S(2)}, u32[]{:S(2)}) collective-permute-start(s32[1032,128]{1,0:T(8,128)} %finish.4), channel_id=1, source_target_pairs={{0,8},{8,0},{16,24},{24,16},{1,9},{9,1},{17,25},{25,17},{2,10},{10... | collective-permute-start | bytes 1585160 | tf_op jit(solution)/shard_map/ppermute | solution.py:572
  125.0 0.8 copy-start.3
  128.8 0.8 copy-start.1
  133.2 0.8 copy-start.2

commit v5 on v4

--- a/solution.py
+++ b/solution.py
@@ -20,7 +20,11 @@
 TOP = 32767.0
 GROUP = 8
 COLUMNS = 2
-VMEM = 56 * 1024 * 1024
+ROWS = 8
+CHUNKS = 4
+UNROLL = 2
+VMEM = 28 * 1024 * 1024
+SMALL = 10 * 1024 * 1024
 
 
 def signed_wave(index, length):
@@ -200,84 +204,98 @@
             plane[p, c, :, lanes] = value[c * HALF : (c + 1) * HALF, p * BLK : (p + 1) * BLK]
 
 
-def offset_forward(pairs, upper, turn):
-    parts = []
-    for low_half, high_half in pairs:
-        first = [low_half[c] + high_half[c] for c in range(2)]
-        second = cmul(low_half[0] - high_half[0], low_half[1] - high_half[1], turn[0], -turn[1])
-        parts += [jnp.concatenate(first, axis=0), jnp.concatenate(second, axis=0)]
-    value = left_product(upper[...], jnp.concatenate(parts, axis=1))
-    return [value[:, n * 2 * BLK : (n + 1) * 2 * BLK] for n in range(len(pairs))]
-
-
-def offset_inverse(columns, lower, turn):
-    value = left_product(lower[...], jnp.concatenate(columns, axis=1))
-    pairs = []
-    for n in range(len(columns)):
-        part = value[:, n * 2 * BLK : (n + 1) * 2 * BLK]
-        first = part[:HALF, :BLK], part[HALF:, :BLK]
-        second = cmul(part[:HALF, BLK:], part[HALF:, BLK:], turn[0], turn[1])
-        pairs.append(
-            (
-                [first[c] + second[c] for c in range(2)],
-                [first[c] - second[c] for c in range(2)],
-            )
-        )
-    return pairs
-
-
-def layer_turn(halves_in, layer_ref, step, a):
-    blocks = layer_ref.shape[2]
-    tall = NH // blocks
-    results = []
-    for p in range(2):
-        parts = [[], []]
-        for at in range(HALF // tall):
-            block = p * (HALF // tall) + at
-            cos, sin = layer_ref[0, step, block, a], layer_ref[1, step, block, a]
-            rows = slice(at * tall, (at + 1) * tall)
-            real, imag = cmul(halves_in[p][0][rows], halves_in[p][1][rows], cos, sin)
-            parts[0].append(real)
-            parts[1].append(imag)
-        results.append([jnp.concatenate(part, axis=0) for part in parts])
-    return results
-
-
-def midpoint_pass(plane, out, phase_refs, forward, inverse, middle_ref, rows):
+def row_blocks(tall):
+    return [slice(at * tall, (at + 1) * tall) for at in range(HALF // tall)]
+
+
+def turn_at(offset_ref, rows):
+    return offset_ref[0, rows], offset_ref[1, rows]
+
+
+def forward_rows(low, high, turn):
+    first = low[0] + high[0], low[1] + high[1]
+    second = cmul(low[0] - high[0], low[1] - high[1], turn[0], -turn[1])
+    return (*first, *second)
+
+
+def inverse_rows(value, rows, turn):
+    upper, below = rows, slice(HALF + rows.start, HALF + rows.stop)
+    first = value[upper, :BLK], value[below, :BLK]
+    second = cmul(value[upper, BLK:], value[below, BLK:], turn[0], turn[1])
+    low = first[0] + second[0], first[1] + second[1]
+    high = first[0] - second[0], first[1] - second[1]
+    return low, high
+
+
+def assembled(blocks):
+    parts = [jnp.concatenate(part, axis=0) for part in zip(*blocks)]
+    return jnp.concatenate(
+        [jnp.concatenate(parts[:2], axis=0), jnp.concatenate(parts[2:], axis=0)], axis=1
+    )
+
+
+def offset_product(table, columns):
+    value = left_product(table[...], jnp.concatenate(columns, axis=1))
+    return [value[:, n * 2 * BLK : (n + 1) * 2 * BLK] for n in range(len(columns))]
+
+
+def layer_turn(pair, layer_ref, step, block, a):
+    half = layer_ref.shape[2] // 2
+    return [
+        cmul(*part, layer_ref[0, step, block + p * half, a], layer_ref[1, step, block + p * half, a])
+        for p, part in enumerate(pair)
+    ]
+
+
+def midpoint_pass(plane, out, phase_refs, forward, inverse, middle_ref):
     outer = middle_ref.shape[1]
-    per_half = HALF // rows
-
-    @pl.loop(0, 2 * per_half, unroll=4)
+    lanes = [slice(a * BLK, (a + 1) * BLK) for a in range(outer)]
+    tall = ROWS * CHUNKS
+    per_half = HALF // tall
+
+    @pl.loop(0, 2 * per_half, unroll=UNROLL)
     def _(at):
         p = at // per_half
-        here = pl.ds(pl.multiple_of((at % per_half) * rows, rows), rows)
-        there = pl.ds(pl.multiple_of(at * rows, rows), rows)
-        lanes = [slice(a * BLK, (a + 1) * BLK) for a in range(outer)]
-        values = [(plane[p, 0, here, lane], plane[p, 1, here, lane]) for lane in lanes]
-        values = small_transform(values, -1)
-        turned = []
-        for a in range(outer):
-            real, imag = cmul(*values[a], middle_ref[0, a : a + 1], -middle_ref[1, a : a + 1])
-            turned.append(jnp.concatenate([real, imag], axis=1))
-        value = right_product(jnp.concatenate(turned, axis=0), forward[...])
-        turned = []
-        for a in range(outer):
-            part = value[a * rows : (a + 1) * rows]
-            real, imag = cmul(
-                part[:, :BLK], part[:, BLK:], phase_refs[0][there, lanes[a]], phase_refs[1][there, lanes[a]]
-            )
-            turned.append(jnp.concatenate([real, imag], axis=1))
-        value = right_product(jnp.concatenate(turned, axis=0), inverse[...])
-        values = []
-        for a in range(outer):
-            part = value[a * rows : (a + 1) * rows]
-            values.append(
-                cmul(part[:, :BLK], part[:, BLK:], middle_ref[0, a : a + 1], middle_ref[1, a : a + 1])
-            )
-        values = small_transform(values, 1)
-        for a in range(outer):
-            out[p, 0, here, lanes[a]] = values[a][0]
-            out[p, 1, here, lanes[a]] = values[a][1]
+        base = pl.multiple_of((at % per_half) * tall, tall)
+        phase_base = pl.multiple_of(at * tall, tall)
+
+        def gathered(pieces):
+            return jnp.concatenate([jnp.concatenate(pair, axis=1) for pair in pieces], axis=0)
+
+        pieces = []
+        for chunk in range(CHUNKS):
+            here = pl.ds(base + chunk * ROWS, ROWS)
+            values = [(plane[p, 0, here, lane], plane[p, 1, here, lane]) for lane in lanes]
+            values = small_transform(values, -1)
+            for a in range(outer):
+                pieces.append(cmul(*values[a], middle_ref[0, a : a + 1], -middle_ref[1, a : a + 1]))
+        value = right_product(gathered(pieces), forward[...])
+        pieces = []
+        for chunk in range(CHUNKS):
+            there = pl.ds(phase_base + chunk * ROWS, ROWS)
+            for a in range(outer):
+                row = (chunk * outer + a) * ROWS
+                part = value[row : row + ROWS]
+                pieces.append(
+                    cmul(
+                        part[:, :BLK], part[:, BLK:],
+                        phase_refs[0][there, lanes[a]], phase_refs[1][there, lanes[a]],
+                    )
+                )
+        value = right_product(gathered(pieces), inverse[...])
+        for chunk in range(CHUNKS):
+            here = pl.ds(base + chunk * ROWS, ROWS)
+            values = []
+            for a in range(outer):
+                row = (chunk * outer + a) * ROWS
+                part = value[row : row + ROWS]
+                values.append(
+                    cmul(part[:, :BLK], part[:, BLK:], middle_ref[0, a : a + 1], middle_ref[1, a : a + 1])
+                )
+            values = small_transform(values, 1)
+            for a in range(outer):
+                out[p, 0, here, lanes[a]] = values[a][0]
+                out[p, 1, here, lanes[a]] = values[a][1]
 
 
 def march_kernel(
@@ -288,82 +306,83 @@
     outer = middle_ref.shape[1]
     steps = layer_ref.shape[1]
     slots = sources * groups * GROUP
-    turn = offset_ref[0], offset_ref[1]
+    tall = NH // layer_ref.shape[2]
 
     scales[...] = scale_of(code_ref[:, :, outer].reshape(slots, BLK))
 
     @pl.loop(0, outer // COLUMNS, unroll=2)
     def _(at):
-        pairs = []
+        columns = []
         for a in range(COLUMNS):
             real, imag = unpacked(code_ref[:, :, at * COLUMNS + a].reshape(slots, BLK))
             scale = scales[...]
             value = jnp.concatenate([real * scale, imag * scale], axis=1)
             moved = dot(pick_ref[...], jnp.concatenate(halves(value), axis=0))
-            pairs.append(
-                (
-                    [moved[:HALF, :BLK], moved[:HALF, BLK:]],
-                    [moved[HALF:, :BLK], moved[HALF:, BLK:]],
+            blocks = []
+            for rows in row_blocks(tall):
+                low, high = moved[rows], moved[HALF + rows.start : HALF + rows.stop]
+                blocks.append(
+                    forward_rows(
+                        (low[:, :BLK], low[:, BLK:]), (high[:, :BLK], high[:, BLK:]),
+                        turn_at(offset_ref, rows),
+                    )
                 )
-            )
-        for a, value in enumerate(offset_forward(pairs, rows_forward, turn)):
+            columns.append(assembled(blocks))
+        for a, value in enumerate(offset_product(rows_forward, columns)):
             store_column(plane, at * COLUMNS + a, value)
 
     for step in range(steps):
-        midpoint_pass(
-            plane, other, (phase_real, phase_imag), lanes_forward, lanes_inverse, middle_ref, 16
-        )
+        midpoint_pass(plane, other, (phase_real, phase_imag), lanes_forward, lanes_inverse, middle_ref)
         if step < steps - 1:
 
             @pl.loop(0, outer // COLUMNS, unroll=2)
             def _(at):
                 places = [at * COLUMNS + a for a in range(COLUMNS)]
-                pairs = offset_inverse([column_of(other, a) for a in places], rows_inverse, turn)
-                pairs = [layer_turn(p, layer_ref, step, a) for p, a in zip(pairs, places)]
-                for a, value in zip(places, offset_forward(pairs, rows_forward, turn)):
+                columns = []
+                for a, value in zip(
+                    places, offset_product(rows_inverse, [column_of(other, a) for a in places])
+                ):
+                    blocks = []
+                    for block, rows in enumerate(row_blocks(tall)):
+                        turn = turn_at(offset_ref, rows)
+                        pair = inverse_rows(value, rows, turn)
+                        blocks.append(forward_rows(*layer_turn(pair, layer_ref, step, block, a), turn))
+                    columns.append(assembled(blocks))
+                for a, value in zip(places, offset_product(rows_forward, columns)):
                     store_column(plane, a, value)
 
 
-def finish_kernel(dest_ref, layer_ref, plane_ref, rows_inverse, offset_ref, out_ref):
+def finish_kernel(dest_ref, layer_ref, plane_ref, rows_inverse, offset_ref, *rest):
+    out_ref = rest[-1]
     here = plane_ref.shape[3] // BLK
-    turn = offset_ref[0], offset_ref[1]
-    pairs = offset_inverse([column_of(plane_ref, at) for at in range(here)], rows_inverse, turn)
+    tall = NH // layer_ref.shape[2]
+    step = layer_ref.shape[1] - 1
+    columns = offset_product(rows_inverse, [column_of(plane_ref, at) for at in range(here)])
     for at in range(here):
-        parts = layer_turn(pairs[at], layer_ref, layer_ref.shape[1] - 1, dest_ref[0] * here + at)
+        found = []
+        for block, rows in enumerate(row_blocks(tall)):
+            pair = inverse_rows(columns[at], rows, turn_at(offset_ref, rows))
+            found.append(layer_turn(pair, layer_ref, step, block, dest_ref[0] * here + at))
         for c in range(2):
-            both = jnp.maximum(jnp.abs(parts[0][c]), jnp.abs(parts[1][c]))
-            code = scale_code(jnp.max(both, axis=0, keepdims=True))
+            biggest = functools.reduce(jnp.maximum, [jnp.abs(part[c]) for pair in found for part in pair])
+            code = scale_code(jnp.max(biggest, axis=0, keepdims=True))
             inverse = inverse_scale_of(code)
-            words = packed(coded(parts[0][c], inverse), coded(parts[1][c], inverse))
             row = at * 2 + c
-            out_ref[pl.ds(row, HALF, 2 * here), :] = words
+            for block, pair in enumerate(found):
+                words = packed(coded(pair[0][c], inverse), coded(pair[1][c], inverse))
+                out_ref[pl.ds(block * tall * 2 * here + row, tall, 2 * here), :] = words
             out_ref[pl.ds(HALF * 2 * here + row, 1), :] = code
 
 
 def result_kernel(freq_ref, code_ref, *rest):
-    out_ref, words, sem = rest[-3:]
-    chunk, tall = out_ref.shape[1:3]
-    per = words.shape[0] // tall - 1
-    at = pl.program_id(0)
-    chunks = per // chunk
-
-    @pl.when(at == 0)
-    def _():
-        copy = pltpu.make_async_copy(code_ref, words, sem)
-        copy.start()
-        copy.wait()
-
-    scale = scale_of(words[per * tall :])[None]
-    rows = pl.ds(pl.multiple_of((at % chunks) * chunk * tall, chunk * tall), chunk * tall)
-    here = words[rows].reshape(chunk, tall, BLK)
-
-    @pl.when(at < chunks)
-    def _():
-        out_ref[0] = unpacked(here)[0] * scale
-
-    @pl.when(at >= chunks)
-    def _():
-        out_ref[0] = unpacked(here)[1] * scale
+    out_ref = rest[-1]
+    per, tall = out_ref.shape[1:3]
+    scale = scale_of(code_ref[per * tall :])[None]
+    for half in range(2):
+
+        @pl.when(pl.program_id(0) == half)
+        def _():
+            out_ref[0] = unpacked(code_ref[: per * tall].reshape(per, tall, BLK))[half] * scale
 
 
 def take_kernel(mine_ref, counts_ref, source_ref, out_ref, sems):
@@ -457,16 +476,23 @@
         out_specs=vmem,
         out_shape=jax.ShapeDtypeStruct((per_device, BLK, BLK), jnp.bfloat16),
         scratch_shapes=[pltpu.SemaphoreType.DMA((per_device,))],
+        compiler_params=pltpu.CompilerParams(vmem_limit_bytes=SMALL),
         name="take_own",
     )(mine.reshape(1), counts, operators)
     data, own = lax.optimization_barrier((data, own))
     cores = 2 if off_count % 2 == 0 else 1
     line = off_count // cores
     assert line & (line - 1) == 0 and fl & (fl - 1) == 0
-    shares = [own] + [
-        lax.ppermute(own, "off", [(i, (i // cores ^ away) * cores + i % cores) for i in range(off_count)])
-        for away in range(1, line)
-    ]
+    shares = [own]
+    for away in range(1, line):
+        low = away & -away
+        shares.append(
+            lax.ppermute(
+                shares[away ^ low],
+                "off",
+                [(i, (i // cores ^ low) * cores + i % cores) for i in range(off_count)],
+            )
+        )
     if cores > 1:
         shares += [lax.ppermute(x, "off", [(i, i ^ 1) for i in range(off_count)]) for x in shares]
 
@@ -500,7 +526,7 @@
             pltpu.VMEM((len(shares) * per_device, BLK, BLK), jnp.bfloat16),
             pltpu.SemaphoreType.DMA((len(shares),)),
         ],
-        compiler_params=pltpu.CompilerParams(vmem_limit_bytes=VMEM),
+        compiler_params=pltpu.CompilerParams(vmem_limit_bytes=SMALL),
         name="contributions",
     )(own_slots, own_bins, data, *shares)
     terms, goal, layers, freq_at = lax.optimization_barrier((terms, goal, layers, off_at * fl + mine))
@@ -545,29 +571,34 @@
         name="march",
     )(layer_turns, terms, pick, phase_real, phase_imag, *tables, middle, offset_turn)
 
-    finish = pl.pallas_call(
-        finish_kernel,
-        grid_spec=pltpu.PrefetchScalarGridSpec(
-            num_scalar_prefetch=1,
-            grid=(1,),
-            in_specs=[
-                smem,
-                pl.BlockSpec((2, 2, HALF, mid_local), lambda i, dest: (0, 0, 0, dest[0])),
-                vmem,
-                vmem,
-            ],
-            out_specs=pl.BlockSpec((rows_out, BLK), lambda i, dest: (0, 0)),
-        ),
-        out_shape=jax.ShapeDtypeStruct((rows_out, BLK), jnp.int32),
-        cost_estimate=pl.CostEstimate(
-            flops=6 * NH * NH * 2 * BLK * here, bytes_accessed=6 * NH * mid_local, transcendentals=0
-        ),
-        name="finish",
-    )
-    got = {}
+    def finish(dest, *before):
+        return pl.pallas_call(
+            finish_kernel,
+            grid_spec=pltpu.PrefetchScalarGridSpec(
+                num_scalar_prefetch=1,
+                grid=(1,),
+                in_specs=[
+                    smem,
+                    pl.BlockSpec((2, 2, HALF, mid_local), lambda i, dest: (0, 0, 0, dest[0])),
+                    vmem,
+                    vmem,
+                ]
+                + [hbm] * len(before),
+                out_specs=pl.BlockSpec((rows_out, BLK), lambda i, dest: (0, 0)),
+            ),
+            out_shape=jax.ShapeDtypeStruct((rows_out, BLK), jnp.int32),
+            cost_estimate=pl.CostEstimate(
+                flops=6 * NH * NH * 2 * BLK * here, bytes_accessed=6 * NH * mid_local, transcendentals=0
+            ),
+            compiler_params=pltpu.CompilerParams(vmem_limit_bytes=SMALL),
+            name="finish",
+        )(dest.reshape(1), layer_turns, plane, tables[1], offset_turn, *before)
+
+    got, before = {}, []
     for ahead in [*range(fl - 1, 0, -1), 0]:
         dest = (mid_at // fl) * fl + (mine ^ ahead)
-        block = finish(dest.reshape(1), layer_turns, plane, tables[1], offset_turn)
+        block = finish(dest, *before)
+        before = [block]
         if ahead:
             block = lax.ppermute(block, "mid", [(s, s ^ ahead) for s in range(mid_count)])
         got[ahead] = block
@@ -580,14 +611,13 @@
             result_kernel,
             grid_spec=pltpu.PrefetchScalarGridSpec(
                 num_scalar_prefetch=1,
-                grid=(NH // (HALF // 2),),
-                in_specs=[hbm] if first else [hbm, hbm],
-                out_specs=pl.BlockSpec((1, HALF // 2, 2 * here, BLK), lambda i, f: (f[0], i, 0, 0)),
-                scratch_shapes=[pltpu.VMEM((rows_out, BLK), jnp.int32), pltpu.SemaphoreType.DMA],
+                grid=(2,),
+                in_specs=[vmem] if first else [vmem, hbm],
+                out_specs=pl.BlockSpec((1, HALF, 2 * here, BLK), lambda i, f: (f[0], i, 0, 0)),
             ),
             out_shape=jax.ShapeDtypeStruct((fl, NH, 2 * here, BLK), jnp.float32),
             input_output_aliases={} if first else {2: 0},
-            compiler_params=pltpu.CompilerParams(vmem_limit_bytes=VMEM),
+            compiler_params=pltpu.CompilerParams(vmem_limit_bytes=SMALL),
             cost_estimate=pl.CostEstimate(
                 flops=4 * NH * mid_local, bytes_accessed=12 * NH * mid_local, transcendentals=0
             ),

time: 139 us -> 127 us (0.914); the launches traced: 137 us -> 126 us
  Pallas kernels: 59.6 us -> 42.6 us
  waiting for transfers between devices: 19 us -> 27.9 us
  starting transfers between devices: 18.5 us -> 16.2 us
    pallas_call x4, Pallas kernels: 12.5 us -> 6.82 us  [finish(): pl.pallas_call(finish_kernel, grid_spec=pltpu.PrefetchScalarGridSpec(num_...]
    pallas_call x4, Pallas kernels: 10.5 us -> 5.19 us  [local(): pl.pallas_call(result_kernel, grid_spec=pltpu.PrefetchScalarGridSpec(num_...]
    ppermute x3, waiting for transfers between devices: 6.46 us -> 11.4 us  [local(): lax.ppermute(block, 'mid', [(s, s ^ ahead) for s in range(mid_count)])]
    pallas_call x1, Pallas kernels: 28.6 us -> 25.8 us  [local(): pl.pallas_call(march_kernel, in_specs=[smem] + [vmem] * 10, out_specs=vme...]
    unnamed x25 -> x27, local copies, waits for them, and re-layouts: 5.47 us -> 8.1 us
    ppermute x3, starting transfers between devices: 4.45 us -> 1.89 us  [local(): lax.ppermute(shares[away ^ low], 'off', [(i, (i // cores ^ low) * cores +...]
    pallas_call x1, Pallas kernels: 5.62 us -> 3.78 us  [local(): pl.pallas_call(contribution_kernel, in_specs=[smem, smem, vmem] + [hbm] *...]
  transfers between devices with their start and end apart: 12 -> 12, of which waited for: 6 -> 7; matrix products, arithmetic and copies ran while one was open for 14% -> 13% of each run, Pallas kernels for 14% -> 8%
where the time goes in v5:
time: 127 us; the launch traced here: 126 us
  Pallas kernels  42.6 us (34%)
  waiting for transfers between devices  27.9 us (22%)
  other arithmetic  17.5 us (14%)
  starting transfers between devices  16.2 us (13%)
  blocking collectives  11 us (9%)
  local copies, waits for them, and re-layouts  10.6 us (8%)
    pallas_call x1, Pallas kernels, local(): pl.pallas_call(march_kernel, in_specs=[smem] + [vmem] * 10, out_specs=vme...  25.8 us
    mul x1, other arithmetic, local(): x * (1.0 / (NH * total_mid))  14 us
    ppermute x3, waiting for transfers between devices, local(): lax.ppermute(block, 'mid', [(s, s ^ ahead) for s in range(mid_count)])  11.4 us
    all_gather x1, blocking collectives, local(): data = lax.all_gather(data, 'mid', axis=0)  11 us
    unnamed x27, local copies, waits for them, and re-layouts  8.1 us
    pallas_call x4, Pallas kernels, finish(): pl.pallas_call(finish_kernel, grid_spec=pltpu.PrefetchScalarGridSpec(num_...  6.82 us
    ppermute x3, waiting for transfers between devices, local(): lax.ppermute(shares[away ^ low], 'off', [(i, (i // cores ^ low) * cores +...  6.8 us
    all_to_all x1, starting transfers between devices, local(): data = lax.all_to_all(data, 'off', split_axis=1, concat_axis=0, tiled=True)  6.33 us
  transfers between devices with their start and end apart: 12, of which 7 were waited for; matrix products, arithmetic and copies ran while one was open for 13% of the time, Pallas kernels for 8%

profile of v5, /device:TPU:0, one launch (start us, length us, event | category | flops | bytes accessed | tf_op | source)
XLA Modules:
  0.0 126.3 jit_solution(2231530778854031910)
XLA Ops:
  1.7 1.0 copy.44
  3.8 6.3 %all-to-all-start = ((bf16[3,8,8,512]{3,2,0,1:T(8,128)(2,1)}), bf16[3,8,8,512]{3,2,0,1:T(8,128)(2,1)S(1)}, u32[]{:S(2)}, u32[]{:S(2)}) async-start(bf16[3,8,8,512]{3,2,0,1:T(8,128)(2,1)} %copy.46), calls=%async_computation | async-start | bytes 393216 | tf_op jit(solution)/shard_map/all_to_all | solution.py:471
  12.9 5.6 %all-to-all-done = bf16[3,8,8,512]{3,2,0,1:T(8,128)(2,1)S(1)} async-done(((bf16[3,8,8,512]{3,2,0,1:T(8,128)(2,1)}), bf16[3,8,8,512]{3,2,0,1:T(8,128)(2,1)S(1)}, u32[]{:S(2)}, u32[]{:S(2)}) %all-to-all-start) | async-done | bytes 196640 | tf_op jit(solution)/shard_map/all_to_all | solution.py:471
  19.5 1.4 %collective-permute-start.1 = (bf16[8,128,128]{2,1,0:T(8,128)(2,1)S(1)}, bf16[8,128,128]{2,1,0:T(8,128)(2,1)S(1)}, u32[]{:S(2)}, u32[]{:S(2)}) collective-permute-start(bf16[8,128,128]{2,1,0:T(8,128)(2,1)S(1)} %take_own.1.rest_0_), channel_id=1, source_target_pairs={{0,4},{1,5},{2,6},{3,7},{4,0},{5,1},{6,2},{7,3},{8,12},{9,13},{10,... | collective-permute-start | bytes 786440 | tf_op jit(solution)/shard_map/ppermute | solution.py:490
  21.5 11.0 %all-gather = bf16[68,8,512]{2,1,0:T(8,128)(2,1)S(1)} all-gather(bf16[17,8,512]{2,1,0:T(8,128)(2,1)S(1)} %pad_maximum_fusion.1), channel_id=2, replica_groups=mesh['mid'=4,'off'=8] {'mid'}, dimensions={0}, use_global_device_ids=true | all-gather | bytes 696320 | tf_op jit(solution)/shard_map/all_gather | solution.py:503
  34.2 5.9 %collective-permute-done.2.rest_3_ = bf16[8,128,128]{2,1,0:T(8,128)(2,1)S(1)} collective-permute-done((bf16[8,128,128]{2,1,0:T(8,128)(2,1)S(1)}, bf16[8,128,128]{2,1,0:T(8,128)(2,1)S(1)}, u32[]{:S(2)}, u32[]{:S(2)}) %collective-permute-start.2) | collective-permute-done | bytes 262176 | tf_op jit(solution)/shard_map/ppermute | solution.py:490
  41.7 3.8 %contributions.1 = s32[4,5,17,8,128]{4,3,2,1,0:T(8,128)} custom-call(s32[40]{0:T(128)S(1)} %get-tuple-element.27.slot_ref, s32[40]{0:T(128)S(1)} %get-tuple-element.26.bin_ref, bf16[16,128,128]{2,1,0:T(8,128)(2,1)S(1)} %bitcast.47, bf16[8,128,128]{2,1,0:T(8,128)(2,1)S(1)} %take_own.1.rest_0_, bf16[8,128,128]{2,1,0:T(8,128)(2,1)S(1)} %collective-permute-done.rest_1_, ...), custom_call_target="tpu_custom_call" | custom-call | tf_op jit(solution)/shard_map/contributions/pallas_call | solution.py:519
  45.6 3.7 %all-to-all-start.1 = ((s32[4,5,17,8,128]{4,3,2,1,0:T(8,128)}), s32[4,5,17,8,128]{4,3,2,1,0:T(8,128)S(1)}, u32[]{:S(2)}, u32[]{:S(2)}) async-start(s32[4,5,17,8,128]{4,3,2,1,0:T(8,128)} %contributions.1), calls=%async_computation.1 | async-start | bytes 2785280 | tf_op jit(solution)/shard_map/all_to_all | solution.py:552
  49.9 14.0 %multiply_multiply_fusion = (f32[256,2048]{1,0:T(8,128)}, f32[256,2048]{1,0:T(8,128)}) fusion(s32[256]{0:T(256)S(1)} %get-tuple-element.34, s32[256]{0:T(256)S(1)} %get-tuple-element.39, pred[256]{0:T(512)(128)(4,1)S(1)} %get-tuple-element.36, s32[256]{0:T(256)S(1)} %get-tuple-element.35, s32[256]{0:T(256)S(1)} %get-tuple-element.38, ...), kind=kLoop, calls=%fused_computation.14 | loop fusion | flops 38797312 | bytes 4235780 | tf_op jit(solution)/shard_map/mul | solution.py:544
  63.8 3.1 %all-to-all-done.1.code_ref = s32[4,5,17,8,128]{4,3,2,1,0:T(8,128)S(1)} async-done(((s32[4,5,17,8,128]{4,3,2,1,0:T(8,128)}), s32[4,5,17,8,128]{4,3,2,1,0:T(8,128)S(1)}, u32[]{:S(2)}, u32[]{:S(2)}) %all-to-all-start.1) | async-done | bytes 1392672 | tf_op jit(solution)/shard_map/all_to_all | solution.py:552
  67.0 1.6 %copy-done.4 = f32[256,2048]{1,0:T(8,128)S(1)} copy-done((f32[256,2048]{1,0:T(8,128)S(1)}, f32[256,2048]{1,0:T(8,128)}, u32[]{:S(2)}) %copy-start.4) | copy-done | bytes 2097176
  68.6 1.6 %copy-done.5 = f32[256,2048]{1,0:T(8,128)S(1)} copy-done((f32[256,2048]{1,0:T(8,128)S(1)}, f32[256,2048]{1,0:T(8,128)}, u32[]{:S(2)}) %copy-start.5) | copy-done | bytes 2097176
  71.2 25.8 %march.1.plane_ref = f32[2,2,128,2048]{3,2,1,0:T(8,128)S(1)} custom-call(f32[2,2,8,16]{3,2,1,0:T(8,128)S(1)} %pad_maximum_fusion.2.layer_ref, s32[4,5,17,8,128]{4,3,2,1,0:T(8,128)S(1)} %all-to-all-done.1.code_ref, bf16[256,320]{1,0:T(8,128)(2,1)S(1)} %fusion.8.pick_ref, f32[256,2048]{1,0:T(8,128)S(1)} %copy-done.5, f32[256,2048]{1,0:T(8,128)S(1)} %copy-done.4, ...), custom_call_target="tpu_custom_call" | custom-call | tf_op jit(solution)/shard_map/march/pallas_call | solution.py:561
  97.0 1.7 %finish.4.rest_0_ = s32[1032,128]{1,0:T(8,128)S(1)} custom-call(s32[1]{0:T(128)} %bitcast.23.dest_ref, f32[2,2,8,16]{3,2,1,0:T(8,128)S(1)} %pad_maximum_fusion.2.layer_ref, f32[2,2,128,2048]{3,2,1,0:T(8,128)S(1)} %march.1.plane_ref, bf16[256,768]{1,0:T(8,128)(2,1)S(1)} %copy-done.2, f32[2,128,128]{2,1,0:T(8,128)S(1)} %copy-done.3), custom_call_target="tpu_custom_call" | custom-call | flops 402653184 | bytes 786432 | tf_op jit(solution)/shard_map/finish/pallas_call | solution.py:575
  98.8 1.5 %collective-permute-start.9 = (s32[1032,128]{1,0:T(8,128)S(1)}, s32[1032,128]{1,0:T(8,128)}, u32[]{:S(2)}, u32[]{:S(2)}) collective-permute-start(s32[1032,128]{1,0:T(8,128)S(1)} %finish.4.rest_0_), channel_id=1, source_target_pairs={{0,24},{8,16},{16,8},{24,0},{1,25},{9,17},{17,9},{25,1},{2,26},{10... | collective-permute-start | bytes 1585160 | tf_op jit(solution)/shard_map/ppermute | solution.py:603
  100.2 1.7 %finish.5.rest_0_ = s32[1032,128]{1,0:T(8,128)S(1)} custom-call(s32[1]{0:T(128)} %bitcast.22.dest_ref, f32[2,2,8,16]{3,2,1,0:T(8,128)S(1)} %pad_maximum_fusion.2.layer_ref, f32[2,2,128,2048]{3,2,1,0:T(8,128)S(1)} %march.1.plane_ref, bf16[256,768]{1,0:T(8,128)(2,1)S(1)} %copy-done.2, f32[2,128,128]{2,1,0:T(8,128)S(1)} %copy-done.3, s32[1032,128]{1,0:T(8,128)S(1)} %finish.4.rest_0_), custom_call_target="tpu_custom_call" | custom-call | flops 402653184 | bytes 786432 | tf_op jit(solution)/shard_map/finish/pallas_call | solution.py:575
  101.9 1.5 %collective-permute-start.8 = (s32[1032,128]{1,0:T(8,128)S(1)}, s32[1032,128]{1,0:T(8,128)S(1)}, u32[]{:S(2)}, u32[]{:S(2)}) collective-permute-start(s32[1032,128]{1,0:T(8,128)S(1)} %finish.5.rest_0_), channel_id=1, source_target_pairs={{0,16},{8,24},{16,0},{24,8},{1,17},{9,25},{17,1},{25,9},{2,18},{10... | collective-permute-start | bytes 1585160 | tf_op jit(solution)/shard_map/ppermute | solution.py:603
  103.5 1.7 %finish.6.rest_0_ = s32[1032,128]{1,0:T(8,128)S(1)} custom-call(s32[1]{0:T(128)} %bitcast.1.dest_ref, f32[2,2,8,16]{3,2,1,0:T(8,128)S(1)} %pad_maximum_fusion.2.layer_ref, f32[2,2,128,2048]{3,2,1,0:T(8,128)S(1)} %march.1.plane_ref, bf16[256,768]{1,0:T(8,128)(2,1)S(1)} %copy-done.2, f32[2,128,128]{2,1,0:T(8,128)S(1)} %copy-done.3, s32[1032,128]{1,0:T(8,128)S(1)} %finish.5.rest_0_), custom_call_target="tpu_custom_call" | custom-call | flops 402653184 | bytes 786432 | tf_op jit(solution)/shard_map/finish/pallas_call | solution.py:575
  105.9 2.2 %copy-done.1 = f32[2,2,128,2048]{3,2,1,0:T(8,128)S(1)} copy-done((f32[2,2,128,2048]{3,2,1,0:T(8,128)S(1)}, f32[2,2,128,2048]{3,2,1,0:T(8,128)}, u32[]{:S(2)}) %copy-start.1) | copy-done | bytes 4194328
  108.1 1.7 %finish.7.code_ref = s32[1032,128]{1,0:T(8,128)S(1)} custom-call(s32[1]{0:T(128)} %bitcast.26.dest_ref, f32[2,2,8,16]{3,2,1,0:T(8,128)S(1)} %pad_maximum_fusion.2.layer_ref, f32[2,2,128,2048]{3,2,1,0:T(8,128)S(1)} %copy-done.1, bf16[256,768]{1,0:T(8,128)(2,1)S(1)} %copy-done.2, f32[2,128,128]{2,1,0:T(8,128)S(1)} %copy-done.3, s32[1032,128]{1,0:T(8,128)S(1)} %finish.6.rest_0_), custom_call_target="tpu_custom_call" | custom-call | flops 402653184 | bytes 786432 | tf_op jit(solution)/shard_map/finish/pallas_call | solution.py:575
  109.8 1.1 result.4.rest_0_
  110.8 4.0 %collective-permute-done.9.code_ref = s32[1032,128]{1,0:T(8,128)} collective-permute-done((s32[1032,128]{1,0:T(8,128)S(1)}, s32[1032,128]{1,0:T(8,128)}, u32[]{:S(2)}, u32[]{:S(2)}) %collective-permute-start.9) | collective-permute-done | bytes 528416 | tf_op jit(solution)/shard_map/ppermute | solution.py:603
  114.8 2.1 %result.5.rest_0_ = f32[4,256,8,128]{3,2,1,0:T(8,128)} custom-call(s32[1]{0:T(128)} %bitcast.25.freq_ref, s32[1032,128]{1,0:T(8,128)} %collective-permute-done.9.code_ref, f32[4,256,8,128]{3,2,1,0:T(8,128)} %result.4.rest_0_), custom_call_target="tpu_custom_call", output_to_operand_aliasing={{}: (2, {})} | custom-call | flops 524288 | bytes 1572864 | tf_op jit(solution)/shard_map/result/pallas_call | solution.py:610
  116.9 7.4 %collective-permute-done.8.code_ref = s32[1032,128]{1,0:T(8,128)S(1)} collective-permute-done((s32[1032,128]{1,0:T(8,128)S(1)}, s32[1032,128]{1,0:T(8,128)S(1)}, u32[]{:S(2)}, u32[]{:S(2)}) %collective-permute-start.8) | collective-permute-done | bytes 528416 | tf_op jit(solution)/shard_map/ppermute | solution.py:603
  (93 shorter events, 14.5 us)
Async XLA Ops:
  0.0 11.2 %copy-start.6 = (bf16[2,16,128,128]{3,2,1,0:T(8,128)(2,1)S(1)}, bf16[2,16,128,128]{3,2,1,0:T(8,128)(2,1)}, u32[]{:S(2)}) copy-start(bf16[2,16,128,128]{3,2,1,0:T(8,128)(2,1)} %source_ref.1) | copy-start | bytes 3145732
  3.8 14.7 %all-to-all-start = ((bf16[3,8,8,512]{3,2,0,1:T(8,128)(2,1)}), bf16[3,8,8,512]{3,2,0,1:T(8,128)(2,1)S(1)}, u32[]{:S(2)}, u32[]{:S(2)}) async-start(bf16[3,8,8,512]{3,2,0,1:T(8,128)(2,1)} %copy.46), calls=%async_computation | async-start | bytes 393216 | tf_op jit(solution)/shard_map/all_to_all | solution.py:471
  19.1 14.7 %collective-permute-start = (bf16[8,128,128]{2,1,0:T(8,128)(2,1)S(1)}, bf16[8,128,128]{2,1,0:T(8,128)(2,1)S(1)}, u32[]{:S(2)}, u32[]{:S(2)}) collective-permute-start(bf16[8,128,128]{2,1,0:T(8,128)(2,1)S(1)} %take_own.1.rest_0_), channel_id=1, source_target_pairs={{0,2},{1,3},{2,0},{3,1},{4,6},{5,7},{6,4},{7,5},{8,10},{9,11},{10,... | collective-permute-start | bytes 786440 | tf_op jit(solution)/shard_map/ppermute | solution.py:490
  19.5 14.0 %collective-permute-start.1 = (bf16[8,128,128]{2,1,0:T(8,128)(2,1)S(1)}, bf16[8,128,128]{2,1,0:T(8,128)(2,1)S(1)}, u32[]{:S(2)}, u32[]{:S(2)}) collective-permute-start(bf16[8,128,128]{2,1,0:T(8,128)(2,1)S(1)} %take_own.1.rest_0_), channel_id=1, source_target_pairs={{0,4},{1,5},{2,6},{3,7},{4,0},{5,1},{6,2},{7,3},{8,12},{9,13},{10,... | collective-permute-start | bytes 786440 | tf_op jit(solution)/shard_map/ppermute | solution.py:490
  20.9 19.7 %collective-permute-start.3 = (bf16[8,128,128]{2,1,0:T(8,128)(2,1)S(1)}, bf16[8,128,128]{2,1,0:T(8,128)(2,1)S(1)}, u32[]{:S(2)}, u32[]{:S(2)}) collective-permute-start(bf16[8,128,128]{2,1,0:T(8,128)(2,1)S(1)} %take_own.1.rest_0_), channel_id=1, source_target_pairs={{0,1},{1,0},{2,3},{3,2},{4,5},{5,4},{6,7},{7,6},{8,9},{9,8},{10,11... | collective-permute-start | bytes 786440 | tf_op jit(solution)/shard_map/ppermute | solution.py:497
  33.6 6.6 %collective-permute-start.2 = (bf16[8,128,128]{2,1,0:T(8,128)(2,1)S(1)}, bf16[8,128,128]{2,1,0:T(8,128)(2,1)S(1)}, u32[]{:S(2)}, u32[]{:S(2)}) collective-permute-start(bf16[8,128,128]{2,1,0:T(8,128)(2,1)S(1)} %collective-permute-done.1.rest_2_), channel_id=1, source_target_pairs={{0,2},{1,3},{2,0},{3,1},{4,6},{5,7},{6,4},{7,5},{8,10},{9,11},{10,... | collective-permute-start | bytes 786440 | tf_op jit(solution)/shard_map/ppermute | solution.py:490
  33.7 7.0 %collective-permute-start.5 = (bf16[8,128,128]{2,1,0:T(8,128)(2,1)S(1)}, bf16[8,128,128]{2,1,0:T(8,128)(2,1)S(1)}, u32[]{:S(2)}, u32[]{:S(2)}) collective-permute-start(bf16[8,128,128]{2,1,0:T(8,128)(2,1)S(1)} %collective-permute-done.1.rest_2_), channel_id=1, source_target_pairs={{0,1},{1,0},{2,3},{3,2},{4,5},{5,4},{6,7},{7,6},{8,9},{9,8},{10,11... | collective-permute-start | bytes 786440 | tf_op jit(solution)/shard_map/ppermute | solution.py:497
  33.7 6.9 %collective-permute-start.4 = (bf16[8,128,128]{2,1,0:T(8,128)(2,1)S(1)}, bf16[8,128,128]{2,1,0:T(8,128)(2,1)S(1)}, u32[]{:S(2)}, u32[]{:S(2)}) collective-permute-start(bf16[8,128,128]{2,1,0:T(8,128)(2,1)S(1)} %collective-permute-done.rest_1_), channel_id=1, source_target_pairs={{0,1},{1,0},{2,3},{3,2},{4,5},{5,4},{6,7},{7,6},{8,9},{9,8},{10,11... | collective-permute-start | bytes 786440 | tf_op jit(solution)/shard_map/ppermute | solution.py:497
  40.2 1.5 %collective-permute-start.6 = (bf16[8,128,128]{2,1,0:T(8,128)(2,1)S(1)}, bf16[8,128,128]{2,1,0:T(8,128)(2,1)S(1)}, u32[]{:S(2)}, u32[]{:S(2)}) collective-permute-start(bf16[8,128,128]{2,1,0:T(8,128)(2,1)S(1)} %collective-permute-done.2.rest_3_), channel_id=1, source_target_pairs={{0,1},{1,0},{2,3},{3,2},{4,5},{5,4},{6,7},{7,6},{8,9},{9,8},{10,11... | collective-permute-start | bytes 786440 | tf_op jit(solution)/shard_map/ppermute | solution.py:497
  45.5 4.0 %copy-start.12 = (f32[2,16]{1,0:T(2,128)S(1)}, f32[2,16]{1,0:T(2,128)}, u32[]{:S(2)}) copy-start(f32[2,16]{1,0:T(2,128)} %param.17) | copy-start | bytes 388
  45.6 21.4 %all-to-all-start.1 = ((s32[4,5,17,8,128]{4,3,2,1,0:T(8,128)}), s32[4,5,17,8,128]{4,3,2,1,0:T(8,128)S(1)}, u32[]{:S(2)}, u32[]{:S(2)}) async-start(s32[4,5,17,8,128]{4,3,2,1,0:T(8,128)} %contributions.1), calls=%async_computation.1 | async-start | bytes 2785280 | tf_op jit(solution)/shard_map/all_to_all | solution.py:552
  49.8 17.2 %copy-start.2 = (bf16[256,768]{1,0:T(8,128)(2,1)S(1)}, bf16[256,768]{1,0:T(8,128)(2,1)}, u32[]{:S(2)}) copy-start(bf16[256,768]{1,0:T(8,128)(2,1)} %constant.233.clone.rows_inverse) | copy-start | bytes 1179652
  49.8 17.2 %copy-start.3 = (f32[2,128,128]{2,1,0:T(8,128)S(1)}, f32[2,128,128]{2,1,0:T(8,128)}, u32[]{:S(2)}) copy-start(f32[2,128,128]{2,1,0:T(8,128)} %constant.237.clone.offset_ref) | copy-start | bytes 393220
  49.8 17.2 %copy-start.7 = (bf16[256,768]{1,0:T(8,128)(2,1)S(1)}, bf16[256,768]{1,0:T(8,128)(2,1)}, u32[]{:S(2)}) copy-start(bf16[256,768]{1,0:T(8,128)(2,1)} %constant.232.clone.rows_forward) | copy-start | bytes 1179652
  49.8 17.1 %copy-start.8 = (bf16[768,256]{1,0:T(8,128)(2,1)S(1)}, bf16[768,256]{1,0:T(8,128)(2,1)}, u32[]{:S(2)}) copy-start(bf16[768,256]{1,0:T(8,128)(2,1)} %constant.234.clone.lanes_forward) | copy-start | bytes 1179652
  49.9 17.1 %copy-start.10 = (f32[2,16,128]{2,1,0:T(8,128)S(1)}, f32[2,16,128]{2,1,0:T(8,128)}, u32[]{:S(2)}) copy-start(f32[2,16,128]{2,1,0:T(8,128)} %constant.236.clone.middle_ref) | copy-start | bytes 49156
  67.0 1.6 %copy-start.4 = (f32[256,2048]{1,0:T(8,128)S(1)}, f32[256,2048]{1,0:T(8,128)}, u32[]{:S(2)}) copy-start(f32[256,2048]{1,0:T(8,128)} %get-tuple-element.19.phase_imag) | copy-start | bytes 6291460
  68.6 1.6 %copy-start.5 = (f32[256,2048]{1,0:T(8,128)S(1)}, f32[256,2048]{1,0:T(8,128)}, u32[]{:S(2)}) copy-start(f32[256,2048]{1,0:T(8,128)} %get-tuple-element.20.phase_real) | copy-start | bytes 6291460
  70.2 1.0 copy-start.9
  97.0 6.5 %copy-start = (f32[2,2,128,2048]{3,2,1,0:T(8,128)}, f32[2,2,128,2048]{3,2,1,0:T(8,128)S(1)}, u32[]{:S(2)}) copy-start(f32[2,2,128,2048]{3,2,1,0:T(8,128)S(1)} %march.1.plane_ref) | copy-start | bytes 12582916
  98.8 16.1 %collective-permute-start.9 = (s32[1032,128]{1,0:T(8,128)S(1)}, s32[1032,128]{1,0:T(8,128)}, u32[]{:S(2)}, u32[]{:S(2)}) collective-permute-start(s32[1032,128]{1,0:T(8,128)S(1)} %finish.4.rest_0_), channel_id=1, source_target_pairs={{0,24},{8,16},{16,8},{24,0},{1,25},{9,17},{17,9},{25,1},{2,26},{10... | collective-permute-start | bytes 1585160 | tf_op jit(solution)/shard_map/ppermute | solution.py:603
  101.9 22.3 %collective-permute-start.8 = (s32[1032,128]{1,0:T(8,128)S(1)}, s32[1032,128]{1,0:T(8,128)S(1)}, u32[]{:S(2)}, u32[]{:S(2)}) collective-permute-start(s32[1032,128]{1,0:T(8,128)S(1)} %finish.5.rest_0_), channel_id=1, source_target_pairs={{0,16},{8,24},{16,0},{24,8},{1,17},{9,25},{17,1},{25,9},{2,18},{10... | collective-permute-start | bytes 1585160 | tf_op jit(solution)/shard_map/ppermute | solution.py:603
  105.2 20.1 %collective-permute-start.7 = (s32[1032,128]{1,0:T(8,128)S(1)}, s32[1032,128]{1,0:T(8,128)S(1)}, u32[]{:S(2)}, u32[]{:S(2)}) collective-permute-start(s32[1032,128]{1,0:T(8,128)S(1)} %finish.6.rest_0_), channel_id=1, source_target_pairs={{0,8},{8,0},{16,24},{24,16},{1,9},{9,1},{17,25},{25,17},{2,10},{10... | collective-permute-start | bytes 1585160 | tf_op jit(solution)/shard_map/ppermute | solution.py:603
  105.9 2.2 %copy-start.1 = (f32[2,2,128,2048]{3,2,1,0:T(8,128)S(1)}, f32[2,2,128,2048]{3,2,1,0:T(8,128)}, u32[]{:S(2)}) copy-start(f32[2,2,128,2048]{3,2,1,0:T(8,128)} %copy-done) | copy-start | bytes 12582916
  (1 other events, 0.7 us)

commit v6 on v5

--- a/solution.py
+++ b/solution.py
@@ -152,8 +152,10 @@
     return (word >> 16).astype(jnp.float32), ((word << 16) >> 16).astype(jnp.float32)
 
 
-def contribution_kernel(slot_ref, bin_ref, data_ref, *rest):
-    *sources, out_ref, held, weight_ref, sems = rest
+def contribution_kernel(place_ref, order_ref, slot_ref, bin_ref, data_ref, *rest, freqs):
+    *sources, held, weight_ref, sems = rest
+    sources, outs = sources[:-freqs], sources[-freqs:]
+    groups, outer = outs[0].shape[0], outs[0].shape[1] - 1
     count = sources[0].shape[0]
     copies = [
         pltpu.make_async_copy(ref, weight_ref.at[pl.ds(n * count, count)], sems.at[n])
@@ -163,8 +165,6 @@
         copy.start()
     for copy in copies:
         copy.wait()
-    freqs, groups = out_ref.shape[:2]
-    outer = out_ref.shape[2] - 1
 
     @pl.loop(0, groups)
     def _(group):
@@ -172,18 +172,19 @@
             slot = slot_ref[group * GROUP + at]
             source = bin_ref[group * GROUP + at]
             held[pl.ds(at, data_ref.shape[1], GROUP), :] = dot(data_ref[source], weight_ref[slot])
-        for f in range(freqs):
-            base = f * 2 * outer * GROUP
-            biggest = jnp.abs(held[pl.ds(base, GROUP), :])
-            for at in range(1, 2 * outer):
-                biggest = jnp.maximum(biggest, jnp.abs(held[pl.ds(base + at * GROUP, GROUP), :]))
+        for away, out_ref in enumerate(outs):
+            base = (place_ref[0] ^ away) * (2 * outer * GROUP)
+
+            def term(at):
+                return held[pl.ds(pl.multiple_of(base + at * GROUP, GROUP), GROUP), :]
+
+            biggest = functools.reduce(jnp.maximum, [jnp.abs(term(at)) for at in range(2 * outer)])
             code = scale_code(biggest)
             inverse = inverse_scale_of(code)
             for a in range(outer):
-                real = held[pl.ds(base + a * GROUP, GROUP), :]
-                imag = held[pl.ds(base + (outer + a) * GROUP, GROUP), :]
-                out_ref[f, group, a] = packed(coded(real, inverse), coded(imag, inverse))
-            out_ref[f, group, outer] = code
+                words = packed(coded(term(a), inverse), coded(term(outer + a), inverse))
+                out_ref[group, order_ref[a]] = words
+            out_ref[group, outer] = code
 
 
 def column_of(plane, a):
@@ -232,6 +233,24 @@
     return jnp.concatenate(
         [jnp.concatenate(parts[:2], axis=0), jnp.concatenate(parts[2:], axis=0)], axis=1
     )
+
+
+def propagator_kernel(omega_ref, real_ref, imag_ref):
+    total = real_ref.shape[1]
+    scale = 1.0 / (NH * total)
+    omega_sq = omega_ref[0] * omega_ref[0]
+
+    @pl.loop(0, NH // GROUP)
+    def _(at):
+        start = pl.multiple_of(at * GROUP, GROUP)
+        row = lax.broadcasted_iota(jnp.int32, (GROUP, BLK), 0) + at * GROUP
+        lane = lax.broadcasted_iota(jnp.int32, (GROUP, BLK), 1)
+        offset_wave = signed_wave(2 * (row % HALF) + row // HALF, NH)
+        for a in range(total // BLK):
+            mid_wave = signed_wave(a + total // BLK * lane, total)
+            real, imag = propagator(omega_sq, mid_wave, offset_wave)
+            real_ref[pl.ds(start, GROUP), a * BLK : (a + 1) * BLK] = real * scale
+            imag_ref[pl.ds(start, GROUP), a * BLK : (a + 1) * BLK] = imag * scale
 
 
 def offset_product(table, columns):
@@ -298,23 +317,27 @@
                 out[p, 1, here, lanes[a]] = values[a][1]
 
 
-def march_kernel(
-    layer_ref, code_ref, pick_ref, phase_real, phase_imag, rows_forward, rows_inverse, lanes_forward,
-    lanes_inverse, middle_ref, offset_ref, other, plane, scales,
-):
-    sources, groups = code_ref.shape[:2]
+def march_kernel(layer_ref, *rest, sources):
+    code_refs, rest = rest[:sources], rest[sources:]
+    (
+        pick_ref, phase_real, phase_imag, rows_forward, rows_inverse, lanes_forward, lanes_inverse,
+        middle_ref, offset_ref, other, plane, scales,
+    ) = rest
+    groups = code_refs[0].shape[0]
     outer = middle_ref.shape[1]
     steps = layer_ref.shape[1]
-    slots = sources * groups * GROUP
     tall = NH // layer_ref.shape[2]
 
-    scales[...] = scale_of(code_ref[:, :, outer].reshape(slots, BLK))
+    def words(a):
+        return jnp.concatenate([ref[:, a].reshape(groups * GROUP, BLK) for ref in code_refs], axis=0)
+
+    scales[...] = scale_of(words(outer))
 
     @pl.loop(0, outer // COLUMNS, unroll=2)
     def _(at):
         columns = []
         for a in range(COLUMNS):
-            real, imag = unpacked(code_ref[:, :, at * COLUMNS + a].reshape(slots, BLK))
+            real, imag = unpacked(words(at * COLUMNS + a))
             scale = scales[...]
             value = jnp.concatenate([real * scale, imag * scale], axis=1)
             moved = dot(pick_ref[...], jnp.concatenate(halves(value), axis=0))
@@ -458,18 +481,6 @@
     smem = pl.BlockSpec(memory_space=pltpu.SMEM)
     vmem = pl.BlockSpec(memory_space=pltpu.VMEM)
     hbm = pl.BlockSpec(memory_space=pl.ANY)
-    pairs = fl * 2
-
-    def extra(whole_numbers, copies):
-        flat = whole_numbers.astype(jnp.bfloat16).reshape(1, 1, 1, -1)
-        flat = jnp.pad(flat, ((0, 0), (0, 0), (0, pairs - 1), (0, mid_local - flat.shape[3])))
-        return jnp.broadcast_to(flat, (1, copies, pairs, mid_local))
-
-    lists = jnp.concatenate([counts[:, None], targets], axis=1)
-    data = bins_data.reshape(bins_local, off_count, pairs, mid_local)
-    data = jnp.concatenate([data, extra(lists, off_count)], axis=0)
-    data = lax.all_to_all(data, "off", split_axis=1, concat_axis=0, tiled=True)
-
     own = pl.pallas_call(
         take_kernel,
         in_specs=[smem, smem, hbm],
@@ -479,7 +490,7 @@
         compiler_params=pltpu.CompilerParams(vmem_limit_bytes=SMALL),
         name="take_own",
     )(mine.reshape(1), counts, operators)
-    data, own = lax.optimization_barrier((data, own))
+    bins_data, own = lax.optimization_barrier((bins_data, own))
     cores = 2 if off_count % 2 == 0 else 1
     line = off_count // cores
     assert line & (line - 1) == 0 and fl & (fl - 1) == 0
@@ -496,16 +507,38 @@
     if cores > 1:
         shares += [lax.ppermute(x, "off", [(i, i ^ 1) for i in range(off_count)]) for x in shares]
 
+    pairs = fl * 2
+
+    def extra(whole_numbers, copies):
+        flat = whole_numbers.astype(jnp.bfloat16).reshape(1, 1, 1, -1)
+        flat = jnp.pad(flat, ((0, 0), (0, 0), (0, pairs - 1), (0, mid_local - flat.shape[3])))
+        return jnp.broadcast_to(flat, (1, copies, pairs, mid_local))
+
+    lists = jnp.concatenate([counts[:, None], targets], axis=1)
+    data = bins_data.reshape(bins_local, off_count, pairs, mid_local)
+    data = jnp.concatenate([data, extra(lists, off_count)], axis=0)
+    data = lax.all_to_all(data, "off", split_axis=1, concat_axis=0, tiled=True)
+
     data = data.reshape(off_count, bins_local + 1, pairs, mid_local)
     lists = data[:, bins_local, 0, : lists.size].astype(jnp.int32).reshape(bins_total, 1 + entries)
     data = data[:, :bins_local].reshape(bins_total, pairs, mid_local)
     data = jnp.concatenate([data, extra(layer_index, 1)[0]], axis=0)
-    data = lax.all_gather(data, "mid", axis=0)
+    assert mid_count & (mid_count - 1) == 0
+    parts = [data] + [
+        lax.ppermute(data, "mid", [(i, i ^ away) for i in range(mid_count)])
+        for away in range(mid_count - 1, 0, -1)
+    ]
+    data = jnp.stack(parts[:1] + parts[:0:-1])
+    partner = jnp.arange(mid_count, dtype=jnp.int32) ^ mid_at
     layers = data[:, bins_total, 0, : layer_index.size].astype(jnp.int32)
+    layers = jnp.sum(
+        jnp.where((partner[:, None] == jnp.arange(mid_count))[:, :, None], layers[None], 0), axis=1
+    )
     layers = layers.reshape(mid_count, *layer_index.shape).transpose(1, 2, 0, 3)
     layers = layers.reshape(*layer_index.shape[:2], outer)
     data = data[:, :bins_total].reshape(mid_count, bins_total, pairs, mid_local // BLK, BLK)
     data = data.transpose(1, 2, 0, 3, 4).reshape(bins_total, pairs * outer, BLK)
+    order = (partner[:, None] * (mid_local // BLK) + jnp.arange(mid_local // BLK)).reshape(outer)
 
     live_total = bins_total * entries // 2
     room = -(-(live_total + (fl - 1) * off_count) // fl)
@@ -516,11 +549,12 @@
     own_slots = lax.dynamic_index_in_dim(slots, mine, 0, False)
     own_bins = lax.dynamic_index_in_dim(bins, mine, 0, False)
     list_groups = room // GROUP
+    shape = jax.ShapeDtypeStruct((list_groups, outer + 1, GROUP, BLK), jnp.int32)
     terms = pl.pallas_call(
-        contribution_kernel,
-        in_specs=[smem, smem, vmem] + [hbm] * len(shares),
-        out_specs=vmem,
-        out_shape=jax.ShapeDtypeStruct((fl, list_groups, outer + 1, GROUP, BLK), jnp.int32),
+        functools.partial(contribution_kernel, freqs=fl),
+        in_specs=[smem, smem, smem, smem, vmem] + [hbm] * len(shares),
+        out_specs=[vmem] * fl,
+        out_shape=[shape] * fl,
         scratch_shapes=[
             pltpu.VMEM((fl * 2 * outer * GROUP, BLK), jnp.float32),
             pltpu.VMEM((len(shares) * per_device, BLK, BLK), jnp.bfloat16),
@@ -528,30 +562,39 @@
         ],
         compiler_params=pltpu.CompilerParams(vmem_limit_bytes=SMALL),
         name="contributions",
-    )(own_slots, own_bins, data, *shares)
-    terms, goal, layers, freq_at = lax.optimization_barrier((terms, goal, layers, off_at * fl + mine))
+    )(mine.reshape(1), order, own_slots, own_bins, data, *shares)
+    terms, goal, layers, freq_at = lax.optimization_barrier(
+        (terms, goal, layers, off_at * fl + mine)
+    )
+    got = {0: terms[0]}
+    for away in range(fl - 1, 0, -1):
+        got[away] = lax.ppermute(terms[away], "mid", [(i, i ^ away) for i in range(mid_count)])
+    terms = [got[away] for away in range(fl)]
+
+    source = jnp.arange(fl, dtype=jnp.int32) ^ mine
+    goal = jnp.sum(jnp.where((source[:, None] == jnp.arange(fl))[:, :, None], goal[None], 0), axis=1)
     pick = (
         jnp.tile(goal.reshape(1, fl * room), (1, 2))
         == lax.broadcasted_iota(jnp.int32, (NH, 2 * fl * room), 0)
     ).astype(jnp.bfloat16)
-
     omega = math.pi * (0.1 + 0.8 * (freq_at.astype(jnp.float32) + 0.5) / freq_total)
-    row = lax.broadcasted_iota(jnp.int32, (NH, total_mid), 0)
-    lane = lax.broadcasted_iota(jnp.int32, (NH, total_mid), 1)
-    offset_wave = signed_wave(2 * (row % HALF) + row // HALF, NH)
-    mid_wave = signed_wave(lane // BLK + outer * (lane % BLK), total_mid)
-    phase_real, phase_imag = propagator(omega * omega, mid_wave, offset_wave)
-    phase_real, phase_imag = (x * (1.0 / (NH * total_mid)) for x in (phase_real, phase_imag))
+    phase_real, phase_imag = pl.pallas_call(
+        propagator_kernel,
+        in_specs=[smem],
+        out_specs=[vmem] * 2,
+        out_shape=[jax.ShapeDtypeStruct((NH, total_mid), jnp.float32)] * 2,
+        compiler_params=pltpu.CompilerParams(vmem_limit_bytes=SMALL),
+        cost_estimate=pl.CostEstimate(
+            flops=60 * NH * total_mid, bytes_accessed=8 * NH * total_mid, transcendentals=10 * NH * total_mid
+        ),
+        name="propagator",
+    )(omega.reshape(1))
 
     layer_total = slowness.shape[1]
     chosen = layers[..., None] == jnp.arange(layer_total)
     slow = jnp.sum(jnp.where(chosen, slowness[:, None, None, :], 0.0), axis=-1)
     turn = 2.0 * dz_cells * omega * (slow - 1.0)
     layer_turns = jnp.stack([jnp.cos(turn), jnp.sin(turn)])
-
-    terms = lax.all_to_all(
-        terms, "mid", split_axis=0, concat_axis=0, axis_index_groups=groups, tiled=True
-    )
 
     middle, offset_turn = twiddle_tables(outer)
     here = mid_local // BLK
@@ -559,8 +602,8 @@
     tables = [jnp.asarray(t) for t in block_tables()]
     middle, offset_turn = jnp.asarray(middle), jnp.asarray(offset_turn)
     plane = pl.pallas_call(
-        march_kernel,
-        in_specs=[smem] + [vmem] * 10,
+        functools.partial(march_kernel, sources=fl),
+        in_specs=[smem] + [vmem] * (fl + 9),
         out_specs=vmem,
         out_shape=jax.ShapeDtypeStruct((2, 2, HALF, total_mid), jnp.float32),
         scratch_shapes=[
@@ -569,7 +612,7 @@
         ],
         compiler_params=pltpu.CompilerParams(vmem_limit_bytes=VMEM),
         name="march",
-    )(layer_turns, terms, pick, phase_real, phase_imag, *tables, middle, offset_turn)
+    )(layer_turns, *terms, pick, phase_real, phase_imag, *tables, middle, offset_turn)
 
     def finish(dest, *before):
         return pl.pallas_call(

time: 127 us -> 116 us (0.913)
  other arithmetic: 17.5 us -> 3.92 us
  Pallas kernels: 42.6 us -> 56.1 us
  blocking collectives: 11 us -> 0 us
  starting transfers between devices: 16.2 us -> 23.2 us
  waiting for transfers between devices: 27.9 us -> 22.4 us
  local copies, waits for them, and re-layouts: 10.6 us -> 9.19 us
    mul x1, other arithmetic: 14 us -> 0.01 us  [local(): partner[:, None] * (mid_local // BLK) + jnp.arange(mid_local // BLK)]
    pallas_call x2 -> x3, Pallas kernels: 29.6 us -> 43.1 us  [the longest x1 25.7 us: local(): pl.pallas_call(functools.partial(march_kernel, sources=fl), in_specs=[sme...]
    all_gather x1 -> x0, blocking collectives: 11 us -> none  [local(): data = lax.all_gather(data, 'mid', axis=0)]
    ppermute x0 -> x6, starting transfers between devices: none -> 7.04 us  [the longest x3 3.55 us: local(): lax.ppermute(data, 'mid', [(i, i ^ away) for i in range(mid_count)])]
    ppermute x3, starting transfers between devices: 1.89 us -> 8.49 us  [local(): lax.ppermute(shares[away ^ low], 'off', [(i, (i // cores ^ low) * cores +...]
    ppermute x0 -> x6, waiting for transfers between devices: none -> 5.72 us  [the longest x3 5.22 us: local(): lax.ppermute(data, 'mid', [(i, i ^ away) for i in range(mid_count)])]
    all_to_all x1, waiting for transfers between devices: 5.57 us -> 1.37 us  [local(): data = lax.all_to_all(data, 'off', split_axis=1, concat_axis=0, tiled=True)]
    all_to_all x1 -> x0, starting transfers between devices: 3.73 us -> none  [local(): lax.all_to_all(terms, 'mid', split_axis=0, concat_axis=0, axis_index_grou...]
  transfers between devices with their start and end apart: 12 -> 17, of which waited for: 7 -> 10; matrix products, arithmetic and copies ran while one was open for 13% -> 6% of each run, Pallas kernels for 8% -> 21%
where the time goes in v6:
time: 116 us; the launch traced here: 115 us
  Pallas kernels  56.1 us (48%)
  starting transfers between devices  23.2 us (20%)
  waiting for transfers between devices  22.4 us (19%)
  local copies, waits for them, and re-layouts  9.19 us (8%)
  other arithmetic  3.92 us (3%)
    pallas_call x1, Pallas kernels, local(): pl.pallas_call(functools.partial(march_kernel, sources=fl), in_specs=[sme...  25.7 us
    pallas_call x1, Pallas kernels, local(): pl.pallas_call(propagator_kernel, in_specs=[smem], out_specs=[vmem] * 2,...  14.6 us
    ppermute x3, waiting for transfers between devices, local(): lax.ppermute(block, 'mid', [(s, s ^ ahead) for s in range(mid_count)])  11.3 us
    ppermute x3, starting transfers between devices, local(): lax.ppermute(shares[away ^ low], 'off', [(i, (i // cores ^ low) * cores +...  8.49 us
    pallas_call x4, Pallas kernels, finish(): pl.pallas_call(finish_kernel, grid_spec=pltpu.PrefetchScalarGridSpec(num_...  6.82 us
    unnamed x26, local copies, waits for them, and re-layouts  5.56 us
    ppermute x3, waiting for transfers between devices, local(): lax.ppermute(data, 'mid', [(i, i ^ away) for i in range(mid_count)])  5.22 us
    pallas_call x4, Pallas kernels, local(): pl.pallas_call(result_kernel, grid_spec=pltpu.PrefetchScalarGridSpec(num_...  5.19 us
  transfers between devices with their start and end apart: 17, of which 10 were waited for; matrix products, arithmetic and copies ran while one was open for 6% of the time, Pallas kernels for 21%

profile of v6, /device:TPU:0, one launch (start us, length us, event | category | flops | bytes accessed | tf_op | source)
XLA Modules:
  0.0 115.2 jit_solution(11820706059972960756)
XLA Ops:
  0.0 1.2 %copy-done.4 = bf16[2,16,128,128]{3,2,1,0:T(8,128)(2,1)S(1)} copy-done((bf16[2,16,128,128]{3,2,1,0:T(8,128)(2,1)S(1)}, bf16[2,16,128,128]{3,2,1,0:T(8,128)(2,1)}, u32[]{:S(2)}) %copy-start.4) | copy-done | bytes 1048600
  2.9 3.1 %collective-permute-start.3 = (bf16[8,128,128]{2,1,0:T(8,128)(2,1)S(1)}, bf16[8,128,128]{2,1,0:T(8,128)(2,1)S(1)}, u32[]{:S(2)}, u32[]{:S(2)}) collective-permute-start(bf16[8,128,128]{2,1,0:T(8,128)(2,1)S(1)} %take_own.1.rest_0_), channel_id=1, source_target_pairs={{0,2},{1,3},{2,0},{3,1},{4,6},{5,7},{6,4},{7,5},{8,10},{9,11},{10,... | collective-permute-start | bytes 786440 | tf_op jit(solution)/shard_map/ppermute | solution.py:501
  6.0 2.6 %collective-permute-start.4 = (bf16[8,128,128]{2,1,0:T(8,128)(2,1)S(1)}, bf16[8,128,128]{2,1,0:T(8,128)(2,1)S(1)}, u32[]{:S(2)}, u32[]{:S(2)}) collective-permute-start(bf16[8,128,128]{2,1,0:T(8,128)(2,1)S(1)} %take_own.1.rest_0_), channel_id=1, source_target_pairs={{0,4},{1,5},{2,6},{3,7},{4,0},{5,1},{6,2},{7,3},{8,12},{9,13},{10,... | collective-permute-start | bytes 786440 | tf_op jit(solution)/shard_map/ppermute | solution.py:501
  12.4 3.4 %all-to-all-start = ((bf16[3,8,8,512]{3,2,0,1:T(8,128)(2,1)}), bf16[3,8,8,512]{3,2,0,1:T(8,128)(2,1)S(1)}, u32[]{:S(2)}, u32[]{:S(2)}) async-start(bf16[3,8,8,512]{3,2,0,1:T(8,128)(2,1)} %copy.46), calls=%async_computation | async-start | bytes 393216 | tf_op jit(solution)/shard_map/all_to_all | solution.py:520
  17.0 3.4 %collective-permute-done.4.rest_2_ = bf16[8,128,128]{2,1,0:T(8,128)(2,1)S(1)} collective-permute-done((bf16[8,128,128]{2,1,0:T(8,128)(2,1)S(1)}, bf16[8,128,128]{2,1,0:T(8,128)(2,1)S(1)}, u32[]{:S(2)}, u32[]{:S(2)}) %collective-permute-start.4) | collective-permute-done | bytes 262176 | tf_op jit(solution)/shard_map/ppermute | solution.py:501
  20.4 2.8 %collective-permute-start.5 = (bf16[8,128,128]{2,1,0:T(8,128)(2,1)S(1)}, bf16[8,128,128]{2,1,0:T(8,128)(2,1)S(1)}, u32[]{:S(2)}, u32[]{:S(2)}) collective-permute-start(bf16[8,128,128]{2,1,0:T(8,128)(2,1)S(1)} %collective-permute-done.4.rest_2_), channel_id=1, source_target_pairs={{0,2},{1,3},{2,0},{3,1},{4,6},{5,7},{6,4},{7,5},{8,10},{9,11},{10,... | collective-permute-start | bytes 786440 | tf_op jit(solution)/shard_map/ppermute | solution.py:501
  23.2 1.4 %all-to-all-done = bf16[3,8,8,512]{3,2,0,1:T(8,128)(2,1)S(1)} async-done(((bf16[3,8,8,512]{3,2,0,1:T(8,128)(2,1)}), bf16[3,8,8,512]{3,2,0,1:T(8,128)(2,1)S(1)}, u32[]{:S(2)}, u32[]{:S(2)}) %all-to-all-start) | async-done | bytes 196640 | tf_op jit(solution)/shard_map/all_to_all | solution.py:520
  25.2 2.5 %collective-permute-start.2 = (bf16[17,8,512]{2,1,0:T(8,128)(2,1)S(1)}, bf16[17,8,512]{2,1,0:T(8,128)(2,1)S(1)}, u32[]{:S(2)}, u32[]{:S(2)}) collective-permute-start(bf16[17,8,512]{2,1,0:T(8,128)(2,1)S(1)} %get-tuple-element.38), channel_id=1, source_target_pairs={{0,24},{8,16},{16,8},{24,0},{1,25},{9,17},{17,9},{25,1},{2,26},{10... | collective-permute-start | bytes 417800 | tf_op jit(solution)/shard_map/ppermute | solution.py:528
  29.6 2.6 %collective-permute-done.2 = bf16[17,8,512]{2,1,0:T(8,128)(2,1)S(1)} collective-permute-done((bf16[17,8,512]{2,1,0:T(8,128)(2,1)S(1)}, bf16[17,8,512]{2,1,0:T(8,128)(2,1)S(1)}, u32[]{:S(2)}, u32[]{:S(2)}) %collective-permute-start.2) | collective-permute-done | bytes 139296 | tf_op jit(solution)/shard_map/ppermute | solution.py:528
  32.2 2.5 %collective-permute-done.1 = bf16[17,8,512]{2,1,0:T(8,128)(2,1)S(1)} collective-permute-done((bf16[17,8,512]{2,1,0:T(8,128)(2,1)S(1)}, bf16[17,8,512]{2,1,0:T(8,128)(2,1)S(1)}, u32[]{:S(2)}, u32[]{:S(2)}) %collective-permute-start.1) | collective-permute-done | bytes 139296 | tf_op jit(solution)/shard_map/ppermute | solution.py:528
  36.6 2.8 %contributions.1 = (s32[5,17,8,128]{3,2,1,0:T(8,128)S(1)}, s32[5,17,8,128]{3,2,1,0:T(8,128)S(1)}, s32[5,17,8,128]{3,2,1,0:T(8,128)S(1)}, s32[5,17,8,128]{3,2,1,0:T(8,128)S(1)}) custom-call(s32[1]{0:T(128)} %bitcast.2.mine_ref.place_ref.freq_ref, s32[16]{0:T(128)S(1)} %add.129.order_ref, s32[40]{0:T(128)S(1)} %get-tuple-element.45.slot_ref, ...), custom_call_target="tpu_custom_call" | custom-call | tf_op jit(solution)/shard_map/contributions/pallas_call | solution.py:553
  40.9 1.5 %collective-permute-start.10 = (s32[5,17,8,128]{3,2,1,0:T(8,128)}, s32[5,17,8,128]{3,2,1,0:T(8,128)S(1)}, u32[]{:S(2)}, u32[]{:S(2)}) collective-permute-start(s32[5,17,8,128]{3,2,1,0:T(8,128)} %copy-done.11), channel_id=1, source_target_pairs={{0,8},{8,0},{16,24},{24,16},{1,9},{9,1},{17,25},{25,17},{2,10},{10... | collective-permute-start | bytes 1044488 | tf_op jit(solution)/shard_map/ppermute | solution.py:571
  43.3 1.2 %collective-permute-start.12 = (s32[5,17,8,128]{3,2,1,0:T(8,128)S(1)}, s32[5,17,8,128]{3,2,1,0:T(8,128)S(1)}, u32[]{:S(2)}, u32[]{:S(2)}) collective-permute-start(s32[5,17,8,128]{3,2,1,0:T(8,128)S(1)} %get-tuple-element.31), channel_id=1, source_target_pairs={{0,24},{8,16},{16,8},{24,0},{1,25},{9,17},{17,9},{25,1},{2,26},{10... | collective-permute-start | bytes 1044488 | tf_op jit(solution)/shard_map/ppermute | solution.py:571
  45.0 14.6 %propagator.1 = (f32[256,2048]{1,0:T(8,128)S(1)}, f32[256,2048]{1,0:T(8,128)S(1)}) custom-call(f32[1]{0:T(128)} %bitcast.27.omega_ref), custom_call_target="tpu_custom_call" | custom-call | flops 31457280 | bytes 4194304 | tf_op jit(solution)/shard_map/propagator/pallas_call | solution.py:581
  60.2 25.7 %march.1.plane_ref = f32[2,2,128,2048]{3,2,1,0:T(8,128)S(1)} custom-call(f32[2,2,8,16]{3,2,1,0:T(8,128)S(1)} %pad_maximum_fusion.3.layer_ref, s32[5,17,8,128]{3,2,1,0:T(8,128)S(1)} %get-tuple-element.28.rest_0_, s32[5,17,8,128]{3,2,1,0:T(8,128)S(1)} %collective-permute-done.10.rest_1_, s32[5,17,8,128]{3,2,1,0:T(8,128)S(1)} %collective-permute-done.11.rest_2_, ...), custom_call_target="tpu_custom_call" | custom-call | tf_op jit(solution)/shard_map/march/pallas_call | solution.py:604
  86.0 1.7 %finish.4.rest_0_ = s32[1032,128]{1,0:T(8,128)S(1)} custom-call(s32[1]{0:T(128)} %bitcast.29.dest_ref, f32[2,2,8,16]{3,2,1,0:T(8,128)S(1)} %pad_maximum_fusion.3.layer_ref, f32[2,2,128,2048]{3,2,1,0:T(8,128)S(1)} %march.1.plane_ref, bf16[256,768]{1,0:T(8,128)(2,1)S(1)} %copy-done.2, f32[2,128,128]{2,1,0:T(8,128)S(1)} %copy-done.3), custom_call_target="tpu_custom_call" | custom-call | flops 402653184 | bytes 786432 | tf_op jit(solution)/shard_map/finish/pallas_call | solution.py:618
  87.7 1.6 %collective-permute-start.15 = (s32[1032,128]{1,0:T(8,128)S(1)}, s32[1032,128]{1,0:T(8,128)}, u32[]{:S(2)}, u32[]{:S(2)}) collective-permute-start(s32[1032,128]{1,0:T(8,128)S(1)} %finish.4.rest_0_), channel_id=1, source_target_pairs={{0,24},{8,16},{16,8},{24,0},{1,25},{9,17},{17,9},{25,1},{2,26},{10... | collective-permute-start | bytes 1585160 | tf_op jit(solution)/shard_map/ppermute | solution.py:646
  89.2 1.7 %finish.5.rest_0_ = s32[1032,128]{1,0:T(8,128)S(1)} custom-call(s32[1]{0:T(128)} %bitcast.28.dest_ref, f32[2,2,8,16]{3,2,1,0:T(8,128)S(1)} %pad_maximum_fusion.3.layer_ref, f32[2,2,128,2048]{3,2,1,0:T(8,128)S(1)} %march.1.plane_ref, bf16[256,768]{1,0:T(8,128)(2,1)S(1)} %copy-done.2, f32[2,128,128]{2,1,0:T(8,128)S(1)} %copy-done.3, s32[1032,128]{1,0:T(8,128)S(1)} %finish.4.rest_0_), custom_call_target="tpu_custom_call" | custom-call | flops 402653184 | bytes 786432 | tf_op jit(solution)/shard_map/finish/pallas_call | solution.py:618
  92.0 1.7 %finish.6.rest_0_ = s32[1032,128]{1,0:T(8,128)S(1)} custom-call(s32[1]{0:T(128)} %bitcast.1.dest_ref, f32[2,2,8,16]{3,2,1,0:T(8,128)S(1)} %pad_maximum_fusion.3.layer_ref, f32[2,2,128,2048]{3,2,1,0:T(8,128)S(1)} %march.1.plane_ref, bf16[256,768]{1,0:T(8,128)(2,1)S(1)} %copy-done.2, f32[2,128,128]{2,1,0:T(8,128)S(1)} %copy-done.3, s32[1032,128]{1,0:T(8,128)S(1)} %finish.5.rest_0_), custom_call_target="tpu_custom_call" | custom-call | flops 402653184 | bytes 786432 | tf_op jit(solution)/shard_map/finish/pallas_call | solution.py:618
  94.8 2.2 %copy-done.1 = f32[2,2,128,2048]{3,2,1,0:T(8,128)S(1)} copy-done((f32[2,2,128,2048]{3,2,1,0:T(8,128)S(1)}, f32[2,2,128,2048]{3,2,1,0:T(8,128)}, u32[]{:S(2)}) %copy-start.1) | copy-done | bytes 4194328
  97.0 1.7 %finish.7.code_ref = s32[1032,128]{1,0:T(8,128)S(1)} custom-call(s32[1]{0:T(128)} %bitcast.32.dest_ref, f32[2,2,8,16]{3,2,1,0:T(8,128)S(1)} %pad_maximum_fusion.3.layer_ref, f32[2,2,128,2048]{3,2,1,0:T(8,128)S(1)} %copy-done.1, bf16[256,768]{1,0:T(8,128)(2,1)S(1)} %copy-done.2, f32[2,128,128]{2,1,0:T(8,128)S(1)} %copy-done.3, s32[1032,128]{1,0:T(8,128)S(1)} %finish.6.rest_0_), custom_call_target="tpu_custom_call" | custom-call | flops 402653184 | bytes 786432 | tf_op jit(solution)/shard_map/finish/pallas_call | solution.py:618
  99.7 4.0 %collective-permute-done.15.code_ref = s32[1032,128]{1,0:T(8,128)} collective-permute-done((s32[1032,128]{1,0:T(8,128)S(1)}, s32[1032,128]{1,0:T(8,128)}, u32[]{:S(2)}, u32[]{:S(2)}) %collective-permute-start.15) | collective-permute-done | bytes 528416 | tf_op jit(solution)/shard_map/ppermute | solution.py:646
  103.7 2.1 %result.5.rest_0_ = f32[4,256,8,128]{3,2,1,0:T(8,128)} custom-call(s32[1]{0:T(128)} %bitcast.31.freq_ref, s32[1032,128]{1,0:T(8,128)} %collective-permute-done.15.code_ref, f32[4,256,8,128]{3,2,1,0:T(8,128)} %result.4.rest_0_), custom_call_target="tpu_custom_call", output_to_operand_aliasing={{}: (2, {})} | custom-call | flops 524288 | bytes 1572864 | tf_op jit(solution)/shard_map/result/pallas_call | solution.py:653
  105.8 7.3 %collective-permute-done.14.code_ref = s32[1032,128]{1,0:T(8,128)S(1)} collective-permute-done((s32[1032,128]{1,0:T(8,128)S(1)}, s32[1032,128]{1,0:T(8,128)S(1)}, u32[]{:S(2)}, u32[]{:S(2)}) %collective-permute-start.14) | collective-permute-done | bytes 528416 | tf_op jit(solution)/shard_map/ppermute | solution.py:646
  (105 shorter events, 19.6 us)
Async XLA Ops:
  2.9 26.6 %collective-permute-start.3 = (bf16[8,128,128]{2,1,0:T(8,128)(2,1)S(1)}, bf16[8,128,128]{2,1,0:T(8,128)(2,1)S(1)}, u32[]{:S(2)}, u32[]{:S(2)}) collective-permute-start(bf16[8,128,128]{2,1,0:T(8,128)(2,1)S(1)} %take_own.1.rest_0_), channel_id=1, source_target_pairs={{0,2},{1,3},{2,0},{3,1},{4,6},{5,7},{6,4},{7,5},{8,10},{9,11},{10,... | collective-permute-start | bytes 786440 | tf_op jit(solution)/shard_map/ppermute | solution.py:501
  6.0 14.4 %collective-permute-start.4 = (bf16[8,128,128]{2,1,0:T(8,128)(2,1)S(1)}, bf16[8,128,128]{2,1,0:T(8,128)(2,1)S(1)}, u32[]{:S(2)}, u32[]{:S(2)}) collective-permute-start(bf16[8,128,128]{2,1,0:T(8,128)(2,1)S(1)} %take_own.1.rest_0_), channel_id=1, source_target_pairs={{0,4},{1,5},{2,6},{3,7},{4,0},{5,1},{6,2},{7,3},{8,12},{9,13},{10,... | collective-permute-start | bytes 786440 | tf_op jit(solution)/shard_map/ppermute | solution.py:501
  11.6 32.8 %copy-start.12 = (f32[2,16]{1,0:T(2,128)S(1)}, f32[2,16]{1,0:T(2,128)}, u32[]{:S(2)}) copy-start(f32[2,16]{1,0:T(2,128)} %param.17) | copy-start | bytes 388
  12.4 12.2 %all-to-all-start = ((bf16[3,8,8,512]{3,2,0,1:T(8,128)(2,1)}), bf16[3,8,8,512]{3,2,0,1:T(8,128)(2,1)S(1)}, u32[]{:S(2)}, u32[]{:S(2)}) async-start(bf16[3,8,8,512]{3,2,0,1:T(8,128)(2,1)} %copy.46), calls=%async_computation | async-start | bytes 393216 | tf_op jit(solution)/shard_map/all_to_all | solution.py:520
  20.4 14.5 %collective-permute-start.5 = (bf16[8,128,128]{2,1,0:T(8,128)(2,1)S(1)}, bf16[8,128,128]{2,1,0:T(8,128)(2,1)S(1)}, u32[]{:S(2)}, u32[]{:S(2)}) collective-permute-start(bf16[8,128,128]{2,1,0:T(8,128)(2,1)S(1)} %collective-permute-done.4.rest_2_), channel_id=1, source_target_pairs={{0,2},{1,3},{2,0},{3,1},{4,6},{5,7},{6,4},{7,5},{8,10},{9,11},{10,... | collective-permute-start | bytes 786440 | tf_op jit(solution)/shard_map/ppermute | solution.py:501
  25.2 7.1 %collective-permute-start.2 = (bf16[17,8,512]{2,1,0:T(8,128)(2,1)S(1)}, bf16[17,8,512]{2,1,0:T(8,128)(2,1)S(1)}, u32[]{:S(2)}, u32[]{:S(2)}) collective-permute-start(bf16[17,8,512]{2,1,0:T(8,128)(2,1)S(1)} %get-tuple-element.38), channel_id=1, source_target_pairs={{0,24},{8,16},{16,8},{24,0},{1,25},{9,17},{17,9},{25,1},{2,26},{10... | collective-permute-start | bytes 417800 | tf_op jit(solution)/shard_map/ppermute | solution.py:528
  27.7 7.1 %collective-permute-start.1 = (bf16[17,8,512]{2,1,0:T(8,128)(2,1)S(1)}, bf16[17,8,512]{2,1,0:T(8,128)(2,1)S(1)}, u32[]{:S(2)}, u32[]{:S(2)}) collective-permute-start(bf16[17,8,512]{2,1,0:T(8,128)(2,1)S(1)} %get-tuple-element.38), channel_id=1, source_target_pairs={{0,16},{8,24},{16,0},{24,8},{1,17},{9,25},{17,1},{25,9},{2,18},{10... | collective-permute-start | bytes 417800 | tf_op jit(solution)/shard_map/ppermute | solution.py:528
  28.2 6.6 %collective-permute-start = (bf16[17,8,512]{2,1,0:T(8,128)(2,1)S(1)}, bf16[17,8,512]{2,1,0:T(8,128)(2,1)S(1)}, u32[]{:S(2)}, u32[]{:S(2)}) collective-permute-start(bf16[17,8,512]{2,1,0:T(8,128)(2,1)S(1)} %get-tuple-element.38), channel_id=1, source_target_pairs={{0,8},{8,0},{16,24},{24,16},{1,9},{9,1},{17,25},{25,17},{2,10},{10... | collective-permute-start | bytes 417800 | tf_op jit(solution)/shard_map/ppermute | solution.py:528
  29.5 6.5 %collective-permute-start.6 = (bf16[8,128,128]{2,1,0:T(8,128)(2,1)S(1)}, bf16[8,128,128]{2,1,0:T(8,128)(2,1)S(1)}, u32[]{:S(2)}, u32[]{:S(2)}) collective-permute-start(bf16[8,128,128]{2,1,0:T(8,128)(2,1)S(1)} %take_own.1.rest_0_), channel_id=1, source_target_pairs={{0,1},{1,0},{2,3},{3,2},{4,5},{5,4},{6,7},{7,6},{8,9},{9,8},{10,11... | collective-permute-start | bytes 786440 | tf_op jit(solution)/shard_map/ppermute | solution.py:508
  32.2 4.1 %collective-permute-start.8 = (bf16[8,128,128]{2,1,0:T(8,128)(2,1)S(1)}, bf16[8,128,128]{2,1,0:T(8,128)(2,1)S(1)}, u32[]{:S(2)}, u32[]{:S(2)}) collective-permute-start(bf16[8,128,128]{2,1,0:T(8,128)(2,1)S(1)} %collective-permute-done.4.rest_2_), channel_id=1, source_target_pairs={{0,1},{1,0},{2,3},{3,2},{4,5},{5,4},{6,7},{7,6},{8,9},{9,8},{10,11... | collective-permute-start | bytes 786440 | tf_op jit(solution)/shard_map/ppermute | solution.py:508
  34.7 1.5 %collective-permute-start.7 = (bf16[8,128,128]{2,1,0:T(8,128)(2,1)S(1)}, bf16[8,128,128]{2,1,0:T(8,128)(2,1)S(1)}, u32[]{:S(2)}, u32[]{:S(2)}) collective-permute-start(bf16[8,128,128]{2,1,0:T(8,128)(2,1)S(1)} %collective-permute-done.3.rest_1_), channel_id=1, source_target_pairs={{0,1},{1,0},{2,3},{3,2},{4,5},{5,4},{6,7},{7,6},{8,9},{9,8},{10,11... | collective-permute-start | bytes 786440 | tf_op jit(solution)/shard_map/ppermute | solution.py:508
  34.9 1.7 %collective-permute-start.9 = (bf16[8,128,128]{2,1,0:T(8,128)(2,1)S(1)}, bf16[8,128,128]{2,1,0:T(8,128)(2,1)S(1)}, u32[]{:S(2)}, u32[]{:S(2)}) collective-permute-start(bf16[8,128,128]{2,1,0:T(8,128)(2,1)S(1)} %collective-permute-done.5.rest_3_), channel_id=1, source_target_pairs={{0,1},{1,0},{2,3},{3,2},{4,5},{5,4},{6,7},{7,6},{8,9},{9,8},{10,11... | collective-permute-start | bytes 786440 | tf_op jit(solution)/shard_map/ppermute | solution.py:508
  40.9 18.7 %collective-permute-start.10 = (s32[5,17,8,128]{3,2,1,0:T(8,128)}, s32[5,17,8,128]{3,2,1,0:T(8,128)S(1)}, u32[]{:S(2)}, u32[]{:S(2)}) collective-permute-start(s32[5,17,8,128]{3,2,1,0:T(8,128)} %copy-done.11), channel_id=1, source_target_pairs={{0,8},{8,0},{16,24},{24,16},{1,9},{9,1},{17,25},{25,17},{2,10},{10... | collective-permute-start | bytes 1044488 | tf_op jit(solution)/shard_map/ppermute | solution.py:571
  42.4 17.7 %collective-permute-start.11 = (s32[5,17,8,128]{3,2,1,0:T(8,128)}, s32[5,17,8,128]{3,2,1,0:T(8,128)S(1)}, u32[]{:S(2)}, u32[]{:S(2)}) collective-permute-start(s32[5,17,8,128]{3,2,1,0:T(8,128)} %copy-done.10), channel_id=1, source_target_pairs={{0,16},{8,24},{16,0},{24,8},{1,17},{9,25},{17,1},{25,9},{2,18},{10... | collective-permute-start | bytes 1044488 | tf_op jit(solution)/shard_map/ppermute | solution.py:571
  43.3 16.9 %collective-permute-start.12 = (s32[5,17,8,128]{3,2,1,0:T(8,128)S(1)}, s32[5,17,8,128]{3,2,1,0:T(8,128)S(1)}, u32[]{:S(2)}, u32[]{:S(2)}) collective-permute-start(s32[5,17,8,128]{3,2,1,0:T(8,128)S(1)} %get-tuple-element.31), channel_id=1, source_target_pairs={{0,24},{8,16},{16,8},{24,0},{1,25},{9,17},{17,9},{25,1},{2,26},{10... | collective-permute-start | bytes 1044488 | tf_op jit(solution)/shard_map/ppermute | solution.py:571
  45.0 15.2 %copy-start.2 = (bf16[256,768]{1,0:T(8,128)(2,1)S(1)}, bf16[256,768]{1,0:T(8,128)(2,1)}, u32[]{:S(2)}) copy-start(bf16[256,768]{1,0:T(8,128)(2,1)} %constant.143.clone.rest_8_.rows_inverse) | copy-start | bytes 1179652
  45.0 15.2 %copy-start.3 = (f32[2,128,128]{2,1,0:T(8,128)S(1)}, f32[2,128,128]{2,1,0:T(8,128)}, u32[]{:S(2)}) copy-start(f32[2,128,128]{2,1,0:T(8,128)} %constant.147.clone.rest_12_.offset_ref) | copy-start | bytes 393220
  45.0 15.2 %copy-start.5 = (bf16[256,768]{1,0:T(8,128)(2,1)S(1)}, bf16[256,768]{1,0:T(8,128)(2,1)}, u32[]{:S(2)}) copy-start(bf16[256,768]{1,0:T(8,128)(2,1)} %constant.142.clone.rest_7_) | copy-start | bytes 1179652
  45.0 15.2 %copy-start.6 = (bf16[768,256]{1,0:T(8,128)(2,1)S(1)}, bf16[768,256]{1,0:T(8,128)(2,1)}, u32[]{:S(2)}) copy-start(bf16[768,256]{1,0:T(8,128)(2,1)} %constant.144.clone.rest_9_) | copy-start | bytes 1179652
  45.0 15.2 %copy-start.7 = (bf16[768,256]{1,0:T(8,128)(2,1)S(1)}, bf16[768,256]{1,0:T(8,128)(2,1)}, u32[]{:S(2)}) copy-start(bf16[768,256]{1,0:T(8,128)(2,1)} %constant.145.clone.rest_10_) | copy-start | bytes 1179652
  45.0 15.2 %copy-start.8 = (f32[2,16,128]{2,1,0:T(8,128)S(1)}, f32[2,16,128]{2,1,0:T(8,128)}, u32[]{:S(2)}) copy-start(f32[2,16,128]{2,1,0:T(8,128)} %constant.146.clone.rest_11_) | copy-start | bytes 49156
  87.7 16.1 %collective-permute-start.15 = (s32[1032,128]{1,0:T(8,128)S(1)}, s32[1032,128]{1,0:T(8,128)}, u32[]{:S(2)}, u32[]{:S(2)}) collective-permute-start(s32[1032,128]{1,0:T(8,128)S(1)} %finish.4.rest_0_), channel_id=1, source_target_pairs={{0,24},{8,16},{16,8},{24,0},{1,25},{9,17},{17,9},{25,1},{2,26},{10... | collective-permute-start | bytes 1585160 | tf_op jit(solution)/shard_map/ppermute | solution.py:646
  90.9 22.2 %collective-permute-start.14 = (s32[1032,128]{1,0:T(8,128)S(1)}, s32[1032,128]{1,0:T(8,128)S(1)}, u32[]{:S(2)}, u32[]{:S(2)}) collective-permute-start(s32[1032,128]{1,0:T(8,128)S(1)} %finish.5.rest_0_), channel_id=1, source_target_pairs={{0,16},{8,24},{16,0},{24,8},{1,17},{9,25},{17,1},{25,9},{2,18},{10... | collective-permute-start | bytes 1585160 | tf_op jit(solution)/shard_map/ppermute | solution.py:646
  93.7 20.5 %collective-permute-start.13 = (s32[1032,128]{1,0:T(8,128)S(1)}, s32[1032,128]{1,0:T(8,128)S(1)}, u32[]{:S(2)}, u32[]{:S(2)}) collective-permute-start(s32[1032,128]{1,0:T(8,128)S(1)} %finish.6.rest_0_), channel_id=1, source_target_pairs={{0,8},{8,0},{16,24},{24,16},{1,9},{9,1},{17,25},{25,17},{2,10},{10... | collective-permute-start | bytes 1585160 | tf_op jit(solution)/shard_map/ppermute | solution.py:646
  (6 other events, 11.6 us)

commit v7 on v6

--- a/solution.py
+++ b/solution.py
@@ -19,10 +19,8 @@
 STEP_LOG = 64.0
 TOP = 32767.0
 GROUP = 8
-COLUMNS = 2
 ROWS = 8
-CHUNKS = 4
-UNROLL = 2
+CHUNKS = 2
 VMEM = 28 * 1024 * 1024
 SMALL = 10 * 1024 * 1024
 
@@ -87,14 +85,49 @@
     return jnp.dot(left, right, preferred_element_type=jnp.float32)
 
 
-def left_product(table, value):
-    high, low = halves(value)
-    return dot(table, jnp.concatenate([high, low, high], axis=0))
-
-
-def right_product(value, table):
-    high, low = halves(value)
-    return dot(jnp.concatenate([high, low, high], axis=1), table)
+def aligned(start, size):
+    return start if isinstance(start, int) else pl.multiple_of(start, size)
+
+
+def pipelined(count, *stages):
+    first, second, third = stages
+    first(0, 0)
+    second(0, 0)
+    first(1, 1)
+
+    @pl.loop(1, count // 2)
+    def _(pair):
+        tile = 2 * pair
+        third(tile - 2, 0)
+        second(tile - 1, 1)
+        first(tile, 0)
+        third(tile - 1, 1)
+        second(tile, 0)
+        first(tile + 1, 1)
+
+    third(count - 2, 0)
+    second(count - 1, 1)
+    third(count - 1, 1)
+
+
+def keep_rows(ref, value):
+    size = value.shape[0]
+    ref[:size], ref[size:] = halves(value)
+
+
+def keep_lanes(ref, value):
+    size = value.shape[1]
+    ref[:, :size], ref[:, size:] = halves(value)
+
+
+def left_product(table, ref):
+    size = ref.shape[0] // 2
+    return dot(table, jnp.concatenate([ref[...], ref[:size]], axis=0))
+
+
+def right_product(ref, table):
+    size = ref.shape[1] // 2
+    return dot(jnp.concatenate([ref[...], ref[:, :size]], axis=1), table)
 
 
 def cmul(real_a, imag_a, real_b, imag_b):
@@ -188,7 +221,7 @@
 
 
 def column_of(plane, a):
-    lanes = pl.ds(pl.multiple_of(a * BLK, BLK), BLK)
+    lanes = pl.ds(aligned(a * BLK, BLK), BLK)
     return jnp.concatenate(
         [
             jnp.concatenate([plane[p, 0, :, lanes], plane[p, 1, :, lanes]], axis=0)
@@ -199,7 +232,7 @@
 
 
 def store_column(plane, a, value):
-    lanes = pl.ds(pl.multiple_of(a * BLK, BLK), BLK)
+    lanes = pl.ds(aligned(a * BLK, BLK), BLK)
     for p in range(2):
         for c in range(2):
             plane[p, c, :, lanes] = value[c * HALF : (c + 1) * HALF, p * BLK : (p + 1) * BLK]
@@ -235,7 +268,17 @@
     )
 
 
-def propagator_kernel(omega_ref, real_ref, imag_ref):
+def propagator_kernel(omega_ref, slow_ref, layers_ref, real_ref, imag_ref, turns_ref):
+    steps, layer_total = slow_ref.shape
+    for step in range(steps):
+        layers = layers_ref[step]
+        slow = functools.reduce(
+            jnp.add, [jnp.where(layers == n, slow_ref[step, n], 0.0) for n in range(layer_total)]
+        )
+        turn = 2.0 * dz_cells * omega_ref[0] * (slow - 1.0)
+        turns_ref[0, step] = jnp.cos(turn)
+        turns_ref[1, step] = jnp.sin(turn)
+
     total = real_ref.shape[1]
     scale = 1.0 / (NH * total)
     omega_sq = omega_ref[0] * omega_ref[0]
@@ -253,11 +296,6 @@
             imag_ref[pl.ds(start, GROUP), a * BLK : (a + 1) * BLK] = imag * scale
 
 
-def offset_product(table, columns):
-    value = left_product(table[...], jnp.concatenate(columns, axis=1))
-    return [value[:, n * 2 * BLK : (n + 1) * 2 * BLK] for n in range(len(columns))]
-
-
 def layer_turn(pair, layer_ref, step, block, a):
     half = layer_ref.shape[2] // 2
     return [
@@ -266,34 +304,37 @@
     ]
 
 
-def midpoint_pass(plane, out, phase_refs, forward, inverse, middle_ref):
+def midpoint_pass(plane, out, phase_refs, forward, inverse, middle_ref, first_kept, second_kept):
     outer = middle_ref.shape[1]
     lanes = [slice(a * BLK, (a + 1) * BLK) for a in range(outer)]
-    tall = ROWS * CHUNKS
+    tall = first_kept[0].shape[0] // outer
     per_half = HALF // tall
-
-    @pl.loop(0, 2 * per_half, unroll=UNROLL)
-    def _(at):
-        p = at // per_half
-        base = pl.multiple_of((at % per_half) * tall, tall)
-        phase_base = pl.multiple_of(at * tall, tall)
-
-        def gathered(pieces):
-            return jnp.concatenate([jnp.concatenate(pair, axis=1) for pair in pieces], axis=0)
-
+    chunks = range(0, tall, ROWS)
+
+    def place(at):
+        return at // per_half, (at % per_half) * tall
+
+    def gathered(pieces):
+        return jnp.concatenate([jnp.concatenate(pair, axis=1) for pair in pieces], axis=0)
+
+    def forward_stage(at, parity):
+        p, base = place(at)
         pieces = []
-        for chunk in range(CHUNKS):
-            here = pl.ds(base + chunk * ROWS, ROWS)
+        for chunk in chunks:
+            here = pl.ds(aligned(base + chunk, ROWS), ROWS)
             values = [(plane[p, 0, here, lane], plane[p, 1, here, lane]) for lane in lanes]
             values = small_transform(values, -1)
             for a in range(outer):
                 pieces.append(cmul(*values[a], middle_ref[0, a : a + 1], -middle_ref[1, a : a + 1]))
-        value = right_product(gathered(pieces), forward[...])
+        keep_lanes(first_kept[parity], gathered(pieces))
+
+    def phase_stage(at, parity):
+        value = right_product(first_kept[parity], forward[...])
         pieces = []
-        for chunk in range(CHUNKS):
-            there = pl.ds(phase_base + chunk * ROWS, ROWS)
+        for chunk in chunks:
+            there = pl.ds(aligned(at * tall + chunk, ROWS), ROWS)
             for a in range(outer):
-                row = (chunk * outer + a) * ROWS
+                row = chunk * outer + a * ROWS
                 part = value[row : row + ROWS]
                 pieces.append(
                     cmul(
@@ -301,12 +342,16 @@
                         phase_refs[0][there, lanes[a]], phase_refs[1][there, lanes[a]],
                     )
                 )
-        value = right_product(gathered(pieces), inverse[...])
-        for chunk in range(CHUNKS):
-            here = pl.ds(base + chunk * ROWS, ROWS)
+        keep_lanes(second_kept[parity], gathered(pieces))
+
+    def inverse_stage(at, parity):
+        p, base = place(at)
+        value = right_product(second_kept[parity], inverse[...])
+        for chunk in chunks:
+            here = pl.ds(aligned(base + chunk, ROWS), ROWS)
             values = []
             for a in range(outer):
-                row = (chunk * outer + a) * ROWS
+                row = chunk * outer + a * ROWS
                 part = value[row : row + ROWS]
                 values.append(
                     cmul(part[:, :BLK], part[:, BLK:], middle_ref[0, a : a + 1], middle_ref[1, a : a + 1])
@@ -316,13 +361,16 @@
                 out[p, 0, here, lanes[a]] = values[a][0]
                 out[p, 1, here, lanes[a]] = values[a][1]
 
+    pipelined(2 * per_half, forward_stage, phase_stage, inverse_stage)
+
 
 def march_kernel(layer_ref, *rest, sources):
     code_refs, rest = rest[:sources], rest[sources:]
     (
         pick_ref, phase_real, phase_imag, rows_forward, rows_inverse, lanes_forward, lanes_inverse,
-        middle_ref, offset_ref, other, plane, scales,
+        middle_ref, offset_ref, other, plane, scales, *kept,
     ) = rest
+    column_first, column_second, row_first, row_second, terms = (kept[n : n + 2] for n in range(0, 10, 2))
     groups = code_refs[0].shape[0]
     outer = middle_ref.shape[1]
     steps = layer_ref.shape[1]
@@ -333,54 +381,57 @@
 
     scales[...] = scale_of(words(outer))
 
-    @pl.loop(0, outer // COLUMNS, unroll=2)
-    def _(at):
-        columns = []
-        for a in range(COLUMNS):
-            real, imag = unpacked(words(at * COLUMNS + a))
-            scale = scales[...]
-            value = jnp.concatenate([real * scale, imag * scale], axis=1)
-            moved = dot(pick_ref[...], jnp.concatenate(halves(value), axis=0))
-            blocks = []
-            for rows in row_blocks(tall):
-                low, high = moved[rows], moved[HALF + rows.start : HALF + rows.stop]
-                blocks.append(
-                    forward_rows(
-                        (low[:, :BLK], low[:, BLK:]), (high[:, :BLK], high[:, BLK:]),
-                        turn_at(offset_ref, rows),
-                    )
+    def decode_stage(a, parity):
+        real, imag = unpacked(words(a))
+        scale = scales[...]
+        keep_rows(terms[parity], jnp.concatenate([real * scale, imag * scale], axis=1))
+
+    def place_stage(a, parity):
+        moved = dot(pick_ref[...], terms[parity][...])
+        blocks = []
+        for rows in row_blocks(tall):
+            low, high = moved[rows], moved[HALF + rows.start : HALF + rows.stop]
+            blocks.append(
+                forward_rows(
+                    (low[:, :BLK], low[:, BLK:]), (high[:, :BLK], high[:, BLK:]), turn_at(offset_ref, rows)
                 )
-            columns.append(assembled(blocks))
-        for a, value in enumerate(offset_product(rows_forward, columns)):
-            store_column(plane, at * COLUMNS + a, value)
+            )
+        keep_rows(column_second[parity], assembled(blocks))
+
+    def store_stage(a, parity):
+        store_column(plane, a, left_product(rows_forward[...], column_second[parity]))
+
+    pipelined(outer, decode_stage, place_stage, store_stage)
 
     for step in range(steps):
-        midpoint_pass(plane, other, (phase_real, phase_imag), lanes_forward, lanes_inverse, middle_ref)
+        midpoint_pass(
+            plane, other, (phase_real, phase_imag), lanes_forward, lanes_inverse, middle_ref, row_first, row_second
+        )
         if step < steps - 1:
 
-            @pl.loop(0, outer // COLUMNS, unroll=2)
-            def _(at):
-                places = [at * COLUMNS + a for a in range(COLUMNS)]
-                columns = []
-                for a, value in zip(
-                    places, offset_product(rows_inverse, [column_of(other, a) for a in places])
-                ):
-                    blocks = []
-                    for block, rows in enumerate(row_blocks(tall)):
-                        turn = turn_at(offset_ref, rows)
-                        pair = inverse_rows(value, rows, turn)
-                        blocks.append(forward_rows(*layer_turn(pair, layer_ref, step, block, a), turn))
-                    columns.append(assembled(blocks))
-                for a, value in zip(places, offset_product(rows_forward, columns)):
-                    store_column(plane, a, value)
+            def load_stage(a, parity):
+                keep_rows(column_first[parity], column_of(other, a))
+
+            def turn_stage(a, parity):
+                value = left_product(rows_inverse[...], column_first[parity])
+                blocks = []
+                for block, rows in enumerate(row_blocks(tall)):
+                    turn = turn_at(offset_ref, rows)
+                    pair = inverse_rows(value, rows, turn)
+                    blocks.append(forward_rows(*layer_turn(pair, layer_ref, step, block, a), turn))
+                keep_rows(column_second[parity], assembled(blocks))
+
+            pipelined(outer, load_stage, turn_stage, store_stage)
 
 
 def finish_kernel(dest_ref, layer_ref, plane_ref, rows_inverse, offset_ref, *rest):
-    out_ref = rest[-1]
+    out_ref, kept = rest[-2:]
     here = plane_ref.shape[3] // BLK
     tall = NH // layer_ref.shape[2]
     step = layer_ref.shape[1] - 1
-    columns = offset_product(rows_inverse, [column_of(plane_ref, at) for at in range(here)])
+    keep_rows(kept, jnp.concatenate([column_of(plane_ref, at) for at in range(here)], axis=1))
+    value = left_product(rows_inverse[...], kept)
+    columns = [value[:, at * 2 * BLK : (at + 1) * 2 * BLK] for at in range(here)]
     for at in range(here):
         found = []
         for block, rows in enumerate(row_blocks(tall)):
@@ -546,9 +597,18 @@
     offs, nth, bins, goal = slot_lists(lists[:, 0], lists[:, 1:], bins_local, fl, per_device, room)
     side = (offs % cores != off_at % cores).astype(jnp.int32) * line
     slots = (side + ((offs // cores) ^ (off_at // cores))) * per_device + nth
+    source = jnp.arange(fl, dtype=jnp.int32) ^ mine
+    goal = jnp.sum(jnp.where((source[:, None] == jnp.arange(fl))[:, :, None], goal[None], 0), axis=1)
+    pick = (
+        jnp.tile(goal.reshape(1, fl * room), (1, 2))
+        == lax.broadcasted_iota(jnp.int32, (NH, 2 * fl * room), 0)
+    ).astype(jnp.bfloat16)
     own_slots = lax.dynamic_index_in_dim(slots, mine, 0, False)
     own_bins = lax.dynamic_index_in_dim(bins, mine, 0, False)
     list_groups = room // GROUP
+    data, order, own_slots, own_bins, layers, pick = lax.optimization_barrier(
+        (data, order, own_slots, own_bins, layers, pick)
+    )
     shape = jax.ShapeDtypeStruct((list_groups, outer + 1, GROUP, BLK), jnp.int32)
     terms = pl.pallas_call(
         functools.partial(contribution_kernel, freqs=fl),
@@ -563,38 +623,25 @@
         compiler_params=pltpu.CompilerParams(vmem_limit_bytes=SMALL),
         name="contributions",
     )(mine.reshape(1), order, own_slots, own_bins, data, *shares)
-    terms, goal, layers, freq_at = lax.optimization_barrier(
-        (terms, goal, layers, off_at * fl + mine)
-    )
+    terms, freq_at = lax.optimization_barrier((terms, off_at * fl + mine))
     got = {0: terms[0]}
     for away in range(fl - 1, 0, -1):
         got[away] = lax.ppermute(terms[away], "mid", [(i, i ^ away) for i in range(mid_count)])
     terms = [got[away] for away in range(fl)]
 
-    source = jnp.arange(fl, dtype=jnp.int32) ^ mine
-    goal = jnp.sum(jnp.where((source[:, None] == jnp.arange(fl))[:, :, None], goal[None], 0), axis=1)
-    pick = (
-        jnp.tile(goal.reshape(1, fl * room), (1, 2))
-        == lax.broadcasted_iota(jnp.int32, (NH, 2 * fl * room), 0)
-    ).astype(jnp.bfloat16)
     omega = math.pi * (0.1 + 0.8 * (freq_at.astype(jnp.float32) + 0.5) / freq_total)
-    phase_real, phase_imag = pl.pallas_call(
+    phase_real, phase_imag, layer_turns = pl.pallas_call(
         propagator_kernel,
-        in_specs=[smem],
-        out_specs=[vmem] * 2,
-        out_shape=[jax.ShapeDtypeStruct((NH, total_mid), jnp.float32)] * 2,
+        in_specs=[smem, smem, vmem],
+        out_specs=[vmem] * 3,
+        out_shape=[jax.ShapeDtypeStruct((NH, total_mid), jnp.float32)] * 2
+        + [jax.ShapeDtypeStruct((2, *layers.shape), jnp.float32)],
         compiler_params=pltpu.CompilerParams(vmem_limit_bytes=SMALL),
         cost_estimate=pl.CostEstimate(
             flops=60 * NH * total_mid, bytes_accessed=8 * NH * total_mid, transcendentals=10 * NH * total_mid
         ),
         name="propagator",
-    )(omega.reshape(1))
-
-    layer_total = slowness.shape[1]
-    chosen = layers[..., None] == jnp.arange(layer_total)
-    slow = jnp.sum(jnp.where(chosen, slowness[:, None, None, :], 0.0), axis=-1)
-    turn = 2.0 * dz_cells * omega * (slow - 1.0)
-    layer_turns = jnp.stack([jnp.cos(turn), jnp.sin(turn)])
+    )(omega.reshape(1), slowness, layers)
 
     middle, offset_turn = twiddle_tables(outer)
     here = mid_local // BLK
@@ -609,6 +656,9 @@
         scratch_shapes=[
             pltpu.VMEM((2, 2, HALF, total_mid), jnp.float32),
             pltpu.VMEM((fl * room, BLK), jnp.float32),
+            *[pltpu.VMEM((2 * NH, 2 * BLK), jnp.bfloat16)] * 4,
+            *[pltpu.VMEM((ROWS * CHUNKS * outer, 4 * BLK), jnp.bfloat16)] * 4,
+            *[pltpu.VMEM((2 * fl * room, 2 * BLK), jnp.bfloat16)] * 2,
         ],
         compiler_params=pltpu.CompilerParams(vmem_limit_bytes=VMEM),
         name="march",
@@ -628,6 +678,7 @@
                 ]
                 + [hbm] * len(before),
                 out_specs=pl.BlockSpec((rows_out, BLK), lambda i, dest: (0, 0)),
+                scratch_shapes=[pltpu.VMEM((2 * NH, 2 * mid_local), jnp.bfloat16)],
             ),
             out_shape=jax.ShapeDtypeStruct((rows_out, BLK), jnp.int32),
             cost_estimate=pl.CostEstimate(

time: 116 us -> 116 us (level)
  Pallas kernels: 56.1 us -> 58.7 us
  local copies, waits for them, and re-layouts: 9.19 us -> 7.74 us
    unnamed x26 -> x22, local copies, waits for them, and re-layouts: 5.56 us -> 4.11 us
where the time goes in v7:
time: 116 us; the launch traced here: 115 us
  Pallas kernels  58.7 us (51%)
  starting transfers between devices  23.2 us (20%)
  waiting for transfers between devices  21.5 us (19%)
  local copies, waits for them, and re-layouts  7.74 us (7%)
  other arithmetic  3.68 us (3%)
    pallas_call x1, Pallas kernels, local(): pl.pallas_call(functools.partial(march_kernel, sources=fl), in_specs=[sme...  26.8 us
    pallas_call x1, Pallas kernels, local(): pl.pallas_call(propagator_kernel, in_specs=[smem, smem, vmem], out_specs=...  15.2 us
    ppermute x3, waiting for transfers between devices, local(): lax.ppermute(block, 'mid', [(s, s ^ ahead) for s in range(mid_count)])  11.3 us
    ppermute x3, starting transfers between devices, local(): lax.ppermute(shares[away ^ low], 'off', [(i, (i // cores ^ low) * cores +...  8.49 us
    pallas_call x4, Pallas kernels, finish(): pl.pallas_call(finish_kernel, grid_spec=pltpu.PrefetchScalarGridSpec(num_...  6.82 us
    pallas_call x4, Pallas kernels, local(): pl.pallas_call(result_kernel, grid_spec=pltpu.PrefetchScalarGridSpec(num_...  5.19 us
    ppermute x3, waiting for transfers between devices, local(): lax.ppermute(data, 'mid', [(i, i ^ away) for i in range(mid_count)])  4.36 us
    unnamed x22, local copies, waits for them, and re-layouts  4.11 us
  transfers between devices with their start and end apart: 17, of which 10 were waited for; matrix products, arithmetic and copies ran while one was open for 6% of the time, Pallas kernels for 21%

profile of v7, /device:TPU:0, one launch (start us, length us, event | category | flops | bytes accessed | tf_op | source)
XLA Modules:
  0.0 115.1 jit_solution(18281807639806805485)
XLA Ops:
  0.0 1.2 %copy-done.4 = bf16[2,16,128,128]{3,2,1,0:T(8,128)(2,1)S(1)} copy-done((bf16[2,16,128,128]{3,2,1,0:T(8,128)(2,1)S(1)}, bf16[2,16,128,128]{3,2,1,0:T(8,128)(2,1)}, u32[]{:S(2)}) %copy-start.4) | copy-done | bytes 1048600
  2.9 3.1 %collective-permute-start.3 = (bf16[8,128,128]{2,1,0:T(8,128)(2,1)S(1)}, bf16[8,128,128]{2,1,0:T(8,128)(2,1)S(1)}, u32[]{:S(2)}, u32[]{:S(2)}) collective-permute-start(bf16[8,128,128]{2,1,0:T(8,128)(2,1)S(1)} %take_own.1.rest_0_), channel_id=1, source_target_pairs={{0,2},{1,3},{2,0},{3,1},{4,6},{5,7},{6,4},{7,5},{8,10},{9,11},{10,... | collective-permute-start | bytes 786440 | tf_op jit(solution)/shard_map/ppermute | solution.py:552
  6.0 2.6 %collective-permute-start.4 = (bf16[8,128,128]{2,1,0:T(8,128)(2,1)S(1)}, bf16[8,128,128]{2,1,0:T(8,128)(2,1)S(1)}, u32[]{:S(2)}, u32[]{:S(2)}) collective-permute-start(bf16[8,128,128]{2,1,0:T(8,128)(2,1)S(1)} %take_own.1.rest_0_), channel_id=1, source_target_pairs={{0,4},{1,5},{2,6},{3,7},{4,0},{5,1},{6,2},{7,3},{8,12},{9,13},{10,... | collective-permute-start | bytes 786440 | tf_op jit(solution)/shard_map/ppermute | solution.py:552
  12.4 3.4 %all-to-all-start = ((bf16[3,8,8,512]{3,2,0,1:T(8,128)(2,1)}), bf16[3,8,8,512]{3,2,0,1:T(8,128)(2,1)S(1)}, u32[]{:S(2)}, u32[]{:S(2)}) async-start(bf16[3,8,8,512]{3,2,0,1:T(8,128)(2,1)} %copy.46), calls=%async_computation | async-start | bytes 393216 | tf_op jit(solution)/shard_map/all_to_all | solution.py:571
  17.0 3.4 %collective-permute-done.4.rest_2_ = bf16[8,128,128]{2,1,0:T(8,128)(2,1)S(1)} collective-permute-done((bf16[8,128,128]{2,1,0:T(8,128)(2,1)S(1)}, bf16[8,128,128]{2,1,0:T(8,128)(2,1)S(1)}, u32[]{:S(2)}, u32[]{:S(2)}) %collective-permute-start.4) | collective-permute-done | bytes 262176 | tf_op jit(solution)/shard_map/ppermute | solution.py:552
  20.4 2.8 %collective-permute-start.5 = (bf16[8,128,128]{2,1,0:T(8,128)(2,1)S(1)}, bf16[8,128,128]{2,1,0:T(8,128)(2,1)S(1)}, u32[]{:S(2)}, u32[]{:S(2)}) collective-permute-start(bf16[8,128,128]{2,1,0:T(8,128)(2,1)S(1)} %collective-permute-done.4.rest_2_), channel_id=1, source_target_pairs={{0,2},{1,3},{2,0},{3,1},{4,6},{5,7},{6,4},{7,5},{8,10},{9,11},{10,... | collective-permute-start | bytes 786440 | tf_op jit(solution)/shard_map/ppermute | solution.py:552
  23.2 1.4 %all-to-all-done = bf16[3,8,8,512]{3,2,0,1:T(8,128)(2,1)S(1)} async-done(((bf16[3,8,8,512]{3,2,0,1:T(8,128)(2,1)}), bf16[3,8,8,512]{3,2,0,1:T(8,128)(2,1)S(1)}, u32[]{:S(2)}, u32[]{:S(2)}) %all-to-all-start) | async-done | bytes 196640 | tf_op jit(solution)/shard_map/all_to_all | solution.py:571
  24.6 2.5 %collective-permute-start.2 = (bf16[17,8,512]{2,1,0:T(8,128)(2,1)S(1)}, bf16[17,8,512]{2,1,0:T(8,128)(2,1)S(1)}, u32[]{:S(2)}, u32[]{:S(2)}) collective-permute-start(bf16[17,8,512]{2,1,0:T(8,128)(2,1)S(1)} %get-tuple-element.48), channel_id=1, source_target_pairs={{0,24},{8,16},{16,8},{24,0},{1,25},{9,17},{17,9},{25,1},{2,26},{10... | collective-permute-start | bytes 417800 | tf_op jit(solution)/shard_map/ppermute | solution.py:579
  29.9 1.8 %collective-permute-done.2 = bf16[17,8,512]{2,1,0:T(8,128)(2,1)S(1)} collective-permute-done((bf16[17,8,512]{2,1,0:T(8,128)(2,1)S(1)}, bf16[17,8,512]{2,1,0:T(8,128)(2,1)S(1)}, u32[]{:S(2)}, u32[]{:S(2)}) %collective-permute-start.2) | collective-permute-done | bytes 139296 | tf_op jit(solution)/shard_map/ppermute | solution.py:579
  31.7 2.5 %collective-permute-done.1 = bf16[17,8,512]{2,1,0:T(8,128)(2,1)S(1)} collective-permute-done((bf16[17,8,512]{2,1,0:T(8,128)(2,1)S(1)}, bf16[17,8,512]{2,1,0:T(8,128)(2,1)S(1)}, u32[]{:S(2)}, u32[]{:S(2)}) %collective-permute-start.1) | collective-permute-done | bytes 139296 | tf_op jit(solution)/shard_map/ppermute | solution.py:579
  36.1 3.6 %contributions.1 = (s32[5,17,8,128]{3,2,1,0:T(8,128)S(1)}, s32[5,17,8,128]{3,2,1,0:T(8,128)}, s32[5,17,8,128]{3,2,1,0:T(8,128)}, s32[5,17,8,128]{3,2,1,0:T(8,128)S(1)}) custom-call(s32[1]{0:T(128)} %bitcast.2.mine_ref.place_ref.freq_ref, s32[16]{0:T(128)S(1)} %add.116.order_ref, s32[40]{0:T(128)S(1)} %get-tuple-element.27.slot_ref, ...), custom_call_target="tpu_custom_call" | custom-call | tf_op jit(solution)/shard_map/contributions/pallas_call | solution.py:613
  39.7 1.6 %collective-permute-start.10 = (s32[5,17,8,128]{3,2,1,0:T(8,128)}, s32[5,17,8,128]{3,2,1,0:T(8,128)S(1)}, u32[]{:S(2)}, u32[]{:S(2)}) collective-permute-start(s32[5,17,8,128]{3,2,1,0:T(8,128)} %get-tuple-element.39), channel_id=1, source_target_pairs={{0,8},{8,0},{16,24},{24,16},{1,9},{9,1},{17,25},{25,17},{2,10},{10... | collective-permute-start | bytes 1044488 | tf_op jit(solution)/shard_map/ppermute | solution.py:629
  42.1 1.2 %collective-permute-start.12 = (s32[5,17,8,128]{3,2,1,0:T(8,128)S(1)}, s32[5,17,8,128]{3,2,1,0:T(8,128)S(1)}, u32[]{:S(2)}, u32[]{:S(2)}) collective-permute-start(s32[5,17,8,128]{3,2,1,0:T(8,128)S(1)} %get-tuple-element.41), channel_id=1, source_target_pairs={{0,24},{8,16},{16,8},{24,0},{1,25},{9,17},{17,9},{25,1},{2,26},{10... | collective-permute-start | bytes 1044488 | tf_op jit(solution)/shard_map/ppermute | solution.py:629
  43.4 15.2 %propagator.1 = (f32[256,2048]{1,0:T(8,128)S(1)}, f32[256,2048]{1,0:T(8,128)S(1)}, f32[2,2,8,16]{3,2,1,0:T(8,128)S(1)}) custom-call(f32[1]{0:T(128)} %bitcast.25.omega_ref, f32[2,16]{1,0:T(2,128)S(1)} %copy-done.10, s32[2,8,16]{2,1,0:T(8,128)S(1)} %copy.50.layers_ref), custom_call_target="tpu_custom_call" | custom-call | flops 31457280 | bytes 4194304 | tf_op jit(solution)/shard_map/propagator/pallas_call | solution.py:633
  59.0 26.8 %march.1.plane_ref = f32[2,2,128,2048]{3,2,1,0:T(8,128)S(1)} custom-call(f32[2,2,8,16]{3,2,1,0:T(8,128)S(1)} %get-tuple-element.37.layer_ref, s32[5,17,8,128]{3,2,1,0:T(8,128)S(1)} %get-tuple-element.38.rest_0_, s32[5,17,8,128]{3,2,1,0:T(8,128)S(1)} %collective-permute-done.10.rest_1_, s32[5,17,8,128]{3,2,1,0:T(8,128)S(1)} %collective-permute-done.11.rest_2_, ...), custom_call_target="tpu_custom_call" | custom-call | tf_op jit(solution)/shard_map/march/pallas_call | solution.py:651
  85.9 1.7 %finish.4.rest_0_ = s32[1032,128]{1,0:T(8,128)S(1)} custom-call(s32[1]{0:T(128)} %bitcast.27.dest_ref, f32[2,2,8,16]{3,2,1,0:T(8,128)S(1)} %get-tuple-element.37.layer_ref, f32[2,2,128,2048]{3,2,1,0:T(8,128)S(1)} %march.1.plane_ref, bf16[256,768]{1,0:T(8,128)(2,1)S(1)} %copy-done.2, f32[2,128,128]{2,1,0:T(8,128)S(1)} %copy-done.3), custom_call_target="tpu_custom_call" | custom-call | flops 402653184 | bytes 786432 | tf_op jit(solution)/shard_map/finish/pallas_call | solution.py:668
  87.6 1.6 %collective-permute-start.15 = (s32[1032,128]{1,0:T(8,128)S(1)}, s32[1032,128]{1,0:T(8,128)}, u32[]{:S(2)}, u32[]{:S(2)}) collective-permute-start(s32[1032,128]{1,0:T(8,128)S(1)} %finish.4.rest_0_), channel_id=1, source_target_pairs={{0,24},{8,16},{16,8},{24,0},{1,25},{9,17},{17,9},{25,1},{2,26},{10... | collective-permute-start | bytes 1585160 | tf_op jit(solution)/shard_map/ppermute | solution.py:697
  89.2 1.7 %finish.5.rest_0_ = s32[1032,128]{1,0:T(8,128)S(1)} custom-call(s32[1]{0:T(128)} %bitcast.26.dest_ref, f32[2,2,8,16]{3,2,1,0:T(8,128)S(1)} %get-tuple-element.37.layer_ref, f32[2,2,128,2048]{3,2,1,0:T(8,128)S(1)} %march.1.plane_ref, bf16[256,768]{1,0:T(8,128)(2,1)S(1)} %copy-done.2, f32[2,128,128]{2,1,0:T(8,128)S(1)} %copy-done.3, s32[1032,128]{1,0:T(8,128)S(1)} %finish.4.rest_0_), custom_call_target="tpu_custom_call" | custom-call | flops 402653184 | bytes 786432 | tf_op jit(solution)/shard_map/finish/pallas_call | solution.py:668
  92.0 1.7 %finish.6.rest_0_ = s32[1032,128]{1,0:T(8,128)S(1)} custom-call(s32[1]{0:T(128)} %bitcast.1.dest_ref, f32[2,2,8,16]{3,2,1,0:T(8,128)S(1)} %get-tuple-element.37.layer_ref, f32[2,2,128,2048]{3,2,1,0:T(8,128)S(1)} %march.1.plane_ref, bf16[256,768]{1,0:T(8,128)(2,1)S(1)} %copy-done.2, f32[2,128,128]{2,1,0:T(8,128)S(1)} %copy-done.3, s32[1032,128]{1,0:T(8,128)S(1)} %finish.5.rest_0_), custom_call_target="tpu_custom_call" | custom-call | flops 402653184 | bytes 786432 | tf_op jit(solution)/shard_map/finish/pallas_call | solution.py:668
  94.7 2.2 %copy-done.1 = f32[2,2,128,2048]{3,2,1,0:T(8,128)S(1)} copy-done((f32[2,2,128,2048]{3,2,1,0:T(8,128)S(1)}, f32[2,2,128,2048]{3,2,1,0:T(8,128)}, u32[]{:S(2)}) %copy-start.1) | copy-done | bytes 4194328
  96.9 1.7 %finish.7.code_ref = s32[1032,128]{1,0:T(8,128)S(1)} custom-call(s32[1]{0:T(128)} %bitcast.30.dest_ref, f32[2,2,8,16]{3,2,1,0:T(8,128)S(1)} %get-tuple-element.37.layer_ref, f32[2,2,128,2048]{3,2,1,0:T(8,128)S(1)} %copy-done.1, bf16[256,768]{1,0:T(8,128)(2,1)S(1)} %copy-done.2, f32[2,128,128]{2,1,0:T(8,128)S(1)} %copy-done.3, s32[1032,128]{1,0:T(8,128)S(1)} %finish.6.rest_0_), custom_call_target="tpu_custom_call" | custom-call | flops 402653184 | bytes 786432 | tf_op jit(solution)/shard_map/finish/pallas_call | solution.py:668
  99.7 4.0 %collective-permute-done.15.code_ref = s32[1032,128]{1,0:T(8,128)} collective-permute-done((s32[1032,128]{1,0:T(8,128)S(1)}, s32[1032,128]{1,0:T(8,128)}, u32[]{:S(2)}, u32[]{:S(2)}) %collective-permute-start.15) | collective-permute-done | bytes 528416 | tf_op jit(solution)/shard_map/ppermute | solution.py:697
  103.7 2.1 %result.5.rest_0_ = f32[4,256,8,128]{3,2,1,0:T(8,128)} custom-call(s32[1]{0:T(128)} %bitcast.29.freq_ref, s32[1032,128]{1,0:T(8,128)} %collective-permute-done.15.code_ref, f32[4,256,8,128]{3,2,1,0:T(8,128)} %result.4.rest_0_), custom_call_target="tpu_custom_call", output_to_operand_aliasing={{}: (2, {})} | custom-call | flops 524288 | bytes 1572864 | tf_op jit(solution)/shard_map/result/pallas_call | solution.py:704
  105.7 7.4 %collective-permute-done.14.code_ref = s32[1032,128]{1,0:T(8,128)S(1)} collective-permute-done((s32[1032,128]{1,0:T(8,128)S(1)}, s32[1032,128]{1,0:T(8,128)S(1)}, u32[]{:S(2)}, u32[]{:S(2)}) %collective-permute-start.14) | collective-permute-done | bytes 528416 | tf_op jit(solution)/shard_map/ppermute | solution.py:697
  (98 shorter events, 17.8 us)
Async XLA Ops:
  2.9 26.9 %collective-permute-start.3 = (bf16[8,128,128]{2,1,0:T(8,128)(2,1)S(1)}, bf16[8,128,128]{2,1,0:T(8,128)(2,1)S(1)}, u32[]{:S(2)}, u32[]{:S(2)}) collective-permute-start(bf16[8,128,128]{2,1,0:T(8,128)(2,1)S(1)} %take_own.1.rest_0_), channel_id=1, source_target_pairs={{0,2},{1,3},{2,0},{3,1},{4,6},{5,7},{6,4},{7,5},{8,10},{9,11},{10,... | collective-permute-start | bytes 786440 | tf_op jit(solution)/shard_map/ppermute | solution.py:552
  6.0 14.4 %collective-permute-start.4 = (bf16[8,128,128]{2,1,0:T(8,128)(2,1)S(1)}, bf16[8,128,128]{2,1,0:T(8,128)(2,1)S(1)}, u32[]{:S(2)}, u32[]{:S(2)}) collective-permute-start(bf16[8,128,128]{2,1,0:T(8,128)(2,1)S(1)} %take_own.1.rest_0_), channel_id=1, source_target_pairs={{0,4},{1,5},{2,6},{3,7},{4,0},{5,1},{6,2},{7,3},{8,12},{9,13},{10,... | collective-permute-start | bytes 786440 | tf_op jit(solution)/shard_map/ppermute | solution.py:552
  11.6 31.7 %copy-start.10 = (f32[2,16]{1,0:T(2,128)S(1)}, f32[2,16]{1,0:T(2,128)}, u32[]{:S(2)}) copy-start(f32[2,16]{1,0:T(2,128)} %slow_ref.1) | copy-start | bytes 388
  12.4 12.2 %all-to-all-start = ((bf16[3,8,8,512]{3,2,0,1:T(8,128)(2,1)}), bf16[3,8,8,512]{3,2,0,1:T(8,128)(2,1)S(1)}, u32[]{:S(2)}, u32[]{:S(2)}) async-start(bf16[3,8,8,512]{3,2,0,1:T(8,128)(2,1)} %copy.46), calls=%async_computation | async-start | bytes 393216 | tf_op jit(solution)/shard_map/all_to_all | solution.py:571
  20.4 14.0 %collective-permute-start.5 = (bf16[8,128,128]{2,1,0:T(8,128)(2,1)S(1)}, bf16[8,128,128]{2,1,0:T(8,128)(2,1)S(1)}, u32[]{:S(2)}, u32[]{:S(2)}) collective-permute-start(bf16[8,128,128]{2,1,0:T(8,128)(2,1)S(1)} %collective-permute-done.4.rest_2_), channel_id=1, source_target_pairs={{0,2},{1,3},{2,0},{3,1},{4,6},{5,7},{6,4},{7,5},{8,10},{9,11},{10,... | collective-permute-start | bytes 786440 | tf_op jit(solution)/shard_map/ppermute | solution.py:552
  24.6 7.1 %collective-permute-start.2 = (bf16[17,8,512]{2,1,0:T(8,128)(2,1)S(1)}, bf16[17,8,512]{2,1,0:T(8,128)(2,1)S(1)}, u32[]{:S(2)}, u32[]{:S(2)}) collective-permute-start(bf16[17,8,512]{2,1,0:T(8,128)(2,1)S(1)} %get-tuple-element.48), channel_id=1, source_target_pairs={{0,24},{8,16},{16,8},{24,0},{1,25},{9,17},{17,9},{25,1},{2,26},{10... | collective-permute-start | bytes 417800 | tf_op jit(solution)/shard_map/ppermute | solution.py:579
  27.1 7.1 %collective-permute-start.1 = (bf16[17,8,512]{2,1,0:T(8,128)(2,1)S(1)}, bf16[17,8,512]{2,1,0:T(8,128)(2,1)S(1)}, u32[]{:S(2)}, u32[]{:S(2)}) collective-permute-start(bf16[17,8,512]{2,1,0:T(8,128)(2,1)S(1)} %get-tuple-element.48), channel_id=1, source_target_pairs={{0,16},{8,24},{16,0},{24,8},{1,17},{9,25},{17,1},{25,9},{2,18},{10... | collective-permute-start | bytes 417800 | tf_op jit(solution)/shard_map/ppermute | solution.py:579
  27.6 6.6 %collective-permute-start = (bf16[17,8,512]{2,1,0:T(8,128)(2,1)S(1)}, bf16[17,8,512]{2,1,0:T(8,128)(2,1)S(1)}, u32[]{:S(2)}, u32[]{:S(2)}) collective-permute-start(bf16[17,8,512]{2,1,0:T(8,128)(2,1)S(1)} %get-tuple-element.48), channel_id=1, source_target_pairs={{0,8},{8,0},{16,24},{24,16},{1,9},{9,1},{17,25},{25,17},{2,10},{10... | collective-permute-start | bytes 417800 | tf_op jit(solution)/shard_map/ppermute | solution.py:579
  29.8 5.7 %collective-permute-start.6 = (bf16[8,128,128]{2,1,0:T(8,128)(2,1)S(1)}, bf16[8,128,128]{2,1,0:T(8,128)(2,1)S(1)}, u32[]{:S(2)}, u32[]{:S(2)}) collective-permute-start(bf16[8,128,128]{2,1,0:T(8,128)(2,1)S(1)} %take_own.1.rest_0_), channel_id=1, source_target_pairs={{0,1},{1,0},{2,3},{3,2},{4,5},{5,4},{6,7},{7,6},{8,9},{9,8},{10,11... | collective-permute-start | bytes 786440 | tf_op jit(solution)/shard_map/ppermute | solution.py:559
  31.7 4.1 %collective-permute-start.8 = (bf16[8,128,128]{2,1,0:T(8,128)(2,1)S(1)}, bf16[8,128,128]{2,1,0:T(8,128)(2,1)S(1)}, u32[]{:S(2)}, u32[]{:S(2)}) collective-permute-start(bf16[8,128,128]{2,1,0:T(8,128)(2,1)S(1)} %collective-permute-done.4.rest_2_), channel_id=1, source_target_pairs={{0,1},{1,0},{2,3},{3,2},{4,5},{5,4},{6,7},{7,6},{8,9},{9,8},{10,11... | collective-permute-start | bytes 786440 | tf_op jit(solution)/shard_map/ppermute | solution.py:559
  34.2 1.5 %collective-permute-start.7 = (bf16[8,128,128]{2,1,0:T(8,128)(2,1)S(1)}, bf16[8,128,128]{2,1,0:T(8,128)(2,1)S(1)}, u32[]{:S(2)}, u32[]{:S(2)}) collective-permute-start(bf16[8,128,128]{2,1,0:T(8,128)(2,1)S(1)} %collective-permute-done.3.rest_1_), channel_id=1, source_target_pairs={{0,1},{1,0},{2,3},{3,2},{4,5},{5,4},{6,7},{7,6},{8,9},{9,8},{10,11... | collective-permute-start | bytes 786440 | tf_op jit(solution)/shard_map/ppermute | solution.py:559
  34.4 1.7 %collective-permute-start.9 = (bf16[8,128,128]{2,1,0:T(8,128)(2,1)S(1)}, bf16[8,128,128]{2,1,0:T(8,128)(2,1)S(1)}, u32[]{:S(2)}, u32[]{:S(2)}) collective-permute-start(bf16[8,128,128]{2,1,0:T(8,128)(2,1)S(1)} %collective-permute-done.5.rest_3_), channel_id=1, source_target_pairs={{0,1},{1,0},{2,3},{3,2},{4,5},{5,4},{6,7},{7,6},{8,9},{9,8},{10,11... | collective-permute-start | bytes 786440 | tf_op jit(solution)/shard_map/ppermute | solution.py:559
  39.7 18.9 %collective-permute-start.10 = (s32[5,17,8,128]{3,2,1,0:T(8,128)}, s32[5,17,8,128]{3,2,1,0:T(8,128)S(1)}, u32[]{:S(2)}, u32[]{:S(2)}) collective-permute-start(s32[5,17,8,128]{3,2,1,0:T(8,128)} %get-tuple-element.39), channel_id=1, source_target_pairs={{0,8},{8,0},{16,24},{24,16},{1,9},{9,1},{17,25},{25,17},{2,10},{10... | collective-permute-start | bytes 1044488 | tf_op jit(solution)/shard_map/ppermute | solution.py:629
  41.2 17.7 %collective-permute-start.11 = (s32[5,17,8,128]{3,2,1,0:T(8,128)}, s32[5,17,8,128]{3,2,1,0:T(8,128)S(1)}, u32[]{:S(2)}, u32[]{:S(2)}) collective-permute-start(s32[5,17,8,128]{3,2,1,0:T(8,128)} %get-tuple-element.40), channel_id=1, source_target_pairs={{0,16},{8,24},{16,0},{24,8},{1,17},{9,25},{17,1},{25,9},{2,18},{10... | collective-permute-start | bytes 1044488 | tf_op jit(solution)/shard_map/ppermute | solution.py:629
  42.1 16.9 %collective-permute-start.12 = (s32[5,17,8,128]{3,2,1,0:T(8,128)S(1)}, s32[5,17,8,128]{3,2,1,0:T(8,128)S(1)}, u32[]{:S(2)}, u32[]{:S(2)}) collective-permute-start(s32[5,17,8,128]{3,2,1,0:T(8,128)S(1)} %get-tuple-element.41), channel_id=1, source_target_pairs={{0,24},{8,16},{16,8},{24,0},{1,25},{9,17},{17,9},{25,1},{2,26},{10... | collective-permute-start | bytes 1044488 | tf_op jit(solution)/shard_map/ppermute | solution.py:629
  43.3 15.7 %copy-start.2 = (bf16[256,768]{1,0:T(8,128)(2,1)S(1)}, bf16[256,768]{1,0:T(8,128)(2,1)}, u32[]{:S(2)}) copy-start(bf16[256,768]{1,0:T(8,128)(2,1)} %constant.135.clone.rest_8_.rows_inverse) | copy-start | bytes 1179652
  43.3 15.7 %copy-start.3 = (f32[2,128,128]{2,1,0:T(8,128)S(1)}, f32[2,128,128]{2,1,0:T(8,128)}, u32[]{:S(2)}) copy-start(f32[2,128,128]{2,1,0:T(8,128)} %constant.139.clone.rest_12_.offset_ref) | copy-start | bytes 393220
  43.3 15.7 %copy-start.5 = (bf16[256,768]{1,0:T(8,128)(2,1)S(1)}, bf16[256,768]{1,0:T(8,128)(2,1)}, u32[]{:S(2)}) copy-start(bf16[256,768]{1,0:T(8,128)(2,1)} %constant.134.clone.rest_7_) | copy-start | bytes 1179652
  43.3 15.7 %copy-start.6 = (bf16[768,256]{1,0:T(8,128)(2,1)S(1)}, bf16[768,256]{1,0:T(8,128)(2,1)}, u32[]{:S(2)}) copy-start(bf16[768,256]{1,0:T(8,128)(2,1)} %constant.136.clone.rest_9_) | copy-start | bytes 1179652
  43.3 15.7 %copy-start.7 = (bf16[768,256]{1,0:T(8,128)(2,1)S(1)}, bf16[768,256]{1,0:T(8,128)(2,1)}, u32[]{:S(2)}) copy-start(bf16[768,256]{1,0:T(8,128)(2,1)} %constant.137.clone.rest_10_) | copy-start | bytes 1179652
  43.4 15.7 %copy-start.8 = (f32[2,16,128]{2,1,0:T(8,128)S(1)}, f32[2,16,128]{2,1,0:T(8,128)}, u32[]{:S(2)}) copy-start(f32[2,16,128]{2,1,0:T(8,128)} %constant.138.clone.rest_11_) | copy-start | bytes 49156
  87.6 16.1 %collective-permute-start.15 = (s32[1032,128]{1,0:T(8,128)S(1)}, s32[1032,128]{1,0:T(8,128)}, u32[]{:S(2)}, u32[]{:S(2)}) collective-permute-start(s32[1032,128]{1,0:T(8,128)S(1)} %finish.4.rest_0_), channel_id=1, source_target_pairs={{0,24},{8,16},{16,8},{24,0},{1,25},{9,17},{17,9},{25,1},{2,26},{10... | collective-permute-start | bytes 1585160 | tf_op jit(solution)/shard_map/ppermute | solution.py:697
  90.9 22.2 %collective-permute-start.14 = (s32[1032,128]{1,0:T(8,128)S(1)}, s32[1032,128]{1,0:T(8,128)S(1)}, u32[]{:S(2)}, u32[]{:S(2)}) collective-permute-start(s32[1032,128]{1,0:T(8,128)S(1)} %finish.5.rest_0_), channel_id=1, source_target_pairs={{0,16},{8,24},{16,0},{24,8},{1,17},{9,25},{17,1},{25,9},{2,18},{10... | collective-permute-start | bytes 1585160 | tf_op jit(solution)/shard_map/ppermute | solution.py:697
  93.7 20.4 %collective-permute-start.13 = (s32[1032,128]{1,0:T(8,128)S(1)}, s32[1032,128]{1,0:T(8,128)S(1)}, u32[]{:S(2)}, u32[]{:S(2)}) collective-permute-start(s32[1032,128]{1,0:T(8,128)S(1)} %finish.6.rest_0_), channel_id=1, source_target_pairs={{0,8},{8,0},{16,24},{24,16},{1,9},{9,1},{17,25},{25,17},{2,10},{10... | collective-permute-start | bytes 1585160 | tf_op jit(solution)/shard_map/ppermute | solution.py:697
  (4 other events, 10.2 us)

commit v8 on v7

--- a/solution.py
+++ b/solution.py
@@ -73,6 +73,7 @@
     middle = np.stack([np.cos(angles), np.sin(angles)]).astype(np.float32)
     rows = 2.0 * np.pi * np.arange(HALF) / NH
     offset = np.stack([np.cos(rows), np.sin(rows)]).astype(np.float32)
+    middle = np.broadcast_to(middle[:, :, None], (2, outer, ROWS, BLK)).copy()
     return middle, np.broadcast_to(offset[:, :, None], (2, HALF, BLK)).copy()
 
 
@@ -132,6 +133,10 @@
 
 def cmul(real_a, imag_a, real_b, imag_b):
     return real_a * real_b - imag_a * imag_b, real_a * imag_b + imag_a * real_b
+
+
+def cmul_conj(real_a, imag_a, real_b, imag_b):
+    return real_a * real_b + imag_a * imag_b, imag_a * real_b - real_a * imag_b
 
 
 def small_transform(values, sign):
@@ -248,7 +253,7 @@
 
 def forward_rows(low, high, turn):
     first = low[0] + high[0], low[1] + high[1]
-    second = cmul(low[0] - high[0], low[1] - high[1], turn[0], -turn[1])
+    second = cmul_conj(low[0] - high[0], low[1] - high[1], *turn)
     return (*first, *second)
 
 
@@ -325,7 +330,7 @@
             values = [(plane[p, 0, here, lane], plane[p, 1, here, lane]) for lane in lanes]
             values = small_transform(values, -1)
             for a in range(outer):
-                pieces.append(cmul(*values[a], middle_ref[0, a : a + 1], -middle_ref[1, a : a + 1]))
+                pieces.append(cmul_conj(*values[a], middle_ref[0, a], middle_ref[1, a]))
         keep_lanes(first_kept[parity], gathered(pieces))
 
     def phase_stage(at, parity):
@@ -354,7 +359,7 @@
                 row = chunk * outer + a * ROWS
                 part = value[row : row + ROWS]
                 values.append(
-                    cmul(part[:, :BLK], part[:, BLK:], middle_ref[0, a : a + 1], middle_ref[1, a : a + 1])
+                    cmul(part[:, :BLK], part[:, BLK:], middle_ref[0, a], middle_ref[1, a])
                 )
             values = small_transform(values, 1)
             for a in range(outer):
@@ -532,6 +537,19 @@
     smem = pl.BlockSpec(memory_space=pltpu.SMEM)
     vmem = pl.BlockSpec(memory_space=pltpu.VMEM)
     hbm = pl.BlockSpec(memory_space=pl.ANY)
+    pairs = fl * 2
+
+    def extra(whole_numbers, copies):
+        flat = whole_numbers.astype(jnp.bfloat16).reshape(1, 1, 1, -1)
+        flat = jnp.pad(flat, ((0, 0), (0, 0), (0, pairs - 1), (0, mid_local - flat.shape[3])))
+        return jnp.broadcast_to(flat, (1, copies, pairs, mid_local))
+
+    lists = lax.optimization_barrier(jnp.concatenate([counts[:, None], targets], axis=1))
+    data = bins_data.reshape(bins_local, off_count, pairs, mid_local)
+    data = jnp.concatenate([data, extra(lists, off_count)], axis=0)
+    data, operators = lax.optimization_barrier((data, operators))
+    data = lax.all_to_all(data, "off", split_axis=1, concat_axis=0, tiled=True)
+
     own = pl.pallas_call(
         take_kernel,
         in_specs=[smem, smem, hbm],
@@ -541,7 +559,6 @@
         compiler_params=pltpu.CompilerParams(vmem_limit_bytes=SMALL),
         name="take_own",
     )(mine.reshape(1), counts, operators)
-    bins_data, own = lax.optimization_barrier((bins_data, own))
     cores = 2 if off_count % 2 == 0 else 1
     line = off_count // cores
     assert line & (line - 1) == 0 and fl & (fl - 1) == 0
@@ -558,17 +575,6 @@
     if cores > 1:
         shares += [lax.ppermute(x, "off", [(i, i ^ 1) for i in range(off_count)]) for x in shares]
 
-    pairs = fl * 2
-
-    def extra(whole_numbers, copies):
-        flat = whole_numbers.astype(jnp.bfloat16).reshape(1, 1, 1, -1)
-        flat = jnp.pad(flat, ((0, 0), (0, 0), (0, pairs - 1), (0, mid_local - flat.shape[3])))
-        return jnp.broadcast_to(flat, (1, copies, pairs, mid_local))
-
-    lists = jnp.concatenate([counts[:, None], targets], axis=1)
-    data = bins_data.reshape(bins_local, off_count, pairs, mid_local)
-    data = jnp.concatenate([data, extra(lists, off_count)], axis=0)
-    data = lax.all_to_all(data, "off", split_axis=1, concat_axis=0, tiled=True)
 
     data = data.reshape(off_count, bins_local + 1, pairs, mid_local)
     lists = data[:, bins_local, 0, : lists.size].astype(jnp.int32).reshape(bins_total, 1 + entries)

time: 116 us -> 119 us (1.026)
  waiting for transfers between devices: 21.5 us -> 24.1 us
    ppermute x3, waiting for transfers between devices: 3.37 us -> 6.01 us  [local(): lax.ppermute(shares[away ^ low], 'off', [(i, (i // cores ^ low) * cores +...]
    unnamed x22 -> x23, local copies, waits for them, and re-layouts: 4.11 us -> 5.15 us
  transfers between devices with their start and end apart: 17 -> 17, of which waited for: 10 -> 10; matrix products, arithmetic and copies ran while one was open for 6% -> 4% of each run, Pallas kernels for 21% -> 21%
where the time goes in v8:
time: 119 us; the launch traced here: 118 us
  Pallas kernels  58.7 us (49%)
  waiting for transfers between devices  24.1 us (20%)
  starting transfers between devices  23.6 us (20%)
  local copies, waits for them, and re-layouts  8.37 us (7%)
  other arithmetic  3.02 us (3%)
    pallas_call x1, Pallas kernels, local(): pl.pallas_call(functools.partial(march_kernel, sources=fl), in_specs=[sme...  26.9 us
    pallas_call x1, Pallas kernels, local(): pl.pallas_call(propagator_kernel, in_specs=[smem, smem, vmem], out_specs=...  15.2 us
    ppermute x3, waiting for transfers between devices, local(): lax.ppermute(block, 'mid', [(s, s ^ ahead) for s in range(mid_count)])  11.3 us
    ppermute x3, starting transfers between devices, local(): lax.ppermute(shares[away ^ low], 'off', [(i, (i // cores ^ low) * cores +...  8.85 us
    pallas_call x4, Pallas kernels, finish(): pl.pallas_call(finish_kernel, grid_spec=pltpu.PrefetchScalarGridSpec(num_...  6.82 us
    ppermute x3, waiting for transfers between devices, local(): lax.ppermute(shares[away ^ low], 'off', [(i, (i // cores ^ low) * cores +...  6.01 us
    pallas_call x4, Pallas kernels, local(): pl.pallas_call(result_kernel, grid_spec=pltpu.PrefetchScalarGridSpec(num_...  5.19 us
    unnamed x23, local copies, waits for them, and re-layouts  5.15 us
  transfers between devices with their start and end apart: 17, of which 10 were waited for; matrix products, arithmetic and copies ran while one was open for 4% of the time, Pallas kernels for 21%

profile of v8, /device:TPU:0, one launch (start us, length us, event | category | flops | bytes accessed | tf_op | source)
XLA Modules:
  0.0 118.2 jit_solution(11978365686731635604)
XLA Ops:
  3.0 1.2 %copy-done.4 = bf16[2,16,128,128]{3,2,1,0:T(8,128)(2,1)S(1)} copy-done((bf16[2,16,128,128]{3,2,1,0:T(8,128)(2,1)S(1)}, bf16[2,16,128,128]{3,2,1,0:T(8,128)(2,1)}, u32[]{:S(2)}) %copy-start.4) | copy-done | bytes 1048600
  5.9 3.1 %collective-permute-start.3 = (bf16[8,128,128]{2,1,0:T(8,128)(2,1)S(1)}, bf16[8,128,128]{2,1,0:T(8,128)(2,1)S(1)}, u32[]{:S(2)}, u32[]{:S(2)}) collective-permute-start(bf16[8,128,128]{2,1,0:T(8,128)(2,1)S(1)} %take_own.1.rest_0_), channel_id=1, source_target_pairs={{0,2},{1,3},{2,0},{3,1},{4,6},{5,7},{6,4},{7,5},{8,10},{9,11},{10,... | collective-permute-start | bytes 786440 | tf_op jit(solution)/shard_map/ppermute | solution.py:569
  9.0 2.6 %collective-permute-start.4 = (bf16[8,128,128]{2,1,0:T(8,128)(2,1)S(1)}, bf16[8,128,128]{2,1,0:T(8,128)(2,1)S(1)}, u32[]{:S(2)}, u32[]{:S(2)}) collective-permute-start(bf16[8,128,128]{2,1,0:T(8,128)(2,1)S(1)} %take_own.1.rest_0_), channel_id=1, source_target_pairs={{0,4},{1,5},{2,6},{3,7},{4,0},{5,1},{6,2},{7,3},{8,12},{9,13},{10,... | collective-permute-start | bytes 786440 | tf_op jit(solution)/shard_map/ppermute | solution.py:569
  12.4 3.4 %all-to-all-start = ((bf16[3,8,8,512]{3,2,0,1:T(8,128)(2,1)}), bf16[3,8,8,512]{3,2,0,1:T(8,128)(2,1)S(1)}, u32[]{:S(2)}, u32[]{:S(2)}) async-start(bf16[3,8,8,512]{3,2,0,1:T(8,128)(2,1)} %copy.46), calls=%async_computation | async-start | bytes 393216 | tf_op jit(solution)/shard_map/all_to_all | solution.py:551
  17.0 6.0 %collective-permute-done.4.rest_2_ = bf16[8,128,128]{2,1,0:T(8,128)(2,1)S(1)} collective-permute-done((bf16[8,128,128]{2,1,0:T(8,128)(2,1)S(1)}, bf16[8,128,128]{2,1,0:T(8,128)(2,1)S(1)}, u32[]{:S(2)}, u32[]{:S(2)}) %collective-permute-start.4) | collective-permute-done | bytes 262176 | tf_op jit(solution)/shard_map/ppermute | solution.py:569
  23.0 3.2 %collective-permute-start.5 = (bf16[8,128,128]{2,1,0:T(8,128)(2,1)S(1)}, bf16[8,128,128]{2,1,0:T(8,128)(2,1)S(1)}, u32[]{:S(2)}, u32[]{:S(2)}) collective-permute-start(bf16[8,128,128]{2,1,0:T(8,128)(2,1)S(1)} %collective-permute-done.4.rest_2_), channel_id=1, source_target_pairs={{0,2},{1,3},{2,0},{3,1},{4,6},{5,7},{6,4},{7,5},{8,10},{9,11},{10,... | collective-permute-start | bytes 786440 | tf_op jit(solution)/shard_map/ppermute | solution.py:569
  26.2 1.4 %all-to-all-done = bf16[3,8,8,512]{3,2,0,1:T(8,128)(2,1)S(1)} async-done(((bf16[3,8,8,512]{3,2,0,1:T(8,128)(2,1)}), bf16[3,8,8,512]{3,2,0,1:T(8,128)(2,1)S(1)}, u32[]{:S(2)}, u32[]{:S(2)}) %all-to-all-start) | async-done | bytes 196640 | tf_op jit(solution)/shard_map/all_to_all | solution.py:551
  27.6 2.5 %collective-permute-start.2 = (bf16[17,8,512]{2,1,0:T(8,128)(2,1)S(1)}, bf16[17,8,512]{2,1,0:T(8,128)(2,1)S(1)}, u32[]{:S(2)}, u32[]{:S(2)}) collective-permute-start(bf16[17,8,512]{2,1,0:T(8,128)(2,1)S(1)} %get-tuple-element.48), channel_id=1, source_target_pairs={{0,24},{8,16},{16,8},{24,0},{1,25},{9,17},{17,9},{25,1},{2,26},{10... | collective-permute-start | bytes 417800 | tf_op jit(solution)/shard_map/ppermute | solution.py:585
  32.9 1.8 %collective-permute-done.2 = bf16[17,8,512]{2,1,0:T(8,128)(2,1)S(1)} collective-permute-done((bf16[17,8,512]{2,1,0:T(8,128)(2,1)S(1)}, bf16[17,8,512]{2,1,0:T(8,128)(2,1)S(1)}, u32[]{:S(2)}, u32[]{:S(2)}) %collective-permute-start.2) | collective-permute-done | bytes 139296 | tf_op jit(solution)/shard_map/ppermute | solution.py:585
  34.7 2.5 %collective-permute-done.1 = bf16[17,8,512]{2,1,0:T(8,128)(2,1)S(1)} collective-permute-done((bf16[17,8,512]{2,1,0:T(8,128)(2,1)S(1)}, bf16[17,8,512]{2,1,0:T(8,128)(2,1)S(1)}, u32[]{:S(2)}, u32[]{:S(2)}) %collective-permute-start.1) | collective-permute-done | bytes 139296 | tf_op jit(solution)/shard_map/ppermute | solution.py:585
  39.1 3.6 %contributions.1 = (s32[5,17,8,128]{3,2,1,0:T(8,128)S(1)}, s32[5,17,8,128]{3,2,1,0:T(8,128)}, s32[5,17,8,128]{3,2,1,0:T(8,128)}, s32[5,17,8,128]{3,2,1,0:T(8,128)S(1)}) custom-call(s32[1]{0:T(128)} %bitcast.2.mine_ref.place_ref.freq_ref, s32[16]{0:T(128)S(1)} %add.116.order_ref, s32[40]{0:T(128)S(1)} %get-tuple-element.27.slot_ref, ...), custom_call_target="tpu_custom_call" | custom-call | tf_op jit(solution)/shard_map/contributions/pallas_call | solution.py:619
  42.7 1.6 %collective-permute-start.10 = (s32[5,17,8,128]{3,2,1,0:T(8,128)}, s32[5,17,8,128]{3,2,1,0:T(8,128)S(1)}, u32[]{:S(2)}, u32[]{:S(2)}) collective-permute-start(s32[5,17,8,128]{3,2,1,0:T(8,128)} %get-tuple-element.39), channel_id=1, source_target_pairs={{0,8},{8,0},{16,24},{24,16},{1,9},{9,1},{17,25},{25,17},{2,10},{10... | collective-permute-start | bytes 1044488 | tf_op jit(solution)/shard_map/ppermute | solution.py:635
  45.1 1.2 collective-permute-start.12
  46.4 15.2 %propagator.1 = (f32[256,2048]{1,0:T(8,128)S(1)}, f32[256,2048]{1,0:T(8,128)S(1)}, f32[2,2,8,16]{3,2,1,0:T(8,128)S(1)}) custom-call(f32[1]{0:T(128)} %bitcast.25.omega_ref, f32[2,16]{1,0:T(2,128)S(1)} %copy-done.10, s32[2,8,16]{2,1,0:T(8,128)S(1)} %copy.50.layers_ref), custom_call_target="tpu_custom_call" | custom-call | flops 31457280 | bytes 4194304 | tf_op jit(solution)/shard_map/propagator/pallas_call | solution.py:639
  62.1 26.9 %march.1.plane_ref = f32[2,2,128,2048]{3,2,1,0:T(8,128)S(1)} custom-call(f32[2,2,8,16]{3,2,1,0:T(8,128)S(1)} %get-tuple-element.37.layer_ref, s32[5,17,8,128]{3,2,1,0:T(8,128)S(1)} %get-tuple-element.38.rest_0_, s32[5,17,8,128]{3,2,1,0:T(8,128)S(1)} %collective-permute-done.10.rest_1_, s32[5,17,8,128]{3,2,1,0:T(8,128)S(1)} %collective-permute-done.11.rest_2_, ...), custom_call_target="tpu_custom_call" | custom-call | tf_op jit(solution)/shard_map/march/pallas_call | solution.py:657
  89.0 1.7 %finish.4.rest_0_ = s32[1032,128]{1,0:T(8,128)S(1)} custom-call(s32[1]{0:T(128)} %bitcast.27.dest_ref, f32[2,2,8,16]{3,2,1,0:T(8,128)S(1)} %get-tuple-element.37.layer_ref, f32[2,2,128,2048]{3,2,1,0:T(8,128)S(1)} %march.1.plane_ref, bf16[256,768]{1,0:T(8,128)(2,1)S(1)} %copy-done.2, f32[2,128,128]{2,1,0:T(8,128)S(1)} %copy-done.3), custom_call_target="tpu_custom_call" | custom-call | flops 402653184 | bytes 786432 | tf_op jit(solution)/shard_map/finish/pallas_call | solution.py:674
  90.7 1.6 %collective-permute-start.15 = (s32[1032,128]{1,0:T(8,128)S(1)}, s32[1032,128]{1,0:T(8,128)}, u32[]{:S(2)}, u32[]{:S(2)}) collective-permute-start(s32[1032,128]{1,0:T(8,128)S(1)} %finish.4.rest_0_), channel_id=1, source_target_pairs={{0,24},{8,16},{16,8},{24,0},{1,25},{9,17},{17,9},{25,1},{2,26},{10... | collective-permute-start | bytes 1585160 | tf_op jit(solution)/shard_map/ppermute | solution.py:703
  92.2 1.7 %finish.5.rest_0_ = s32[1032,128]{1,0:T(8,128)S(1)} custom-call(s32[1]{0:T(128)} %bitcast.26.dest_ref, f32[2,2,8,16]{3,2,1,0:T(8,128)S(1)} %get-tuple-element.37.layer_ref, f32[2,2,128,2048]{3,2,1,0:T(8,128)S(1)} %march.1.plane_ref, bf16[256,768]{1,0:T(8,128)(2,1)S(1)} %copy-done.2, f32[2,128,128]{2,1,0:T(8,128)S(1)} %copy-done.3, s32[1032,128]{1,0:T(8,128)S(1)} %finish.4.rest_0_), custom_call_target="tpu_custom_call" | custom-call | flops 402653184 | bytes 786432 | tf_op jit(solution)/shard_map/finish/pallas_call | solution.py:674
  95.1 1.7 %finish.6.rest_0_ = s32[1032,128]{1,0:T(8,128)S(1)} custom-call(s32[1]{0:T(128)} %bitcast.1.dest_ref, f32[2,2,8,16]{3,2,1,0:T(8,128)S(1)} %get-tuple-element.37.layer_ref, f32[2,2,128,2048]{3,2,1,0:T(8,128)S(1)} %march.1.plane_ref, bf16[256,768]{1,0:T(8,128)(2,1)S(1)} %copy-done.2, f32[2,128,128]{2,1,0:T(8,128)S(1)} %copy-done.3, s32[1032,128]{1,0:T(8,128)S(1)} %finish.5.rest_0_), custom_call_target="tpu_custom_call" | custom-call | flops 402653184 | bytes 786432 | tf_op jit(solution)/shard_map/finish/pallas_call | solution.py:674
  97.8 2.2 %copy-done.1 = f32[2,2,128,2048]{3,2,1,0:T(8,128)S(1)} copy-done((f32[2,2,128,2048]{3,2,1,0:T(8,128)S(1)}, f32[2,2,128,2048]{3,2,1,0:T(8,128)}, u32[]{:S(2)}) %copy-start.1) | copy-done | bytes 4194328
  100.0 1.7 %finish.7.code_ref = s32[1032,128]{1,0:T(8,128)S(1)} custom-call(s32[1]{0:T(128)} %bitcast.30.dest_ref, f32[2,2,8,16]{3,2,1,0:T(8,128)S(1)} %get-tuple-element.37.layer_ref, f32[2,2,128,2048]{3,2,1,0:T(8,128)S(1)} %copy-done.1, bf16[256,768]{1,0:T(8,128)(2,1)S(1)} %copy-done.2, f32[2,128,128]{2,1,0:T(8,128)S(1)} %copy-done.3, s32[1032,128]{1,0:T(8,128)S(1)} %finish.6.rest_0_), custom_call_target="tpu_custom_call" | custom-call | flops 402653184 | bytes 786432 | tf_op jit(solution)/shard_map/finish/pallas_call | solution.py:674
  102.7 4.0 %collective-permute-done.15.code_ref = s32[1032,128]{1,0:T(8,128)} collective-permute-done((s32[1032,128]{1,0:T(8,128)S(1)}, s32[1032,128]{1,0:T(8,128)}, u32[]{:S(2)}, u32[]{:S(2)}) %collective-permute-start.15) | collective-permute-done | bytes 528416 | tf_op jit(solution)/shard_map/ppermute | solution.py:703
  106.7 2.1 %result.5.rest_0_ = f32[4,256,8,128]{3,2,1,0:T(8,128)} custom-call(s32[1]{0:T(128)} %bitcast.29.freq_ref, s32[1032,128]{1,0:T(8,128)} %collective-permute-done.15.code_ref, f32[4,256,8,128]{3,2,1,0:T(8,128)} %result.4.rest_0_), custom_call_target="tpu_custom_call", output_to_operand_aliasing={{}: (2, {})} | custom-call | flops 524288 | bytes 1572864 | tf_op jit(solution)/shard_map/result/pallas_call | solution.py:710
  108.8 7.3 %collective-permute-done.14.code_ref = s32[1032,128]{1,0:T(8,128)S(1)} collective-permute-done((s32[1032,128]{1,0:T(8,128)S(1)}, s32[1032,128]{1,0:T(8,128)S(1)}, u32[]{:S(2)}, u32[]{:S(2)}) %collective-permute-start.14) | collective-permute-done | bytes 528416 | tf_op jit(solution)/shard_map/ppermute | solution.py:703
  (97 shorter events, 17.8 us)
Async XLA Ops:
  5.9 40.4 %copy-start.10 = (f32[2,16]{1,0:T(2,128)S(1)}, f32[2,16]{1,0:T(2,128)}, u32[]{:S(2)}) copy-start(f32[2,16]{1,0:T(2,128)} %slow_ref.1) | copy-start | bytes 388
  5.9 26.9 %collective-permute-start.3 = (bf16[8,128,128]{2,1,0:T(8,128)(2,1)S(1)}, bf16[8,128,128]{2,1,0:T(8,128)(2,1)S(1)}, u32[]{:S(2)}, u32[]{:S(2)}) collective-permute-start(bf16[8,128,128]{2,1,0:T(8,128)(2,1)S(1)} %take_own.1.rest_0_), channel_id=1, source_target_pairs={{0,2},{1,3},{2,0},{3,1},{4,6},{5,7},{6,4},{7,5},{8,10},{9,11},{10,... | collective-permute-start | bytes 786440 | tf_op jit(solution)/shard_map/ppermute | solution.py:569
  9.0 14.0 %collective-permute-start.4 = (bf16[8,128,128]{2,1,0:T(8,128)(2,1)S(1)}, bf16[8,128,128]{2,1,0:T(8,128)(2,1)S(1)}, u32[]{:S(2)}, u32[]{:S(2)}) collective-permute-start(bf16[8,128,128]{2,1,0:T(8,128)(2,1)S(1)} %take_own.1.rest_0_), channel_id=1, source_target_pairs={{0,4},{1,5},{2,6},{3,7},{4,0},{5,1},{6,2},{7,3},{8,12},{9,13},{10,... | collective-permute-start | bytes 786440 | tf_op jit(solution)/shard_map/ppermute | solution.py:569
  12.4 15.2 %all-to-all-start = ((bf16[3,8,8,512]{3,2,0,1:T(8,128)(2,1)}), bf16[3,8,8,512]{3,2,0,1:T(8,128)(2,1)S(1)}, u32[]{:S(2)}, u32[]{:S(2)}) async-start(bf16[3,8,8,512]{3,2,0,1:T(8,128)(2,1)} %copy.46), calls=%async_computation | async-start | bytes 393216 | tf_op jit(solution)/shard_map/all_to_all | solution.py:551
  23.0 14.4 %collective-permute-start.5 = (bf16[8,128,128]{2,1,0:T(8,128)(2,1)S(1)}, bf16[8,128,128]{2,1,0:T(8,128)(2,1)S(1)}, u32[]{:S(2)}, u32[]{:S(2)}) collective-permute-start(bf16[8,128,128]{2,1,0:T(8,128)(2,1)S(1)} %collective-permute-done.4.rest_2_), channel_id=1, source_target_pairs={{0,2},{1,3},{2,0},{3,1},{4,6},{5,7},{6,4},{7,5},{8,10},{9,11},{10,... | collective-permute-start | bytes 786440 | tf_op jit(solution)/shard_map/ppermute | solution.py:569
  27.6 7.1 %collective-permute-start.2 = (bf16[17,8,512]{2,1,0:T(8,128)(2,1)S(1)}, bf16[17,8,512]{2,1,0:T(8,128)(2,1)S(1)}, u32[]{:S(2)}, u32[]{:S(2)}) collective-permute-start(bf16[17,8,512]{2,1,0:T(8,128)(2,1)S(1)} %get-tuple-element.48), channel_id=1, source_target_pairs={{0,24},{8,16},{16,8},{24,0},{1,25},{9,17},{17,9},{25,1},{2,26},{10... | collective-permute-start | bytes 417800 | tf_op jit(solution)/shard_map/ppermute | solution.py:585
  30.1 7.1 %collective-permute-start.1 = (bf16[17,8,512]{2,1,0:T(8,128)(2,1)S(1)}, bf16[17,8,512]{2,1,0:T(8,128)(2,1)S(1)}, u32[]{:S(2)}, u32[]{:S(2)}) collective-permute-start(bf16[17,8,512]{2,1,0:T(8,128)(2,1)S(1)} %get-tuple-element.48), channel_id=1, source_target_pairs={{0,16},{8,24},{16,0},{24,8},{1,17},{9,25},{17,1},{25,9},{2,18},{10... | collective-permute-start | bytes 417800 | tf_op jit(solution)/shard_map/ppermute | solution.py:585
  30.7 6.7 %collective-permute-start = (bf16[17,8,512]{2,1,0:T(8,128)(2,1)S(1)}, bf16[17,8,512]{2,1,0:T(8,128)(2,1)S(1)}, u32[]{:S(2)}, u32[]{:S(2)}) collective-permute-start(bf16[17,8,512]{2,1,0:T(8,128)(2,1)S(1)} %get-tuple-element.48), channel_id=1, source_target_pairs={{0,8},{8,0},{16,24},{24,16},{1,9},{9,1},{17,25},{25,17},{2,10},{10... | collective-permute-start | bytes 417800 | tf_op jit(solution)/shard_map/ppermute | solution.py:585
  32.8 5.7 %collective-permute-start.6 = (bf16[8,128,128]{2,1,0:T(8,128)(2,1)S(1)}, bf16[8,128,128]{2,1,0:T(8,128)(2,1)S(1)}, u32[]{:S(2)}, u32[]{:S(2)}) collective-permute-start(bf16[8,128,128]{2,1,0:T(8,128)(2,1)S(1)} %take_own.1.rest_0_), channel_id=1, source_target_pairs={{0,1},{1,0},{2,3},{3,2},{4,5},{5,4},{6,7},{7,6},{8,9},{9,8},{10,11... | collective-permute-start | bytes 786440 | tf_op jit(solution)/shard_map/ppermute | solution.py:576
  34.7 4.1 %collective-permute-start.8 = (bf16[8,128,128]{2,1,0:T(8,128)(2,1)S(1)}, bf16[8,128,128]{2,1,0:T(8,128)(2,1)S(1)}, u32[]{:S(2)}, u32[]{:S(2)}) collective-permute-start(bf16[8,128,128]{2,1,0:T(8,128)(2,1)S(1)} %collective-permute-done.4.rest_2_), channel_id=1, source_target_pairs={{0,1},{1,0},{2,3},{3,2},{4,5},{5,4},{6,7},{7,6},{8,9},{9,8},{10,11... | collective-permute-start | bytes 786440 | tf_op jit(solution)/shard_map/ppermute | solution.py:576
  37.2 1.5 %collective-permute-start.7 = (bf16[8,128,128]{2,1,0:T(8,128)(2,1)S(1)}, bf16[8,128,128]{2,1,0:T(8,128)(2,1)S(1)}, u32[]{:S(2)}, u32[]{:S(2)}) collective-permute-start(bf16[8,128,128]{2,1,0:T(8,128)(2,1)S(1)} %collective-permute-done.3.rest_1_), channel_id=1, source_target_pairs={{0,1},{1,0},{2,3},{3,2},{4,5},{5,4},{6,7},{7,6},{8,9},{9,8},{10,11... | collective-permute-start | bytes 786440 | tf_op jit(solution)/shard_map/ppermute | solution.py:576
  37.4 1.7 %collective-permute-start.9 = (bf16[8,128,128]{2,1,0:T(8,128)(2,1)S(1)}, bf16[8,128,128]{2,1,0:T(8,128)(2,1)S(1)}, u32[]{:S(2)}, u32[]{:S(2)}) collective-permute-start(bf16[8,128,128]{2,1,0:T(8,128)(2,1)S(1)} %collective-permute-done.5.rest_3_), channel_id=1, source_target_pairs={{0,1},{1,0},{2,3},{3,2},{4,5},{5,4},{6,7},{7,6},{8,9},{9,8},{10,11... | collective-permute-start | bytes 786440 | tf_op jit(solution)/shard_map/ppermute | solution.py:576
  42.7 18.9 %collective-permute-start.10 = (s32[5,17,8,128]{3,2,1,0:T(8,128)}, s32[5,17,8,128]{3,2,1,0:T(8,128)S(1)}, u32[]{:S(2)}, u32[]{:S(2)}) collective-permute-start(s32[5,17,8,128]{3,2,1,0:T(8,128)} %get-tuple-element.39), channel_id=1, source_target_pairs={{0,8},{8,0},{16,24},{24,16},{1,9},{9,1},{17,25},{25,17},{2,10},{10... | collective-permute-start | bytes 1044488 | tf_op jit(solution)/shard_map/ppermute | solution.py:635
  44.3 17.7 %collective-permute-start.11 = (s32[5,17,8,128]{3,2,1,0:T(8,128)}, s32[5,17,8,128]{3,2,1,0:T(8,128)S(1)}, u32[]{:S(2)}, u32[]{:S(2)}) collective-permute-start(s32[5,17,8,128]{3,2,1,0:T(8,128)} %get-tuple-element.40), channel_id=1, source_target_pairs={{0,16},{8,24},{16,0},{24,8},{1,17},{9,25},{17,1},{25,9},{2,18},{10... | collective-permute-start | bytes 1044488 | tf_op jit(solution)/shard_map/ppermute | solution.py:635
  45.1 16.9 %collective-permute-start.12 = (s32[5,17,8,128]{3,2,1,0:T(8,128)S(1)}, s32[5,17,8,128]{3,2,1,0:T(8,128)S(1)}, u32[]{:S(2)}, u32[]{:S(2)}) collective-permute-start(s32[5,17,8,128]{3,2,1,0:T(8,128)S(1)} %get-tuple-element.41), channel_id=1, source_target_pairs={{0,24},{8,16},{16,8},{24,0},{1,25},{9,17},{17,9},{25,1},{2,26},{10... | collective-permute-start | bytes 1044488 | tf_op jit(solution)/shard_map/ppermute | solution.py:635
  46.3 15.7 %copy-start.2 = (bf16[256,768]{1,0:T(8,128)(2,1)S(1)}, bf16[256,768]{1,0:T(8,128)(2,1)}, u32[]{:S(2)}) copy-start(bf16[256,768]{1,0:T(8,128)(2,1)} %constant.135.clone.rest_8_.rows_inverse) | copy-start | bytes 1179652
  46.3 15.7 %copy-start.3 = (f32[2,128,128]{2,1,0:T(8,128)S(1)}, f32[2,128,128]{2,1,0:T(8,128)}, u32[]{:S(2)}) copy-start(f32[2,128,128]{2,1,0:T(8,128)} %constant.139.clone.rest_12_.offset_ref) | copy-start | bytes 393220
  46.4 15.7 %copy-start.5 = (bf16[256,768]{1,0:T(8,128)(2,1)S(1)}, bf16[256,768]{1,0:T(8,128)(2,1)}, u32[]{:S(2)}) copy-start(bf16[256,768]{1,0:T(8,128)(2,1)} %constant.134.clone.rest_7_) | copy-start | bytes 1179652
  46.4 15.7 %copy-start.6 = (bf16[768,256]{1,0:T(8,128)(2,1)S(1)}, bf16[768,256]{1,0:T(8,128)(2,1)}, u32[]{:S(2)}) copy-start(bf16[768,256]{1,0:T(8,128)(2,1)} %constant.136.clone.rest_9_) | copy-start | bytes 1179652
  46.4 15.7 %copy-start.7 = (bf16[768,256]{1,0:T(8,128)(2,1)S(1)}, bf16[768,256]{1,0:T(8,128)(2,1)}, u32[]{:S(2)}) copy-start(bf16[768,256]{1,0:T(8,128)(2,1)} %constant.137.clone.rest_10_) | copy-start | bytes 1179652
  46.4 15.7 %copy-start.8 = (f32[2,16,8,128]{3,2,1,0:T(8,128)S(1)}, f32[2,16,8,128]{3,2,1,0:T(8,128)}, u32[]{:S(2)}) copy-start(f32[2,16,8,128]{3,2,1,0:T(8,128)} %constant.138.clone.rest_11_) | copy-start | bytes 393220
  90.7 16.1 %collective-permute-start.15 = (s32[1032,128]{1,0:T(8,128)S(1)}, s32[1032,128]{1,0:T(8,128)}, u32[]{:S(2)}, u32[]{:S(2)}) collective-permute-start(s32[1032,128]{1,0:T(8,128)S(1)} %finish.4.rest_0_), channel_id=1, source_target_pairs={{0,24},{8,16},{16,8},{24,0},{1,25},{9,17},{17,9},{25,1},{2,26},{10... | collective-permute-start | bytes 1585160 | tf_op jit(solution)/shard_map/ppermute | solution.py:703
  94.0 22.2 %collective-permute-start.14 = (s32[1032,128]{1,0:T(8,128)S(1)}, s32[1032,128]{1,0:T(8,128)S(1)}, u32[]{:S(2)}, u32[]{:S(2)}) collective-permute-start(s32[1032,128]{1,0:T(8,128)S(1)} %finish.5.rest_0_), channel_id=1, source_target_pairs={{0,16},{8,24},{16,0},{24,8},{1,17},{9,25},{17,1},{25,9},{2,18},{10... | collective-permute-start | bytes 1585160 | tf_op jit(solution)/shard_map/ppermute | solution.py:703
  96.8 20.4 %collective-permute-start.13 = (s32[1032,128]{1,0:T(8,128)S(1)}, s32[1032,128]{1,0:T(8,128)S(1)}, u32[]{:S(2)}, u32[]{:S(2)}) collective-permute-start(s32[1032,128]{1,0:T(8,128)S(1)} %finish.6.rest_0_), channel_id=1, source_target_pairs={{0,8},{8,0},{16,24},{24,16},{1,9},{9,1},{17,25},{25,17},{2,10},{10... | collective-permute-start | bytes 1585160 | tf_op jit(solution)/shard_map/ppermute | solution.py:703
  (4 other events, 10.2 us)

commit v9 on v7

--- a/solution.py
+++ b/solution.py
@@ -16,6 +16,8 @@
 damping = 0.1
 
 HALF = NH // 2
+RADIX = 8
+TALL = NH // RADIX
 STEP_LOG = 64.0
 TOP = 32767.0
 GROUP = 8
@@ -54,14 +56,14 @@
 
 
 def block_tables():
-    index = np.arange(BLK)
-    angles = 2.0 * np.pi * (np.outer(index, index) % BLK) / BLK
-    cos, sin = np.cos(angles), np.sin(angles)
-    upper = np.block([[cos, sin], [-sin, cos]])
-    lower = np.block([[cos, -sin], [sin, cos]])
     tables = []
-    for axis, pair in ((1, (upper, lower)), (0, (lower, upper))):
-        for table in pair:
+    for axis, size in ((1, TALL), (0, BLK)):
+        index = np.arange(size)
+        angles = 2.0 * np.pi * (np.outer(index, index) % size) / size
+        cos, sin = np.cos(angles), np.sin(angles)
+        upper = np.block([[cos, sin], [-sin, cos]])
+        lower = np.block([[cos, -sin], [sin, cos]])
+        for table in (upper, lower) if axis == 1 else (lower, upper):
             high, low = halves_np(table)
             tables.append(np.concatenate([high, high, low], axis=axis))
     return tables
@@ -71,9 +73,10 @@
     ka, b = np.arange(outer)[:, None], np.arange(BLK)[None, :]
     angles = 2.0 * np.pi * ka * b / (outer * BLK)
     middle = np.stack([np.cos(angles), np.sin(angles)]).astype(np.float32)
-    rows = 2.0 * np.pi * np.arange(HALF) / NH
+    rows = 2.0 * np.pi * np.outer(np.arange(RADIX), np.arange(TALL)) / NH
     offset = np.stack([np.cos(rows), np.sin(rows)]).astype(np.float32)
-    return middle, np.broadcast_to(offset[:, :, None], (2, HALF, BLK)).copy()
+    middle = np.broadcast_to(middle[:, :, None], (2, outer, ROWS, BLK)).copy()
+    return middle, np.broadcast_to(offset[..., None], (2, RADIX, TALL, BLK)).copy()
 
 
 def halves(value):
@@ -132,6 +135,10 @@
 
 def cmul(real_a, imag_a, real_b, imag_b):
     return real_a * real_b - imag_a * imag_b, real_a * imag_b + imag_a * real_b
+
+
+def cmul_conj(real_a, imag_a, real_b, imag_b):
+    return real_a * real_b + imag_a * imag_b, imag_a * real_b - real_a * imag_b
 
 
 def small_transform(values, sign):
@@ -220,54 +227,6 @@
             out_ref[group, outer] = code
 
 
-def column_of(plane, a):
-    lanes = pl.ds(aligned(a * BLK, BLK), BLK)
-    return jnp.concatenate(
-        [
-            jnp.concatenate([plane[p, 0, :, lanes], plane[p, 1, :, lanes]], axis=0)
-            for p in range(2)
-        ],
-        axis=1,
-    )
-
-
-def store_column(plane, a, value):
-    lanes = pl.ds(aligned(a * BLK, BLK), BLK)
-    for p in range(2):
-        for c in range(2):
-            plane[p, c, :, lanes] = value[c * HALF : (c + 1) * HALF, p * BLK : (p + 1) * BLK]
-
-
-def row_blocks(tall):
-    return [slice(at * tall, (at + 1) * tall) for at in range(HALF // tall)]
-
-
-def turn_at(offset_ref, rows):
-    return offset_ref[0, rows], offset_ref[1, rows]
-
-
-def forward_rows(low, high, turn):
-    first = low[0] + high[0], low[1] + high[1]
-    second = cmul(low[0] - high[0], low[1] - high[1], turn[0], -turn[1])
-    return (*first, *second)
-
-
-def inverse_rows(value, rows, turn):
-    upper, below = rows, slice(HALF + rows.start, HALF + rows.stop)
-    first = value[upper, :BLK], value[below, :BLK]
-    second = cmul(value[upper, BLK:], value[below, BLK:], turn[0], turn[1])
-    low = first[0] + second[0], first[1] + second[1]
-    high = first[0] - second[0], first[1] - second[1]
-    return low, high
-
-
-def assembled(blocks):
-    parts = [jnp.concatenate(part, axis=0) for part in zip(*blocks)]
-    return jnp.concatenate(
-        [jnp.concatenate(parts[:2], axis=0), jnp.concatenate(parts[2:], axis=0)], axis=1
-    )
-
-
 def propagator_kernel(omega_ref, slow_ref, layers_ref, real_ref, imag_ref, turns_ref):
     steps, layer_total = slow_ref.shape
     for step in range(steps):
@@ -288,7 +247,7 @@
         start = pl.multiple_of(at * GROUP, GROUP)
         row = lax.broadcasted_iota(jnp.int32, (GROUP, BLK), 0) + at * GROUP
         lane = lax.broadcasted_iota(jnp.int32, (GROUP, BLK), 1)
-        offset_wave = signed_wave(2 * (row % HALF) + row // HALF, NH)
+        offset_wave = signed_wave(RADIX * (row % TALL) + row // TALL, NH)
         for a in range(total // BLK):
             mid_wave = signed_wave(a + total // BLK * lane, total)
             real, imag = propagator(omega_sq, mid_wave, offset_wave)
@@ -296,11 +255,57 @@
             imag_ref[pl.ds(start, GROUP), a * BLK : (a + 1) * BLK] = imag * scale
 
 
-def layer_turn(pair, layer_ref, step, block, a):
-    half = layer_ref.shape[2] // 2
+def column_of(plane, a):
+    lanes = pl.ds(aligned(a * BLK, BLK), BLK)
+    return jnp.concatenate(
+        [jnp.concatenate([plane[q, 0, :, lanes], plane[q, 1, :, lanes]], axis=0) for q in range(RADIX)],
+        axis=1,
+    )
+
+
+def store_column(plane, a, value):
+    lanes = pl.ds(aligned(a * BLK, BLK), BLK)
+    for q in range(RADIX):
+        for c in range(2):
+            plane[q, c, :, lanes] = value[c * TALL : (c + 1) * TALL, q * BLK : (q + 1) * BLK]
+
+
+def row_starts():
+    return range(0, TALL, ROWS)
+
+
+def forward_rows(values, offset_ref, start):
+    rows = slice(start, start + ROWS)
+    values = small_transform(values, -1)
+    return values[:1] + [
+        cmul_conj(*values[q], offset_ref[0, q, rows], offset_ref[1, q, rows]) for q in range(1, RADIX)
+    ]
+
+
+def inverse_rows(value, offset_ref, start):
+    rows, below = slice(start, start + ROWS), slice(TALL + start, TALL + start + ROWS)
+    values = []
+    for q in range(RADIX):
+        part = value[rows, q * BLK : (q + 1) * BLK], value[below, q * BLK : (q + 1) * BLK]
+        values.append(cmul(*part, offset_ref[0, q, rows], offset_ref[1, q, rows]) if q else part)
+    return small_transform(values, 1)
+
+
+def assembled(blocks):
+    return jnp.concatenate(
+        [
+            jnp.concatenate([values[q][c] for c in range(2) for values in blocks], axis=0)
+            for q in range(RADIX)
+        ],
+        axis=1,
+    )
+
+
+def layer_turn(values, layer_ref, step, a):
+    per = RADIX // layer_ref.shape[2]
     return [
-        cmul(*part, layer_ref[0, step, block + p * half, a], layer_ref[1, step, block + p * half, a])
-        for p, part in enumerate(pair)
+        cmul(*part, layer_ref[0, step, g // per, a], layer_ref[1, step, g // per, a])
+        for g, part in enumerate(values)
     ]
 
 
@@ -308,7 +313,7 @@
     outer = middle_ref.shape[1]
     lanes = [slice(a * BLK, (a + 1) * BLK) for a in range(outer)]
     tall = first_kept[0].shape[0] // outer
-    per_half = HALF // tall
+    per_half = TALL // tall
     chunks = range(0, tall, ROWS)
 
     def place(at):
@@ -325,7 +330,7 @@
             values = [(plane[p, 0, here, lane], plane[p, 1, here, lane]) for lane in lanes]
             values = small_transform(values, -1)
             for a in range(outer):
-                pieces.append(cmul(*values[a], middle_ref[0, a : a + 1], -middle_ref[1, a : a + 1]))
+                pieces.append(cmul_conj(*values[a], middle_ref[0, a], middle_ref[1, a]))
         keep_lanes(first_kept[parity], gathered(pieces))
 
     def phase_stage(at, parity):
@@ -354,14 +359,14 @@
                 row = chunk * outer + a * ROWS
                 part = value[row : row + ROWS]
                 values.append(
-                    cmul(part[:, :BLK], part[:, BLK:], middle_ref[0, a : a + 1], middle_ref[1, a : a + 1])
+                    cmul(part[:, :BLK], part[:, BLK:], middle_ref[0, a], middle_ref[1, a])
                 )
             values = small_transform(values, 1)
             for a in range(outer):
                 out[p, 0, here, lanes[a]] = values[a][0]
                 out[p, 1, here, lanes[a]] = values[a][1]
 
-    pipelined(2 * per_half, forward_stage, phase_stage, inverse_stage)
+    pipelined(RADIX * per_half, forward_stage, phase_stage, inverse_stage)
 
 
 def march_kernel(layer_ref, *rest, sources):
@@ -374,7 +379,6 @@
     groups = code_refs[0].shape[0]
     outer = middle_ref.shape[1]
     steps = layer_ref.shape[1]
-    tall = NH // layer_ref.shape[2]
 
     def words(a):
         return jnp.concatenate([ref[:, a].reshape(groups * GROUP, BLK) for ref in code_refs], axis=0)
@@ -389,13 +393,12 @@
     def place_stage(a, parity):
         moved = dot(pick_ref[...], terms[parity][...])
         blocks = []
-        for rows in row_blocks(tall):
-            low, high = moved[rows], moved[HALF + rows.start : HALF + rows.stop]
-            blocks.append(
-                forward_rows(
-                    (low[:, :BLK], low[:, BLK:]), (high[:, :BLK], high[:, BLK:]), turn_at(offset_ref, rows)
-                )
-            )
+        for start in row_starts():
+            values = []
+            for g in range(RADIX):
+                part = moved[g * TALL + start : g * TALL + start + ROWS]
+                values.append((part[:, :BLK], part[:, BLK:]))
+            blocks.append(forward_rows(values, offset_ref, start))
         keep_rows(column_second[parity], assembled(blocks))
 
     def store_stage(a, parity):
@@ -415,10 +418,9 @@
             def turn_stage(a, parity):
                 value = left_product(rows_inverse[...], column_first[parity])
                 blocks = []
-                for block, rows in enumerate(row_blocks(tall)):
-                    turn = turn_at(offset_ref, rows)
-                    pair = inverse_rows(value, rows, turn)
-                    blocks.append(forward_rows(*layer_turn(pair, layer_ref, step, block, a), turn))
+                for start in row_starts():
+                    values = layer_turn(inverse_rows(value, offset_ref, start), layer_ref, step, a)
+                    blocks.append(forward_rows(values, offset_ref, start))
                 keep_rows(column_second[parity], assembled(blocks))
 
             pipelined(outer, load_stage, turn_stage, store_stage)
@@ -427,24 +429,29 @@
 def finish_kernel(dest_ref, layer_ref, plane_ref, rows_inverse, offset_ref, *rest):
     out_ref, kept = rest[-2:]
     here = plane_ref.shape[3] // BLK
-    tall = NH // layer_ref.shape[2]
     step = layer_ref.shape[1] - 1
     keep_rows(kept, jnp.concatenate([column_of(plane_ref, at) for at in range(here)], axis=1))
     value = left_product(rows_inverse[...], kept)
-    columns = [value[:, at * 2 * BLK : (at + 1) * 2 * BLK] for at in range(here)]
     for at in range(here):
-        found = []
-        for block, rows in enumerate(row_blocks(tall)):
-            pair = inverse_rows(columns[at], rows, turn_at(offset_ref, rows))
-            found.append(layer_turn(pair, layer_ref, step, block, dest_ref[0] * here + at))
+        column = value[:, at * RADIX * BLK : (at + 1) * RADIX * BLK]
+        found = [
+            layer_turn(inverse_rows(column, offset_ref, start), layer_ref, step, dest_ref[0] * here + at)
+            for start in row_starts()
+        ]
         for c in range(2):
-            biggest = functools.reduce(jnp.maximum, [jnp.abs(part[c]) for pair in found for part in pair])
+            biggest = functools.reduce(
+                jnp.maximum, [jnp.abs(part[c]) for values in found for part in values]
+            )
             code = scale_code(jnp.max(biggest, axis=0, keepdims=True))
             inverse = inverse_scale_of(code)
             row = at * 2 + c
-            for block, pair in enumerate(found):
-                words = packed(coded(pair[0][c], inverse), coded(pair[1][c], inverse))
-                out_ref[pl.ds(block * tall * 2 * here + row, tall, 2 * here), :] = words
+            for start, values in zip(row_starts(), found):
+                for g in range(RADIX // 2):
+                    words = packed(
+                        coded(values[g][c], inverse), coded(values[g + RADIX // 2][c], inverse)
+                    )
+                    first = (g * TALL + start) * 2 * here + row
+                    out_ref[pl.ds(first, ROWS, 2 * here), :] = words
             out_ref[pl.ds(HALF * 2 * here + row, 1), :] = code
 
 
@@ -521,7 +528,7 @@
     total_mid = mid_local * mid_count
     outer = total_mid // BLK
     mid_at, off_at = lax.axis_index("mid"), lax.axis_index("off")
-    assert mid_count % fl == 0 and (bins_local * entries) % fl == 0
+    assert RADIX % layer_index.shape[1] == 0 and mid_count % fl == 0 and (bins_local * entries) % fl == 0
     mine = mid_at % fl
     rounds = mid_count // fl
     groups = (
@@ -565,11 +572,10 @@
         flat = jnp.pad(flat, ((0, 0), (0, 0), (0, pairs - 1), (0, mid_local - flat.shape[3])))
         return jnp.broadcast_to(flat, (1, copies, pairs, mid_local))
 
-    lists = jnp.concatenate([counts[:, None], targets], axis=1)
+    lists = lax.optimization_barrier(jnp.concatenate([counts[:, None], targets], axis=1))
     data = bins_data.reshape(bins_local, off_count, pairs, mid_local)
     data = jnp.concatenate([data, extra(lists, off_count)], axis=0)
     data = lax.all_to_all(data, "off", split_axis=1, concat_axis=0, tiled=True)
-
     data = data.reshape(off_count, bins_local + 1, pairs, mid_local)
     lists = data[:, bins_local, 0, : lists.size].astype(jnp.int32).reshape(bins_total, 1 + entries)
     data = data[:, :bins_local].reshape(bins_total, pairs, mid_local)
@@ -652,11 +658,11 @@
         functools.partial(march_kernel, sources=fl),
         in_specs=[smem] + [vmem] * (fl + 9),
         out_specs=vmem,
-        out_shape=jax.ShapeDtypeStruct((2, 2, HALF, total_mid), jnp.float32),
+        out_shape=jax.ShapeDtypeStruct((RADIX, 2, TALL, total_mid), jnp.float32),
         scratch_shapes=[
-            pltpu.VMEM((2, 2, HALF, total_mid), jnp.float32),
+            pltpu.VMEM((RADIX, 2, TALL, total_mid), jnp.float32),
             pltpu.VMEM((fl * room, BLK), jnp.float32),
-            *[pltpu.VMEM((2 * NH, 2 * BLK), jnp.bfloat16)] * 4,
+            *[pltpu.VMEM((4 * TALL, RADIX * BLK), jnp.bfloat16)] * 4,
             *[pltpu.VMEM((ROWS * CHUNKS * outer, 4 * BLK), jnp.bfloat16)] * 4,
             *[pltpu.VMEM((2 * fl * room, 2 * BLK), jnp.bfloat16)] * 2,
         ],
@@ -672,13 +678,13 @@
                 grid=(1,),
                 in_specs=[
                     smem,
-                    pl.BlockSpec((2, 2, HALF, mid_local), lambda i, dest: (0, 0, 0, dest[0])),
+                    pl.BlockSpec((RADIX, 2, TALL, mid_local), lambda i, dest: (0, 0, 0, dest[0])),
                     vmem,
                     vmem,
                 ]
                 + [hbm] * len(before),
                 out_specs=pl.BlockSpec((rows_out, BLK), lambda i, dest: (0, 0)),
-                scratch_shapes=[pltpu.VMEM((2 * NH, 2 * mid_local), jnp.bfloat16)],
+                scratch_shapes=[pltpu.VMEM((4 * TALL, RADIX * mid_local), jnp.bfloat16)],
             ),
             out_shape=jax.ShapeDtypeStruct((rows_out, BLK), jnp.int32),
             cost_estimate=pl.CostEstimate(

time: 116 us -> 117 us (level)
    pallas_call x1, Pallas kernels: 26.8 us -> 28.4 us  [local(): pl.pallas_call(functools.partial(march_kernel, sources=fl), in_specs=[sme...]
  transfers between devices with their start and end apart: 17 -> 17, of which waited for: 10 -> 10; matrix products, arithmetic and copies ran while one was open for 6% -> 6% of each run, Pallas kernels for 21% -> 20%
where the time goes in v9:
time: 117 us
  Pallas kernels  59.4 us (51%)
  starting transfers between devices  23.2 us (20%)
  waiting for transfers between devices  22.5 us (19%)
  local copies, waits for them, and re-layouts  8.38 us (7%)
  other arithmetic  3.02 us (3%)
    pallas_call x1, Pallas kernels, local(): pl.pallas_call(functools.partial(march_kernel, sources=fl), in_specs=[sme...  28.4 us
    pallas_call x1, Pallas kernels, local(): pl.pallas_call(propagator_kernel, in_specs=[smem, smem, vmem], out_specs=...  15.2 us
    ppermute x3, waiting for transfers between devices, local(): lax.ppermute(block, 'mid', [(s, s ^ ahead) for s in range(mid_count)])  12.3 us
    ppermute x3, starting transfers between devices, local(): lax.ppermute(shares[away ^ low], 'off', [(i, (i // cores ^ low) * cores +...  8.49 us
    pallas_call x4, Pallas kernels, finish(): pl.pallas_call(finish_kernel, grid_spec=pltpu.PrefetchScalarGridSpec(num_...  6.87 us
    ppermute x3, waiting for transfers between devices, local(): lax.ppermute(data, 'mid', [(i, i ^ away) for i in range(mid_count)])  4.35 us
    pallas_call x4, Pallas kernels, local(): pl.pallas_call(result_kernel, grid_spec=pltpu.PrefetchScalarGridSpec(num_...  4.15 us
    unnamed x22, local copies, waits for them, and re-layouts  4.11 us
  transfers between devices with their start and end apart: 17, of which 10 were waited for; matrix products, arithmetic and copies ran while one was open for 6% of the time, Pallas kernels for 20%

profile of v9, /device:TPU:0, one launch (start us, length us, event | category | flops | bytes accessed | tf_op | source)
XLA Modules:
  0.0 116.9 jit_solution(14955214913934288202)
XLA Ops:
  0.0 1.2 %copy-done.3 = bf16[2,16,128,128]{3,2,1,0:T(8,128)(2,1)S(1)} copy-done((bf16[2,16,128,128]{3,2,1,0:T(8,128)(2,1)S(1)}, bf16[2,16,128,128]{3,2,1,0:T(8,128)(2,1)}, u32[]{:S(2)}) %copy-start.3) | copy-done | bytes 1048600
  2.9 3.1 %collective-permute-start.3 = (bf16[8,128,128]{2,1,0:T(8,128)(2,1)S(1)}, bf16[8,128,128]{2,1,0:T(8,128)(2,1)S(1)}, u32[]{:S(2)}, u32[]{:S(2)}) collective-permute-start(bf16[8,128,128]{2,1,0:T(8,128)(2,1)S(1)} %take_own.1.rest_0_), channel_id=1, source_target_pairs={{0,2},{1,3},{2,0},{3,1},{4,6},{5,7},{6,4},{7,5},{8,10},{9,11},{10,... | collective-permute-start | bytes 786440 | tf_op jit(solution)/shard_map/ppermute | solution.py:559
  6.0 2.6 %collective-permute-start.4 = (bf16[8,128,128]{2,1,0:T(8,128)(2,1)S(1)}, bf16[8,128,128]{2,1,0:T(8,128)(2,1)S(1)}, u32[]{:S(2)}, u32[]{:S(2)}) collective-permute-start(bf16[8,128,128]{2,1,0:T(8,128)(2,1)S(1)} %take_own.1.rest_0_), channel_id=1, source_target_pairs={{0,4},{1,5},{2,6},{3,7},{4,0},{5,1},{6,2},{7,3},{8,12},{9,13},{10,... | collective-permute-start | bytes 786440 | tf_op jit(solution)/shard_map/ppermute | solution.py:559
  12.3 3.4 %all-to-all-start = ((bf16[3,8,8,512]{3,2,0,1:T(8,128)(2,1)}), bf16[3,8,8,512]{3,2,0,1:T(8,128)(2,1)S(1)}, u32[]{:S(2)}, u32[]{:S(2)}) async-start(bf16[3,8,8,512]{3,2,0,1:T(8,128)(2,1)} %copy.46), calls=%async_computation | async-start | bytes 393216 | tf_op jit(solution)/shard_map/all_to_all | solution.py:578
  17.0 3.4 %collective-permute-done.4.rest_2_ = bf16[8,128,128]{2,1,0:T(8,128)(2,1)S(1)} collective-permute-done((bf16[8,128,128]{2,1,0:T(8,128)(2,1)S(1)}, bf16[8,128,128]{2,1,0:T(8,128)(2,1)S(1)}, u32[]{:S(2)}, u32[]{:S(2)}) %collective-permute-start.4) | collective-permute-done | bytes 262176 | tf_op jit(solution)/shard_map/ppermute | solution.py:559
  20.4 2.8 %collective-permute-start.5 = (bf16[8,128,128]{2,1,0:T(8,128)(2,1)S(1)}, bf16[8,128,128]{2,1,0:T(8,128)(2,1)S(1)}, u32[]{:S(2)}, u32[]{:S(2)}) collective-permute-start(bf16[8,128,128]{2,1,0:T(8,128)(2,1)S(1)} %collective-permute-done.4.rest_2_), channel_id=1, source_target_pairs={{0,2},{1,3},{2,0},{3,1},{4,6},{5,7},{6,4},{7,5},{8,10},{9,11},{10,... | collective-permute-start | bytes 786440 | tf_op jit(solution)/shard_map/ppermute | solution.py:559
  23.2 1.4 %all-to-all-done = bf16[3,8,8,512]{3,2,0,1:T(8,128)(2,1)S(1)} async-done(((bf16[3,8,8,512]{3,2,0,1:T(8,128)(2,1)}), bf16[3,8,8,512]{3,2,0,1:T(8,128)(2,1)S(1)}, u32[]{:S(2)}, u32[]{:S(2)}) %all-to-all-start) | async-done | bytes 196640 | tf_op jit(solution)/shard_map/all_to_all | solution.py:578
  24.6 2.5 %collective-permute-start.2 = (bf16[17,8,512]{2,1,0:T(8,128)(2,1)S(1)}, bf16[17,8,512]{2,1,0:T(8,128)(2,1)S(1)}, u32[]{:S(2)}, u32[]{:S(2)}) collective-permute-start(bf16[17,8,512]{2,1,0:T(8,128)(2,1)S(1)} %get-tuple-element.48), channel_id=1, source_target_pairs={{0,24},{8,16},{16,8},{24,0},{1,25},{9,17},{17,9},{25,1},{2,26},{10... | collective-permute-start | bytes 417800 | tf_op jit(solution)/shard_map/ppermute | solution.py:585
  29.9 1.8 %collective-permute-done.2 = bf16[17,8,512]{2,1,0:T(8,128)(2,1)S(1)} collective-permute-done((bf16[17,8,512]{2,1,0:T(8,128)(2,1)S(1)}, bf16[17,8,512]{2,1,0:T(8,128)(2,1)S(1)}, u32[]{:S(2)}, u32[]{:S(2)}) %collective-permute-start.2) | collective-permute-done | bytes 139296 | tf_op jit(solution)/shard_map/ppermute | solution.py:585
  31.7 2.5 %collective-permute-done.1 = bf16[17,8,512]{2,1,0:T(8,128)(2,1)S(1)} collective-permute-done((bf16[17,8,512]{2,1,0:T(8,128)(2,1)S(1)}, bf16[17,8,512]{2,1,0:T(8,128)(2,1)S(1)}, u32[]{:S(2)}, u32[]{:S(2)}) %collective-permute-start.1) | collective-permute-done | bytes 139296 | tf_op jit(solution)/shard_map/ppermute | solution.py:585
  36.1 3.7 %contributions.1 = (s32[5,17,8,128]{3,2,1,0:T(8,128)S(1)}, s32[5,17,8,128]{3,2,1,0:T(8,128)}, s32[5,17,8,128]{3,2,1,0:T(8,128)}, s32[5,17,8,128]{3,2,1,0:T(8,128)}) custom-call(s32[1]{0:T(128)} %bitcast.2.mine_ref.place_ref.freq_ref, s32[16]{0:T(128)S(1)} %add.116.order_ref, s32[40]{0:T(128)S(1)} %get-tuple-element.27.slot_ref, ...), custom_call_target="tpu_custom_call" | custom-call | tf_op jit(solution)/shard_map/contributions/pallas_call | solution.py:619
  39.8 1.6 %collective-permute-start.10 = (s32[5,17,8,128]{3,2,1,0:T(8,128)}, s32[5,17,8,128]{3,2,1,0:T(8,128)S(1)}, u32[]{:S(2)}, u32[]{:S(2)}) collective-permute-start(s32[5,17,8,128]{3,2,1,0:T(8,128)} %get-tuple-element.39), channel_id=1, source_target_pairs={{0,8},{8,0},{16,24},{24,16},{1,9},{9,1},{17,25},{25,17},{2,10},{10... | collective-permute-start | bytes 1044488 | tf_op jit(solution)/shard_map/ppermute | solution.py:635
  42.2 1.2 collective-permute-start.12
  43.5 15.2 %propagator.1 = (f32[256,2048]{1,0:T(8,128)S(1)}, f32[256,2048]{1,0:T(8,128)S(1)}, f32[2,2,8,16]{3,2,1,0:T(8,128)S(1)}) custom-call(f32[1]{0:T(128)} %bitcast.25.omega_ref, f32[2,16]{1,0:T(2,128)S(1)} %copy-done.10, s32[2,8,16]{2,1,0:T(8,128)S(1)} %copy.50.layers_ref), custom_call_target="tpu_custom_call" | custom-call | flops 31457280 | bytes 4194304 | tf_op jit(solution)/shard_map/propagator/pallas_call | solution.py:639
  59.1 28.4 %march.1.plane_ref = f32[8,2,32,2048]{3,2,1,0:T(8,128)S(1)} custom-call(f32[2,2,8,16]{3,2,1,0:T(8,128)S(1)} %get-tuple-element.37.layer_ref, s32[5,17,8,128]{3,2,1,0:T(8,128)S(1)} %get-tuple-element.38.rest_0_, s32[5,17,8,128]{3,2,1,0:T(8,128)S(1)} %collective-permute-done.10.rest_1_, s32[5,17,8,128]{3,2,1,0:T(8,128)S(1)} %collective-permute-done.11.rest_2_, ...), custom_call_target="tpu_custom_call" | custom-call | tf_op jit(solution)/shard_map/march/pallas_call | solution.py:657
  87.6 1.7 %finish.4.rest_0_ = s32[1032,128]{1,0:T(8,128)S(1)} custom-call(s32[1]{0:T(128)} %bitcast.27.dest_ref, f32[2,2,8,16]{3,2,1,0:T(8,128)S(1)} %get-tuple-element.37.layer_ref, f32[8,2,32,2048]{3,2,1,0:T(8,128)S(1)} %march.1.plane_ref, bf16[64,192]{1,0:T(8,128)(2,1)S(1)} %copy-done.4, f32[2,8,32,128]{3,2,1,0:T(8,128)S(1)} %copy-done.2), custom_call_target="tpu_custom_call" | custom-call | flops 402653184 | bytes 786432 | tf_op jit(solution)/shard_map/finish/pallas_call | solution.py:674
  89.3 1.6 %collective-permute-start.15 = (s32[1032,128]{1,0:T(8,128)S(1)}, s32[1032,128]{1,0:T(8,128)S(1)}, u32[]{:S(2)}, u32[]{:S(2)}) collective-permute-start(s32[1032,128]{1,0:T(8,128)S(1)} %finish.4.rest_0_), channel_id=1, source_target_pairs={{0,24},{8,16},{16,8},{24,0},{1,25},{9,17},{17,9},{25,1},{2,26},{10... | collective-permute-start | bytes 1585160 | tf_op jit(solution)/shard_map/ppermute | solution.py:703
  90.9 1.7 %finish.5.rest_0_ = s32[1032,128]{1,0:T(8,128)S(1)} custom-call(s32[1]{0:T(128)} %bitcast.26.dest_ref, f32[2,2,8,16]{3,2,1,0:T(8,128)S(1)} %get-tuple-element.37.layer_ref, f32[8,2,32,2048]{3,2,1,0:T(8,128)S(1)} %march.1.plane_ref, bf16[64,192]{1,0:T(8,128)(2,1)S(1)} %copy-done.4, f32[2,8,32,128]{3,2,1,0:T(8,128)S(1)} %copy-done.2, ...), custom_call_target="tpu_custom_call" | custom-call | flops 402653184 | bytes 786432 | tf_op jit(solution)/shard_map/finish/pallas_call | solution.py:674
  92.6 1.1 collective-permute-start.14
  93.8 1.7 %finish.6.rest_0_ = s32[1032,128]{1,0:T(8,128)S(1)} custom-call(s32[1]{0:T(128)} %bitcast.1.dest_ref, f32[2,2,8,16]{3,2,1,0:T(8,128)S(1)} %get-tuple-element.37.layer_ref, f32[8,2,32,2048]{3,2,1,0:T(8,128)S(1)} %march.1.plane_ref, bf16[64,192]{1,0:T(8,128)(2,1)S(1)} %copy-done.4, f32[2,8,32,128]{3,2,1,0:T(8,128)S(1)} %copy-done.2, s32[1032,128]{1,0:T(8,128)S(1)} %finish.5.rest_0_), custom_call_target="tpu_custom_call" | custom-call | flops 402653184 | bytes 786432 | tf_op jit(solution)/shard_map/finish/pallas_call | solution.py:674
  96.5 2.2 %copy-done.1 = f32[8,2,32,2048]{3,2,1,0:T(8,128)S(1)} copy-done((f32[8,2,32,2048]{3,2,1,0:T(8,128)S(1)}, f32[8,2,32,2048]{3,2,1,0:T(8,128)}, u32[]{:S(2)}) %copy-start.1) | copy-done | bytes 4194328
  98.6 1.7 %finish.7.code_ref = s32[1032,128]{1,0:T(8,128)S(1)} custom-call(s32[1]{0:T(128)} %bitcast.30.dest_ref, f32[2,2,8,16]{3,2,1,0:T(8,128)S(1)} %get-tuple-element.37.layer_ref, f32[8,2,32,2048]{3,2,1,0:T(8,128)S(1)} %copy-done.1, bf16[64,192]{1,0:T(8,128)(2,1)S(1)} %copy-done.4, f32[2,8,32,128]{3,2,1,0:T(8,128)S(1)} %copy-done.2, s32[1032,128]{1,0:T(8,128)S(1)} %finish.6.rest_0_), custom_call_target="tpu_custom_call" | custom-call | flops 402653184 | bytes 786432 | tf_op jit(solution)/shard_map/finish/pallas_call | solution.py:674
  101.4 3.9 %collective-permute-done.15.code_ref = s32[1032,128]{1,0:T(8,128)S(1)} collective-permute-done((s32[1032,128]{1,0:T(8,128)S(1)}, s32[1032,128]{1,0:T(8,128)S(1)}, u32[]{:S(2)}, u32[]{:S(2)}) %collective-permute-start.15) | collective-permute-done | bytes 528416 | tf_op jit(solution)/shard_map/ppermute | solution.py:703
  106.3 8.5 %collective-permute-done.14.code_ref = s32[1032,128]{1,0:T(8,128)S(1)} collective-permute-done((s32[1032,128]{1,0:T(8,128)S(1)}, s32[1032,128]{1,0:T(8,128)S(1)}, u32[]{:S(2)}, u32[]{:S(2)}) %collective-permute-start.14) | collective-permute-done | bytes 528416 | tf_op jit(solution)/shard_map/ppermute | solution.py:703
  (97 shorter events, 17.7 us)
Async XLA Ops:
  2.9 26.9 %collective-permute-start.3 = (bf16[8,128,128]{2,1,0:T(8,128)(2,1)S(1)}, bf16[8,128,128]{2,1,0:T(8,128)(2,1)S(1)}, u32[]{:S(2)}, u32[]{:S(2)}) collective-permute-start(bf16[8,128,128]{2,1,0:T(8,128)(2,1)S(1)} %take_own.1.rest_0_), channel_id=1, source_target_pairs={{0,2},{1,3},{2,0},{3,1},{4,6},{5,7},{6,4},{7,5},{8,10},{9,11},{10,... | collective-permute-start | bytes 786440 | tf_op jit(solution)/shard_map/ppermute | solution.py:559
  6.0 14.4 %collective-permute-start.4 = (bf16[8,128,128]{2,1,0:T(8,128)(2,1)S(1)}, bf16[8,128,128]{2,1,0:T(8,128)(2,1)S(1)}, u32[]{:S(2)}, u32[]{:S(2)}) collective-permute-start(bf16[8,128,128]{2,1,0:T(8,128)(2,1)S(1)} %take_own.1.rest_0_), channel_id=1, source_target_pairs={{0,4},{1,5},{2,6},{3,7},{4,0},{5,1},{6,2},{7,3},{8,12},{9,13},{10,... | collective-permute-start | bytes 786440 | tf_op jit(solution)/shard_map/ppermute | solution.py:559
  11.6 31.8 %copy-start.10 = (f32[2,16]{1,0:T(2,128)S(1)}, f32[2,16]{1,0:T(2,128)}, u32[]{:S(2)}) copy-start(f32[2,16]{1,0:T(2,128)} %slow_ref.1) | copy-start | bytes 388
  12.3 12.2 %all-to-all-start = ((bf16[3,8,8,512]{3,2,0,1:T(8,128)(2,1)}), bf16[3,8,8,512]{3,2,0,1:T(8,128)(2,1)S(1)}, u32[]{:S(2)}, u32[]{:S(2)}) async-start(bf16[3,8,8,512]{3,2,0,1:T(8,128)(2,1)} %copy.46), calls=%async_computation | async-start | bytes 393216 | tf_op jit(solution)/shard_map/all_to_all | solution.py:578
  20.4 14.0 %collective-permute-start.5 = (bf16[8,128,128]{2,1,0:T(8,128)(2,1)S(1)}, bf16[8,128,128]{2,1,0:T(8,128)(2,1)S(1)}, u32[]{:S(2)}, u32[]{:S(2)}) collective-permute-start(bf16[8,128,128]{2,1,0:T(8,128)(2,1)S(1)} %collective-permute-done.4.rest_2_), channel_id=1, source_target_pairs={{0,2},{1,3},{2,0},{3,1},{4,6},{5,7},{6,4},{7,5},{8,10},{9,11},{10,... | collective-permute-start | bytes 786440 | tf_op jit(solution)/shard_map/ppermute | solution.py:559
  24.6 7.0 %collective-permute-start.2 = (bf16[17,8,512]{2,1,0:T(8,128)(2,1)S(1)}, bf16[17,8,512]{2,1,0:T(8,128)(2,1)S(1)}, u32[]{:S(2)}, u32[]{:S(2)}) collective-permute-start(bf16[17,8,512]{2,1,0:T(8,128)(2,1)S(1)} %get-tuple-element.48), channel_id=1, source_target_pairs={{0,24},{8,16},{16,8},{24,0},{1,25},{9,17},{17,9},{25,1},{2,26},{10... | collective-permute-start | bytes 417800 | tf_op jit(solution)/shard_map/ppermute | solution.py:585
  27.1 7.1 %collective-permute-start.1 = (bf16[17,8,512]{2,1,0:T(8,128)(2,1)S(1)}, bf16[17,8,512]{2,1,0:T(8,128)(2,1)S(1)}, u32[]{:S(2)}, u32[]{:S(2)}) collective-permute-start(bf16[17,8,512]{2,1,0:T(8,128)(2,1)S(1)} %get-tuple-element.48), channel_id=1, source_target_pairs={{0,16},{8,24},{16,0},{24,8},{1,17},{9,25},{17,1},{25,9},{2,18},{10... | collective-permute-start | bytes 417800 | tf_op jit(solution)/shard_map/ppermute | solution.py:585
  27.6 6.6 %collective-permute-start = (bf16[17,8,512]{2,1,0:T(8,128)(2,1)S(1)}, bf16[17,8,512]{2,1,0:T(8,128)(2,1)S(1)}, u32[]{:S(2)}, u32[]{:S(2)}) collective-permute-start(bf16[17,8,512]{2,1,0:T(8,128)(2,1)S(1)} %get-tuple-element.48), channel_id=1, source_target_pairs={{0,8},{8,0},{16,24},{24,16},{1,9},{9,1},{17,25},{25,17},{2,10},{10... | collective-permute-start | bytes 417800 | tf_op jit(solution)/shard_map/ppermute | solution.py:585
  29.8 5.7 %collective-permute-start.6 = (bf16[8,128,128]{2,1,0:T(8,128)(2,1)S(1)}, bf16[8,128,128]{2,1,0:T(8,128)(2,1)S(1)}, u32[]{:S(2)}, u32[]{:S(2)}) collective-permute-start(bf16[8,128,128]{2,1,0:T(8,128)(2,1)S(1)} %take_own.1.rest_0_), channel_id=1, source_target_pairs={{0,1},{1,0},{2,3},{3,2},{4,5},{5,4},{6,7},{7,6},{8,9},{9,8},{10,11... | collective-permute-start | bytes 786440 | tf_op jit(solution)/shard_map/ppermute | solution.py:566
  31.7 4.1 %collective-permute-start.8 = (bf16[8,128,128]{2,1,0:T(8,128)(2,1)S(1)}, bf16[8,128,128]{2,1,0:T(8,128)(2,1)S(1)}, u32[]{:S(2)}, u32[]{:S(2)}) collective-permute-start(bf16[8,128,128]{2,1,0:T(8,128)(2,1)S(1)} %collective-permute-done.4.rest_2_), channel_id=1, source_target_pairs={{0,1},{1,0},{2,3},{3,2},{4,5},{5,4},{6,7},{7,6},{8,9},{9,8},{10,11... | collective-permute-start | bytes 786440 | tf_op jit(solution)/shard_map/ppermute | solution.py:566
  34.2 1.5 %collective-permute-start.7 = (bf16[8,128,128]{2,1,0:T(8,128)(2,1)S(1)}, bf16[8,128,128]{2,1,0:T(8,128)(2,1)S(1)}, u32[]{:S(2)}, u32[]{:S(2)}) collective-permute-start(bf16[8,128,128]{2,1,0:T(8,128)(2,1)S(1)} %collective-permute-done.3.rest_1_), channel_id=1, source_target_pairs={{0,1},{1,0},{2,3},{3,2},{4,5},{5,4},{6,7},{7,6},{8,9},{9,8},{10,11... | collective-permute-start | bytes 786440 | tf_op jit(solution)/shard_map/ppermute | solution.py:566
  34.4 1.7 %collective-permute-start.9 = (bf16[8,128,128]{2,1,0:T(8,128)(2,1)S(1)}, bf16[8,128,128]{2,1,0:T(8,128)(2,1)S(1)}, u32[]{:S(2)}, u32[]{:S(2)}) collective-permute-start(bf16[8,128,128]{2,1,0:T(8,128)(2,1)S(1)} %collective-permute-done.5.rest_3_), channel_id=1, source_target_pairs={{0,1},{1,0},{2,3},{3,2},{4,5},{5,4},{6,7},{7,6},{8,9},{9,8},{10,11... | collective-permute-start | bytes 786440 | tf_op jit(solution)/shard_map/ppermute | solution.py:566
  39.8 18.9 %collective-permute-start.10 = (s32[5,17,8,128]{3,2,1,0:T(8,128)}, s32[5,17,8,128]{3,2,1,0:T(8,128)S(1)}, u32[]{:S(2)}, u32[]{:S(2)}) collective-permute-start(s32[5,17,8,128]{3,2,1,0:T(8,128)} %get-tuple-element.39), channel_id=1, source_target_pairs={{0,8},{8,0},{16,24},{24,16},{1,9},{9,1},{17,25},{25,17},{2,10},{10... | collective-permute-start | bytes 1044488 | tf_op jit(solution)/shard_map/ppermute | solution.py:635
  41.3 17.7 %collective-permute-start.11 = (s32[5,17,8,128]{3,2,1,0:T(8,128)}, s32[5,17,8,128]{3,2,1,0:T(8,128)S(1)}, u32[]{:S(2)}, u32[]{:S(2)}) collective-permute-start(s32[5,17,8,128]{3,2,1,0:T(8,128)} %get-tuple-element.40), channel_id=1, source_target_pairs={{0,16},{8,24},{16,0},{24,8},{1,17},{9,25},{17,1},{25,9},{2,18},{10... | collective-permute-start | bytes 1044488 | tf_op jit(solution)/shard_map/ppermute | solution.py:635
  42.2 16.9 %collective-permute-start.12 = (s32[5,17,8,128]{3,2,1,0:T(8,128)}, s32[5,17,8,128]{3,2,1,0:T(8,128)S(1)}, u32[]{:S(2)}, u32[]{:S(2)}) collective-permute-start(s32[5,17,8,128]{3,2,1,0:T(8,128)} %get-tuple-element.41), channel_id=1, source_target_pairs={{0,24},{8,16},{16,8},{24,0},{1,25},{9,17},{17,9},{25,1},{2,26},{10... | collective-permute-start | bytes 1044488 | tf_op jit(solution)/shard_map/ppermute | solution.py:635
  43.4 15.7 %copy-start.2 = (f32[2,8,32,128]{3,2,1,0:T(8,128)S(1)}, f32[2,8,32,128]{3,2,1,0:T(8,128)}, u32[]{:S(2)}) copy-start(f32[2,8,32,128]{3,2,1,0:T(8,128)} %constant.139.clone.rest_12_.offset_ref) | copy-start | bytes 786436
  43.4 15.7 %copy-start.4 = (bf16[64,192]{1,0:T(8,128)(2,1)S(1)}, bf16[64,192]{1,0:T(8,128)(2,1)}, u32[]{:S(2)}) copy-start(bf16[64,192]{1,0:T(8,128)(2,1)} %constant.135.clone.rest_8_.rows_inverse) | copy-start | bytes 73732
  43.4 15.7 %copy-start.5 = (bf16[768,256]{1,0:T(8,128)(2,1)S(1)}, bf16[768,256]{1,0:T(8,128)(2,1)}, u32[]{:S(2)}) copy-start(bf16[768,256]{1,0:T(8,128)(2,1)} %constant.136.clone.rest_9_) | copy-start | bytes 1179652
  43.4 15.7 %copy-start.6 = (bf16[768,256]{1,0:T(8,128)(2,1)S(1)}, bf16[768,256]{1,0:T(8,128)(2,1)}, u32[]{:S(2)}) copy-start(bf16[768,256]{1,0:T(8,128)(2,1)} %constant.137.clone.rest_10_) | copy-start | bytes 1179652
  43.4 15.7 %copy-start.7 = (f32[2,16,8,128]{3,2,1,0:T(8,128)S(1)}, f32[2,16,8,128]{3,2,1,0:T(8,128)}, u32[]{:S(2)}) copy-start(f32[2,16,8,128]{3,2,1,0:T(8,128)} %constant.138.clone.rest_11_) | copy-start | bytes 393220
  43.5 15.7 %copy-start.8 = (bf16[64,192]{1,0:T(8,128)(2,1)S(1)}, bf16[64,192]{1,0:T(8,128)(2,1)}, u32[]{:S(2)}) copy-start(bf16[64,192]{1,0:T(8,128)(2,1)} %constant.134.clone.rest_7_) | copy-start | bytes 73732
  89.3 16.0 %collective-permute-start.15 = (s32[1032,128]{1,0:T(8,128)S(1)}, s32[1032,128]{1,0:T(8,128)S(1)}, u32[]{:S(2)}, u32[]{:S(2)}) collective-permute-start(s32[1032,128]{1,0:T(8,128)S(1)} %finish.4.rest_0_), channel_id=1, source_target_pairs={{0,24},{8,16},{16,8},{24,0},{1,25},{9,17},{17,9},{25,1},{2,26},{10... | collective-permute-start | bytes 1585160 | tf_op jit(solution)/shard_map/ppermute | solution.py:703
  92.6 22.2 %collective-permute-start.14 = (s32[1032,128]{1,0:T(8,128)S(1)}, s32[1032,128]{1,0:T(8,128)S(1)}, u32[]{:S(2)}, u32[]{:S(2)}) collective-permute-start(s32[1032,128]{1,0:T(8,128)S(1)} %finish.5.rest_0_), channel_id=1, source_target_pairs={{0,16},{8,24},{16,0},{24,8},{1,17},{9,25},{17,1},{25,9},{2,18},{10... | collective-permute-start | bytes 1585160 | tf_op jit(solution)/shard_map/ppermute | solution.py:703
  95.5 20.3 %collective-permute-start.13 = (s32[1032,128]{1,0:T(8,128)S(1)}, s32[1032,128]{1,0:T(8,128)S(1)}, u32[]{:S(2)}, u32[]{:S(2)}) collective-permute-start(s32[1032,128]{1,0:T(8,128)S(1)} %finish.6.rest_0_), channel_id=1, source_target_pairs={{0,8},{8,0},{16,24},{24,16},{1,9},{9,1},{17,25},{25,17},{2,10},{10... | collective-permute-start | bytes 1585160 | tf_op jit(solution)/shard_map/ppermute | solution.py:703
  (4 other events, 10.2 us)

commit v10 on v7

--- a/solution.py
+++ b/solution.py
@@ -63,7 +63,7 @@
     for axis, pair in ((1, (upper, lower)), (0, (lower, upper))):
         for table in pair:
             high, low = halves_np(table)
-            tables.append(np.concatenate([high, high, low], axis=axis))
+            tables.append(np.concatenate([high, high, low], axis=axis).astype(np.float32))
     return tables
 
 
@@ -77,8 +77,9 @@
 
 
 def halves(value):
-    high = value.astype(jnp.bfloat16)
-    return high, (value - high.astype(jnp.float32)).astype(jnp.bfloat16)
+    wide = value * 65537.0
+    high = wide - (wide - value)
+    return high, value - high
 
 
 def dot(left, right):
@@ -602,7 +603,7 @@
     pick = (
         jnp.tile(goal.reshape(1, fl * room), (1, 2))
         == lax.broadcasted_iota(jnp.int32, (NH, 2 * fl * room), 0)
-    ).astype(jnp.bfloat16)
+    ).astype(jnp.float32)
     own_slots = lax.dynamic_index_in_dim(slots, mine, 0, False)
     own_bins = lax.dynamic_index_in_dim(bins, mine, 0, False)
     list_groups = room // GROUP
@@ -656,9 +657,9 @@
         scratch_shapes=[
             pltpu.VMEM((2, 2, HALF, total_mid), jnp.float32),
             pltpu.VMEM((fl * room, BLK), jnp.float32),
-            *[pltpu.VMEM((2 * NH, 2 * BLK), jnp.bfloat16)] * 4,
-            *[pltpu.VMEM((ROWS * CHUNKS * outer, 4 * BLK), jnp.bfloat16)] * 4,
-            *[pltpu.VMEM((2 * fl * room, 2 * BLK), jnp.bfloat16)] * 2,
+            *[pltpu.VMEM((2 * NH, 2 * BLK), jnp.float32)] * 4,
+            *[pltpu.VMEM((ROWS * CHUNKS * outer, 4 * BLK), jnp.float32)] * 4,
+            *[pltpu.VMEM((2 * fl * room, 2 * BLK), jnp.float32)] * 2,
         ],
         compiler_params=pltpu.CompilerParams(vmem_limit_bytes=VMEM),
         name="march",
@@ -678,7 +679,7 @@
                 ]
                 + [hbm] * len(before),
                 out_specs=pl.BlockSpec((rows_out, BLK), lambda i, dest: (0, 0)),
-                scratch_shapes=[pltpu.VMEM((2 * NH, 2 * mid_local), jnp.bfloat16)],
+                scratch_shapes=[pltpu.VMEM((2 * NH, 2 * mid_local), jnp.float32)],
             ),
             out_shape=jax.ShapeDtypeStruct((rows_out, BLK), jnp.int32),
             cost_estimate=pl.CostEstimate(

time: 116 us -> 119 us (1.026)
  Pallas kernels: 58.7 us -> 61.1 us
    pallas_call x1, Pallas kernels: 26.8 us -> 28.1 us  [local(): pl.pallas_call(functools.partial(march_kernel, sources=fl), in_specs=[sme...]
    unnamed x22 -> x28, local copies, waits for them, and re-layouts: 4.11 us -> 4.18 us
  transfers between devices with their start and end apart: 17 -> 17, of which waited for: 10 -> 8; matrix products, arithmetic and copies ran while one was open for 6% -> 7% of each run, Pallas kernels for 21% -> 22%
where the time goes in v10:
time: 119 us; the launch traced here: 118 us
  Pallas kernels  61.1 us (51%)
  starting transfers between devices  23.4 us (20%)
  waiting for transfers between devices  21 us (18%)
  local copies, waits for them, and re-layouts  7.81 us (7%)
  other arithmetic  4.36 us (4%)
    pallas_call x1, Pallas kernels, local(): pl.pallas_call(functools.partial(march_kernel, sources=fl), in_specs=[sme...  28.1 us
    pallas_call x1, Pallas kernels, local(): pl.pallas_call(propagator_kernel, in_specs=[smem, smem, vmem], out_specs=...  15.2 us
    ppermute x3, waiting for transfers between devices, local(): lax.ppermute(block, 'mid', [(s, s ^ ahead) for s in range(mid_count)])  11.6 us
    ppermute x3, starting transfers between devices, local(): lax.ppermute(shares[away ^ low], 'off', [(i, (i // cores ^ low) * cores +...  8.49 us
    pallas_call x4, Pallas kernels, finish(): pl.pallas_call(finish_kernel, grid_spec=pltpu.PrefetchScalarGridSpec(num_...  6.88 us
    pallas_call x4, Pallas kernels, local(): pl.pallas_call(result_kernel, grid_spec=pltpu.PrefetchScalarGridSpec(num_...  6.23 us
    ppermute x3, waiting for transfers between devices, local(): lax.ppermute(data, 'mid', [(i, i ^ away) for i in range(mid_count)])  4.22 us
    unnamed x28, local copies, waits for them, and re-layouts  4.18 us
  transfers between devices with their start and end apart: 17, of which 8 were waited for; matrix products, arithmetic and copies ran while one was open for 7% of the time, Pallas kernels for 22%

profile of v10, /device:TPU:0, one launch (start us, length us, event | category | flops | bytes accessed | tf_op | source)
XLA Modules:
  0.0 118.1 jit_solution(16504781745693696902)
XLA Ops:
  0.0 1.2 %copy-done.4 = bf16[2,16,128,128]{3,2,1,0:T(8,128)(2,1)S(1)} copy-done((bf16[2,16,128,128]{3,2,1,0:T(8,128)(2,1)S(1)}, bf16[2,16,128,128]{3,2,1,0:T(8,128)(2,1)}, u32[]{:S(2)}) %copy-start.4) | copy-done | bytes 1048600
  2.9 3.1 %collective-permute-start.3 = (bf16[8,128,128]{2,1,0:T(8,128)(2,1)S(1)}, bf16[8,128,128]{2,1,0:T(8,128)(2,1)S(1)}, u32[]{:S(2)}, u32[]{:S(2)}) collective-permute-start(bf16[8,128,128]{2,1,0:T(8,128)(2,1)S(1)} %take_own.1.rest_0_), channel_id=1, source_target_pairs={{0,2},{1,3},{2,0},{3,1},{4,6},{5,7},{6,4},{7,5},{8,10},{9,11},{10,... | collective-permute-start | bytes 786440 | tf_op jit(solution)/shard_map/ppermute | solution.py:553
  6.0 2.6 %collective-permute-start.4 = (bf16[8,128,128]{2,1,0:T(8,128)(2,1)S(1)}, bf16[8,128,128]{2,1,0:T(8,128)(2,1)S(1)}, u32[]{:S(2)}, u32[]{:S(2)}) collective-permute-start(bf16[8,128,128]{2,1,0:T(8,128)(2,1)S(1)} %take_own.1.rest_0_), channel_id=1, source_target_pairs={{0,4},{1,5},{2,6},{3,7},{4,0},{5,1},{6,2},{7,3},{8,12},{9,13},{10,... | collective-permute-start | bytes 786440 | tf_op jit(solution)/shard_map/ppermute | solution.py:553
  12.4 3.5 %all-to-all-start = ((bf16[3,8,8,512]{3,2,0,1:T(8,128)(2,1)}), bf16[3,8,8,512]{3,2,0,1:T(8,128)(2,1)S(1)}, u32[]{:S(2)}, u32[]{:S(2)}) async-start(bf16[3,8,8,512]{3,2,0,1:T(8,128)(2,1)} %copy.46), calls=%async_computation | async-start | bytes 393216 | tf_op jit(solution)/shard_map/all_to_all | solution.py:572
  17.1 3.2 %collective-permute-done.4.rest_2_ = bf16[8,128,128]{2,1,0:T(8,128)(2,1)S(1)} collective-permute-done((bf16[8,128,128]{2,1,0:T(8,128)(2,1)S(1)}, bf16[8,128,128]{2,1,0:T(8,128)(2,1)S(1)}, u32[]{:S(2)}, u32[]{:S(2)}) %collective-permute-start.4) | collective-permute-done | bytes 262176 | tf_op jit(solution)/shard_map/ppermute | solution.py:553
  20.4 2.8 %collective-permute-start.5 = (bf16[8,128,128]{2,1,0:T(8,128)(2,1)S(1)}, bf16[8,128,128]{2,1,0:T(8,128)(2,1)S(1)}, u32[]{:S(2)}, u32[]{:S(2)}) collective-permute-start(bf16[8,128,128]{2,1,0:T(8,128)(2,1)S(1)} %collective-permute-done.4.rest_2_), channel_id=1, source_target_pairs={{0,2},{1,3},{2,0},{3,1},{4,6},{5,7},{6,4},{7,5},{8,10},{9,11},{10,... | collective-permute-start | bytes 786440 | tf_op jit(solution)/shard_map/ppermute | solution.py:553
  23.2 1.4 %all-to-all-done = bf16[3,8,8,512]{3,2,0,1:T(8,128)(2,1)S(1)} async-done(((bf16[3,8,8,512]{3,2,0,1:T(8,128)(2,1)}), bf16[3,8,8,512]{3,2,0,1:T(8,128)(2,1)S(1)}, u32[]{:S(2)}, u32[]{:S(2)}) %all-to-all-start) | async-done | bytes 196640 | tf_op jit(solution)/shard_map/all_to_all | solution.py:572
  24.6 2.5 %collective-permute-start.2 = (bf16[17,8,512]{2,1,0:T(8,128)(2,1)S(1)}, bf16[17,8,512]{2,1,0:T(8,128)(2,1)S(1)}, u32[]{:S(2)}, u32[]{:S(2)}) collective-permute-start(bf16[17,8,512]{2,1,0:T(8,128)(2,1)S(1)} %get-tuple-element.48), channel_id=1, source_target_pairs={{0,24},{8,16},{16,8},{24,0},{1,25},{9,17},{17,9},{25,1},{2,26},{10... | collective-permute-start | bytes 417800 | tf_op jit(solution)/shard_map/ppermute | solution.py:580
  29.9 1.7 %collective-permute-done.2 = bf16[17,8,512]{2,1,0:T(8,128)(2,1)S(1)} collective-permute-done((bf16[17,8,512]{2,1,0:T(8,128)(2,1)S(1)}, bf16[17,8,512]{2,1,0:T(8,128)(2,1)S(1)}, u32[]{:S(2)}, u32[]{:S(2)}) %collective-permute-start.2) | collective-permute-done | bytes 139296 | tf_op jit(solution)/shard_map/ppermute | solution.py:580
  31.5 2.5 %collective-permute-done.1 = bf16[17,8,512]{2,1,0:T(8,128)(2,1)S(1)} collective-permute-done((bf16[17,8,512]{2,1,0:T(8,128)(2,1)S(1)}, bf16[17,8,512]{2,1,0:T(8,128)(2,1)S(1)}, u32[]{:S(2)}, u32[]{:S(2)}) %collective-permute-start.1) | collective-permute-done | bytes 139296 | tf_op jit(solution)/shard_map/ppermute | solution.py:580
  36.1 3.7 %contributions.1 = (s32[5,17,8,128]{3,2,1,0:T(8,128)S(1)}, s32[5,17,8,128]{3,2,1,0:T(8,128)}, s32[5,17,8,128]{3,2,1,0:T(8,128)}, s32[5,17,8,128]{3,2,1,0:T(8,128)}) custom-call(s32[1]{0:T(128)} %bitcast.2.mine_ref.place_ref.freq_ref, s32[16]{0:T(128)S(1)} %add.116.order_ref, s32[40]{0:T(128)S(1)} %get-tuple-element.27.slot_ref, ...), custom_call_target="tpu_custom_call" | custom-call | tf_op jit(solution)/shard_map/contributions/pallas_call | solution.py:614
  39.8 1.6 %collective-permute-start.10 = (s32[5,17,8,128]{3,2,1,0:T(8,128)}, s32[5,17,8,128]{3,2,1,0:T(8,128)S(1)}, u32[]{:S(2)}, u32[]{:S(2)}) collective-permute-start(s32[5,17,8,128]{3,2,1,0:T(8,128)} %get-tuple-element.39), channel_id=1, source_target_pairs={{0,8},{8,0},{16,24},{24,16},{1,9},{9,1},{17,25},{25,17},{2,10},{10... | collective-permute-start | bytes 1044488 | tf_op jit(solution)/shard_map/ppermute | solution.py:630
  43.5 15.2 %propagator.1 = (f32[256,2048]{1,0:T(8,128)S(1)}, f32[256,2048]{1,0:T(8,128)S(1)}, f32[2,2,8,16]{3,2,1,0:T(8,128)S(1)}) custom-call(f32[1]{0:T(128)} %bitcast.25.omega_ref, f32[2,16]{1,0:T(2,128)S(1)} %copy-done.10, s32[2,8,16]{2,1,0:T(8,128)S(1)} %copy.50.layers_ref), custom_call_target="tpu_custom_call" | custom-call | flops 31457280 | bytes 4194304 | tf_op jit(solution)/shard_map/propagator/pallas_call | solution.py:634
  59.4 28.1 %march.1.plane_ref = f32[2,2,128,2048]{3,2,1,0:T(8,128)S(1)} custom-call(f32[2,2,8,16]{3,2,1,0:T(8,128)S(1)} %get-tuple-element.37.layer_ref, s32[5,17,8,128]{3,2,1,0:T(8,128)S(1)} %get-tuple-element.38.rest_0_, s32[5,17,8,128]{3,2,1,0:T(8,128)S(1)} %collective-permute-done.10.rest_1_, s32[5,17,8,128]{3,2,1,0:T(8,128)S(1)} %collective-permute-done.11.rest_2_, ...), custom_call_target="tpu_custom_call" | custom-call | tf_op jit(solution)/shard_map/march/pallas_call | solution.py:652
  87.5 1.7 %finish.4.rest_0_ = s32[1032,128]{1,0:T(8,128)S(1)} custom-call(s32[1]{0:T(128)} %bitcast.27.dest_ref, f32[2,2,8,16]{3,2,1,0:T(8,128)S(1)} %get-tuple-element.37.layer_ref, f32[2,2,128,2048]{3,2,1,0:T(8,128)S(1)} %march.1.plane_ref, f32[256,768]{1,0:T(8,128)S(1)} %copy-done.2, f32[2,128,128]{2,1,0:T(8,128)S(1)} %copy-done.3), custom_call_target="tpu_custom_call" | custom-call | flops 402653184 | bytes 786432 | tf_op jit(solution)/shard_map/finish/pallas_call | solution.py:669
  89.2 1.5 %collective-permute-start.15 = (s32[1032,128]{1,0:T(8,128)S(1)}, s32[1032,128]{1,0:T(8,128)}, u32[]{:S(2)}, u32[]{:S(2)}) collective-permute-start(s32[1032,128]{1,0:T(8,128)S(1)} %finish.4.rest_0_), channel_id=1, source_target_pairs={{0,24},{8,16},{16,8},{24,0},{1,25},{9,17},{17,9},{25,1},{2,26},{10... | collective-permute-start | bytes 1585160 | tf_op jit(solution)/shard_map/ppermute | solution.py:698
  90.7 1.7 %finish.5.rest_0_ = s32[1032,128]{1,0:T(8,128)S(1)} custom-call(s32[1]{0:T(128)} %bitcast.26.dest_ref, f32[2,2,8,16]{3,2,1,0:T(8,128)S(1)} %get-tuple-element.37.layer_ref, f32[2,2,128,2048]{3,2,1,0:T(8,128)S(1)} %march.1.plane_ref, f32[256,768]{1,0:T(8,128)S(1)} %copy-done.2, f32[2,128,128]{2,1,0:T(8,128)S(1)} %copy-done.3, s32[1032,128]{1,0:T(8,128)S(1)} %finish.4.rest_0_), custom_call_target="tpu_custom_call" | custom-call | flops 402653184 | bytes 786432 | tf_op jit(solution)/shard_map/finish/pallas_call | solution.py:669
  93.5 1.7 %finish.6.rest_0_ = s32[1032,128]{1,0:T(8,128)S(1)} custom-call(s32[1]{0:T(128)} %bitcast.1.dest_ref, f32[2,2,8,16]{3,2,1,0:T(8,128)S(1)} %get-tuple-element.37.layer_ref, f32[2,2,128,2048]{3,2,1,0:T(8,128)S(1)} %march.1.plane_ref, f32[256,768]{1,0:T(8,128)S(1)} %copy-done.2, f32[2,128,128]{2,1,0:T(8,128)S(1)} %copy-done.3, s32[1032,128]{1,0:T(8,128)S(1)} %finish.5.rest_0_), custom_call_target="tpu_custom_call" | custom-call | flops 402653184 | bytes 786432 | tf_op jit(solution)/shard_map/finish/pallas_call | solution.py:669
  96.3 2.2 %copy-done.1 = f32[2,2,128,2048]{3,2,1,0:T(8,128)S(1)} copy-done((f32[2,2,128,2048]{3,2,1,0:T(8,128)S(1)}, f32[2,2,128,2048]{3,2,1,0:T(8,128)}, u32[]{:S(2)}) %copy-start.1) | copy-done | bytes 4194328
  98.5 1.7 %finish.7.code_ref = s32[1032,128]{1,0:T(8,128)S(1)} custom-call(s32[1]{0:T(128)} %bitcast.30.dest_ref, f32[2,2,8,16]{3,2,1,0:T(8,128)S(1)} %get-tuple-element.37.layer_ref, f32[2,2,128,2048]{3,2,1,0:T(8,128)S(1)} %copy-done.1, f32[256,768]{1,0:T(8,128)S(1)} %copy-done.2, f32[2,128,128]{2,1,0:T(8,128)S(1)} %copy-done.3, s32[1032,128]{1,0:T(8,128)S(1)} %finish.6.rest_0_), custom_call_target="tpu_custom_call" | custom-call | flops 402653184 | bytes 786432 | tf_op jit(solution)/shard_map/finish/pallas_call | solution.py:669
  101.3 3.9 %collective-permute-done.15.code_ref = s32[1032,128]{1,0:T(8,128)} collective-permute-done((s32[1032,128]{1,0:T(8,128)S(1)}, s32[1032,128]{1,0:T(8,128)}, u32[]{:S(2)}, u32[]{:S(2)}) %collective-permute-start.15) | collective-permute-done | bytes 528416 | tf_op jit(solution)/shard_map/ppermute | solution.py:698
  105.3 2.1 %result.5.rest_0_ = f32[4,256,8,128]{3,2,1,0:T(8,128)} custom-call(s32[1]{0:T(128)} %bitcast.29.freq_ref, s32[1032,128]{1,0:T(8,128)} %collective-permute-done.15.code_ref, f32[4,256,8,128]{3,2,1,0:T(8,128)} %result.4.rest_0_), custom_call_target="tpu_custom_call", output_to_operand_aliasing={{}: (2, {})} | custom-call | flops 524288 | bytes 1572864 | tf_op jit(solution)/shard_map/result/pallas_call | solution.py:705
  107.3 7.6 %collective-permute-done.14.code_ref = s32[1032,128]{1,0:T(8,128)} collective-permute-done((s32[1032,128]{1,0:T(8,128)S(1)}, s32[1032,128]{1,0:T(8,128)}, u32[]{:S(2)}, u32[]{:S(2)}) %collective-permute-start.14) | collective-permute-done | bytes 528416 | tf_op jit(solution)/shard_map/ppermute | solution.py:698
  114.9 2.1 %result.6.rest_0_ = f32[4,256,8,128]{3,2,1,0:T(8,128)} custom-call(s32[1]{0:T(128)} %bitcast.28.freq_ref, s32[1032,128]{1,0:T(8,128)} %collective-permute-done.14.code_ref, f32[4,256,8,128]{3,2,1,0:T(8,128)} %result.5.rest_0_), custom_call_target="tpu_custom_call", output_to_operand_aliasing={{}: (2, {})} | custom-call | flops 524288 | bytes 1572864 | tf_op jit(solution)/shard_map/result/pallas_call | solution.py:705
  (104 shorter events, 18.3 us)
Async XLA Ops:
  2.9 26.9 %collective-permute-start.3 = (bf16[8,128,128]{2,1,0:T(8,128)(2,1)S(1)}, bf16[8,128,128]{2,1,0:T(8,128)(2,1)S(1)}, u32[]{:S(2)}, u32[]{:S(2)}) collective-permute-start(bf16[8,128,128]{2,1,0:T(8,128)(2,1)S(1)} %take_own.1.rest_0_), channel_id=1, source_target_pairs={{0,2},{1,3},{2,0},{3,1},{4,6},{5,7},{6,4},{7,5},{8,10},{9,11},{10,... | collective-permute-start | bytes 786440 | tf_op jit(solution)/shard_map/ppermute | solution.py:553
  6.0 14.4 %collective-permute-start.4 = (bf16[8,128,128]{2,1,0:T(8,128)(2,1)S(1)}, bf16[8,128,128]{2,1,0:T(8,128)(2,1)S(1)}, u32[]{:S(2)}, u32[]{:S(2)}) collective-permute-start(bf16[8,128,128]{2,1,0:T(8,128)(2,1)S(1)} %take_own.1.rest_0_), channel_id=1, source_target_pairs={{0,4},{1,5},{2,6},{3,7},{4,0},{5,1},{6,2},{7,3},{8,12},{9,13},{10,... | collective-permute-start | bytes 786440 | tf_op jit(solution)/shard_map/ppermute | solution.py:553
  12.4 31.1 %copy-start.10 = (f32[2,16]{1,0:T(2,128)S(1)}, f32[2,16]{1,0:T(2,128)}, u32[]{:S(2)}) copy-start(f32[2,16]{1,0:T(2,128)} %slow_ref.1) | copy-start | bytes 388
  12.4 12.2 %all-to-all-start = ((bf16[3,8,8,512]{3,2,0,1:T(8,128)(2,1)}), bf16[3,8,8,512]{3,2,0,1:T(8,128)(2,1)S(1)}, u32[]{:S(2)}, u32[]{:S(2)}) async-start(bf16[3,8,8,512]{3,2,0,1:T(8,128)(2,1)} %copy.46), calls=%async_computation | async-start | bytes 393216 | tf_op jit(solution)/shard_map/all_to_all | solution.py:572
  20.4 13.8 %collective-permute-start.5 = (bf16[8,128,128]{2,1,0:T(8,128)(2,1)S(1)}, bf16[8,128,128]{2,1,0:T(8,128)(2,1)S(1)}, u32[]{:S(2)}, u32[]{:S(2)}) collective-permute-start(bf16[8,128,128]{2,1,0:T(8,128)(2,1)S(1)} %collective-permute-done.4.rest_2_), channel_id=1, source_target_pairs={{0,2},{1,3},{2,0},{3,1},{4,6},{5,7},{6,4},{7,5},{8,10},{9,11},{10,... | collective-permute-start | bytes 786440 | tf_op jit(solution)/shard_map/ppermute | solution.py:553
  24.6 6.9 %collective-permute-start.2 = (bf16[17,8,512]{2,1,0:T(8,128)(2,1)S(1)}, bf16[17,8,512]{2,1,0:T(8,128)(2,1)S(1)}, u32[]{:S(2)}, u32[]{:S(2)}) collective-permute-start(bf16[17,8,512]{2,1,0:T(8,128)(2,1)S(1)} %get-tuple-element.48), channel_id=1, source_target_pairs={{0,24},{8,16},{16,8},{24,0},{1,25},{9,17},{17,9},{25,1},{2,26},{10... | collective-permute-start | bytes 417800 | tf_op jit(solution)/shard_map/ppermute | solution.py:580
  27.1 6.9 %collective-permute-start.1 = (bf16[17,8,512]{2,1,0:T(8,128)(2,1)S(1)}, bf16[17,8,512]{2,1,0:T(8,128)(2,1)S(1)}, u32[]{:S(2)}, u32[]{:S(2)}) collective-permute-start(bf16[17,8,512]{2,1,0:T(8,128)(2,1)S(1)} %get-tuple-element.48), channel_id=1, source_target_pairs={{0,16},{8,24},{16,0},{24,8},{1,17},{9,25},{17,1},{25,9},{2,18},{10... | collective-permute-start | bytes 417800 | tf_op jit(solution)/shard_map/ppermute | solution.py:580
  27.6 6.5 %collective-permute-start = (bf16[17,8,512]{2,1,0:T(8,128)(2,1)S(1)}, bf16[17,8,512]{2,1,0:T(8,128)(2,1)S(1)}, u32[]{:S(2)}, u32[]{:S(2)}) collective-permute-start(bf16[17,8,512]{2,1,0:T(8,128)(2,1)S(1)} %get-tuple-element.48), channel_id=1, source_target_pairs={{0,8},{8,0},{16,24},{24,16},{1,9},{9,1},{17,25},{25,17},{2,10},{10... | collective-permute-start | bytes 417800 | tf_op jit(solution)/shard_map/ppermute | solution.py:580
  29.8 6.3 %collective-permute-start.6 = (bf16[8,128,128]{2,1,0:T(8,128)(2,1)S(1)}, bf16[8,128,128]{2,1,0:T(8,128)(2,1)S(1)}, u32[]{:S(2)}, u32[]{:S(2)}) collective-permute-start(bf16[8,128,128]{2,1,0:T(8,128)(2,1)S(1)} %take_own.1.rest_0_), channel_id=1, source_target_pairs={{0,1},{1,0},{2,3},{3,2},{4,5},{5,4},{6,7},{7,6},{8,9},{9,8},{10,11... | collective-permute-start | bytes 786440 | tf_op jit(solution)/shard_map/ppermute | solution.py:560
  31.5 4.6 %collective-permute-start.8 = (bf16[8,128,128]{2,1,0:T(8,128)(2,1)S(1)}, bf16[8,128,128]{2,1,0:T(8,128)(2,1)S(1)}, u32[]{:S(2)}, u32[]{:S(2)}) collective-permute-start(bf16[8,128,128]{2,1,0:T(8,128)(2,1)S(1)} %collective-permute-done.4.rest_2_), channel_id=1, source_target_pairs={{0,1},{1,0},{2,3},{3,2},{4,5},{5,4},{6,7},{7,6},{8,9},{9,8},{10,11... | collective-permute-start | bytes 786440 | tf_op jit(solution)/shard_map/ppermute | solution.py:560
  34.1 2.1 %collective-permute-start.7 = (bf16[8,128,128]{2,1,0:T(8,128)(2,1)S(1)}, bf16[8,128,128]{2,1,0:T(8,128)(2,1)S(1)}, u32[]{:S(2)}, u32[]{:S(2)}) collective-permute-start(bf16[8,128,128]{2,1,0:T(8,128)(2,1)S(1)} %collective-permute-done.3.rest_1_), channel_id=1, source_target_pairs={{0,1},{1,0},{2,3},{3,2},{4,5},{5,4},{6,7},{7,6},{8,9},{9,8},{10,11... | collective-permute-start | bytes 786440 | tf_op jit(solution)/shard_map/ppermute | solution.py:560
  34.2 1.9 %collective-permute-start.9 = (bf16[8,128,128]{2,1,0:T(8,128)(2,1)S(1)}, bf16[8,128,128]{2,1,0:T(8,128)(2,1)S(1)}, u32[]{:S(2)}, u32[]{:S(2)}) collective-permute-start(bf16[8,128,128]{2,1,0:T(8,128)(2,1)S(1)} %collective-permute-done.5.rest_3_), channel_id=1, source_target_pairs={{0,1},{1,0},{2,3},{3,2},{4,5},{5,4},{6,7},{7,6},{8,9},{9,8},{10,11... | collective-permute-start | bytes 786440 | tf_op jit(solution)/shard_map/ppermute | solution.py:560
  39.8 18.9 %collective-permute-start.10 = (s32[5,17,8,128]{3,2,1,0:T(8,128)}, s32[5,17,8,128]{3,2,1,0:T(8,128)S(1)}, u32[]{:S(2)}, u32[]{:S(2)}) collective-permute-start(s32[5,17,8,128]{3,2,1,0:T(8,128)} %get-tuple-element.39), channel_id=1, source_target_pairs={{0,8},{8,0},{16,24},{24,16},{1,9},{9,1},{17,25},{25,17},{2,10},{10... | collective-permute-start | bytes 1044488 | tf_op jit(solution)/shard_map/ppermute | solution.py:630
  41.4 17.9 %collective-permute-start.11 = (s32[5,17,8,128]{3,2,1,0:T(8,128)}, s32[5,17,8,128]{3,2,1,0:T(8,128)S(1)}, u32[]{:S(2)}, u32[]{:S(2)}) collective-permute-start(s32[5,17,8,128]{3,2,1,0:T(8,128)} %get-tuple-element.40), channel_id=1, source_target_pairs={{0,16},{8,24},{16,0},{24,8},{1,17},{9,25},{17,1},{25,9},{2,18},{10... | collective-permute-start | bytes 1044488 | tf_op jit(solution)/shard_map/ppermute | solution.py:630
  42.2 17.1 %collective-permute-start.12 = (s32[5,17,8,128]{3,2,1,0:T(8,128)}, s32[5,17,8,128]{3,2,1,0:T(8,128)S(1)}, u32[]{:S(2)}, u32[]{:S(2)}) collective-permute-start(s32[5,17,8,128]{3,2,1,0:T(8,128)} %get-tuple-element.41), channel_id=1, source_target_pairs={{0,24},{8,16},{16,8},{24,0},{1,25},{9,17},{17,9},{25,1},{2,26},{10... | collective-permute-start | bytes 1044488 | tf_op jit(solution)/shard_map/ppermute | solution.py:630
  43.5 15.8 %copy-start.2 = (f32[256,768]{1,0:T(8,128)S(1)}, f32[256,768]{1,0:T(8,128)}, u32[]{:S(2)}) copy-start(f32[256,768]{1,0:T(8,128)} %constant.135.clone.rest_8_.rows_inverse) | copy-start | bytes 2359300
  43.5 15.8 %copy-start.3 = (f32[2,128,128]{2,1,0:T(8,128)S(1)}, f32[2,128,128]{2,1,0:T(8,128)}, u32[]{:S(2)}) copy-start(f32[2,128,128]{2,1,0:T(8,128)} %constant.139.clone.rest_12_.offset_ref) | copy-start | bytes 393220
  43.5 15.8 %copy-start.5 = (f32[256,768]{1,0:T(8,128)S(1)}, f32[256,768]{1,0:T(8,128)}, u32[]{:S(2)}) copy-start(f32[256,768]{1,0:T(8,128)} %constant.134.clone.rest_7_) | copy-start | bytes 2359300
  43.5 15.8 %copy-start.6 = (f32[768,256]{1,0:T(8,128)S(1)}, f32[768,256]{1,0:T(8,128)}, u32[]{:S(2)}) copy-start(f32[768,256]{1,0:T(8,128)} %constant.136.clone.rest_9_) | copy-start | bytes 2359300
  43.5 15.8 %copy-start.7 = (f32[768,256]{1,0:T(8,128)S(1)}, f32[768,256]{1,0:T(8,128)}, u32[]{:S(2)}) copy-start(f32[768,256]{1,0:T(8,128)} %constant.137.clone.rest_10_) | copy-start | bytes 2359300
  43.5 15.8 %copy-start.8 = (f32[2,16,128]{2,1,0:T(8,128)S(1)}, f32[2,16,128]{2,1,0:T(8,128)}, u32[]{:S(2)}) copy-start(f32[2,16,128]{2,1,0:T(8,128)} %constant.138.clone.rest_11_) | copy-start | bytes 49156
  89.2 16.1 %collective-permute-start.15 = (s32[1032,128]{1,0:T(8,128)S(1)}, s32[1032,128]{1,0:T(8,128)}, u32[]{:S(2)}, u32[]{:S(2)}) collective-permute-start(s32[1032,128]{1,0:T(8,128)S(1)} %finish.4.rest_0_), channel_id=1, source_target_pairs={{0,24},{8,16},{16,8},{24,0},{1,25},{9,17},{17,9},{25,1},{2,26},{10... | collective-permute-start | bytes 1585160 | tf_op jit(solution)/shard_map/ppermute | solution.py:698
  92.5 22.5 %collective-permute-start.14 = (s32[1032,128]{1,0:T(8,128)S(1)}, s32[1032,128]{1,0:T(8,128)}, u32[]{:S(2)}, u32[]{:S(2)}) collective-permute-start(s32[1032,128]{1,0:T(8,128)S(1)} %finish.5.rest_0_), channel_id=1, source_target_pairs={{0,16},{8,24},{16,0},{24,8},{1,17},{9,25},{17,1},{25,9},{2,18},{10... | collective-permute-start | bytes 1585160 | tf_op jit(solution)/shard_map/ppermute | solution.py:698
  95.2 21.8 %collective-permute-start.13 = (s32[1032,128]{1,0:T(8,128)S(1)}, s32[1032,128]{1,0:T(8,128)S(1)}, u32[]{:S(2)}, u32[]{:S(2)}) collective-permute-start(s32[1032,128]{1,0:T(8,128)S(1)} %finish.6.rest_0_), channel_id=1, source_target_pairs={{0,8},{8,0},{16,24},{24,16},{1,9},{9,1},{17,25},{25,17},{2,10},{10... | collective-permute-start | bytes 1585160 | tf_op jit(solution)/shard_map/ppermute | solution.py:698
  (7 other events, 14.1 us)

commit v11 on v6

--- a/solution.py
+++ b/solution.py
@@ -235,7 +235,17 @@
     )
 
 
-def propagator_kernel(omega_ref, real_ref, imag_ref):
+def propagator_kernel(omega_ref, slow_ref, layers_ref, real_ref, imag_ref, turns_ref):
+    steps, layer_total = slow_ref.shape
+    for step in range(steps):
+        layers = layers_ref[step]
+        slow = functools.reduce(
+            jnp.add, [jnp.where(layers == n, slow_ref[step, n], 0.0) for n in range(layer_total)]
+        )
+        turn = 2.0 * dz_cells * omega_ref[0] * (slow - 1.0)
+        turns_ref[0, step] = jnp.cos(turn)
+        turns_ref[1, step] = jnp.sin(turn)
+
     total = real_ref.shape[1]
     scale = 1.0 / (NH * total)
     omega_sq = omega_ref[0] * omega_ref[0]
@@ -546,9 +556,18 @@
     offs, nth, bins, goal = slot_lists(lists[:, 0], lists[:, 1:], bins_local, fl, per_device, room)
     side = (offs % cores != off_at % cores).astype(jnp.int32) * line
     slots = (side + ((offs // cores) ^ (off_at // cores))) * per_device + nth
+    source = jnp.arange(fl, dtype=jnp.int32) ^ mine
+    goal = jnp.sum(jnp.where((source[:, None] == jnp.arange(fl))[:, :, None], goal[None], 0), axis=1)
+    pick = (
+        jnp.tile(goal.reshape(1, fl * room), (1, 2))
+        == lax.broadcasted_iota(jnp.int32, (NH, 2 * fl * room), 0)
+    ).astype(jnp.bfloat16)
     own_slots = lax.dynamic_index_in_dim(slots, mine, 0, False)
     own_bins = lax.dynamic_index_in_dim(bins, mine, 0, False)
     list_groups = room // GROUP
+    data, order, own_slots, own_bins, layers, pick = lax.optimization_barrier(
+        (data, order, own_slots, own_bins, layers, pick)
+    )
     shape = jax.ShapeDtypeStruct((list_groups, outer + 1, GROUP, BLK), jnp.int32)
     terms = pl.pallas_call(
         functools.partial(contribution_kernel, freqs=fl),
@@ -563,38 +582,25 @@
         compiler_params=pltpu.CompilerParams(vmem_limit_bytes=SMALL),
         name="contributions",
     )(mine.reshape(1), order, own_slots, own_bins, data, *shares)
-    terms, goal, layers, freq_at = lax.optimization_barrier(
-        (terms, goal, layers, off_at * fl + mine)
-    )
+    terms, freq_at = lax.optimization_barrier((terms, off_at * fl + mine))
     got = {0: terms[0]}
     for away in range(fl - 1, 0, -1):
         got[away] = lax.ppermute(terms[away], "mid", [(i, i ^ away) for i in range(mid_count)])
     terms = [got[away] for away in range(fl)]
 
-    source = jnp.arange(fl, dtype=jnp.int32) ^ mine
-    goal = jnp.sum(jnp.where((source[:, None] == jnp.arange(fl))[:, :, None], goal[None], 0), axis=1)
-    pick = (
-        jnp.tile(goal.reshape(1, fl * room), (1, 2))
-        == lax.broadcasted_iota(jnp.int32, (NH, 2 * fl * room), 0)
-    ).astype(jnp.bfloat16)
     omega = math.pi * (0.1 + 0.8 * (freq_at.astype(jnp.float32) + 0.5) / freq_total)
-    phase_real, phase_imag = pl.pallas_call(
+    phase_real, phase_imag, layer_turns = pl.pallas_call(
         propagator_kernel,
-        in_specs=[smem],
-        out_specs=[vmem] * 2,
-        out_shape=[jax.ShapeDtypeStruct((NH, total_mid), jnp.float32)] * 2,
+        in_specs=[smem, smem, vmem],
+        out_specs=[vmem] * 3,
+        out_shape=[jax.ShapeDtypeStruct((NH, total_mid), jnp.float32)] * 2
+        + [jax.ShapeDtypeStruct((2, *layers.shape), jnp.float32)],
         compiler_params=pltpu.CompilerParams(vmem_limit_bytes=SMALL),
         cost_estimate=pl.CostEstimate(
             flops=60 * NH * total_mid, bytes_accessed=8 * NH * total_mid, transcendentals=10 * NH * total_mid
         ),
         name="propagator",
-    )(omega.reshape(1))
-
-    layer_total = slowness.shape[1]
-    chosen = layers[..., None] == jnp.arange(layer_total)
-    slow = jnp.sum(jnp.where(chosen, slowness[:, None, None, :], 0.0), axis=-1)
-    turn = 2.0 * dz_cells * omega * (slow - 1.0)
-    layer_turns = jnp.stack([jnp.cos(turn), jnp.sin(turn)])
+    )(omega.reshape(1), slowness, layers)
 
     middle, offset_turn = twiddle_tables(outer)
     here = mid_local // BLK

time: 116 us -> 114 us (0.983)
  local copies, waits for them, and re-layouts: 9.19 us -> 7.74 us
    unnamed x26 -> x22, local copies, waits for them, and re-layouts: 5.56 us -> 4.11 us
  transfers between devices with their start and end apart: 17 -> 17, of which waited for: 10 -> 10; matrix products, arithmetic and copies ran while one was open for 6% -> 6% of each run, Pallas kernels for 21% -> 22%
where the time goes in v11:
time: 114 us
  Pallas kernels  57.2 us (50%)
  starting transfers between devices  23.2 us (20%)
  waiting for transfers between devices  21.5 us (19%)
  local copies, waits for them, and re-layouts  7.74 us (7%)
  other arithmetic  3.68 us (3%)
    pallas_call x1, Pallas kernels, local(): pl.pallas_call(functools.partial(march_kernel, sources=fl), in_specs=[sme...  25.4 us
    pallas_call x1, Pallas kernels, local(): pl.pallas_call(propagator_kernel, in_specs=[smem, smem, vmem], out_specs=...  15.2 us
    ppermute x3, waiting for transfers between devices, local(): lax.ppermute(block, 'mid', [(s, s ^ ahead) for s in range(mid_count)])  11.3 us
    ppermute x3, starting transfers between devices, local(): lax.ppermute(shares[away ^ low], 'off', [(i, (i // cores ^ low) * cores +...  8.49 us
    pallas_call x4, Pallas kernels, finish(): pl.pallas_call(finish_kernel, grid_spec=pltpu.PrefetchScalarGridSpec(num_...  6.82 us
    pallas_call x4, Pallas kernels, local(): pl.pallas_call(result_kernel, grid_spec=pltpu.PrefetchScalarGridSpec(num_...  5.19 us
    ppermute x3, waiting for transfers between devices, local(): lax.ppermute(data, 'mid', [(i, i ^ away) for i in range(mid_count)])  4.36 us
    unnamed x22, local copies, waits for them, and re-layouts  4.11 us
  transfers between devices with their start and end apart: 17, of which 10 were waited for; matrix products, arithmetic and copies ran while one was open for 6% of the time, Pallas kernels for 22%

profile of v11, /device:TPU:0, one launch (start us, length us, event | category | flops | bytes accessed | tf_op | source)
XLA Modules:
  0.0 113.7 jit_solution(7337529733162211707)
XLA Ops:
  0.0 1.2 %copy-done.4 = bf16[2,16,128,128]{3,2,1,0:T(8,128)(2,1)S(1)} copy-done((bf16[2,16,128,128]{3,2,1,0:T(8,128)(2,1)S(1)}, bf16[2,16,128,128]{3,2,1,0:T(8,128)(2,1)}, u32[]{:S(2)}) %copy-start.4) | copy-done | bytes 1048600
  2.9 3.1 %collective-permute-start.3 = (bf16[8,128,128]{2,1,0:T(8,128)(2,1)S(1)}, bf16[8,128,128]{2,1,0:T(8,128)(2,1)S(1)}, u32[]{:S(2)}, u32[]{:S(2)}) collective-permute-start(bf16[8,128,128]{2,1,0:T(8,128)(2,1)S(1)} %take_own.1.rest_0_), channel_id=1, source_target_pairs={{0,2},{1,3},{2,0},{3,1},{4,6},{5,7},{6,4},{7,5},{8,10},{9,11},{10,... | collective-permute-start | bytes 786440 | tf_op jit(solution)/shard_map/ppermute | solution.py:511
  6.0 2.6 %collective-permute-start.4 = (bf16[8,128,128]{2,1,0:T(8,128)(2,1)S(1)}, bf16[8,128,128]{2,1,0:T(8,128)(2,1)S(1)}, u32[]{:S(2)}, u32[]{:S(2)}) collective-permute-start(bf16[8,128,128]{2,1,0:T(8,128)(2,1)S(1)} %take_own.1.rest_0_), channel_id=1, source_target_pairs={{0,4},{1,5},{2,6},{3,7},{4,0},{5,1},{6,2},{7,3},{8,12},{9,13},{10,... | collective-permute-start | bytes 786440 | tf_op jit(solution)/shard_map/ppermute | solution.py:511
  12.4 3.4 %all-to-all-start = ((bf16[3,8,8,512]{3,2,0,1:T(8,128)(2,1)}), bf16[3,8,8,512]{3,2,0,1:T(8,128)(2,1)S(1)}, u32[]{:S(2)}, u32[]{:S(2)}) async-start(bf16[3,8,8,512]{3,2,0,1:T(8,128)(2,1)} %copy.46), calls=%async_computation | async-start | bytes 393216 | tf_op jit(solution)/shard_map/all_to_all | solution.py:530
  17.0 3.4 %collective-permute-done.4.rest_2_ = bf16[8,128,128]{2,1,0:T(8,128)(2,1)S(1)} collective-permute-done((bf16[8,128,128]{2,1,0:T(8,128)(2,1)S(1)}, bf16[8,128,128]{2,1,0:T(8,128)(2,1)S(1)}, u32[]{:S(2)}, u32[]{:S(2)}) %collective-permute-start.4) | collective-permute-done | bytes 262176 | tf_op jit(solution)/shard_map/ppermute | solution.py:511
  20.4 2.8 %collective-permute-start.5 = (bf16[8,128,128]{2,1,0:T(8,128)(2,1)S(1)}, bf16[8,128,128]{2,1,0:T(8,128)(2,1)S(1)}, u32[]{:S(2)}, u32[]{:S(2)}) collective-permute-start(bf16[8,128,128]{2,1,0:T(8,128)(2,1)S(1)} %collective-permute-done.4.rest_2_), channel_id=1, source_target_pairs={{0,2},{1,3},{2,0},{3,1},{4,6},{5,7},{6,4},{7,5},{8,10},{9,11},{10,... | collective-permute-start | bytes 786440 | tf_op jit(solution)/shard_map/ppermute | solution.py:511
  23.2 1.4 %all-to-all-done = bf16[3,8,8,512]{3,2,0,1:T(8,128)(2,1)S(1)} async-done(((bf16[3,8,8,512]{3,2,0,1:T(8,128)(2,1)}), bf16[3,8,8,512]{3,2,0,1:T(8,128)(2,1)S(1)}, u32[]{:S(2)}, u32[]{:S(2)}) %all-to-all-start) | async-done | bytes 196640 | tf_op jit(solution)/shard_map/all_to_all | solution.py:530
  24.6 2.5 %collective-permute-start.2 = (bf16[17,8,512]{2,1,0:T(8,128)(2,1)S(1)}, bf16[17,8,512]{2,1,0:T(8,128)(2,1)S(1)}, u32[]{:S(2)}, u32[]{:S(2)}) collective-permute-start(bf16[17,8,512]{2,1,0:T(8,128)(2,1)S(1)} %get-tuple-element.48), channel_id=1, source_target_pairs={{0,24},{8,16},{16,8},{24,0},{1,25},{9,17},{17,9},{25,1},{2,26},{10... | collective-permute-start | bytes 417800 | tf_op jit(solution)/shard_map/ppermute | solution.py:538
  29.9 1.8 %collective-permute-done.2 = bf16[17,8,512]{2,1,0:T(8,128)(2,1)S(1)} collective-permute-done((bf16[17,8,512]{2,1,0:T(8,128)(2,1)S(1)}, bf16[17,8,512]{2,1,0:T(8,128)(2,1)S(1)}, u32[]{:S(2)}, u32[]{:S(2)}) %collective-permute-start.2) | collective-permute-done | bytes 139296 | tf_op jit(solution)/shard_map/ppermute | solution.py:538
  31.7 2.5 %collective-permute-done.1 = bf16[17,8,512]{2,1,0:T(8,128)(2,1)S(1)} collective-permute-done((bf16[17,8,512]{2,1,0:T(8,128)(2,1)S(1)}, bf16[17,8,512]{2,1,0:T(8,128)(2,1)S(1)}, u32[]{:S(2)}, u32[]{:S(2)}) %collective-permute-start.1) | collective-permute-done | bytes 139296 | tf_op jit(solution)/shard_map/ppermute | solution.py:538
  36.1 3.6 %contributions.1 = (s32[5,17,8,128]{3,2,1,0:T(8,128)S(1)}, s32[5,17,8,128]{3,2,1,0:T(8,128)}, s32[5,17,8,128]{3,2,1,0:T(8,128)}, s32[5,17,8,128]{3,2,1,0:T(8,128)S(1)}) custom-call(s32[1]{0:T(128)} %bitcast.2.mine_ref.place_ref.freq_ref, s32[16]{0:T(128)S(1)} %add.116.order_ref, s32[40]{0:T(128)S(1)} %get-tuple-element.27.slot_ref, ...), custom_call_target="tpu_custom_call" | custom-call | tf_op jit(solution)/shard_map/contributions/pallas_call | solution.py:572
  39.7 1.6 %collective-permute-start.10 = (s32[5,17,8,128]{3,2,1,0:T(8,128)}, s32[5,17,8,128]{3,2,1,0:T(8,128)S(1)}, u32[]{:S(2)}, u32[]{:S(2)}) collective-permute-start(s32[5,17,8,128]{3,2,1,0:T(8,128)} %get-tuple-element.39), channel_id=1, source_target_pairs={{0,8},{8,0},{16,24},{24,16},{1,9},{9,1},{17,25},{25,17},{2,10},{10... | collective-permute-start | bytes 1044488 | tf_op jit(solution)/shard_map/ppermute | solution.py:588
  42.1 1.2 %collective-permute-start.12 = (s32[5,17,8,128]{3,2,1,0:T(8,128)S(1)}, s32[5,17,8,128]{3,2,1,0:T(8,128)S(1)}, u32[]{:S(2)}, u32[]{:S(2)}) collective-permute-start(s32[5,17,8,128]{3,2,1,0:T(8,128)S(1)} %get-tuple-element.41), channel_id=1, source_target_pairs={{0,24},{8,16},{16,8},{24,0},{1,25},{9,17},{17,9},{25,1},{2,26},{10... | collective-permute-start | bytes 1044488 | tf_op jit(solution)/shard_map/ppermute | solution.py:588
  43.4 15.2 %propagator.1 = (f32[256,2048]{1,0:T(8,128)S(1)}, f32[256,2048]{1,0:T(8,128)S(1)}, f32[2,2,8,16]{3,2,1,0:T(8,128)S(1)}) custom-call(f32[1]{0:T(128)} %bitcast.25.omega_ref, f32[2,16]{1,0:T(2,128)S(1)} %copy-done.10, s32[2,8,16]{2,1,0:T(8,128)S(1)} %copy.50.layers_ref), custom_call_target="tpu_custom_call" | custom-call | flops 31457280 | bytes 4194304 | tf_op jit(solution)/shard_map/propagator/pallas_call | solution.py:592
  59.0 25.4 %march.1.plane_ref = f32[2,2,128,2048]{3,2,1,0:T(8,128)S(1)} custom-call(f32[2,2,8,16]{3,2,1,0:T(8,128)S(1)} %get-tuple-element.37.layer_ref, s32[5,17,8,128]{3,2,1,0:T(8,128)S(1)} %get-tuple-element.38.rest_0_, s32[5,17,8,128]{3,2,1,0:T(8,128)S(1)} %collective-permute-done.10.rest_1_, s32[5,17,8,128]{3,2,1,0:T(8,128)S(1)} %collective-permute-done.11.rest_2_, ...), custom_call_target="tpu_custom_call" | custom-call | tf_op jit(solution)/shard_map/march/pallas_call | solution.py:610
  84.4 1.7 %finish.4.rest_0_ = s32[1032,128]{1,0:T(8,128)S(1)} custom-call(s32[1]{0:T(128)} %bitcast.27.dest_ref, f32[2,2,8,16]{3,2,1,0:T(8,128)S(1)} %get-tuple-element.37.layer_ref, f32[2,2,128,2048]{3,2,1,0:T(8,128)S(1)} %march.1.plane_ref, bf16[256,768]{1,0:T(8,128)(2,1)S(1)} %copy-done.2, f32[2,128,128]{2,1,0:T(8,128)S(1)} %copy-done.3), custom_call_target="tpu_custom_call" | custom-call | flops 402653184 | bytes 786432 | tf_op jit(solution)/shard_map/finish/pallas_call | solution.py:624
  86.2 1.6 %collective-permute-start.15 = (s32[1032,128]{1,0:T(8,128)S(1)}, s32[1032,128]{1,0:T(8,128)}, u32[]{:S(2)}, u32[]{:S(2)}) collective-permute-start(s32[1032,128]{1,0:T(8,128)S(1)} %finish.4.rest_0_), channel_id=1, source_target_pairs={{0,24},{8,16},{16,8},{24,0},{1,25},{9,17},{17,9},{25,1},{2,26},{10... | collective-permute-start | bytes 1585160 | tf_op jit(solution)/shard_map/ppermute | solution.py:652
  87.7 1.7 %finish.5.rest_0_ = s32[1032,128]{1,0:T(8,128)S(1)} custom-call(s32[1]{0:T(128)} %bitcast.26.dest_ref, f32[2,2,8,16]{3,2,1,0:T(8,128)S(1)} %get-tuple-element.37.layer_ref, f32[2,2,128,2048]{3,2,1,0:T(8,128)S(1)} %march.1.plane_ref, bf16[256,768]{1,0:T(8,128)(2,1)S(1)} %copy-done.2, f32[2,128,128]{2,1,0:T(8,128)S(1)} %copy-done.3, s32[1032,128]{1,0:T(8,128)S(1)} %finish.4.rest_0_), custom_call_target="tpu_custom_call" | custom-call | flops 402653184 | bytes 786432 | tf_op jit(solution)/shard_map/finish/pallas_call | solution.py:624
  90.6 1.7 %finish.6.rest_0_ = s32[1032,128]{1,0:T(8,128)S(1)} custom-call(s32[1]{0:T(128)} %bitcast.1.dest_ref, f32[2,2,8,16]{3,2,1,0:T(8,128)S(1)} %get-tuple-element.37.layer_ref, f32[2,2,128,2048]{3,2,1,0:T(8,128)S(1)} %march.1.plane_ref, bf16[256,768]{1,0:T(8,128)(2,1)S(1)} %copy-done.2, f32[2,128,128]{2,1,0:T(8,128)S(1)} %copy-done.3, s32[1032,128]{1,0:T(8,128)S(1)} %finish.5.rest_0_), custom_call_target="tpu_custom_call" | custom-call | flops 402653184 | bytes 786432 | tf_op jit(solution)/shard_map/finish/pallas_call | solution.py:624
  93.3 2.2 %copy-done.1 = f32[2,2,128,2048]{3,2,1,0:T(8,128)S(1)} copy-done((f32[2,2,128,2048]{3,2,1,0:T(8,128)S(1)}, f32[2,2,128,2048]{3,2,1,0:T(8,128)}, u32[]{:S(2)}) %copy-start.1) | copy-done | bytes 4194328
  95.5 1.7 %finish.7.code_ref = s32[1032,128]{1,0:T(8,128)S(1)} custom-call(s32[1]{0:T(128)} %bitcast.30.dest_ref, f32[2,2,8,16]{3,2,1,0:T(8,128)S(1)} %get-tuple-element.37.layer_ref, f32[2,2,128,2048]{3,2,1,0:T(8,128)S(1)} %copy-done.1, bf16[256,768]{1,0:T(8,128)(2,1)S(1)} %copy-done.2, f32[2,128,128]{2,1,0:T(8,128)S(1)} %copy-done.3, s32[1032,128]{1,0:T(8,128)S(1)} %finish.6.rest_0_), custom_call_target="tpu_custom_call" | custom-call | flops 402653184 | bytes 786432 | tf_op jit(solution)/shard_map/finish/pallas_call | solution.py:624
  98.2 4.0 %collective-permute-done.15.code_ref = s32[1032,128]{1,0:T(8,128)} collective-permute-done((s32[1032,128]{1,0:T(8,128)S(1)}, s32[1032,128]{1,0:T(8,128)}, u32[]{:S(2)}, u32[]{:S(2)}) %collective-permute-start.15) | collective-permute-done | bytes 528416 | tf_op jit(solution)/shard_map/ppermute | solution.py:652
  102.2 2.1 %result.5.rest_0_ = f32[4,256,8,128]{3,2,1,0:T(8,128)} custom-call(s32[1]{0:T(128)} %bitcast.29.freq_ref, s32[1032,128]{1,0:T(8,128)} %collective-permute-done.15.code_ref, f32[4,256,8,128]{3,2,1,0:T(8,128)} %result.4.rest_0_), custom_call_target="tpu_custom_call", output_to_operand_aliasing={{}: (2, {})} | custom-call | flops 524288 | bytes 1572864 | tf_op jit(solution)/shard_map/result/pallas_call | solution.py:659
  104.3 7.3 %collective-permute-done.14.code_ref = s32[1032,128]{1,0:T(8,128)S(1)} collective-permute-done((s32[1032,128]{1,0:T(8,128)S(1)}, s32[1032,128]{1,0:T(8,128)S(1)}, u32[]{:S(2)}, u32[]{:S(2)}) %collective-permute-start.14) | collective-permute-done | bytes 528416 | tf_op jit(solution)/shard_map/ppermute | solution.py:652
  (98 shorter events, 17.8 us)
Async XLA Ops:
  2.9 26.9 %collective-permute-start.3 = (bf16[8,128,128]{2,1,0:T(8,128)(2,1)S(1)}, bf16[8,128,128]{2,1,0:T(8,128)(2,1)S(1)}, u32[]{:S(2)}, u32[]{:S(2)}) collective-permute-start(bf16[8,128,128]{2,1,0:T(8,128)(2,1)S(1)} %take_own.1.rest_0_), channel_id=1, source_target_pairs={{0,2},{1,3},{2,0},{3,1},{4,6},{5,7},{6,4},{7,5},{8,10},{9,11},{10,... | collective-permute-start | bytes 786440 | tf_op jit(solution)/shard_map/ppermute | solution.py:511
  6.0 14.4 %collective-permute-start.4 = (bf16[8,128,128]{2,1,0:T(8,128)(2,1)S(1)}, bf16[8,128,128]{2,1,0:T(8,128)(2,1)S(1)}, u32[]{:S(2)}, u32[]{:S(2)}) collective-permute-start(bf16[8,128,128]{2,1,0:T(8,128)(2,1)S(1)} %take_own.1.rest_0_), channel_id=1, source_target_pairs={{0,4},{1,5},{2,6},{3,7},{4,0},{5,1},{6,2},{7,3},{8,12},{9,13},{10,... | collective-permute-start | bytes 786440 | tf_op jit(solution)/shard_map/ppermute | solution.py:511
  11.6 31.7 %copy-start.10 = (f32[2,16]{1,0:T(2,128)S(1)}, f32[2,16]{1,0:T(2,128)}, u32[]{:S(2)}) copy-start(f32[2,16]{1,0:T(2,128)} %slow_ref.1) | copy-start | bytes 388
  12.4 12.2 %all-to-all-start = ((bf16[3,8,8,512]{3,2,0,1:T(8,128)(2,1)}), bf16[3,8,8,512]{3,2,0,1:T(8,128)(2,1)S(1)}, u32[]{:S(2)}, u32[]{:S(2)}) async-start(bf16[3,8,8,512]{3,2,0,1:T(8,128)(2,1)} %copy.46), calls=%async_computation | async-start | bytes 393216 | tf_op jit(solution)/shard_map/all_to_all | solution.py:530
  20.4 14.0 %collective-permute-start.5 = (bf16[8,128,128]{2,1,0:T(8,128)(2,1)S(1)}, bf16[8,128,128]{2,1,0:T(8,128)(2,1)S(1)}, u32[]{:S(2)}, u32[]{:S(2)}) collective-permute-start(bf16[8,128,128]{2,1,0:T(8,128)(2,1)S(1)} %collective-permute-done.4.rest_2_), channel_id=1, source_target_pairs={{0,2},{1,3},{2,0},{3,1},{4,6},{5,7},{6,4},{7,5},{8,10},{9,11},{10,... | collective-permute-start | bytes 786440 | tf_op jit(solution)/shard_map/ppermute | solution.py:511
  24.6 7.1 %collective-permute-start.2 = (bf16[17,8,512]{2,1,0:T(8,128)(2,1)S(1)}, bf16[17,8,512]{2,1,0:T(8,128)(2,1)S(1)}, u32[]{:S(2)}, u32[]{:S(2)}) collective-permute-start(bf16[17,8,512]{2,1,0:T(8,128)(2,1)S(1)} %get-tuple-element.48), channel_id=1, source_target_pairs={{0,24},{8,16},{16,8},{24,0},{1,25},{9,17},{17,9},{25,1},{2,26},{10... | collective-permute-start | bytes 417800 | tf_op jit(solution)/shard_map/ppermute | solution.py:538
  27.1 7.1 %collective-permute-start.1 = (bf16[17,8,512]{2,1,0:T(8,128)(2,1)S(1)}, bf16[17,8,512]{2,1,0:T(8,128)(2,1)S(1)}, u32[]{:S(2)}, u32[]{:S(2)}) collective-permute-start(bf16[17,8,512]{2,1,0:T(8,128)(2,1)S(1)} %get-tuple-element.48), channel_id=1, source_target_pairs={{0,16},{8,24},{16,0},{24,8},{1,17},{9,25},{17,1},{25,9},{2,18},{10... | collective-permute-start | bytes 417800 | tf_op jit(solution)/shard_map/ppermute | solution.py:538
  27.6 6.6 %collective-permute-start = (bf16[17,8,512]{2,1,0:T(8,128)(2,1)S(1)}, bf16[17,8,512]{2,1,0:T(8,128)(2,1)S(1)}, u32[]{:S(2)}, u32[]{:S(2)}) collective-permute-start(bf16[17,8,512]{2,1,0:T(8,128)(2,1)S(1)} %get-tuple-element.48), channel_id=1, source_target_pairs={{0,8},{8,0},{16,24},{24,16},{1,9},{9,1},{17,25},{25,17},{2,10},{10... | collective-permute-start | bytes 417800 | tf_op jit(solution)/shard_map/ppermute | solution.py:538
  29.8 5.7 %collective-permute-start.6 = (bf16[8,128,128]{2,1,0:T(8,128)(2,1)S(1)}, bf16[8,128,128]{2,1,0:T(8,128)(2,1)S(1)}, u32[]{:S(2)}, u32[]{:S(2)}) collective-permute-start(bf16[8,128,128]{2,1,0:T(8,128)(2,1)S(1)} %take_own.1.rest_0_), channel_id=1, source_target_pairs={{0,1},{1,0},{2,3},{3,2},{4,5},{5,4},{6,7},{7,6},{8,9},{9,8},{10,11... | collective-permute-start | bytes 786440 | tf_op jit(solution)/shard_map/ppermute | solution.py:518
  31.7 4.1 %collective-permute-start.8 = (bf16[8,128,128]{2,1,0:T(8,128)(2,1)S(1)}, bf16[8,128,128]{2,1,0:T(8,128)(2,1)S(1)}, u32[]{:S(2)}, u32[]{:S(2)}) collective-permute-start(bf16[8,128,128]{2,1,0:T(8,128)(2,1)S(1)} %collective-permute-done.4.rest_2_), channel_id=1, source_target_pairs={{0,1},{1,0},{2,3},{3,2},{4,5},{5,4},{6,7},{7,6},{8,9},{9,8},{10,11... | collective-permute-start | bytes 786440 | tf_op jit(solution)/shard_map/ppermute | solution.py:518
  34.2 1.5 %collective-permute-start.7 = (bf16[8,128,128]{2,1,0:T(8,128)(2,1)S(1)}, bf16[8,128,128]{2,1,0:T(8,128)(2,1)S(1)}, u32[]{:S(2)}, u32[]{:S(2)}) collective-permute-start(bf16[8,128,128]{2,1,0:T(8,128)(2,1)S(1)} %collective-permute-done.3.rest_1_), channel_id=1, source_target_pairs={{0,1},{1,0},{2,3},{3,2},{4,5},{5,4},{6,7},{7,6},{8,9},{9,8},{10,11... | collective-permute-start | bytes 786440 | tf_op jit(solution)/shard_map/ppermute | solution.py:518
  34.4 1.7 %collective-permute-start.9 = (bf16[8,128,128]{2,1,0:T(8,128)(2,1)S(1)}, bf16[8,128,128]{2,1,0:T(8,128)(2,1)S(1)}, u32[]{:S(2)}, u32[]{:S(2)}) collective-permute-start(bf16[8,128,128]{2,1,0:T(8,128)(2,1)S(1)} %collective-permute-done.5.rest_3_), channel_id=1, source_target_pairs={{0,1},{1,0},{2,3},{3,2},{4,5},{5,4},{6,7},{7,6},{8,9},{9,8},{10,11... | collective-permute-start | bytes 786440 | tf_op jit(solution)/shard_map/ppermute | solution.py:518
  39.7 18.9 %collective-permute-start.10 = (s32[5,17,8,128]{3,2,1,0:T(8,128)}, s32[5,17,8,128]{3,2,1,0:T(8,128)S(1)}, u32[]{:S(2)}, u32[]{:S(2)}) collective-permute-start(s32[5,17,8,128]{3,2,1,0:T(8,128)} %get-tuple-element.39), channel_id=1, source_target_pairs={{0,8},{8,0},{16,24},{24,16},{1,9},{9,1},{17,25},{25,17},{2,10},{10... | collective-permute-start | bytes 1044488 | tf_op jit(solution)/shard_map/ppermute | solution.py:588
  41.2 17.7 %collective-permute-start.11 = (s32[5,17,8,128]{3,2,1,0:T(8,128)}, s32[5,17,8,128]{3,2,1,0:T(8,128)S(1)}, u32[]{:S(2)}, u32[]{:S(2)}) collective-permute-start(s32[5,17,8,128]{3,2,1,0:T(8,128)} %get-tuple-element.40), channel_id=1, source_target_pairs={{0,16},{8,24},{16,0},{24,8},{1,17},{9,25},{17,1},{25,9},{2,18},{10... | collective-permute-start | bytes 1044488 | tf_op jit(solution)/shard_map/ppermute | solution.py:588
  42.1 16.9 %collective-permute-start.12 = (s32[5,17,8,128]{3,2,1,0:T(8,128)S(1)}, s32[5,17,8,128]{3,2,1,0:T(8,128)S(1)}, u32[]{:S(2)}, u32[]{:S(2)}) collective-permute-start(s32[5,17,8,128]{3,2,1,0:T(8,128)S(1)} %get-tuple-element.41), channel_id=1, source_target_pairs={{0,24},{8,16},{16,8},{24,0},{1,25},{9,17},{17,9},{25,1},{2,26},{10... | collective-permute-start | bytes 1044488 | tf_op jit(solution)/shard_map/ppermute | solution.py:588
  43.3 15.7 %copy-start.2 = (bf16[256,768]{1,0:T(8,128)(2,1)S(1)}, bf16[256,768]{1,0:T(8,128)(2,1)}, u32[]{:S(2)}) copy-start(bf16[256,768]{1,0:T(8,128)(2,1)} %constant.135.clone.rest_8_.rows_inverse) | copy-start | bytes 1179652
  43.3 15.7 %copy-start.3 = (f32[2,128,128]{2,1,0:T(8,128)S(1)}, f32[2,128,128]{2,1,0:T(8,128)}, u32[]{:S(2)}) copy-start(f32[2,128,128]{2,1,0:T(8,128)} %constant.139.clone.rest_12_.offset_ref) | copy-start | bytes 393220
  43.3 15.7 %copy-start.5 = (bf16[256,768]{1,0:T(8,128)(2,1)S(1)}, bf16[256,768]{1,0:T(8,128)(2,1)}, u32[]{:S(2)}) copy-start(bf16[256,768]{1,0:T(8,128)(2,1)} %constant.134.clone.rest_7_) | copy-start | bytes 1179652
  43.3 15.7 %copy-start.6 = (bf16[768,256]{1,0:T(8,128)(2,1)S(1)}, bf16[768,256]{1,0:T(8,128)(2,1)}, u32[]{:S(2)}) copy-start(bf16[768,256]{1,0:T(8,128)(2,1)} %constant.136.clone.rest_9_) | copy-start | bytes 1179652
  43.3 15.7 %copy-start.7 = (bf16[768,256]{1,0:T(8,128)(2,1)S(1)}, bf16[768,256]{1,0:T(8,128)(2,1)}, u32[]{:S(2)}) copy-start(bf16[768,256]{1,0:T(8,128)(2,1)} %constant.137.clone.rest_10_) | copy-start | bytes 1179652
  43.4 15.7 %copy-start.8 = (f32[2,16,128]{2,1,0:T(8,128)S(1)}, f32[2,16,128]{2,1,0:T(8,128)}, u32[]{:S(2)}) copy-start(f32[2,16,128]{2,1,0:T(8,128)} %constant.138.clone.rest_11_) | copy-start | bytes 49156
  86.2 16.1 %collective-permute-start.15 = (s32[1032,128]{1,0:T(8,128)S(1)}, s32[1032,128]{1,0:T(8,128)}, u32[]{:S(2)}, u32[]{:S(2)}) collective-permute-start(s32[1032,128]{1,0:T(8,128)S(1)} %finish.4.rest_0_), channel_id=1, source_target_pairs={{0,24},{8,16},{16,8},{24,0},{1,25},{9,17},{17,9},{25,1},{2,26},{10... | collective-permute-start | bytes 1585160 | tf_op jit(solution)/shard_map/ppermute | solution.py:652
  89.4 22.2 %collective-permute-start.14 = (s32[1032,128]{1,0:T(8,128)S(1)}, s32[1032,128]{1,0:T(8,128)S(1)}, u32[]{:S(2)}, u32[]{:S(2)}) collective-permute-start(s32[1032,128]{1,0:T(8,128)S(1)} %finish.5.rest_0_), channel_id=1, source_target_pairs={{0,16},{8,24},{16,0},{24,8},{1,17},{9,25},{17,1},{25,9},{2,18},{10... | collective-permute-start | bytes 1585160 | tf_op jit(solution)/shard_map/ppermute | solution.py:652
  92.3 20.4 %collective-permute-start.13 = (s32[1032,128]{1,0:T(8,128)S(1)}, s32[1032,128]{1,0:T(8,128)S(1)}, u32[]{:S(2)}, u32[]{:S(2)}) collective-permute-start(s32[1032,128]{1,0:T(8,128)S(1)} %finish.6.rest_0_), channel_id=1, source_target_pairs={{0,8},{8,0},{16,24},{24,16},{1,9},{9,1},{17,25},{25,17},{2,10},{10... | collective-permute-start | bytes 1585160 | tf_op jit(solution)/shard_map/ppermute | solution.py:652
  (4 other events, 10.2 us)

commit v12 on v11

--- a/solution.py
+++ b/solution.py
@@ -19,10 +19,10 @@
 STEP_LOG = 64.0
 TOP = 32767.0
 GROUP = 8
-COLUMNS = 2
+COLUMNS = 4
 ROWS = 8
-CHUNKS = 4
-UNROLL = 2
+CHUNKS = 8
+UNROLL = 1
 VMEM = 28 * 1024 * 1024
 SMALL = 10 * 1024 * 1024
 
@@ -343,7 +343,7 @@
 
     scales[...] = scale_of(words(outer))
 
-    @pl.loop(0, outer // COLUMNS, unroll=2)
+    @pl.loop(0, outer // COLUMNS, unroll=1)
     def _(at):
         columns = []
         for a in range(COLUMNS):
@@ -368,7 +368,7 @@
         midpoint_pass(plane, other, (phase_real, phase_imag), lanes_forward, lanes_inverse, middle_ref)
         if step < steps - 1:
 
-            @pl.loop(0, outer // COLUMNS, unroll=2)
+            @pl.loop(0, outer // COLUMNS, unroll=1)
             def _(at):
                 places = [at * COLUMNS + a for a in range(COLUMNS)]
                 columns = []

time: 114 us -> 113 us (level)
  Pallas kernels: 57.2 us -> 55.7 us
    pallas_call x1, Pallas kernels: 25.4 us -> 23.9 us  [local(): pl.pallas_call(functools.partial(march_kernel, sources=fl), in_specs=[sme...]
  transfers between devices with their start and end apart: 17 -> 17, of which waited for: 10 -> 10; matrix products, arithmetic and copies ran while one was open for 6% -> 7% of each run, Pallas kernels for 22% -> 22%
where the time goes in v12:
time: 113 us; the launch traced here: 112 us
  Pallas kernels  55.7 us (49%)
  starting transfers between devices  23.2 us (21%)
  waiting for transfers between devices  21.4 us (19%)
  local copies, waits for them, and re-layouts  7.74 us (7%)
  other arithmetic  3.68 us (3%)
    pallas_call x1, Pallas kernels, local(): pl.pallas_call(functools.partial(march_kernel, sources=fl), in_specs=[sme...  23.9 us
    pallas_call x1, Pallas kernels, local(): pl.pallas_call(propagator_kernel, in_specs=[smem, smem, vmem], out_specs=...  15.2 us
    ppermute x3, waiting for transfers between devices, local(): lax.ppermute(block, 'mid', [(s, s ^ ahead) for s in range(mid_count)])  11.3 us
    ppermute x3, starting transfers between devices, local(): lax.ppermute(shares[away ^ low], 'off', [(i, (i // cores ^ low) * cores +...  8.49 us
    pallas_call x4, Pallas kernels, finish(): pl.pallas_call(finish_kernel, grid_spec=pltpu.PrefetchScalarGridSpec(num_...  6.82 us
    pallas_call x4, Pallas kernels, local(): pl.pallas_call(result_kernel, grid_spec=pltpu.PrefetchScalarGridSpec(num_...  5.19 us
    ppermute x3, waiting for transfers between devices, local(): lax.ppermute(data, 'mid', [(i, i ^ away) for i in range(mid_count)])  4.36 us
    unnamed x22, local copies, waits for them, and re-layouts  4.11 us
  transfers between devices with their start and end apart: 17, of which 10 were waited for; matrix products, arithmetic and copies ran while one was open for 7% of the time, Pallas kernels for 22%

profile of v12, /device:TPU:0, one launch (start us, length us, event | category | flops | bytes accessed | tf_op | source)
XLA Modules:
  0.0 112.2 jit_solution(1347970696129712116)
XLA Ops:
  0.0 1.2 %copy-done.4 = bf16[2,16,128,128]{3,2,1,0:T(8,128)(2,1)S(1)} copy-done((bf16[2,16,128,128]{3,2,1,0:T(8,128)(2,1)S(1)}, bf16[2,16,128,128]{3,2,1,0:T(8,128)(2,1)}, u32[]{:S(2)}) %copy-start.4) | copy-done | bytes 1048600
  2.9 3.1 %collective-permute-start.3 = (bf16[8,128,128]{2,1,0:T(8,128)(2,1)S(1)}, bf16[8,128,128]{2,1,0:T(8,128)(2,1)S(1)}, u32[]{:S(2)}, u32[]{:S(2)}) collective-permute-start(bf16[8,128,128]{2,1,0:T(8,128)(2,1)S(1)} %take_own.1.rest_0_), channel_id=1, source_target_pairs={{0,2},{1,3},{2,0},{3,1},{4,6},{5,7},{6,4},{7,5},{8,10},{9,11},{10,... | collective-permute-start | bytes 786440 | tf_op jit(solution)/shard_map/ppermute | solution.py:511
  6.0 2.6 %collective-permute-start.4 = (bf16[8,128,128]{2,1,0:T(8,128)(2,1)S(1)}, bf16[8,128,128]{2,1,0:T(8,128)(2,1)S(1)}, u32[]{:S(2)}, u32[]{:S(2)}) collective-permute-start(bf16[8,128,128]{2,1,0:T(8,128)(2,1)S(1)} %take_own.1.rest_0_), channel_id=1, source_target_pairs={{0,4},{1,5},{2,6},{3,7},{4,0},{5,1},{6,2},{7,3},{8,12},{9,13},{10,... | collective-permute-start | bytes 786440 | tf_op jit(solution)/shard_map/ppermute | solution.py:511
  12.4 3.4 %all-to-all-start = ((bf16[3,8,8,512]{3,2,0,1:T(8,128)(2,1)}), bf16[3,8,8,512]{3,2,0,1:T(8,128)(2,1)S(1)}, u32[]{:S(2)}, u32[]{:S(2)}) async-start(bf16[3,8,8,512]{3,2,0,1:T(8,128)(2,1)} %copy.46), calls=%async_computation | async-start | bytes 393216 | tf_op jit(solution)/shard_map/all_to_all | solution.py:530
  17.0 3.4 %collective-permute-done.4.rest_2_ = bf16[8,128,128]{2,1,0:T(8,128)(2,1)S(1)} collective-permute-done((bf16[8,128,128]{2,1,0:T(8,128)(2,1)S(1)}, bf16[8,128,128]{2,1,0:T(8,128)(2,1)S(1)}, u32[]{:S(2)}, u32[]{:S(2)}) %collective-permute-start.4) | collective-permute-done | bytes 262176 | tf_op jit(solution)/shard_map/ppermute | solution.py:511
  20.4 2.8 %collective-permute-start.5 = (bf16[8,128,128]{2,1,0:T(8,128)(2,1)S(1)}, bf16[8,128,128]{2,1,0:T(8,128)(2,1)S(1)}, u32[]{:S(2)}, u32[]{:S(2)}) collective-permute-start(bf16[8,128,128]{2,1,0:T(8,128)(2,1)S(1)} %collective-permute-done.4.rest_2_), channel_id=1, source_target_pairs={{0,2},{1,3},{2,0},{3,1},{4,6},{5,7},{6,4},{7,5},{8,10},{9,11},{10,... | collective-permute-start | bytes 786440 | tf_op jit(solution)/shard_map/ppermute | solution.py:511
  23.2 1.4 %all-to-all-done = bf16[3,8,8,512]{3,2,0,1:T(8,128)(2,1)S(1)} async-done(((bf16[3,8,8,512]{3,2,0,1:T(8,128)(2,1)}), bf16[3,8,8,512]{3,2,0,1:T(8,128)(2,1)S(1)}, u32[]{:S(2)}, u32[]{:S(2)}) %all-to-all-start) | async-done | bytes 196640 | tf_op jit(solution)/shard_map/all_to_all | solution.py:530
  24.6 2.5 %collective-permute-start.2 = (bf16[17,8,512]{2,1,0:T(8,128)(2,1)S(1)}, bf16[17,8,512]{2,1,0:T(8,128)(2,1)S(1)}, u32[]{:S(2)}, u32[]{:S(2)}) collective-permute-start(bf16[17,8,512]{2,1,0:T(8,128)(2,1)S(1)} %get-tuple-element.48), channel_id=1, source_target_pairs={{0,24},{8,16},{16,8},{24,0},{1,25},{9,17},{17,9},{25,1},{2,26},{10... | collective-permute-start | bytes 417800 | tf_op jit(solution)/shard_map/ppermute | solution.py:538
  29.9 1.8 %collective-permute-done.2 = bf16[17,8,512]{2,1,0:T(8,128)(2,1)S(1)} collective-permute-done((bf16[17,8,512]{2,1,0:T(8,128)(2,1)S(1)}, bf16[17,8,512]{2,1,0:T(8,128)(2,1)S(1)}, u32[]{:S(2)}, u32[]{:S(2)}) %collective-permute-start.2) | collective-permute-done | bytes 139296 | tf_op jit(solution)/shard_map/ppermute | solution.py:538
  31.7 2.5 %collective-permute-done.1 = bf16[17,8,512]{2,1,0:T(8,128)(2,1)S(1)} collective-permute-done((bf16[17,8,512]{2,1,0:T(8,128)(2,1)S(1)}, bf16[17,8,512]{2,1,0:T(8,128)(2,1)S(1)}, u32[]{:S(2)}, u32[]{:S(2)}) %collective-permute-start.1) | collective-permute-done | bytes 139296 | tf_op jit(solution)/shard_map/ppermute | solution.py:538
  36.1 3.6 %contributions.1 = (s32[5,17,8,128]{3,2,1,0:T(8,128)S(1)}, s32[5,17,8,128]{3,2,1,0:T(8,128)}, s32[5,17,8,128]{3,2,1,0:T(8,128)}, s32[5,17,8,128]{3,2,1,0:T(8,128)S(1)}) custom-call(s32[1]{0:T(128)} %bitcast.2.mine_ref.place_ref.freq_ref, s32[16]{0:T(128)S(1)} %add.116.order_ref, s32[40]{0:T(128)S(1)} %get-tuple-element.27.slot_ref, ...), custom_call_target="tpu_custom_call" | custom-call | tf_op jit(solution)/shard_map/contributions/pallas_call | solution.py:572
  39.7 1.6 %collective-permute-start.10 = (s32[5,17,8,128]{3,2,1,0:T(8,128)}, s32[5,17,8,128]{3,2,1,0:T(8,128)S(1)}, u32[]{:S(2)}, u32[]{:S(2)}) collective-permute-start(s32[5,17,8,128]{3,2,1,0:T(8,128)} %get-tuple-element.39), channel_id=1, source_target_pairs={{0,8},{8,0},{16,24},{24,16},{1,9},{9,1},{17,25},{25,17},{2,10},{10... | collective-permute-start | bytes 1044488 | tf_op jit(solution)/shard_map/ppermute | solution.py:588
  42.1 1.2 %collective-permute-start.12 = (s32[5,17,8,128]{3,2,1,0:T(8,128)S(1)}, s32[5,17,8,128]{3,2,1,0:T(8,128)S(1)}, u32[]{:S(2)}, u32[]{:S(2)}) collective-permute-start(s32[5,17,8,128]{3,2,1,0:T(8,128)S(1)} %get-tuple-element.41), channel_id=1, source_target_pairs={{0,24},{8,16},{16,8},{24,0},{1,25},{9,17},{17,9},{25,1},{2,26},{10... | collective-permute-start | bytes 1044488 | tf_op jit(solution)/shard_map/ppermute | solution.py:588
  43.4 15.2 %propagator.1 = (f32[256,2048]{1,0:T(8,128)S(1)}, f32[256,2048]{1,0:T(8,128)S(1)}, f32[2,2,8,16]{3,2,1,0:T(8,128)S(1)}) custom-call(f32[1]{0:T(128)} %bitcast.25.omega_ref, f32[2,16]{1,0:T(2,128)S(1)} %copy-done.10, s32[2,8,16]{2,1,0:T(8,128)S(1)} %copy.50.layers_ref), custom_call_target="tpu_custom_call" | custom-call | flops 31457280 | bytes 4194304 | tf_op jit(solution)/shard_map/propagator/pallas_call | solution.py:592
  59.0 23.9 %march.1.plane_ref = f32[2,2,128,2048]{3,2,1,0:T(8,128)S(1)} custom-call(f32[2,2,8,16]{3,2,1,0:T(8,128)S(1)} %get-tuple-element.37.layer_ref, s32[5,17,8,128]{3,2,1,0:T(8,128)S(1)} %get-tuple-element.38.rest_0_, s32[5,17,8,128]{3,2,1,0:T(8,128)S(1)} %collective-permute-done.10.rest_1_, s32[5,17,8,128]{3,2,1,0:T(8,128)S(1)} %collective-permute-done.11.rest_2_, ...), custom_call_target="tpu_custom_call" | custom-call | tf_op jit(solution)/shard_map/march/pallas_call | solution.py:610
  82.9 1.7 %finish.4.rest_0_ = s32[1032,128]{1,0:T(8,128)S(1)} custom-call(s32[1]{0:T(128)} %bitcast.27.dest_ref, f32[2,2,8,16]{3,2,1,0:T(8,128)S(1)} %get-tuple-element.37.layer_ref, f32[2,2,128,2048]{3,2,1,0:T(8,128)S(1)} %march.1.plane_ref, bf16[256,768]{1,0:T(8,128)(2,1)S(1)} %copy-done.2, f32[2,128,128]{2,1,0:T(8,128)S(1)} %copy-done.3), custom_call_target="tpu_custom_call" | custom-call | flops 402653184 | bytes 786432 | tf_op jit(solution)/shard_map/finish/pallas_call | solution.py:624
  84.6 1.6 %collective-permute-start.15 = (s32[1032,128]{1,0:T(8,128)S(1)}, s32[1032,128]{1,0:T(8,128)}, u32[]{:S(2)}, u32[]{:S(2)}) collective-permute-start(s32[1032,128]{1,0:T(8,128)S(1)} %finish.4.rest_0_), channel_id=1, source_target_pairs={{0,24},{8,16},{16,8},{24,0},{1,25},{9,17},{17,9},{25,1},{2,26},{10... | collective-permute-start | bytes 1585160 | tf_op jit(solution)/shard_map/ppermute | solution.py:652
  86.2 1.7 %finish.5.rest_0_ = s32[1032,128]{1,0:T(8,128)S(1)} custom-call(s32[1]{0:T(128)} %bitcast.26.dest_ref, f32[2,2,8,16]{3,2,1,0:T(8,128)S(1)} %get-tuple-element.37.layer_ref, f32[2,2,128,2048]{3,2,1,0:T(8,128)S(1)} %march.1.plane_ref, bf16[256,768]{1,0:T(8,128)(2,1)S(1)} %copy-done.2, f32[2,128,128]{2,1,0:T(8,128)S(1)} %copy-done.3, s32[1032,128]{1,0:T(8,128)S(1)} %finish.4.rest_0_), custom_call_target="tpu_custom_call" | custom-call | flops 402653184 | bytes 786432 | tf_op jit(solution)/shard_map/finish/pallas_call | solution.py:624
  89.1 1.7 %finish.6.rest_0_ = s32[1032,128]{1,0:T(8,128)S(1)} custom-call(s32[1]{0:T(128)} %bitcast.1.dest_ref, f32[2,2,8,16]{3,2,1,0:T(8,128)S(1)} %get-tuple-element.37.layer_ref, f32[2,2,128,2048]{3,2,1,0:T(8,128)S(1)} %march.1.plane_ref, bf16[256,768]{1,0:T(8,128)(2,1)S(1)} %copy-done.2, f32[2,128,128]{2,1,0:T(8,128)S(1)} %copy-done.3, s32[1032,128]{1,0:T(8,128)S(1)} %finish.5.rest_0_), custom_call_target="tpu_custom_call" | custom-call | flops 402653184 | bytes 786432 | tf_op jit(solution)/shard_map/finish/pallas_call | solution.py:624
  91.8 2.2 %copy-done.1 = f32[2,2,128,2048]{3,2,1,0:T(8,128)S(1)} copy-done((f32[2,2,128,2048]{3,2,1,0:T(8,128)S(1)}, f32[2,2,128,2048]{3,2,1,0:T(8,128)}, u32[]{:S(2)}) %copy-start.1) | copy-done | bytes 4194328
  93.9 1.7 %finish.7.code_ref = s32[1032,128]{1,0:T(8,128)S(1)} custom-call(s32[1]{0:T(128)} %bitcast.30.dest_ref, f32[2,2,8,16]{3,2,1,0:T(8,128)S(1)} %get-tuple-element.37.layer_ref, f32[2,2,128,2048]{3,2,1,0:T(8,128)S(1)} %copy-done.1, bf16[256,768]{1,0:T(8,128)(2,1)S(1)} %copy-done.2, f32[2,128,128]{2,1,0:T(8,128)S(1)} %copy-done.3, s32[1032,128]{1,0:T(8,128)S(1)} %finish.6.rest_0_), custom_call_target="tpu_custom_call" | custom-call | flops 402653184 | bytes 786432 | tf_op jit(solution)/shard_map/finish/pallas_call | solution.py:624
  96.7 4.0 %collective-permute-done.15.code_ref = s32[1032,128]{1,0:T(8,128)} collective-permute-done((s32[1032,128]{1,0:T(8,128)S(1)}, s32[1032,128]{1,0:T(8,128)}, u32[]{:S(2)}, u32[]{:S(2)}) %collective-permute-start.15) | collective-permute-done | bytes 528416 | tf_op jit(solution)/shard_map/ppermute | solution.py:652
  100.7 2.1 %result.5.rest_0_ = f32[4,256,8,128]{3,2,1,0:T(8,128)} custom-call(s32[1]{0:T(128)} %bitcast.29.freq_ref, s32[1032,128]{1,0:T(8,128)} %collective-permute-done.15.code_ref, f32[4,256,8,128]{3,2,1,0:T(8,128)} %result.4.rest_0_), custom_call_target="tpu_custom_call", output_to_operand_aliasing={{}: (2, {})} | custom-call | flops 524288 | bytes 1572864 | tf_op jit(solution)/shard_map/result/pallas_call | solution.py:659
  102.8 7.3 %collective-permute-done.14.code_ref = s32[1032,128]{1,0:T(8,128)S(1)} collective-permute-done((s32[1032,128]{1,0:T(8,128)S(1)}, s32[1032,128]{1,0:T(8,128)S(1)}, u32[]{:S(2)}, u32[]{:S(2)}) %collective-permute-start.14) | collective-permute-done | bytes 528416 | tf_op jit(solution)/shard_map/ppermute | solution.py:652
  (98 shorter events, 17.8 us)
Async XLA Ops:
  2.9 26.9 %collective-permute-start.3 = (bf16[8,128,128]{2,1,0:T(8,128)(2,1)S(1)}, bf16[8,128,128]{2,1,0:T(8,128)(2,1)S(1)}, u32[]{:S(2)}, u32[]{:S(2)}) collective-permute-start(bf16[8,128,128]{2,1,0:T(8,128)(2,1)S(1)} %take_own.1.rest_0_), channel_id=1, source_target_pairs={{0,2},{1,3},{2,0},{3,1},{4,6},{5,7},{6,4},{7,5},{8,10},{9,11},{10,... | collective-permute-start | bytes 786440 | tf_op jit(solution)/shard_map/ppermute | solution.py:511
  6.0 14.4 %collective-permute-start.4 = (bf16[8,128,128]{2,1,0:T(8,128)(2,1)S(1)}, bf16[8,128,128]{2,1,0:T(8,128)(2,1)S(1)}, u32[]{:S(2)}, u32[]{:S(2)}) collective-permute-start(bf16[8,128,128]{2,1,0:T(8,128)(2,1)S(1)} %take_own.1.rest_0_), channel_id=1, source_target_pairs={{0,4},{1,5},{2,6},{3,7},{4,0},{5,1},{6,2},{7,3},{8,12},{9,13},{10,... | collective-permute-start | bytes 786440 | tf_op jit(solution)/shard_map/ppermute | solution.py:511
  11.6 31.7 %copy-start.10 = (f32[2,16]{1,0:T(2,128)S(1)}, f32[2,16]{1,0:T(2,128)}, u32[]{:S(2)}) copy-start(f32[2,16]{1,0:T(2,128)} %slow_ref.1) | copy-start | bytes 388
  12.4 12.2 %all-to-all-start = ((bf16[3,8,8,512]{3,2,0,1:T(8,128)(2,1)}), bf16[3,8,8,512]{3,2,0,1:T(8,128)(2,1)S(1)}, u32[]{:S(2)}, u32[]{:S(2)}) async-start(bf16[3,8,8,512]{3,2,0,1:T(8,128)(2,1)} %copy.46), calls=%async_computation | async-start | bytes 393216 | tf_op jit(solution)/shard_map/all_to_all | solution.py:530
  20.4 14.0 %collective-permute-start.5 = (bf16[8,128,128]{2,1,0:T(8,128)(2,1)S(1)}, bf16[8,128,128]{2,1,0:T(8,128)(2,1)S(1)}, u32[]{:S(2)}, u32[]{:S(2)}) collective-permute-start(bf16[8,128,128]{2,1,0:T(8,128)(2,1)S(1)} %collective-permute-done.4.rest_2_), channel_id=1, source_target_pairs={{0,2},{1,3},{2,0},{3,1},{4,6},{5,7},{6,4},{7,5},{8,10},{9,11},{10,... | collective-permute-start | bytes 786440 | tf_op jit(solution)/shard_map/ppermute | solution.py:511
  24.6 7.1 %collective-permute-start.2 = (bf16[17,8,512]{2,1,0:T(8,128)(2,1)S(1)}, bf16[17,8,512]{2,1,0:T(8,128)(2,1)S(1)}, u32[]{:S(2)}, u32[]{:S(2)}) collective-permute-start(bf16[17,8,512]{2,1,0:T(8,128)(2,1)S(1)} %get-tuple-element.48), channel_id=1, source_target_pairs={{0,24},{8,16},{16,8},{24,0},{1,25},{9,17},{17,9},{25,1},{2,26},{10... | collective-permute-start | bytes 417800 | tf_op jit(solution)/shard_map/ppermute | solution.py:538
  27.1 7.1 %collective-permute-start.1 = (bf16[17,8,512]{2,1,0:T(8,128)(2,1)S(1)}, bf16[17,8,512]{2,1,0:T(8,128)(2,1)S(1)}, u32[]{:S(2)}, u32[]{:S(2)}) collective-permute-start(bf16[17,8,512]{2,1,0:T(8,128)(2,1)S(1)} %get-tuple-element.48), channel_id=1, source_target_pairs={{0,16},{8,24},{16,0},{24,8},{1,17},{9,25},{17,1},{25,9},{2,18},{10... | collective-permute-start | bytes 417800 | tf_op jit(solution)/shard_map/ppermute | solution.py:538
  27.6 6.6 %collective-permute-start = (bf16[17,8,512]{2,1,0:T(8,128)(2,1)S(1)}, bf16[17,8,512]{2,1,0:T(8,128)(2,1)S(1)}, u32[]{:S(2)}, u32[]{:S(2)}) collective-permute-start(bf16[17,8,512]{2,1,0:T(8,128)(2,1)S(1)} %get-tuple-element.48), channel_id=1, source_target_pairs={{0,8},{8,0},{16,24},{24,16},{1,9},{9,1},{17,25},{25,17},{2,10},{10... | collective-permute-start | bytes 417800 | tf_op jit(solution)/shard_map/ppermute | solution.py:538
  29.8 5.7 %collective-permute-start.6 = (bf16[8,128,128]{2,1,0:T(8,128)(2,1)S(1)}, bf16[8,128,128]{2,1,0:T(8,128)(2,1)S(1)}, u32[]{:S(2)}, u32[]{:S(2)}) collective-permute-start(bf16[8,128,128]{2,1,0:T(8,128)(2,1)S(1)} %take_own.1.rest_0_), channel_id=1, source_target_pairs={{0,1},{1,0},{2,3},{3,2},{4,5},{5,4},{6,7},{7,6},{8,9},{9,8},{10,11... | collective-permute-start | bytes 786440 | tf_op jit(solution)/shard_map/ppermute | solution.py:518
  31.7 4.1 %collective-permute-start.8 = (bf16[8,128,128]{2,1,0:T(8,128)(2,1)S(1)}, bf16[8,128,128]{2,1,0:T(8,128)(2,1)S(1)}, u32[]{:S(2)}, u32[]{:S(2)}) collective-permute-start(bf16[8,128,128]{2,1,0:T(8,128)(2,1)S(1)} %collective-permute-done.4.rest_2_), channel_id=1, source_target_pairs={{0,1},{1,0},{2,3},{3,2},{4,5},{5,4},{6,7},{7,6},{8,9},{9,8},{10,11... | collective-permute-start | bytes 786440 | tf_op jit(solution)/shard_map/ppermute | solution.py:518
  34.2 1.5 %collective-permute-start.7 = (bf16[8,128,128]{2,1,0:T(8,128)(2,1)S(1)}, bf16[8,128,128]{2,1,0:T(8,128)(2,1)S(1)}, u32[]{:S(2)}, u32[]{:S(2)}) collective-permute-start(bf16[8,128,128]{2,1,0:T(8,128)(2,1)S(1)} %collective-permute-done.3.rest_1_), channel_id=1, source_target_pairs={{0,1},{1,0},{2,3},{3,2},{4,5},{5,4},{6,7},{7,6},{8,9},{9,8},{10,11... | collective-permute-start | bytes 786440 | tf_op jit(solution)/shard_map/ppermute | solution.py:518
  34.4 1.7 %collective-permute-start.9 = (bf16[8,128,128]{2,1,0:T(8,128)(2,1)S(1)}, bf16[8,128,128]{2,1,0:T(8,128)(2,1)S(1)}, u32[]{:S(2)}, u32[]{:S(2)}) collective-permute-start(bf16[8,128,128]{2,1,0:T(8,128)(2,1)S(1)} %collective-permute-done.5.rest_3_), channel_id=1, source_target_pairs={{0,1},{1,0},{2,3},{3,2},{4,5},{5,4},{6,7},{7,6},{8,9},{9,8},{10,11... | collective-permute-start | bytes 786440 | tf_op jit(solution)/shard_map/ppermute | solution.py:518
  39.7 18.9 %collective-permute-start.10 = (s32[5,17,8,128]{3,2,1,0:T(8,128)}, s32[5,17,8,128]{3,2,1,0:T(8,128)S(1)}, u32[]{:S(2)}, u32[]{:S(2)}) collective-permute-start(s32[5,17,8,128]{3,2,1,0:T(8,128)} %get-tuple-element.39), channel_id=1, source_target_pairs={{0,8},{8,0},{16,24},{24,16},{1,9},{9,1},{17,25},{25,17},{2,10},{10... | collective-permute-start | bytes 1044488 | tf_op jit(solution)/shard_map/ppermute | solution.py:588
  41.2 17.7 %collective-permute-start.11 = (s32[5,17,8,128]{3,2,1,0:T(8,128)}, s32[5,17,8,128]{3,2,1,0:T(8,128)S(1)}, u32[]{:S(2)}, u32[]{:S(2)}) collective-permute-start(s32[5,17,8,128]{3,2,1,0:T(8,128)} %get-tuple-element.40), channel_id=1, source_target_pairs={{0,16},{8,24},{16,0},{24,8},{1,17},{9,25},{17,1},{25,9},{2,18},{10... | collective-permute-start | bytes 1044488 | tf_op jit(solution)/shard_map/ppermute | solution.py:588
  42.1 16.9 %collective-permute-start.12 = (s32[5,17,8,128]{3,2,1,0:T(8,128)S(1)}, s32[5,17,8,128]{3,2,1,0:T(8,128)S(1)}, u32[]{:S(2)}, u32[]{:S(2)}) collective-permute-start(s32[5,17,8,128]{3,2,1,0:T(8,128)S(1)} %get-tuple-element.41), channel_id=1, source_target_pairs={{0,24},{8,16},{16,8},{24,0},{1,25},{9,17},{17,9},{25,1},{2,26},{10... | collective-permute-start | bytes 1044488 | tf_op jit(solution)/shard_map/ppermute | solution.py:588
  43.3 15.7 %copy-start.2 = (bf16[256,768]{1,0:T(8,128)(2,1)S(1)}, bf16[256,768]{1,0:T(8,128)(2,1)}, u32[]{:S(2)}) copy-start(bf16[256,768]{1,0:T(8,128)(2,1)} %constant.135.clone.rest_8_.rows_inverse) | copy-start | bytes 1179652
  43.3 15.7 %copy-start.3 = (f32[2,128,128]{2,1,0:T(8,128)S(1)}, f32[2,128,128]{2,1,0:T(8,128)}, u32[]{:S(2)}) copy-start(f32[2,128,128]{2,1,0:T(8,128)} %constant.139.clone.rest_12_.offset_ref) | copy-start | bytes 393220
  43.3 15.7 %copy-start.5 = (bf16[256,768]{1,0:T(8,128)(2,1)S(1)}, bf16[256,768]{1,0:T(8,128)(2,1)}, u32[]{:S(2)}) copy-start(bf16[256,768]{1,0:T(8,128)(2,1)} %constant.134.clone.rest_7_) | copy-start | bytes 1179652
  43.3 15.7 %copy-start.6 = (bf16[768,256]{1,0:T(8,128)(2,1)S(1)}, bf16[768,256]{1,0:T(8,128)(2,1)}, u32[]{:S(2)}) copy-start(bf16[768,256]{1,0:T(8,128)(2,1)} %constant.136.clone.rest_9_) | copy-start | bytes 1179652
  43.3 15.7 %copy-start.7 = (bf16[768,256]{1,0:T(8,128)(2,1)S(1)}, bf16[768,256]{1,0:T(8,128)(2,1)}, u32[]{:S(2)}) copy-start(bf16[768,256]{1,0:T(8,128)(2,1)} %constant.137.clone.rest_10_) | copy-start | bytes 1179652
  43.4 15.7 %copy-start.8 = (f32[2,16,128]{2,1,0:T(8,128)S(1)}, f32[2,16,128]{2,1,0:T(8,128)}, u32[]{:S(2)}) copy-start(f32[2,16,128]{2,1,0:T(8,128)} %constant.138.clone.rest_11_) | copy-start | bytes 49156
  84.6 16.1 %collective-permute-start.15 = (s32[1032,128]{1,0:T(8,128)S(1)}, s32[1032,128]{1,0:T(8,128)}, u32[]{:S(2)}, u32[]{:S(2)}) collective-permute-start(s32[1032,128]{1,0:T(8,128)S(1)} %finish.4.rest_0_), channel_id=1, source_target_pairs={{0,24},{8,16},{16,8},{24,0},{1,25},{9,17},{17,9},{25,1},{2,26},{10... | collective-permute-start | bytes 1585160 | tf_op jit(solution)/shard_map/ppermute | solution.py:652
  87.9 22.2 %collective-permute-start.14 = (s32[1032,128]{1,0:T(8,128)S(1)}, s32[1032,128]{1,0:T(8,128)S(1)}, u32[]{:S(2)}, u32[]{:S(2)}) collective-permute-start(s32[1032,128]{1,0:T(8,128)S(1)} %finish.5.rest_0_), channel_id=1, source_target_pairs={{0,16},{8,24},{16,0},{24,8},{1,17},{9,25},{17,1},{25,9},{2,18},{10... | collective-permute-start | bytes 1585160 | tf_op jit(solution)/shard_map/ppermute | solution.py:652
  90.8 20.4 %collective-permute-start.13 = (s32[1032,128]{1,0:T(8,128)S(1)}, s32[1032,128]{1,0:T(8,128)S(1)}, u32[]{:S(2)}, u32[]{:S(2)}) collective-permute-start(s32[1032,128]{1,0:T(8,128)S(1)} %finish.6.rest_0_), channel_id=1, source_target_pairs={{0,8},{8,0},{16,24},{24,16},{1,9},{9,1},{17,25},{25,17},{2,10},{10... | collective-permute-start | bytes 1585160 | tf_op jit(solution)/shard_map/ppermute | solution.py:652
  (4 other events, 10.2 us)

commit v13 on v12

--- a/solution.py
+++ b/solution.py
@@ -19,9 +19,9 @@
 STEP_LOG = 64.0
 TOP = 32767.0
 GROUP = 8
-COLUMNS = 4
+COLUMNS = 8
 ROWS = 8
-CHUNKS = 8
+CHUNKS = 16
 UNROLL = 1
 VMEM = 28 * 1024 * 1024
 SMALL = 10 * 1024 * 1024

time: 113 us -> 111 us (0.982)
  Pallas kernels: 55.7 us -> 54.5 us
    pallas_call x1, Pallas kernels: 23.9 us -> 22.6 us  [local(): pl.pallas_call(functools.partial(march_kernel, sources=fl), in_specs=[sme...]
where the time goes in v13:
time: 111 us
  Pallas kernels  54.5 us (49%)
  starting transfers between devices  23.2 us (21%)
  waiting for transfers between devices  21.5 us (19%)
  local copies, waits for them, and re-layouts  7.74 us (7%)
  other arithmetic  3.68 us (3%)
    pallas_call x1, Pallas kernels, local(): pl.pallas_call(functools.partial(march_kernel, sources=fl), in_specs=[sme...  22.6 us
    pallas_call x1, Pallas kernels, local(): pl.pallas_call(propagator_kernel, in_specs=[smem, smem, vmem], out_specs=...  15.2 us
    ppermute x3, waiting for transfers between devices, local(): lax.ppermute(block, 'mid', [(s, s ^ ahead) for s in range(mid_count)])  11.3 us
    ppermute x3, starting transfers between devices, local(): lax.ppermute(shares[away ^ low], 'off', [(i, (i // cores ^ low) * cores +...  8.49 us
    pallas_call x4, Pallas kernels, finish(): pl.pallas_call(finish_kernel, grid_spec=pltpu.PrefetchScalarGridSpec(num_...  6.83 us
    pallas_call x4, Pallas kernels, local(): pl.pallas_call(result_kernel, grid_spec=pltpu.PrefetchScalarGridSpec(num_...  5.19 us
    ppermute x3, waiting for transfers between devices, local(): lax.ppermute(data, 'mid', [(i, i ^ away) for i in range(mid_count)])  4.36 us
    unnamed x22, local copies, waits for them, and re-layouts  4.11 us
  transfers between devices with their start and end apart: 17, of which 10 were waited for; matrix products, arithmetic and copies ran while one was open for 7% of the time, Pallas kernels for 22%

profile of v13, /device:TPU:0, one launch (start us, length us, event | category | flops | bytes accessed | tf_op | source)
XLA Modules:
  0.0 111.0 jit_solution(1350662328743703680)
XLA Ops:
  0.0 1.2 %copy-done.4 = bf16[2,16,128,128]{3,2,1,0:T(8,128)(2,1)S(1)} copy-done((bf16[2,16,128,128]{3,2,1,0:T(8,128)(2,1)S(1)}, bf16[2,16,128,128]{3,2,1,0:T(8,128)(2,1)}, u32[]{:S(2)}) %copy-start.4) | copy-done | bytes 1048600
  2.9 3.1 %collective-permute-start.3 = (bf16[8,128,128]{2,1,0:T(8,128)(2,1)S(1)}, bf16[8,128,128]{2,1,0:T(8,128)(2,1)S(1)}, u32[]{:S(2)}, u32[]{:S(2)}) collective-permute-start(bf16[8,128,128]{2,1,0:T(8,128)(2,1)S(1)} %take_own.1.rest_0_), channel_id=1, source_target_pairs={{0,2},{1,3},{2,0},{3,1},{4,6},{5,7},{6,4},{7,5},{8,10},{9,11},{10,... | collective-permute-start | bytes 786440 | tf_op jit(solution)/shard_map/ppermute | solution.py:511
  6.0 2.6 %collective-permute-start.4 = (bf16[8,128,128]{2,1,0:T(8,128)(2,1)S(1)}, bf16[8,128,128]{2,1,0:T(8,128)(2,1)S(1)}, u32[]{:S(2)}, u32[]{:S(2)}) collective-permute-start(bf16[8,128,128]{2,1,0:T(8,128)(2,1)S(1)} %take_own.1.rest_0_), channel_id=1, source_target_pairs={{0,4},{1,5},{2,6},{3,7},{4,0},{5,1},{6,2},{7,3},{8,12},{9,13},{10,... | collective-permute-start | bytes 786440 | tf_op jit(solution)/shard_map/ppermute | solution.py:511
  12.4 3.4 %all-to-all-start = ((bf16[3,8,8,512]{3,2,0,1:T(8,128)(2,1)}), bf16[3,8,8,512]{3,2,0,1:T(8,128)(2,1)S(1)}, u32[]{:S(2)}, u32[]{:S(2)}) async-start(bf16[3,8,8,512]{3,2,0,1:T(8,128)(2,1)} %copy.46), calls=%async_computation | async-start | bytes 393216 | tf_op jit(solution)/shard_map/all_to_all | solution.py:530
  17.0 3.4 %collective-permute-done.4.rest_2_ = bf16[8,128,128]{2,1,0:T(8,128)(2,1)S(1)} collective-permute-done((bf16[8,128,128]{2,1,0:T(8,128)(2,1)S(1)}, bf16[8,128,128]{2,1,0:T(8,128)(2,1)S(1)}, u32[]{:S(2)}, u32[]{:S(2)}) %collective-permute-start.4) | collective-permute-done | bytes 262176 | tf_op jit(solution)/shard_map/ppermute | solution.py:511
  20.4 2.8 %collective-permute-start.5 = (bf16[8,128,128]{2,1,0:T(8,128)(2,1)S(1)}, bf16[8,128,128]{2,1,0:T(8,128)(2,1)S(1)}, u32[]{:S(2)}, u32[]{:S(2)}) collective-permute-start(bf16[8,128,128]{2,1,0:T(8,128)(2,1)S(1)} %collective-permute-done.4.rest_2_), channel_id=1, source_target_pairs={{0,2},{1,3},{2,0},{3,1},{4,6},{5,7},{6,4},{7,5},{8,10},{9,11},{10,... | collective-permute-start | bytes 786440 | tf_op jit(solution)/shard_map/ppermute | solution.py:511
  23.2 1.4 %all-to-all-done = bf16[3,8,8,512]{3,2,0,1:T(8,128)(2,1)S(1)} async-done(((bf16[3,8,8,512]{3,2,0,1:T(8,128)(2,1)}), bf16[3,8,8,512]{3,2,0,1:T(8,128)(2,1)S(1)}, u32[]{:S(2)}, u32[]{:S(2)}) %all-to-all-start) | async-done | bytes 196640 | tf_op jit(solution)/shard_map/all_to_all | solution.py:530
  24.6 2.5 %collective-permute-start.2 = (bf16[17,8,512]{2,1,0:T(8,128)(2,1)S(1)}, bf16[17,8,512]{2,1,0:T(8,128)(2,1)S(1)}, u32[]{:S(2)}, u32[]{:S(2)}) collective-permute-start(bf16[17,8,512]{2,1,0:T(8,128)(2,1)S(1)} %get-tuple-element.48), channel_id=1, source_target_pairs={{0,24},{8,16},{16,8},{24,0},{1,25},{9,17},{17,9},{25,1},{2,26},{10... | collective-permute-start | bytes 417800 | tf_op jit(solution)/shard_map/ppermute | solution.py:538
  29.9 1.8 %collective-permute-done.2 = bf16[17,8,512]{2,1,0:T(8,128)(2,1)S(1)} collective-permute-done((bf16[17,8,512]{2,1,0:T(8,128)(2,1)S(1)}, bf16[17,8,512]{2,1,0:T(8,128)(2,1)S(1)}, u32[]{:S(2)}, u32[]{:S(2)}) %collective-permute-start.2) | collective-permute-done | bytes 139296 | tf_op jit(solution)/shard_map/ppermute | solution.py:538
  31.7 2.5 %collective-permute-done.1 = bf16[17,8,512]{2,1,0:T(8,128)(2,1)S(1)} collective-permute-done((bf16[17,8,512]{2,1,0:T(8,128)(2,1)S(1)}, bf16[17,8,512]{2,1,0:T(8,128)(2,1)S(1)}, u32[]{:S(2)}, u32[]{:S(2)}) %collective-permute-start.1) | collective-permute-done | bytes 139296 | tf_op jit(solution)/shard_map/ppermute | solution.py:538
  36.1 3.6 %contributions.1 = (s32[5,17,8,128]{3,2,1,0:T(8,128)S(1)}, s32[5,17,8,128]{3,2,1,0:T(8,128)}, s32[5,17,8,128]{3,2,1,0:T(8,128)}, s32[5,17,8,128]{3,2,1,0:T(8,128)S(1)}) custom-call(s32[1]{0:T(128)} %bitcast.2.mine_ref.place_ref.freq_ref, s32[16]{0:T(128)S(1)} %add.116.order_ref, s32[40]{0:T(128)S(1)} %get-tuple-element.27.slot_ref, ...), custom_call_target="tpu_custom_call" | custom-call | tf_op jit(solution)/shard_map/contributions/pallas_call | solution.py:572
  39.7 1.6 %collective-permute-start.10 = (s32[5,17,8,128]{3,2,1,0:T(8,128)}, s32[5,17,8,128]{3,2,1,0:T(8,128)S(1)}, u32[]{:S(2)}, u32[]{:S(2)}) collective-permute-start(s32[5,17,8,128]{3,2,1,0:T(8,128)} %get-tuple-element.39), channel_id=1, source_target_pairs={{0,8},{8,0},{16,24},{24,16},{1,9},{9,1},{17,25},{25,17},{2,10},{10... | collective-permute-start | bytes 1044488 | tf_op jit(solution)/shard_map/ppermute | solution.py:588
  42.1 1.2 %collective-permute-start.12 = (s32[5,17,8,128]{3,2,1,0:T(8,128)S(1)}, s32[5,17,8,128]{3,2,1,0:T(8,128)S(1)}, u32[]{:S(2)}, u32[]{:S(2)}) collective-permute-start(s32[5,17,8,128]{3,2,1,0:T(8,128)S(1)} %get-tuple-element.41), channel_id=1, source_target_pairs={{0,24},{8,16},{16,8},{24,0},{1,25},{9,17},{17,9},{25,1},{2,26},{10... | collective-permute-start | bytes 1044488 | tf_op jit(solution)/shard_map/ppermute | solution.py:588
  43.4 15.2 %propagator.1 = (f32[256,2048]{1,0:T(8,128)S(1)}, f32[256,2048]{1,0:T(8,128)S(1)}, f32[2,2,8,16]{3,2,1,0:T(8,128)S(1)}) custom-call(f32[1]{0:T(128)} %bitcast.25.omega_ref, f32[2,16]{1,0:T(2,128)S(1)} %copy-done.10, s32[2,8,16]{2,1,0:T(8,128)S(1)} %copy.50.layers_ref), custom_call_target="tpu_custom_call" | custom-call | flops 31457280 | bytes 4194304 | tf_op jit(solution)/shard_map/propagator/pallas_call | solution.py:592
  59.0 22.6 %march.1.plane_ref = f32[2,2,128,2048]{3,2,1,0:T(8,128)S(1)} custom-call(f32[2,2,8,16]{3,2,1,0:T(8,128)S(1)} %get-tuple-element.37.layer_ref, s32[5,17,8,128]{3,2,1,0:T(8,128)S(1)} %get-tuple-element.38.rest_0_, s32[5,17,8,128]{3,2,1,0:T(8,128)S(1)} %collective-permute-done.10.rest_1_, s32[5,17,8,128]{3,2,1,0:T(8,128)S(1)} %collective-permute-done.11.rest_2_, ...), custom_call_target="tpu_custom_call" | custom-call | tf_op jit(solution)/shard_map/march/pallas_call | solution.py:610
  81.7 1.7 %finish.4.rest_0_ = s32[1032,128]{1,0:T(8,128)S(1)} custom-call(s32[1]{0:T(128)} %bitcast.27.dest_ref, f32[2,2,8,16]{3,2,1,0:T(8,128)S(1)} %get-tuple-element.37.layer_ref, f32[2,2,128,2048]{3,2,1,0:T(8,128)S(1)} %march.1.plane_ref, bf16[256,768]{1,0:T(8,128)(2,1)S(1)} %copy-done.2, f32[2,128,128]{2,1,0:T(8,128)S(1)} %copy-done.3), custom_call_target="tpu_custom_call" | custom-call | flops 402653184 | bytes 786432 | tf_op jit(solution)/shard_map/finish/pallas_call | solution.py:624
  83.4 1.6 %collective-permute-start.15 = (s32[1032,128]{1,0:T(8,128)S(1)}, s32[1032,128]{1,0:T(8,128)}, u32[]{:S(2)}, u32[]{:S(2)}) collective-permute-start(s32[1032,128]{1,0:T(8,128)S(1)} %finish.4.rest_0_), channel_id=1, source_target_pairs={{0,24},{8,16},{16,8},{24,0},{1,25},{9,17},{17,9},{25,1},{2,26},{10... | collective-permute-start | bytes 1585160 | tf_op jit(solution)/shard_map/ppermute | solution.py:652
  85.0 1.7 %finish.5.rest_0_ = s32[1032,128]{1,0:T(8,128)S(1)} custom-call(s32[1]{0:T(128)} %bitcast.26.dest_ref, f32[2,2,8,16]{3,2,1,0:T(8,128)S(1)} %get-tuple-element.37.layer_ref, f32[2,2,128,2048]{3,2,1,0:T(8,128)S(1)} %march.1.plane_ref, bf16[256,768]{1,0:T(8,128)(2,1)S(1)} %copy-done.2, f32[2,128,128]{2,1,0:T(8,128)S(1)} %copy-done.3, s32[1032,128]{1,0:T(8,128)S(1)} %finish.4.rest_0_), custom_call_target="tpu_custom_call" | custom-call | flops 402653184 | bytes 786432 | tf_op jit(solution)/shard_map/finish/pallas_call | solution.py:624
  87.9 1.7 %finish.6.rest_0_ = s32[1032,128]{1,0:T(8,128)S(1)} custom-call(s32[1]{0:T(128)} %bitcast.1.dest_ref, f32[2,2,8,16]{3,2,1,0:T(8,128)S(1)} %get-tuple-element.37.layer_ref, f32[2,2,128,2048]{3,2,1,0:T(8,128)S(1)} %march.1.plane_ref, bf16[256,768]{1,0:T(8,128)(2,1)S(1)} %copy-done.2, f32[2,128,128]{2,1,0:T(8,128)S(1)} %copy-done.3, s32[1032,128]{1,0:T(8,128)S(1)} %finish.5.rest_0_), custom_call_target="tpu_custom_call" | custom-call | flops 402653184 | bytes 786432 | tf_op jit(solution)/shard_map/finish/pallas_call | solution.py:624
  90.5 2.2 %copy-done.1 = f32[2,2,128,2048]{3,2,1,0:T(8,128)S(1)} copy-done((f32[2,2,128,2048]{3,2,1,0:T(8,128)S(1)}, f32[2,2,128,2048]{3,2,1,0:T(8,128)}, u32[]{:S(2)}) %copy-start.1) | copy-done | bytes 4194328
  92.7 1.7 %finish.7.code_ref = s32[1032,128]{1,0:T(8,128)S(1)} custom-call(s32[1]{0:T(128)} %bitcast.30.dest_ref, f32[2,2,8,16]{3,2,1,0:T(8,128)S(1)} %get-tuple-element.37.layer_ref, f32[2,2,128,2048]{3,2,1,0:T(8,128)S(1)} %copy-done.1, bf16[256,768]{1,0:T(8,128)(2,1)S(1)} %copy-done.2, f32[2,128,128]{2,1,0:T(8,128)S(1)} %copy-done.3, s32[1032,128]{1,0:T(8,128)S(1)} %finish.6.rest_0_), custom_call_target="tpu_custom_call" | custom-call | flops 402653184 | bytes 786432 | tf_op jit(solution)/shard_map/finish/pallas_call | solution.py:624
  95.5 4.0 %collective-permute-done.15.code_ref = s32[1032,128]{1,0:T(8,128)} collective-permute-done((s32[1032,128]{1,0:T(8,128)S(1)}, s32[1032,128]{1,0:T(8,128)}, u32[]{:S(2)}, u32[]{:S(2)}) %collective-permute-start.15) | collective-permute-done | bytes 528416 | tf_op jit(solution)/shard_map/ppermute | solution.py:652
  99.5 2.1 %result.5.rest_0_ = f32[4,256,8,128]{3,2,1,0:T(8,128)} custom-call(s32[1]{0:T(128)} %bitcast.29.freq_ref, s32[1032,128]{1,0:T(8,128)} %collective-permute-done.15.code_ref, f32[4,256,8,128]{3,2,1,0:T(8,128)} %result.4.rest_0_), custom_call_target="tpu_custom_call", output_to_operand_aliasing={{}: (2, {})} | custom-call | flops 524288 | bytes 1572864 | tf_op jit(solution)/shard_map/result/pallas_call | solution.py:659
  101.6 7.3 %collective-permute-done.14.code_ref = s32[1032,128]{1,0:T(8,128)S(1)} collective-permute-done((s32[1032,128]{1,0:T(8,128)S(1)}, s32[1032,128]{1,0:T(8,128)S(1)}, u32[]{:S(2)}, u32[]{:S(2)}) %collective-permute-start.14) | collective-permute-done | bytes 528416 | tf_op jit(solution)/shard_map/ppermute | solution.py:652
  (98 shorter events, 17.8 us)
Async XLA Ops:
  2.9 26.9 %collective-permute-start.3 = (bf16[8,128,128]{2,1,0:T(8,128)(2,1)S(1)}, bf16[8,128,128]{2,1,0:T(8,128)(2,1)S(1)}, u32[]{:S(2)}, u32[]{:S(2)}) collective-permute-start(bf16[8,128,128]{2,1,0:T(8,128)(2,1)S(1)} %take_own.1.rest_0_), channel_id=1, source_target_pairs={{0,2},{1,3},{2,0},{3,1},{4,6},{5,7},{6,4},{7,5},{8,10},{9,11},{10,... | collective-permute-start | bytes 786440 | tf_op jit(solution)/shard_map/ppermute | solution.py:511
  6.0 14.4 %collective-permute-start.4 = (bf16[8,128,128]{2,1,0:T(8,128)(2,1)S(1)}, bf16[8,128,128]{2,1,0:T(8,128)(2,1)S(1)}, u32[]{:S(2)}, u32[]{:S(2)}) collective-permute-start(bf16[8,128,128]{2,1,0:T(8,128)(2,1)S(1)} %take_own.1.rest_0_), channel_id=1, source_target_pairs={{0,4},{1,5},{2,6},{3,7},{4,0},{5,1},{6,2},{7,3},{8,12},{9,13},{10,... | collective-permute-start | bytes 786440 | tf_op jit(solution)/shard_map/ppermute | solution.py:511
  11.6 31.7 %copy-start.10 = (f32[2,16]{1,0:T(2,128)S(1)}, f32[2,16]{1,0:T(2,128)}, u32[]{:S(2)}) copy-start(f32[2,16]{1,0:T(2,128)} %slow_ref.1) | copy-start | bytes 388
  12.4 12.2 %all-to-all-start = ((bf16[3,8,8,512]{3,2,0,1:T(8,128)(2,1)}), bf16[3,8,8,512]{3,2,0,1:T(8,128)(2,1)S(1)}, u32[]{:S(2)}, u32[]{:S(2)}) async-start(bf16[3,8,8,512]{3,2,0,1:T(8,128)(2,1)} %copy.46), calls=%async_computation | async-start | bytes 393216 | tf_op jit(solution)/shard_map/all_to_all | solution.py:530
  20.4 14.0 %collective-permute-start.5 = (bf16[8,128,128]{2,1,0:T(8,128)(2,1)S(1)}, bf16[8,128,128]{2,1,0:T(8,128)(2,1)S(1)}, u32[]{:S(2)}, u32[]{:S(2)}) collective-permute-start(bf16[8,128,128]{2,1,0:T(8,128)(2,1)S(1)} %collective-permute-done.4.rest_2_), channel_id=1, source_target_pairs={{0,2},{1,3},{2,0},{3,1},{4,6},{5,7},{6,4},{7,5},{8,10},{9,11},{10,... | collective-permute-start | bytes 786440 | tf_op jit(solution)/shard_map/ppermute | solution.py:511
  24.6 7.1 %collective-permute-start.2 = (bf16[17,8,512]{2,1,0:T(8,128)(2,1)S(1)}, bf16[17,8,512]{2,1,0:T(8,128)(2,1)S(1)}, u32[]{:S(2)}, u32[]{:S(2)}) collective-permute-start(bf16[17,8,512]{2,1,0:T(8,128)(2,1)S(1)} %get-tuple-element.48), channel_id=1, source_target_pairs={{0,24},{8,16},{16,8},{24,0},{1,25},{9,17},{17,9},{25,1},{2,26},{10... | collective-permute-start | bytes 417800 | tf_op jit(solution)/shard_map/ppermute | solution.py:538
  27.1 7.1 %collective-permute-start.1 = (bf16[17,8,512]{2,1,0:T(8,128)(2,1)S(1)}, bf16[17,8,512]{2,1,0:T(8,128)(2,1)S(1)}, u32[]{:S(2)}, u32[]{:S(2)}) collective-permute-start(bf16[17,8,512]{2,1,0:T(8,128)(2,1)S(1)} %get-tuple-element.48), channel_id=1, source_target_pairs={{0,16},{8,24},{16,0},{24,8},{1,17},{9,25},{17,1},{25,9},{2,18},{10... | collective-permute-start | bytes 417800 | tf_op jit(solution)/shard_map/ppermute | solution.py:538
  27.6 6.6 %collective-permute-start = (bf16[17,8,512]{2,1,0:T(8,128)(2,1)S(1)}, bf16[17,8,512]{2,1,0:T(8,128)(2,1)S(1)}, u32[]{:S(2)}, u32[]{:S(2)}) collective-permute-start(bf16[17,8,512]{2,1,0:T(8,128)(2,1)S(1)} %get-tuple-element.48), channel_id=1, source_target_pairs={{0,8},{8,0},{16,24},{24,16},{1,9},{9,1},{17,25},{25,17},{2,10},{10... | collective-permute-start | bytes 417800 | tf_op jit(solution)/shard_map/ppermute | solution.py:538
  29.8 5.7 %collective-permute-start.6 = (bf16[8,128,128]{2,1,0:T(8,128)(2,1)S(1)}, bf16[8,128,128]{2,1,0:T(8,128)(2,1)S(1)}, u32[]{:S(2)}, u32[]{:S(2)}) collective-permute-start(bf16[8,128,128]{2,1,0:T(8,128)(2,1)S(1)} %take_own.1.rest_0_), channel_id=1, source_target_pairs={{0,1},{1,0},{2,3},{3,2},{4,5},{5,4},{6,7},{7,6},{8,9},{9,8},{10,11... | collective-permute-start | bytes 786440 | tf_op jit(solution)/shard_map/ppermute | solution.py:518
  31.7 4.1 %collective-permute-start.8 = (bf16[8,128,128]{2,1,0:T(8,128)(2,1)S(1)}, bf16[8,128,128]{2,1,0:T(8,128)(2,1)S(1)}, u32[]{:S(2)}, u32[]{:S(2)}) collective-permute-start(bf16[8,128,128]{2,1,0:T(8,128)(2,1)S(1)} %collective-permute-done.4.rest_2_), channel_id=1, source_target_pairs={{0,1},{1,0},{2,3},{3,2},{4,5},{5,4},{6,7},{7,6},{8,9},{9,8},{10,11... | collective-permute-start | bytes 786440 | tf_op jit(solution)/shard_map/ppermute | solution.py:518
  34.2 1.5 %collective-permute-start.7 = (bf16[8,128,128]{2,1,0:T(8,128)(2,1)S(1)}, bf16[8,128,128]{2,1,0:T(8,128)(2,1)S(1)}, u32[]{:S(2)}, u32[]{:S(2)}) collective-permute-start(bf16[8,128,128]{2,1,0:T(8,128)(2,1)S(1)} %collective-permute-done.3.rest_1_), channel_id=1, source_target_pairs={{0,1},{1,0},{2,3},{3,2},{4,5},{5,4},{6,7},{7,6},{8,9},{9,8},{10,11... | collective-permute-start | bytes 786440 | tf_op jit(solution)/shard_map/ppermute | solution.py:518
  34.4 1.7 %collective-permute-start.9 = (bf16[8,128,128]{2,1,0:T(8,128)(2,1)S(1)}, bf16[8,128,128]{2,1,0:T(8,128)(2,1)S(1)}, u32[]{:S(2)}, u32[]{:S(2)}) collective-permute-start(bf16[8,128,128]{2,1,0:T(8,128)(2,1)S(1)} %collective-permute-done.5.rest_3_), channel_id=1, source_target_pairs={{0,1},{1,0},{2,3},{3,2},{4,5},{5,4},{6,7},{7,6},{8,9},{9,8},{10,11... | collective-permute-start | bytes 786440 | tf_op jit(solution)/shard_map/ppermute | solution.py:518
  39.7 18.9 %collective-permute-start.10 = (s32[5,17,8,128]{3,2,1,0:T(8,128)}, s32[5,17,8,128]{3,2,1,0:T(8,128)S(1)}, u32[]{:S(2)}, u32[]{:S(2)}) collective-permute-start(s32[5,17,8,128]{3,2,1,0:T(8,128)} %get-tuple-element.39), channel_id=1, source_target_pairs={{0,8},{8,0},{16,24},{24,16},{1,9},{9,1},{17,25},{25,17},{2,10},{10... | collective-permute-start | bytes 1044488 | tf_op jit(solution)/shard_map/ppermute | solution.py:588
  41.2 17.7 %collective-permute-start.11 = (s32[5,17,8,128]{3,2,1,0:T(8,128)}, s32[5,17,8,128]{3,2,1,0:T(8,128)S(1)}, u32[]{:S(2)}, u32[]{:S(2)}) collective-permute-start(s32[5,17,8,128]{3,2,1,0:T(8,128)} %get-tuple-element.40), channel_id=1, source_target_pairs={{0,16},{8,24},{16,0},{24,8},{1,17},{9,25},{17,1},{25,9},{2,18},{10... | collective-permute-start | bytes 1044488 | tf_op jit(solution)/shard_map/ppermute | solution.py:588
  42.1 16.9 %collective-permute-start.12 = (s32[5,17,8,128]{3,2,1,0:T(8,128)S(1)}, s32[5,17,8,128]{3,2,1,0:T(8,128)S(1)}, u32[]{:S(2)}, u32[]{:S(2)}) collective-permute-start(s32[5,17,8,128]{3,2,1,0:T(8,128)S(1)} %get-tuple-element.41), channel_id=1, source_target_pairs={{0,24},{8,16},{16,8},{24,0},{1,25},{9,17},{17,9},{25,1},{2,26},{10... | collective-permute-start | bytes 1044488 | tf_op jit(solution)/shard_map/ppermute | solution.py:588
  43.3 15.7 %copy-start.2 = (bf16[256,768]{1,0:T(8,128)(2,1)S(1)}, bf16[256,768]{1,0:T(8,128)(2,1)}, u32[]{:S(2)}) copy-start(bf16[256,768]{1,0:T(8,128)(2,1)} %constant.135.clone.rest_8_.rows_inverse) | copy-start | bytes 1179652
  43.3 15.7 %copy-start.3 = (f32[2,128,128]{2,1,0:T(8,128)S(1)}, f32[2,128,128]{2,1,0:T(8,128)}, u32[]{:S(2)}) copy-start(f32[2,128,128]{2,1,0:T(8,128)} %constant.139.clone.rest_12_.offset_ref) | copy-start | bytes 393220
  43.3 15.7 %copy-start.5 = (bf16[256,768]{1,0:T(8,128)(2,1)S(1)}, bf16[256,768]{1,0:T(8,128)(2,1)}, u32[]{:S(2)}) copy-start(bf16[256,768]{1,0:T(8,128)(2,1)} %constant.134.clone.rest_7_) | copy-start | bytes 1179652
  43.3 15.7 %copy-start.6 = (bf16[768,256]{1,0:T(8,128)(2,1)S(1)}, bf16[768,256]{1,0:T(8,128)(2,1)}, u32[]{:S(2)}) copy-start(bf16[768,256]{1,0:T(8,128)(2,1)} %constant.136.clone.rest_9_) | copy-start | bytes 1179652
  43.3 15.7 %copy-start.7 = (bf16[768,256]{1,0:T(8,128)(2,1)S(1)}, bf16[768,256]{1,0:T(8,128)(2,1)}, u32[]{:S(2)}) copy-start(bf16[768,256]{1,0:T(8,128)(2,1)} %constant.137.clone.rest_10_) | copy-start | bytes 1179652
  43.4 15.7 %copy-start.8 = (f32[2,16,128]{2,1,0:T(8,128)S(1)}, f32[2,16,128]{2,1,0:T(8,128)}, u32[]{:S(2)}) copy-start(f32[2,16,128]{2,1,0:T(8,128)} %constant.138.clone.rest_11_) | copy-start | bytes 49156
  83.4 16.1 %collective-permute-start.15 = (s32[1032,128]{1,0:T(8,128)S(1)}, s32[1032,128]{1,0:T(8,128)}, u32[]{:S(2)}, u32[]{:S(2)}) collective-permute-start(s32[1032,128]{1,0:T(8,128)S(1)} %finish.4.rest_0_), channel_id=1, source_target_pairs={{0,24},{8,16},{16,8},{24,0},{1,25},{9,17},{17,9},{25,1},{2,26},{10... | collective-permute-start | bytes 1585160 | tf_op jit(solution)/shard_map/ppermute | solution.py:652
  86.7 22.2 %collective-permute-start.14 = (s32[1032,128]{1,0:T(8,128)S(1)}, s32[1032,128]{1,0:T(8,128)S(1)}, u32[]{:S(2)}, u32[]{:S(2)}) collective-permute-start(s32[1032,128]{1,0:T(8,128)S(1)} %finish.5.rest_0_), channel_id=1, source_target_pairs={{0,16},{8,24},{16,0},{24,8},{1,17},{9,25},{17,1},{25,9},{2,18},{10... | collective-permute-start | bytes 1585160 | tf_op jit(solution)/shard_map/ppermute | solution.py:652
  89.6 20.4 %collective-permute-start.13 = (s32[1032,128]{1,0:T(8,128)S(1)}, s32[1032,128]{1,0:T(8,128)S(1)}, u32[]{:S(2)}, u32[]{:S(2)}) collective-permute-start(s32[1032,128]{1,0:T(8,128)S(1)} %finish.6.rest_0_), channel_id=1, source_target_pairs={{0,8},{8,0},{16,24},{24,16},{1,9},{9,1},{17,25},{25,17},{2,10},{10... | collective-permute-start | bytes 1585160 | tf_op jit(solution)/shard_map/ppermute | solution.py:652
  (4 other events, 10.2 us)
